TPU v7x, 32 devices: a whole 2x2x4 slice. The times are simulated.
32 devices in a mesh: req: 4 (over y, x), blk: 8 (over z, core).
Axes of the slice: x: 2, y: 2, z: 4, core: 2. Of those that a mesh axis runs over, the one named last changes fastest.
Arguments:
- tokens: bfloat16 [4, 1024, 2048], P('req', 'blk'), may hold values from -6 to 6
- block_ids: int32 [4, 16], P('req', 'blk'), may hold values from 0 to 15, as said below
- lengths: int32 [4], P('req'), may hold values from 513 to 1024, as said below
- page_table: int32 [4, 2, 16], P('req'), may hold values from 0 to 31, as said below
- qkv_weight: bfloat16 [2048, 3072], P(('req', 'blk')), may hold values from -0.125 to 0.125
- q_gain: float32 [256], replicated
- k_gain: float32 [256], replicated
Outputs:
- attended: bfloat16 [4, 1024, 2048], P('req', 'blk')
- kv_cache: bfloat16 [4, 32, 64, 512], P('req', 'blk')
Inputs may be any that keep to these rules, and one draw needn't show every extreme that they name: `lengths`: one prompt has length exactly 1024. `block_ids`: the two entries of one device are b and 15 - b; over a prompt the first entries are a permutation of 0 to 7. `page_table`: each prompt's entries are a permutation of 0 to 31.
All inputs are finite; a program needn't handle non-finite values.
Results may differ from a plain program's by a relative error of at most 0.013.
The roundings to bfloat16 on the way count: a program that leaves them out, or rounds other values in their place, can miss the bound.
Values may be sent and summed in bfloat16 or wider, within the bound.
No kernel may reach another device: no remote copies, remote signals or barrier semaphores. Data moves between devices by JAX's collectives and lax.ppermute only.
A program may use at most 128 MiB of HBM per device.

v0:
```python
import math

import jax
import jax.numpy as jnp
from jax import lax
from jax.sharding import PartitionSpec as P

H = 8
KVH = 2
HD = 256


ROPE_BASE = 1000000.0
NORM_EPS = 1e-06
FLOOR_SCORE = -1e30


def head_norm(tensor, scale_gain):
    return (
        tensor
        * lax.rsqrt(jnp.mean(tensor * tensor, axis=-1, keepdims=True) + NORM_EPS)
        * scale_gain
    )


def rotary(tensor, positions):
    half_dim = tensor.shape[-1] // 2
    channel = jnp.arange(half_dim).astype(jnp.float32)
    inverse = jnp.power(jnp.float32(ROPE_BASE), -2.0 * channel / tensor.shape[-1])
    angles = positions.astype(jnp.float32)[:, None] * inverse[None, :]
    cosine = jnp.cos(angles)[:, None, :]
    sine_part = jnp.sin(angles)[:, None, :]
    front_half = tensor[..., :half_dim]
    second = tensor[..., half_dim:]
    return jnp.concatenate(
        [front_half * cosine - second * sine_part, second * cosine + front_half * sine_part], -1
    )


def body(tokens, block_ids, lengths, page_table, qkv_weight, q_gain, k_gain):
    local_rows = tokens[0]
    row_count = local_rows.shape[0]
    blk_rows = row_count // 2
    groups = H // KVH
    projected = jnp.dot(
        local_rows,
        lax.all_gather(qkv_weight, ("req", "blk"), axis=0, tiled=True),
        preferred_element_type=jnp.float32,
    )
    own_ids = block_ids[0]
    positions = (
        own_ids[:, None] * blk_rows + jnp.arange(blk_rows, dtype=jnp.int32)[None, :]
    ).reshape(row_count)
    length = lengths[0]
    query_raw = projected[:, : H * HD].reshape(row_count, H, HD)
    key_raw = projected[:, H * HD : (H + KVH) * HD].reshape(row_count, KVH, HD)
    value_raw = projected[:, (H + KVH) * HD :].reshape(row_count, KVH, HD)
    queries = (
        rotary(head_norm(query_raw, q_gain), positions)
        .astype(jnp.bfloat16)
        .reshape(row_count, KVH, groups, HD)
    )
    send_keys = (
        rotary(head_norm(key_raw, k_gain), positions)
        .astype(jnp.bfloat16)
        .reshape(row_count, KVH * HD)
    )
    send_values = head_norm(value_raw, 1.0).astype(jnp.bfloat16).reshape(row_count, KVH * HD)
    all_ids = lax.all_gather(block_ids, "blk", axis=1, tiled=True)[0]
    table_size = all_ids.shape[0]
    slot_count = page_table.shape[1] * page_table.shape[2] // lax.axis_size("blk")
    my_slots = lax.axis_index("blk") * slot_count + jnp.arange(slot_count, dtype=jnp.int32)
    slot_match = page_table[0][None, :, :] == my_slots[:, None, None]
    head_grid = jnp.arange(page_table.shape[1], dtype=jnp.int32)[None, :, None]
    block_grid = jnp.arange(page_table.shape[2], dtype=jnp.int32)[None, None, :]
    slot_head = jnp.sum(jnp.where(slot_match, head_grid, 0), axis=(1, 2))
    slot_block = jnp.sum(jnp.where(slot_match, block_grid, 0), axis=(1, 2))
    query_live = positions < length
    running_max = jnp.full((row_count, KVH, groups), FLOOR_SCORE, jnp.float32)
    running_sum = jnp.zeros((row_count, KVH, groups), jnp.float32)
    weighted = jnp.zeros((row_count, KVH, groups, HD), jnp.float32)
    pages_out = jnp.zeros((slot_count, blk_rows, 2 * HD), jnp.bfloat16)
    piece_keys = lax.all_gather(send_keys, "blk", axis=0, tiled=True)
    piece_values = lax.all_gather(send_values, "blk", axis=0, tiled=True)
    piece_rows = piece_keys.shape[0]
    global_rows = jnp.arange(piece_rows, dtype=jnp.int32)
    block_index = global_rows // blk_rows
    lookup = jnp.sum(
        jnp.where(
            block_index[:, None] == jnp.arange(table_size, dtype=jnp.int32)[None, :],
            all_ids[None, :],
            0,
        ),
        1,
    )
    key_pos = lookup * blk_rows + global_rows % blk_rows
    key_heads = piece_keys.reshape(piece_rows, KVH, HD)
    value_heads = piece_values.reshape(piece_rows, KVH, HD)
    key_block = math.gcd(piece_rows, 512)

    def one_block(block_number, running):
        block_keys = lax.dynamic_slice_in_dim(key_heads, block_number * key_block, key_block, 0)
        block_values = lax.dynamic_slice_in_dim(value_heads, block_number * key_block, key_block, 0)
        block_pos = lax.dynamic_slice_in_dim(key_pos, block_number * key_block, key_block, 0)
        allowed = (block_pos[None, :] <= positions[:, None]) & (block_pos[None, :] < length)
        old_max, old_sum, old_weighted = running
        scores = jnp.einsum(
            "rgad,kgd->rgak", queries, block_keys, preferred_element_type=jnp.float32
        )
        mask_full = allowed[:, None, None, :]
        new_max = jnp.maximum(old_max, jnp.max(jnp.where(mask_full, scores, FLOOR_SCORE), -1))
        rescale = jnp.exp(old_max - new_max)
        weights = jnp.where(mask_full, jnp.exp(scores - new_max[..., None]), 0.0)
        new_sum = old_sum * rescale + jnp.sum(weights, -1)
        product = jnp.einsum(
            "rgak,kgd->rgad",
            weights.astype(jnp.bfloat16),
            block_values,
            preferred_element_type=jnp.float32,
        )
        return (new_max, new_sum, old_weighted * rescale[..., None] + product)

    running_max, running_sum, weighted = lax.fori_loop(
        0, piece_rows // key_block, one_block, (running_max, running_sum, weighted)
    )
    paired = jnp.concatenate([key_heads, value_heads], -1)
    row_numbers = jnp.arange(piece_rows, dtype=jnp.int32)
    page_offsets = jnp.arange(blk_rows, dtype=jnp.int32)
    page_list = []
    for slot_number in range(slot_count):
        target = slot_block[slot_number] * blk_rows
        is_start = key_pos == target
        present = jnp.any(is_start)
        first_row = jnp.sum(jnp.where(is_start, row_numbers, 0))
        rows_here = lax.dynamic_slice_in_dim(paired, first_row, blk_rows, 0)
        chosen = lax.dynamic_index_in_dim(rows_here, slot_head[slot_number], 1, keepdims=False)
        live_rows = target + page_offsets < length
        chosen = jnp.where(live_rows[:, None], chosen, jnp.zeros_like(chosen))
        page_list.append(jnp.where(present, chosen, pages_out[slot_number]))
    running_max, running_sum, weighted, pages_out = (
        running_max,
        running_sum,
        weighted,
        jnp.stack(page_list),
    )
    divisor = jnp.where(query_live[:, None, None], running_sum, 1.0)
    attended = jnp.where(query_live[:, None, None, None], weighted / divisor[..., None], 0.0)
    attended = attended.reshape(row_count, H * HD).astype(jnp.bfloat16)
    return (attended[None], pages_out[None])


def solution(mesh):
    in_specs = (
        P("req", "blk", None),
        P("req", "blk"),
        P("req"),
        P("req", None, None),
        P(("req", "blk"), None),
        P(),
        P(),
    )
    out_specs = (P("req", "blk", None), P("req", "blk", None, None))
    return jax.shard_map(body, mesh=mesh, in_specs=in_specs, out_specs=out_specs, check_vma=False)
```

profile of v0, /device:TPU:0, one launch (start us, length us, event | category | flops | bytes accessed | tf_op | source)
XLA Modules:
  0.0 189.0 jit_solution(11061576137823461064)
XLA Ops:
  7.2 0.7 all-gather.4.cloned.1.call-update
  8.0 0.7 multiply_bitcast_fusion
  8.8 0.9 fusion.38
  9.7 0.7 fusion.48
  12.9 1.2 dynamic-slice
  14.8 0.8 bitcast_dynamic-update-slice_fusion
  15.6 10.7 %all-reduce = s32[16]{0:T(128)S(1)} all-reduce(s32[16]{0:T(128)S(1)} %bitcast_dynamic-update-slice_fusion), channel_id=1, replica_groups=mesh['req'=4,'blk'=8] {'blk'}, use_global_device_ids=true, to_apply=%add | all-reduce | flops 16 | bytes 128
  26.3 83.5 %all-gather.4.cloned.1.call-done = bf16[2048,3072]{1,0:T(8,128)(2,1)} async-done(((bf16[64,3072]{1,0:T(8,128)(2,1)}), bf16[2048,3072]{1,0:T(8,128)(2,1)}) %all-gather.4.cloned.1.call-update) | async-done | bytes 12582928 | tf_op jit(solution)/shard_map/all_gather | solution.py:47
  109.8 6.4 %fusion.21 = f32[128,3072]{1,0:T(8,128)S(1)} fusion(bf16[2048,3072]{1,0:T(8,128)(2,1)} %all-gather.4.cloned.1.call-done, bf16[1,128,2048]{2,1,0:T(8,128)(2,1)S(1)} %copy-done), kind=kOutput, calls=%fused_computation.41 | convolution fusion | flops 1610612736 | bytes 14680064 | tf_op jit(solution)/shard_map/dot_general | solution.py:45
  116.9 0.7 multiply_convert_fusion
  117.8 0.7 fusion.43
  120.4 0.8 copy.65
  129.2 0.7 select_reduce_fusion.1
  141.2 1.5 copy.84
  142.7 21.2 %all-gather.6.cloned.1.call-done = bf16[1024,512]{0,1:T(8,128)(2,1)} async-done(((bf16[128,512]{0,1:T(8,128)(2,1)}), bf16[1024,512]{0,1:T(8,128)(2,1)}) %all-gather.6.cloned.1.call-update) | async-done | bytes 1048592 | tf_op jit(solution)/shard_map/all_gather | solution.py:83
  163.9 2.3 %fusion.24 = (bf16[64,1,512]{0,2,1:T(8,128)(2,1)}, bf16[64,1,512]{0,2,1:T(8,128)(2,1)S(1)}, bf16[64,1,512]{0,2,1:T(8,128)(2,1)S(1)}, bf16[64,1,512]{0,2,1:T(8,128)(2,1)S(1)}) fusion(s32[]{:T(128)S(6)} %select_n.218, s32[]{:T(128)S(6)} %select_n.221, bf16[1024,2,256]{0,2,1:T(8,128)(2,1)} %bitcast.99, bf16[1024,2,256]{0,2,1:T(8,128)(2,1)S(1)} %bitcast.97, ...), kind=kLoop, calls=%fused_computation.51 | loop fusion | flops 524288 | bytes 2359328 | tf_op jit(solution)/shard_map/concatenate | solution.py:126
  166.2 1.6 copy.76
  167.8 0.7 copy.77
  168.8 9.0 %while.18 = (s32[]{:T(128)}, f32[128,2,4]{0,2,1:T(4,128)S(1)}, f32[128,2,4]{0,2,1:T(4,128)S(1)}, f32[128,2,4,256]{0,3,2,1:T(8,128)S(1)}, s32[1024]{0:T(1024)S(1)...) while((s32[]{:T(128)}, f32[128,2,4]{0,2,1:T(4,128)S(1)}, ...), condition=%wide.region_7.8_spmd.clone, body=%wide.region_4.0_spmd.clone.sunk | while | flops 541988480 | bytes 10298591 | solution.py:123
  168.8 0.7 iota_add_fusion.4
  169.6 0.7 broadcast_compare_fusion.10
  170.5 1.6 fusion.61
  172.5 0.7 fusion.64
  173.3 0.7 iota_add_fusion.4
  174.1 0.7 broadcast_compare_fusion.10
  175.0 1.6 fusion.61
  177.0 0.7 fusion.64
  178.0 1.0 copy.83
  179.6 0.7 fusion.29
  180.3 0.7 fusion.28
  181.0 0.7 fusion.27
  181.7 0.7 maximum_bitcast_fusion
  (84 shorter events, 8.6 us)
Async XLA Ops:
  7.2 102.6 %copy-start = (bf16[1,128,2048]{2,1,0:T(8,128)(2,1)S(1)}, bf16[1,128,2048]{2,1,0:T(8,128)(2,1)}, u32[]{:S(2)}) copy-start(bf16[1,128,2048]{2,1,0:T(8,128)(2,1)} %param.9) | copy-start | bytes 1572868
  7.2 102.6 %all-gather.4.cloned.1.call-start = ((), (), s32[]{:S(2)}) async-start(), calls=%async_computation | async-start | bytes 12976128 | tf_op jit(solution)/shard_map/all_gather | solution.py:47
  7.9 133.3 %all-gather.8.cloned.1.call-start = ((), (), s32[]{:S(2)}) async-start(), calls=%async_computation.2 | async-start | bytes 1179648 | tf_op jit(solution)/shard_map/all_gather | solution.py:84
  8.6 124.7 %copy-start.9 = (s32[2]{0:T(128)}, s32[2]{0:T(128)S(1)}, u32[]{:S(2)}) copy-start(s32[2]{0:T(128)S(1)} %multiply_bitcast_fusion) | copy-start | bytes 28
  116.2 3.7 %copy-start.7 = (f32[256]{0:T(256)S(1)}, f32[256]{0:T(256)}, u32[]{:S(2)}) copy-start(f32[256]{0:T(256)} %param.15) | copy-start | bytes 3076
  117.6 46.3 %all-gather.6.cloned.1.call-start = ((), (), s32[]{:S(2)}) async-start(), calls=%async_computation.1 | async-start | bytes 1179648 | tf_op jit(solution)/shard_map/all_gather | solution.py:83
  139.9 0.8 copy-start.8
  177.8 1.2 copy-start.2
  177.8 1.2 copy-start.6
  177.8 1.8 copy-start.1
  177.8 1.8 copy-start.5
  177.8 2.5 %copy-start.4 = (pred[64]{0:T(512)(128)(4,1)S(1)}, pred[64]{0:T(512)(128)(4,1)}, u32[]{:S(2)}) copy-start(pred[64]{0:T(512)(128)(4,1)} %get-tuple-element.333) | copy-start | bytes 196
  177.8 3.2 %copy-start.3 = (pred[64]{0:T(512)(128)(4,1)S(1)}, pred[64]{0:T(512)(128)(4,1)}, u32[]{:S(2)}) copy-start(pred[64]{0:T(512)(128)(4,1)} %get-tuple-element.332) | copy-start | bytes 196
Sparse Core Ops, SparseCore 0:
  11.0 98.7 all-gather.3
  117.7 20.3 all-gather.7
  140.3 23.5 all-gather.5
where the time goes:
time: 190 us; the launch traced here: 189 us
  waiting for transfers between devices  105 us (55%)
  between operations  33.3 us (18%)
  other arithmetic  17.6 us (9%)
  matrix products  11 us (6%)
  local copies, waits for them, and re-layouts  10.7 us (6%)
  blocking collectives  10.7 us (6%)
    all_gather x1, waiting for transfers between devices, body(): lax.all_gather(qkv_weight, ('req', 'blk'), axis=0, tiled=True)  83.5 us
    all_gather x1, waiting for transfers between devices, body(): piece_keys = lax.all_gather(send_keys, 'blk', axis=0, tiled=True)  21.2 us
    unnamed x1, blocking collectives  10.7 us
    dot_general x1, matrix products, body(): jnp.dot(local_rows, lax.all_gather(qkv_weight, ('req', 'blk'), axis=0, ti...  6.37 us
    unnamed x26, local copies, waits for them, and re-layouts  3.9 us
  transfers between devices with their start and end apart: 3, of which 2 were waited for; matrix products, arithmetic and copies ran while one was open for 7% of the time, Pallas kernels for 0%

commit v1 on v0

v1 whole, which is shorter than its diff:
```python
import functools

import jax
import jax.numpy as jnp
from jax import lax
from jax.experimental import pallas as pl
from jax.experimental.pallas import tpu as pltpu
from jax.sharding import PartitionSpec as P

H = 8
KVH = 2
HD = 256
GROUPS = H // KVH
TEAM = 4
ROPE_BASE = 1000000.0
NORM_EPS = 1e-06
FLOOR_SCORE = -1e30
VMEM_LIMIT = 56 * 1024 * 1024

ANY = pl.BlockSpec(memory_space=pl.ANY)
VMEM = pl.BlockSpec(memory_space=pltpu.VMEM)
SMEM = pl.BlockSpec(memory_space=pltpu.SMEM)


def params():
    return pltpu.CompilerParams(vmem_limit_bytes=VMEM_LIMIT)


def place():
    blk = lax.axis_index("blk")
    return lax.axis_index("req"), blk // TEAM, (blk // 2) % 2, blk % 2


def q_start(pair, core):
    return pl.multiple_of((pair * 2 + core) * 2 * HD, 2 * HD)


def kv_start(pair, core):
    return pl.multiple_of(H * HD + core * KVH * HD + pair * HD, HD)


def pack_kernel(w_ref, *outs):
    _, _, pair, core = place()
    for k in range(1, TEAM):
        to_pair, to_core = pair ^ (k // 2), core ^ (k % 2)
        outs[k - 1][...] = w_ref[:, pl.ds(kv_start(to_pair, to_core), HD)]
        outs[TEAM - 2 + k][...] = w_ref[:, pl.ds(q_start(to_pair, to_core), 2 * HD)]


def team_kernel(is_kv, w_ref, *refs):
    _, _, pair, core = place()
    out = refs[-1]
    rows = w_ref.shape[0]
    width = out.shape[1]
    start = kv_start(pair, core) if is_kv else q_start(pair, core)
    member = pair * 2 + core
    out[pl.ds(pl.multiple_of(member * rows, rows), rows), :] = w_ref[:, pl.ds(start, width)]
    for k in range(1, TEAM):
        out[pl.ds(pl.multiple_of((member ^ k) * rows, rows), rows), :] = refs[k - 1][...]


def project_kernel(n_out, pieces, is_kv, *refs):
    tokens = refs[:TEAM]
    weights = refs[TEAM : TEAM + len(pieces)]
    gain_ref, cos_ref, sin_ref, out, x_all, w_all, x_sem, w_sem = refs[TEAM + len(pieces) :]
    req, outer, _, core = place()
    rows = tokens[0].shape[0]
    copies = []
    for k in range(TEAM):
        slot = (core ^ (k % 2)) + (k // 2) * 2
        copies.append(
            pltpu.make_async_copy(
                tokens[k], x_all.at[pl.ds(pl.multiple_of(slot * rows, rows), rows), :], x_sem.at[k]
            )
        )
    depth = weights[0].shape[0]
    for i, (dr, ko) in enumerate(pieces):
        from_outer = lax.rem(outer + n_out - ko, n_out)
        index = (req ^ dr) * n_out + from_outer
        copies.append(
            pltpu.make_async_copy(
                weights[i], w_all.at[pl.ds(pl.multiple_of(index * depth, depth), depth), :], w_sem.at[i]
            )
        )
    for copy in copies:
        copy.start()
    for copy in copies:
        copy.wait()
    half = HD // 2
    for j in range(TEAM):
        mine = slice(j * rows, (j + 1) * rows)
        product = jnp.dot(x_all[mine, :], w_all[...], preferred_element_type=jnp.float32)
        cosine, sine = cos_ref[mine, :], sin_ref[mine, :]
        gain = gain_ref[...]
        if is_kv:
            is_key = core == 0
            cosine = jnp.where(is_key, cosine, 1.0)
            sine = jnp.where(is_key, sine, 0.0)
            gain = jnp.where(is_key, gain, 1.0)
        for h in range(out.shape[1] // HD):
            head = product[:, h * HD : (h + 1) * HD]
            mean = jnp.mean(head * head, axis=-1, keepdims=True)
            head = head * lax.rsqrt(mean + NORM_EPS) * gain
            front, second = head[:, :half], head[:, half:]
            out[mine, h * HD : h * HD + half] = (front * cosine - second * sine).astype(jnp.bfloat16)
            out[mine, h * HD + half : (h + 1) * HD] = (second * cosine + front * sine).astype(jnp.bfloat16)


def load_kv(n_out, mine, other, store, sems, core):
    rows = mine[0].shape[0]
    copies = []
    for k in range(n_out):
        here = pl.ds(k * rows, rows)
        copies.append(pltpu.make_async_copy(mine[k], store.at[core, here, :], sems.at[0, k]))
        copies.append(pltpu.make_async_copy(other[k], store.at[1 - core, here, :], sems.at[1, k]))
    for copy in copies:
        copy.start()
    for copy in copies:
        copy.wait()


def attend_kernel(n_out, parts, *refs):
    mine, other = refs[:n_out], refs[n_out : 2 * n_out]
    q_ref, qpos_ref, kpos_ref, length_ref = refs[2 * n_out : 2 * n_out + 4]
    outs = refs[2 * n_out + 4 : 2 * n_out + 4 + len(parts)]
    store, sems = refs[2 * n_out + 4 + len(parts) :]
    _, _, _, core = place()
    load_kv(n_out, mine, other, store, sems, core)
    length = length_ref[0]
    rows = outs[0].shape[0]
    key_pos = kpos_ref[...]
    key_pos = jnp.where(key_pos < length, key_pos, jnp.iinfo(jnp.int32).max)
    for part, out in zip(parts, outs):
        slot = (core ^ (part % 2)) + (part // 2) * 2
        here = pl.ds(pl.multiple_of(slot * rows, rows), rows)
        query_pos = qpos_ref[here, :]
        allowed = key_pos <= query_pos
        live = query_pos < length
        for h in range(2):
            cols = slice(h * HD, (h + 1) * HD)
            scores = lax.dot_general(
                q_ref[here, cols], store[0], (((1,), (1,)), ((), ())), preferred_element_type=jnp.float32
            )
            scores = jnp.where(allowed, scores, FLOOR_SCORE)
            row_max = jnp.max(scores, axis=-1, keepdims=True)
            weights = jnp.where(allowed, jnp.exp(scores - row_max), 0.0)
            row_sum = jnp.sum(weights, axis=-1, keepdims=True)
            summed = jnp.dot(weights.astype(jnp.bfloat16), store[1], preferred_element_type=jnp.float32)
            divisor = jnp.where(live, row_sum, 1.0)
            out[:, cols] = jnp.where(live, summed / divisor, 0.0).astype(jnp.bfloat16)


def pages_kernel(n_out, blk_rows, *refs):
    mine, other = refs[:n_out], refs[n_out : 2 * n_out]
    info_ref, own, away, store, sems = refs[2 * n_out :]
    _, _, _, core = place()
    load_kv(n_out, mine, other, store, sems, core)
    slots = own.shape[0]
    row = lax.broadcasted_iota(jnp.int32, (blk_rows, HD), 0)
    for target, base in ((own, 0), (away, slots)):
        for i in range(slots):
            start = pl.multiple_of(info_ref[1, base + i] * blk_rows, blk_rows)
            live = row < info_ref[2, base + i]
            for half in range(2):
                page = store[half, pl.ds(start, blk_rows), :].astype(jnp.float32)
                page = jnp.where(live, page, 0.0).astype(jnp.bfloat16)
                target[i, :, half * HD : (half + 1) * HD] = page


def finish_kernel(a0, a1, a2, a3, own_pages, got_pages, info_ref, att_out, page_out):
    _, _, pair, core = place()
    member = pair * 2 + core
    for k, part in enumerate((a0, a1, a2, a3)):
        att_out[:, pl.ds(pl.multiple_of((member ^ k) * 2 * HD, 2 * HD), 2 * HD)] = part[...]
    for i in range(page_out.shape[0]):
        here = info_ref[0, i] == pair

        @pl.when(here)
        def _():
            page_out[i] = own_pages[i]

        @pl.when(jnp.logical_not(here))
        def _():
            page_out[i] = got_pages[i]


def body(tokens, block_ids, lengths, page_table, qkv_weight, q_gain, k_gain):
    n_req, n_blk = lax.axis_size("req"), lax.axis_size("blk")
    n_out = n_blk // TEAM
    bf16 = jnp.bfloat16
    shape = jax.ShapeDtypeStruct
    blk = lax.axis_index("blk")
    pair = (blk // 2) % 2

    def in_team(array, k):
        return lax.ppermute(array, "blk", [(i, i ^ k) for i in range(n_blk)])

    def in_req(array, k):
        return lax.ppermute(array, "req", [(i, i ^ k) for i in range(n_req)])

    def across(array, k):
        return lax.ppermute(array, "blk", [(i, (i + TEAM * k) % n_blk) for i in range(n_blk)])

    w_rows = qkv_weight.shape[0]
    packed = pl.pallas_call(
        pack_kernel,
        out_shape=[shape((w_rows, HD), bf16)] * 3 + [shape((w_rows, 2 * HD), bf16)] * 3,
        in_specs=[VMEM],
        out_specs=[VMEM] * 6,
        compiler_params=params(),
        name="pack",
    )(qkv_weight)

    def gather_weight(parts, is_kv):
        width = HD if is_kv else 2 * HD
        got = [in_team(part, k + 1) for k, part in enumerate(parts)]
        team = pl.pallas_call(
            functools.partial(team_kernel, is_kv),
            out_shape=shape((TEAM * w_rows, width), bf16),
            in_specs=[VMEM] * TEAM,
            out_specs=VMEM,
            compiler_params=params(),
            name="team",
        )(qkv_weight, *got)
        pieces = {}
        for ko in range(n_out):
            piece = team if ko == 0 else across(team, ko)
            pieces[(0, ko)] = piece
            for dr in (1, 2):
                pieces[(dr, ko)] = in_req(piece, dr)
            first = 1 + ko % 2
            pieces[(3, ko)] = in_req(pieces[(first, ko)], 3 - first)
        return pieces

    kv_pieces = gather_weight(packed[:3], True)
    own = tokens[0]
    rows = own.shape[0]
    far = in_team(own, 2)
    team_tokens = [own, in_team(own, 1), far, in_team(far, 1)]
    q_pieces = gather_weight(packed[3:], False)

    blk_rows = rows // block_ids.shape[1]
    near_ids = in_team(block_ids, 1)
    is_first = blk % 2 == 0
    chip_ids = jnp.where(
        is_first, jnp.concatenate([block_ids, near_ids], 1), jnp.concatenate([near_ids, block_ids], 1)
    )
    team_ids = jnp.concatenate([chip_ids, in_team(chip_ids, 2)], 1)
    all_ids = jnp.concatenate([team_ids] + [across(team_ids, k) for k in range(1, n_out)], 1)[0]
    offsets = jnp.arange(blk_rows, dtype=jnp.int32)
    key_pos = (all_ids[:, None] * blk_rows + offsets[None, :]).reshape(1, -1)
    query_pos = (team_ids[0][:, None] * blk_rows + offsets[None, :]).reshape(-1, 1)
    half = HD // 2
    inverse = jnp.power(jnp.float32(ROPE_BASE), -2.0 * jnp.arange(half).astype(jnp.float32) / HD)
    angles = query_pos.astype(jnp.float32) * inverse[None, :]
    cosine, sine = jnp.cos(angles), jnp.sin(angles)

    def project(pieces, is_kv, gain):
        keys = sorted(pieces)
        width = HD if is_kv else 2 * HD
        depth = TEAM * w_rows
        return pl.pallas_call(
            functools.partial(project_kernel, n_out, keys, is_kv),
            out_shape=shape((TEAM * rows, width), bf16),
            in_specs=[ANY] * (TEAM + len(keys)) + [VMEM] * 3,
            out_specs=VMEM,
            scratch_shapes=[
                pltpu.VMEM((TEAM * rows, own.shape[1]), bf16),
                pltpu.VMEM((depth * len(keys), width), bf16),
                pltpu.SemaphoreType.DMA((TEAM,)),
                pltpu.SemaphoreType.DMA((len(keys),)),
            ],
            cost_estimate=pl.CostEstimate(
                flops=2 * TEAM * rows * own.shape[1] * width, bytes_accessed=6 << 20, transcendentals=0
            ),
            compiler_params=params(),
            name="project_kv" if is_kv else "project_q",
        )(*team_tokens, *[pieces[k] for k in keys], gain[None, :], cosine, sine)

    made = project(kv_pieces, True, k_gain)
    mine = [made] + [across(made, k) for k in range(1, n_out)]
    other = [in_team(part, 1) for part in mine]

    table = page_table[0].reshape(-1)
    per_head = page_table.shape[2]
    slot_count = page_table.shape[1] * per_head // n_blk
    wanted = jnp.concatenate(
        [b * slot_count + jnp.arange(slot_count, dtype=jnp.int32) for b in (blk, blk ^ 2)]
    )
    flat = jnp.sum(
        jnp.where(wanted[:, None] == table[None, :], jnp.arange(table.shape[0], dtype=jnp.int32)[None, :], 0), 1
    )
    block = flat % per_head
    where = jnp.sum(
        jnp.where(block[:, None] == all_ids[None, :], jnp.arange(per_head, dtype=jnp.int32)[None, :], 0), 1
    )
    info = jnp.stack([flat // per_head, where, lengths[0] - block * blk_rows])

    total = TEAM * rows * n_out
    store = [pltpu.VMEM((2, total, HD), bf16), pltpu.SemaphoreType.DMA((2, n_out))]
    page_shape = shape((slot_count, blk_rows, 2 * HD), bf16)
    own_pages, away_pages = pl.pallas_call(
        functools.partial(pages_kernel, n_out, blk_rows),
        out_shape=[page_shape, page_shape],
        in_specs=[ANY] * (2 * n_out) + [SMEM],
        out_specs=[VMEM, VMEM],
        scratch_shapes=store,
        cost_estimate=pl.CostEstimate(flops=0, bytes_accessed=4 << 20, transcendentals=0),
        compiler_params=params(),
        name="pages",
    )(*mine, *other, info)
    got_pages = in_team(away_pages, 2)

    queries = project(q_pieces, False, q_gain)

    def attend(parts):
        return pl.pallas_call(
            functools.partial(attend_kernel, n_out, parts),
            out_shape=[shape((rows, 2 * HD), bf16)] * len(parts),
            in_specs=[ANY] * (2 * n_out) + [VMEM] * 3 + [SMEM],
            out_specs=[VMEM] * len(parts),
            scratch_shapes=store,
            cost_estimate=pl.CostEstimate(
                flops=8 * HD * rows * total * len(parts), bytes_accessed=4 << 20, transcendentals=0
            ),
            compiler_params=params(),
            name="attend",
        )(*mine, *other, queries, query_pos, key_pos, lengths)

    to_far, to_diag = attend((2, 3))
    from_far, from_diag = in_team(to_far, 2), in_team(to_diag, 3)
    kept, to_near = attend((0, 1))
    from_near = in_team(to_near, 1)

    attended, pages = pl.pallas_call(
        finish_kernel,
        out_shape=[shape((rows, H * HD), bf16), page_shape],
        in_specs=[VMEM] * 6 + [SMEM],
        out_specs=[VMEM] * 2,
        compiler_params=params(),
        name="finish",
    )(kept, from_near, from_far, from_diag, own_pages, got_pages, info)
    return attended[None], pages[None]


def solution(mesh):
    in_specs = (
        P("req", "blk", None),
        P("req", "blk"),
        P("req"),
        P("req", None, None),
        P(("req", "blk"), None),
        P(),
        P(),
    )
    out_specs = (P("req", "blk", None), P("req", "blk", None, None))
    return jax.shard_map(body, mesh=mesh, in_specs=in_specs, out_specs=out_specs, check_vma=False)
```

time: 190 us -> 109 us (0.57)
  waiting for transfers between devices: 105 us -> 33.1 us
  starting transfers between devices: 0.12 us -> 32.3 us
  between operations: 33.3 us -> 1.6 us
  Pallas kernels: 0 us -> 30.5 us
  other arithmetic: 17.6 us -> 4.55 us
  matrix products: 11 us -> 0 us
  blocking collectives: 10.7 us -> 0 us
  local copies, waits for them, and re-layouts: 10.7 us -> 6.88 us
    all_gather x3 -> x0, waiting for transfers between devices: 105 us -> none  [the longest x1 83.5 us: body(): lax.all_gather(qkv_weight, ('req', 'blk'), axis=0, tiled=True)]
    ppermute x0 -> x33, waiting for transfers between devices: none -> 33.1 us  [the longest x17 13.6 us: in_team(): return lax.ppermute(array, 'blk', [(i, i ^ k) for i in range(n_blk)])]
    ppermute x0 -> x33, starting transfers between devices: none -> 32.3 us  [the longest x12 15.9 us: in_req(): return lax.ppermute(array, 'req', [(i, i ^ k) for i in range(n_req)])]
    pallas_call x0 -> x9, Pallas kernels: none -> 30.5 us  [the longest x2 10.1 us: project(): pl.pallas_call(functools.partial(project_kernel, n_out, keys, is_kv), out...]
    dot_general x5 -> x0, matrix products: 11 us -> none  [the longest x1 6.37 us: body(): jnp.dot(local_rows, lax.all_gather(qkv_weight, ('req', 'blk'), axis=0, ti...]
    unnamed x1 -> x0, blocking collectives: 10.7 us -> none
    reduce_sum x9 -> x2, other arithmetic: 3.72 us -> 0.37 us  [the longest x1 0.18 us: body(): jnp.sum(jnp.where(wanted[:, None] == table[None, :], jnp.arange(table.sha...]
    lt x5 -> x0, other arithmetic: 2.7 us -> none  [the longest x2 1.45 us: one_block(): block_pos[None, :] < length]
  transfers between devices with their start and end apart: 3 -> 33, of which waited for: 2 -> 13; matrix products, arithmetic and copies ran while one was open for 7% -> 6% of each run, Pallas kernels for 0% -> 26%
where the time goes in v1:
time: 109 us
  waiting for transfers between devices  33.1 us (30%)
  starting transfers between devices  32.3 us (30%)
  Pallas kernels  30.5 us (28%)
  local copies, waits for them, and re-layouts  6.88 us (6%)
  other arithmetic  4.55 us (4%)
  between operations  1.6 us (1%)
    ppermute x12, starting transfers between devices, in_req(): return lax.ppermute(array, 'req', [(i, i ^ k) for i in range(n_req)])  15.9 us
    ppermute x17, waiting for transfers between devices, in_team(): return lax.ppermute(array, 'blk', [(i, i ^ k) for i in range(n_blk)])  13.6 us
    ppermute x4, waiting for transfers between devices, across(): lax.ppermute(array, 'blk', [(i, (i + TEAM * k) % n_blk) for i in range(n_...  12.3 us
    ppermute x17, starting transfers between devices, in_team(): return lax.ppermute(array, 'blk', [(i, i ^ k) for i in range(n_blk)])  10.5 us
    pallas_call x2, Pallas kernels, project(): pl.pallas_call(functools.partial(project_kernel, n_out, keys, is_kv), out...  10.1 us
    pallas_call x2, Pallas kernels, attend(): pl.pallas_call(functools.partial(attend_kernel, n_out, parts), out_shape=...  10.1 us
    ppermute x12, waiting for transfers between devices, in_req(): return lax.ppermute(array, 'req', [(i, i ^ k) for i in range(n_req)])  7.2 us
    ppermute x4, starting transfers between devices, across(): lax.ppermute(array, 'blk', [(i, (i + TEAM * k) % n_blk) for i in range(n_...  5.97 us
  transfers between devices with their start and end apart: 33, of which 13 were waited for; matrix products, arithmetic and copies ran while one was open for 6% of the time, Pallas kernels for 26%

profile of v1, /device:TPU:0, one launch (start us, length us, event | category | flops | bytes accessed | tf_op | source)
XLA Modules:
  0.0 108.9 jit_solution(13025447273909064797)
XLA Ops:
  0.6 3.1 %collective-permute-start.1 = (bf16[128,2048]{1,0:T(8,128)(2,1)}, bf16[128,2048]{1,0:T(8,128)(2,1)S(1)}, u32[]{:S(2)}, u32[]{:S(2)}) collective-permute-start(bf16[128,2048]{1,0:T(8,128)(2,1)} %bitcast.28), channel_id=1, source_target_pairs={{0,2},{1,3},{2,0},{3,1},{4,6},{5,7},{6,4},{7,5},{8,10},{9,11},{10,... | collective-permute-start | bytes 1572872 | tf_op jit(solution)/shard_map/ppermute | solution.py:196
  3.7 1.7 %pack.1 = (bf16[64,256]{1,0:T(8,128)(2,1)}, bf16[64,256]{1,0:T(8,128)(2,1)}, bf16[64,256]{1,0:T(8,128)(2,1)}, bf16[64,512]{1,0:T(8,128)(2,1)}, bf16[64,512]{1,0:T(8,128)(2,1)}, /*index=5*/bf16[64,512]{1,0:T(8,128)(2,1)}) custom-call(bf16[64,3072]{1,0:T(8,128)(2,1)} %w_ref.5), custom_call_target="tpu_custom_call" | custom-call | tf_op jit(solution)/shard_map/pack/pallas_call | solution.py:205
  5.5 1.8 %collective-permute-start.5 = (bf16[64,256]{1,0:T(8,128)(2,1)}, bf16[64,256]{1,0:T(8,128)(2,1)S(1)}, u32[]{:S(2)}, u32[]{:S(2)}) collective-permute-start(bf16[64,256]{1,0:T(8,128)(2,1)} %get-tuple-element.18), channel_id=1, source_target_pairs={{0,3},{1,2},{2,1},{3,0},{4,7},{5,6},{6,5},{7,4},{8,11},{9,10},{10,... | collective-permute-start | bytes 98312 | tf_op jit(solution)/shard_map/ppermute | solution.py:196
  11.3 6.1 %collective-permute-done.4.refs_1_ = bf16[64,256]{1,0:T(8,128)(2,1)S(1)} collective-permute-done((bf16[64,256]{1,0:T(8,128)(2,1)}, bf16[64,256]{1,0:T(8,128)(2,1)S(1)}, u32[]{:S(2)}, u32[]{:S(2)}) %collective-permute-start.4) | collective-permute-done | bytes 32800 | tf_op jit(solution)/shard_map/ppermute | solution.py:196
  17.4 2.0 %collective-permute-start.14 = (s32[1,4]{1,0:T(1,128)S(1)}, s32[1,4]{1,0:T(1,128)S(1)}, u32[]{:S(2)}, u32[]{:S(2)}) collective-permute-start(s32[1,4]{1,0:T(1,128)S(1)} %broadcast_select_fusion), channel_id=1, source_target_pairs={{0,2},{1,3},{2,0},{3,1},{4,6},{5,7},{6,4},{7,5},{8,10},{9,11},{10,... | collective-permute-start | bytes 56 | tf_op jit(solution)/shard_map/ppermute | solution.py:196
  19.5 1.7 %team.2.refs_4_ = bf16[256,256]{1,0:T(8,128)(2,1)} custom-call(bf16[64,3072]{1,0:T(8,128)(2,1)} %w_ref.5, bf16[64,256]{1,0:T(8,128)(2,1)} %copy-done.28, bf16[64,256]{1,0:T(8,128)(2,1)} %copy-done.29, bf16[64,256]{1,0:T(8,128)(2,1)} %copy-done.30), custom_call_target="tpu_custom_call" | custom-call | tf_op jit(solution)/shard_map/team/pallas_call | solution.py:217
  22.0 3.0 %collective-permute-start.6 = (bf16[256,256]{1,0:T(8,128)(2,1)}, bf16[256,256]{1,0:T(8,128)(2,1)S(1)}, u32[]{:S(2)}, u32[]{:S(2)}) collective-permute-start(bf16[256,256]{1,0:T(8,128)(2,1)} %team.2.refs_4_), channel_id=1, source_target_pairs={{0,4},{1,5},{2,6},{3,7},{4,0},{5,1},{6,2},{7,3},{8,12},{9,13},{10,... | collective-permute-start | bytes 393224 | tf_op jit(solution)/shard_map/ppermute | solution.py:202
  25.0 1.5 %collective-permute-start.7 = (bf16[256,256]{1,0:T(8,128)(2,1)}, bf16[256,256]{1,0:T(8,128)(2,1)S(1)}, u32[]{:S(2)}, u32[]{:S(2)}) collective-permute-start(bf16[256,256]{1,0:T(8,128)(2,1)} %team.2.refs_4_), channel_id=1, source_target_pairs={{0,8},{8,0},{16,24},{24,16},{1,9},{9,1},{17,25},{25,17},{2,10},{10... | collective-permute-start | bytes 393224 | tf_op jit(solution)/shard_map/ppermute | solution.py:199
  26.5 1.5 %collective-permute-start.9 = (bf16[256,256]{1,0:T(8,128)(2,1)}, bf16[256,256]{1,0:T(8,128)(2,1)S(1)}, u32[]{:S(2)}, u32[]{:S(2)}) collective-permute-start(bf16[256,256]{1,0:T(8,128)(2,1)} %team.2.refs_4_), channel_id=1, source_target_pairs={{0,16},{8,24},{16,0},{24,8},{1,17},{9,25},{17,1},{25,9},{2,18},{10... | collective-permute-start | bytes 393224 | tf_op jit(solution)/shard_map/ppermute | solution.py:199
  29.3 1.8 %team.3.refs_4_ = bf16[256,512]{1,0:T(8,128)(2,1)} custom-call(bf16[64,3072]{1,0:T(8,128)(2,1)} %w_ref.5, bf16[64,512]{1,0:T(8,128)(2,1)} %copy-done.25, bf16[64,512]{1,0:T(8,128)(2,1)} %copy-done.26, bf16[64,512]{1,0:T(8,128)(2,1)} %copy-done.27), custom_call_target="tpu_custom_call" | custom-call | tf_op jit(solution)/shard_map/team/pallas_call | solution.py:217
  31.6 1.6 %collective-permute-start.8 = (bf16[256,256]{1,0:T(8,128)(2,1)S(1)}, bf16[256,256]{1,0:T(8,128)(2,1)S(1)}, u32[]{:S(2)}, u32[]{:S(2)}) collective-permute-start(bf16[256,256]{1,0:T(8,128)(2,1)S(1)} %collective-permute-done.6.refs_5_), channel_id=1, source_target_pairs={{0,8},{8,0},{16,24},{24,16},{1,9},{9,1},{17,25},{25,17},{2,10},{10... | collective-permute-start | bytes 393224 | tf_op jit(solution)/shard_map/ppermute | solution.py:199
  33.3 1.5 %collective-permute-start.10 = (bf16[256,256]{1,0:T(8,128)(2,1)S(1)}, bf16[256,256]{1,0:T(8,128)(2,1)}, u32[]{:S(2)}, u32[]{:S(2)}) collective-permute-start(bf16[256,256]{1,0:T(8,128)(2,1)S(1)} %collective-permute-done.6.refs_5_), channel_id=1, source_target_pairs={{0,16},{8,24},{16,0},{24,8},{1,17},{9,25},{17,1},{25,9},{2,18},{10... | collective-permute-start | bytes 393224 | tf_op jit(solution)/shard_map/ppermute | solution.py:199
  34.9 1.7 %collective-permute-done.8.refs_7_ = bf16[256,256]{1,0:T(8,128)(2,1)S(1)} collective-permute-done((bf16[256,256]{1,0:T(8,128)(2,1)S(1)}, bf16[256,256]{1,0:T(8,128)(2,1)S(1)}, u32[]{:S(2)}, u32[]{:S(2)}) %collective-permute-start.8) | collective-permute-done | bytes 131104 | tf_op jit(solution)/shard_map/ppermute | solution.py:199
  36.7 1.6 %collective-permute-start.11 = (bf16[256,256]{1,0:T(8,128)(2,1)S(1)}, bf16[256,256]{1,0:T(8,128)(2,1)S(1)}, u32[]{:S(2)}, u32[]{:S(2)}) collective-permute-start(bf16[256,256]{1,0:T(8,128)(2,1)S(1)} %collective-permute-done.7.refs_6_), channel_id=1, source_target_pairs={{0,16},{8,24},{16,0},{24,8},{1,17},{9,25},{17,1},{25,9},{2,18},{10... | collective-permute-start | bytes 393224 | tf_op jit(solution)/shard_map/ppermute | solution.py:199
  39.8 1.8 %multiply_sine_fusion = (f32[512,128]{1,0:T(8,128)}, f32[512,128]{1,0:T(8,128)}) fusion(f32[128]{0:T(128)S(1)} %multiply_power_fusion, f32[512]{0:T(512)S(1)} %convert_element_type.19), kind=kLoop, calls=%fused_computation | loop fusion | flops 65536 | bytes 526848 | tf_op jit(solution)/shard_map/sin | solution.py:256
  41.7 1.6 %collective-permute-start.22 = (bf16[256,512]{1,0:T(8,128)(2,1)S(1)}, bf16[256,512]{1,0:T(8,128)(2,1)S(1)}, u32[]{:S(2)}, u32[]{:S(2)}) collective-permute-start(bf16[256,512]{1,0:T(8,128)(2,1)S(1)} %copy-done.4), channel_id=1, source_target_pairs={{0,8},{8,0},{16,24},{24,16},{1,9},{9,1},{17,25},{25,17},{2,10},{10... | collective-permute-start | bytes 786440 | tf_op jit(solution)/shard_map/ppermute | solution.py:199
  43.2 2.9 %collective-permute-done.21.refs_5_ = bf16[256,512]{1,0:T(8,128)(2,1)S(1)} collective-permute-done((bf16[256,512]{1,0:T(8,128)(2,1)}, bf16[256,512]{1,0:T(8,128)(2,1)S(1)}, u32[]{:S(2)}, u32[]{:S(2)}) %collective-permute-start.21) | collective-permute-done | bytes 262176 | tf_op jit(solution)/shard_map/ppermute | solution.py:202
  46.1 1.6 %collective-permute-start.25 = (bf16[256,512]{1,0:T(8,128)(2,1)S(1)}, bf16[256,512]{1,0:T(8,128)(2,1)S(1)}, u32[]{:S(2)}, u32[]{:S(2)}) collective-permute-start(bf16[256,512]{1,0:T(8,128)(2,1)S(1)} %collective-permute-done.21.refs_5_), channel_id=1, source_target_pairs={{0,16},{8,24},{16,0},{24,8},{1,17},{9,25},{17,1},{25,9},{2,18},{10... | collective-permute-start | bytes 786440 | tf_op jit(solution)/shard_map/ppermute | solution.py:199
  48.7 4.6 %project_kv.1.refs_0_ = bf16[512,256]{1,0:T(8,128)(2,1)} custom-call(bf16[128,2048]{1,0:T(8,128)(2,1)} %bitcast.29, bf16[128,2048]{1,0:T(8,128)(2,1)} %copy-done.2, bf16[128,2048]{1,0:T(8,128)(2,1)} %copy-done.1, bf16[128,2048]{1,0:T(8,128)(2,1)} %copy-done.3, bf16[256,256]{1,0:T(8,128)(2,1)} %team.2.refs_4_, bf16[256,256]{1,0:T(8,128)(2,1)} %copy-done.16, ...), custom_call_target="tpu_custom_call" | custom-call | flops 536870912 | bytes 6291456 | tf_op jit(solution)/shard_map/project_kv/pallas_call | solution.py:262
  55.5 2.4 %collective-permute-start.28 = (s32[1,8]{1,0:T(1,128)S(1)}, s32[1,8]{1,0:T(1,128)S(1)}, u32[]{:S(2)}, u32[]{:S(2)}) collective-permute-start(s32[1,8]{1,0:T(1,128)S(1)} %copy-done.35), channel_id=1, source_target_pairs={{0,4},{1,5},{2,6},{3,7},{4,0},{5,1},{6,2},{7,3},{8,12},{9,13},{10,... | collective-permute-start | bytes 104 | tf_op jit(solution)/shard_map/ppermute | solution.py:202
  58.0 8.8 %collective-permute-done.28 = s32[1,8]{1,0:T(1,128)S(1)} collective-permute-done((s32[1,8]{1,0:T(1,128)S(1)}, s32[1,8]{1,0:T(1,128)S(1)}, u32[]{:S(2)}, u32[]{:S(2)}) %collective-permute-start.28) | collective-permute-done | bytes 64 | tf_op jit(solution)/shard_map/ppermute | solution.py:202
  67.3 1.6 %collective-permute-start.23 = (bf16[256,512]{1,0:T(8,128)(2,1)S(1)}, bf16[256,512]{1,0:T(8,128)(2,1)S(1)}, u32[]{:S(2)}, u32[]{:S(2)}) collective-permute-start(bf16[256,512]{1,0:T(8,128)(2,1)S(1)} %collective-permute-done.21.refs_5_), channel_id=1, source_target_pairs={{0,8},{8,0},{16,24},{24,16},{1,9},{9,1},{17,25},{25,17},{2,10},{10... | collective-permute-start | bytes 786440 | tf_op jit(solution)/shard_map/ppermute | solution.py:199
  68.9 1.5 %collective-permute-start.26 = (bf16[256,512]{1,0:T(8,128)(2,1)S(1)}, bf16[256,512]{1,0:T(8,128)(2,1)S(1)}, u32[]{:S(2)}, u32[]{:S(2)}) collective-permute-start(bf16[256,512]{1,0:T(8,128)(2,1)S(1)} %collective-permute-done.22.refs_6_), channel_id=1, source_target_pairs={{0,16},{8,24},{16,0},{24,8},{1,17},{9,25},{17,1},{25,9},{2,18},{10... | collective-permute-start | bytes 786440 | tf_op jit(solution)/shard_map/ppermute | solution.py:199
  73.2 2.8 %pages.1 = (bf16[4,64,512]{2,1,0:T(8,128)(2,1)}, bf16[4,64,512]{2,1,0:T(8,128)(2,1)}) custom-call(bf16[512,256]{1,0:T(8,128)(2,1)} %project_kv.1.refs_0_, bf16[512,256]{1,0:T(8,128)(2,1)} %copy-done.12, bf16[512,256]{1,0:T(8,128)(2,1)} %copy-done.13, bf16[512,256]{1,0:T(8,128)(2,1)} %copy-done.15, s32[3,8]{1,0:T(4,128)} %pad_add_fusion.refs_4_.info_ref), custom_call_target="tpu_custom_call" | custom-call | bytes 4194304 | tf_op jit(solution)/shard_map/pages/pallas_call | solution.py:302
  76.6 4.0 %collective-permute-done.26.refs_10_ = bf16[256,512]{1,0:T(8,128)(2,1)S(1)} collective-permute-done((bf16[256,512]{1,0:T(8,128)(2,1)S(1)}, bf16[256,512]{1,0:T(8,128)(2,1)S(1)}, u32[]{:S(2)}, u32[]{:S(2)}) %collective-permute-start.26) | collective-permute-done | bytes 262176 | tf_op jit(solution)/shard_map/ppermute | solution.py:199
  81.6 5.5 %project_q.1.refs_4_ = bf16[512,512]{1,0:T(8,128)(2,1)} custom-call(bf16[128,2048]{1,0:T(8,128)(2,1)} %bitcast.30, bf16[128,2048]{1,0:T(8,128)(2,1)} %copy-done.2, bf16[128,2048]{1,0:T(8,128)(2,1)} %copy-done.1, bf16[128,2048]{1,0:T(8,128)(2,1)} %copy-done.3, bf16[256,512]{1,0:T(8,128)(2,1)} %team.3.refs_4_, bf16[256,512]{1,0:T(8,128)(2,1)} %copy-done.5, ...), custom_call_target="tpu_custom_call" | custom-call | flops 1073741824 | bytes 6291456 | tf_op jit(solution)/shard_map/project_q/pallas_call | solution.py:262
  87.1 5.1 %attend.2 = (bf16[128,512]{1,0:T(8,128)(2,1)}, bf16[128,512]{1,0:T(8,128)(2,1)}) custom-call(bf16[512,256]{1,0:T(8,128)(2,1)} %project_kv.1.refs_0_, bf16[512,256]{1,0:T(8,128)(2,1)} %copy-done.12, bf16[512,256]{1,0:T(8,128)(2,1)} %copy-done.13, bf16[512,256]{1,0:T(8,128)(2,1)} %copy-done.15, bf16[512,512]{1,0:T(8,128)(2,1)} %project_q.1.refs_4_, ...), custom_call_target="tpu_custom_call" | custom-call | flops 536870912 | bytes 4194304 | tf_op jit(solution)/shard_map/attend/pallas_call | solution.py:317
  92.2 5.1 %attend.3 = (bf16[128,512]{1,0:T(8,128)(2,1)}, bf16[128,512]{1,0:T(8,128)(2,1)}) custom-call(bf16[512,256]{1,0:T(8,128)(2,1)} %project_kv.1.refs_0_, bf16[512,256]{1,0:T(8,128)(2,1)} %copy-done.12, bf16[512,256]{1,0:T(8,128)(2,1)} %copy-done.13, bf16[512,256]{1,0:T(8,128)(2,1)} %copy-done.15, bf16[512,512]{1,0:T(8,128)(2,1)} %project_q.1.refs_4_, ...), custom_call_target="tpu_custom_call" | custom-call | flops 536870912 | bytes 4194304 | tf_op jit(solution)/shard_map/attend/pallas_call | solution.py:317
  97.4 1.8 %collective-permute-start.31 = (bf16[128,512]{1,0:T(8,128)(2,1)}, bf16[128,512]{1,0:T(8,128)(2,1)S(1)}, u32[]{:S(2)}, u32[]{:S(2)}) collective-permute-start(bf16[128,512]{1,0:T(8,128)(2,1)} %get-tuple-element.25), channel_id=1, source_target_pairs={{0,3},{1,2},{2,1},{3,0},{4,7},{5,6},{6,5},{7,4},{8,11},{9,10},{10,... | collective-permute-start | bytes 393224 | tf_op jit(solution)/shard_map/ppermute | solution.py:196
  99.2 4.6 %collective-permute-done.30.a2 = bf16[128,512]{1,0:T(8,128)(2,1)S(1)} collective-permute-done((bf16[128,512]{1,0:T(8,128)(2,1)}, bf16[128,512]{1,0:T(8,128)(2,1)S(1)}, u32[]{:S(2)}, u32[]{:S(2)}) %collective-permute-start.30) | collective-permute-done | bytes 131104 | tf_op jit(solution)/shard_map/ppermute | solution.py:196
  103.9 2.0 %collective-permute-done.31.a3 = bf16[128,512]{1,0:T(8,128)(2,1)S(1)} collective-permute-done((bf16[128,512]{1,0:T(8,128)(2,1)}, bf16[128,512]{1,0:T(8,128)(2,1)S(1)}, u32[]{:S(2)}, u32[]{:S(2)}) %collective-permute-start.31) | collective-permute-done | bytes 131104 | tf_op jit(solution)/shard_map/ppermute | solution.py:196
  106.7 2.3 %finish.1 = (bf16[128,2048]{1,0:T(8,128)(2,1)}, bf16[4,64,512]{2,1,0:T(8,128)(2,1)}) custom-call(bf16[128,512]{1,0:T(8,128)(2,1)} %get-tuple-element.22.a0, bf16[128,512]{1,0:T(8,128)(2,1)} %copy-done.22, bf16[128,512]{1,0:T(8,128)(2,1)} %copy-done.23, bf16[128,512]{1,0:T(8,128)(2,1)} %copy-done.24, bf16[4,64,512]{2,1,0:T(8,128)(2,1)} %get-tuple-element.26.own_pages, ...), custom_call_target="tpu_custom_call" | custom-call | tf_op jit(solution)/shard_map/finish/pallas_call | solution.py:335
  (133 shorter events, 16.7 us)
Async XLA Ops:
  0.6 27.5 %collective-permute-start.1 = (bf16[128,2048]{1,0:T(8,128)(2,1)}, bf16[128,2048]{1,0:T(8,128)(2,1)S(1)}, u32[]{:S(2)}, u32[]{:S(2)}) collective-permute-start(bf16[128,2048]{1,0:T(8,128)(2,1)} %bitcast.28), channel_id=1, source_target_pairs={{0,2},{1,3},{2,0},{3,1},{4,6},{5,7},{6,4},{7,5},{8,10},{9,11},{10,... | collective-permute-start | bytes 1572872 | tf_op jit(solution)/shard_map/ppermute | solution.py:196
  5.5 4.7 %collective-permute-start.3 = (bf16[64,256]{1,0:T(8,128)(2,1)}, bf16[64,256]{1,0:T(8,128)(2,1)S(1)}, u32[]{:S(2)}, u32[]{:S(2)}) collective-permute-start(bf16[64,256]{1,0:T(8,128)(2,1)} %get-tuple-element.16), channel_id=1, source_target_pairs={{0,1},{1,0},{2,3},{3,2},{4,5},{5,4},{6,7},{7,6},{8,9},{9,8},{10,11... | collective-permute-start | bytes 98312 | tf_op jit(solution)/shard_map/ppermute | solution.py:196
  5.5 11.9 %collective-permute-start.4 = (bf16[64,256]{1,0:T(8,128)(2,1)}, bf16[64,256]{1,0:T(8,128)(2,1)S(1)}, u32[]{:S(2)}, u32[]{:S(2)}) collective-permute-start(bf16[64,256]{1,0:T(8,128)(2,1)} %get-tuple-element.17), channel_id=1, source_target_pairs={{0,2},{1,3},{2,0},{3,1},{4,6},{5,7},{6,4},{7,5},{8,10},{9,11},{10,... | collective-permute-start | bytes 98312 | tf_op jit(solution)/shard_map/ppermute | solution.py:196
  5.5 11.9 %collective-permute-start.5 = (bf16[64,256]{1,0:T(8,128)(2,1)}, bf16[64,256]{1,0:T(8,128)(2,1)S(1)}, u32[]{:S(2)}, u32[]{:S(2)}) collective-permute-start(bf16[64,256]{1,0:T(8,128)(2,1)} %get-tuple-element.18), channel_id=1, source_target_pairs={{0,3},{1,2},{2,1},{3,0},{4,7},{5,6},{6,5},{7,4},{8,11},{9,10},{10,... | collective-permute-start | bytes 98312 | tf_op jit(solution)/shard_map/ppermute | solution.py:196
  7.3 2.6 %collective-permute-start.13 = (s32[1,2]{1,0:T(1,128)}, s32[1,2]{1,0:T(1,128)S(1)}, u32[]{:S(2)}, u32[]{:S(2)}) collective-permute-start(s32[1,2]{1,0:T(1,128)} %param.8), channel_id=1, source_target_pairs={{0,1},{1,0},{2,3},{3,2},{4,5},{5,4},{6,7},{7,6},{8,9},{9,8},{10,11... | collective-permute-start | bytes 32 | tf_op jit(solution)/shard_map/ppermute | solution.py:196
  9.9 15.0 %collective-permute-start.18 = (bf16[64,512]{1,0:T(8,128)(2,1)}, bf16[64,512]{1,0:T(8,128)(2,1)S(1)}, u32[]{:S(2)}, u32[]{:S(2)}) collective-permute-start(bf16[64,512]{1,0:T(8,128)(2,1)} %get-tuple-element.19), channel_id=1, source_target_pairs={{0,1},{1,0},{2,3},{3,2},{4,5},{5,4},{6,7},{7,6},{8,9},{9,8},{10,11... | collective-permute-start | bytes 196616 | tf_op jit(solution)/shard_map/ppermute | solution.py:196
  10.2 16.2 %collective-permute-start.19 = (bf16[64,512]{1,0:T(8,128)(2,1)}, bf16[64,512]{1,0:T(8,128)(2,1)S(1)}, u32[]{:S(2)}, u32[]{:S(2)}) collective-permute-start(bf16[64,512]{1,0:T(8,128)(2,1)} %get-tuple-element.20), channel_id=1, source_target_pairs={{0,2},{1,3},{2,0},{3,1},{4,6},{5,7},{6,4},{7,5},{8,10},{9,11},{10,... | collective-permute-start | bytes 196616 | tf_op jit(solution)/shard_map/ppermute | solution.py:196
  17.4 10.6 %collective-permute-start.20 = (bf16[64,512]{1,0:T(8,128)(2,1)}, bf16[64,512]{1,0:T(8,128)(2,1)S(1)}, u32[]{:S(2)}, u32[]{:S(2)}) collective-permute-start(bf16[64,512]{1,0:T(8,128)(2,1)} %get-tuple-element.21), channel_id=1, source_target_pairs={{0,3},{1,2},{2,1},{3,0},{4,7},{5,6},{6,5},{7,4},{8,11},{9,10},{10,... | collective-permute-start | bytes 196616 | tf_op jit(solution)/shard_map/ppermute | solution.py:196
  17.4 4.6 %collective-permute-start.14 = (s32[1,4]{1,0:T(1,128)S(1)}, s32[1,4]{1,0:T(1,128)S(1)}, u32[]{:S(2)}, u32[]{:S(2)}) collective-permute-start(s32[1,4]{1,0:T(1,128)S(1)} %broadcast_select_fusion), channel_id=1, source_target_pairs={{0,2},{1,3},{2,0},{3,1},{4,6},{5,7},{6,4},{7,5},{8,10},{9,11},{10,... | collective-permute-start | bytes 56 | tf_op jit(solution)/shard_map/ppermute | solution.py:196
  22.0 9.6 %collective-permute-start.6 = (bf16[256,256]{1,0:T(8,128)(2,1)}, bf16[256,256]{1,0:T(8,128)(2,1)S(1)}, u32[]{:S(2)}, u32[]{:S(2)}) collective-permute-start(bf16[256,256]{1,0:T(8,128)(2,1)} %team.2.refs_4_), channel_id=1, source_target_pairs={{0,4},{1,5},{2,6},{3,7},{4,0},{5,1},{6,2},{7,3},{8,12},{9,13},{10,... | collective-permute-start | bytes 393224 | tf_op jit(solution)/shard_map/ppermute | solution.py:202
  25.0 6.7 %collective-permute-start.7 = (bf16[256,256]{1,0:T(8,128)(2,1)}, bf16[256,256]{1,0:T(8,128)(2,1)S(1)}, u32[]{:S(2)}, u32[]{:S(2)}) collective-permute-start(bf16[256,256]{1,0:T(8,128)(2,1)} %team.2.refs_4_), channel_id=1, source_target_pairs={{0,8},{8,0},{16,24},{24,16},{1,9},{9,1},{17,25},{25,17},{2,10},{10... | collective-permute-start | bytes 393224 | tf_op jit(solution)/shard_map/ppermute | solution.py:199
  26.5 6.8 %collective-permute-start.9 = (bf16[256,256]{1,0:T(8,128)(2,1)}, bf16[256,256]{1,0:T(8,128)(2,1)S(1)}, u32[]{:S(2)}, u32[]{:S(2)}) collective-permute-start(bf16[256,256]{1,0:T(8,128)(2,1)} %team.2.refs_4_), channel_id=1, source_target_pairs={{0,16},{8,24},{16,0},{24,8},{1,17},{9,25},{17,1},{25,9},{2,18},{10... | collective-permute-start | bytes 393224 | tf_op jit(solution)/shard_map/ppermute | solution.py:199
  28.0 19.7 %collective-permute-start = (bf16[128,2048]{1,0:T(8,128)(2,1)S(1)}, bf16[128,2048]{1,0:T(8,128)(2,1)S(1)}, u32[]{:S(2)}, u32[]{:S(2)}) collective-permute-start(bf16[128,2048]{1,0:T(8,128)(2,1)S(1)} %bitcast.31), channel_id=1, source_target_pairs={{0,1},{1,0},{2,3},{3,2},{4,5},{5,4},{6,7},{7,6},{8,9},{9,8},{10,11... | collective-permute-start | bytes 1572872 | tf_op jit(solution)/shard_map/ppermute | solution.py:196
  28.1 19.6 %collective-permute-start.2 = (bf16[128,2048]{1,0:T(8,128)(2,1)S(1)}, bf16[128,2048]{1,0:T(8,128)(2,1)S(1)}, u32[]{:S(2)}, u32[]{:S(2)}) collective-permute-start(bf16[128,2048]{1,0:T(8,128)(2,1)S(1)} %collective-permute-done.1.refs_2_), channel_id=1, source_target_pairs={{0,1},{1,0},{2,3},{3,2},{4,5},{5,4},{6,7},{7,6},{8,9},{9,8},{10,11... | collective-permute-start | bytes 1572872 | tf_op jit(solution)/shard_map/ppermute | solution.py:196
  31.6 14.5 %collective-permute-start.21 = (bf16[256,512]{1,0:T(8,128)(2,1)}, bf16[256,512]{1,0:T(8,128)(2,1)S(1)}, u32[]{:S(2)}, u32[]{:S(2)}) collective-permute-start(bf16[256,512]{1,0:T(8,128)(2,1)} %team.3.refs_4_), channel_id=1, source_target_pairs={{0,4},{1,5},{2,6},{3,7},{4,0},{5,1},{6,2},{7,3},{8,12},{9,13},{10,... | collective-permute-start | bytes 786440 | tf_op jit(solution)/shard_map/ppermute | solution.py:202
  31.6 5.0 %collective-permute-start.8 = (bf16[256,256]{1,0:T(8,128)(2,1)S(1)}, bf16[256,256]{1,0:T(8,128)(2,1)S(1)}, u32[]{:S(2)}, u32[]{:S(2)}) collective-permute-start(bf16[256,256]{1,0:T(8,128)(2,1)S(1)} %collective-permute-done.6.refs_5_), channel_id=1, source_target_pairs={{0,8},{8,0},{16,24},{24,16},{1,9},{9,1},{17,25},{25,17},{2,10},{10... | collective-permute-start | bytes 393224 | tf_op jit(solution)/shard_map/ppermute | solution.py:199
  33.3 5.6 %collective-permute-start.10 = (bf16[256,256]{1,0:T(8,128)(2,1)S(1)}, bf16[256,256]{1,0:T(8,128)(2,1)}, u32[]{:S(2)}, u32[]{:S(2)}) collective-permute-start(bf16[256,256]{1,0:T(8,128)(2,1)S(1)} %collective-permute-done.6.refs_5_), channel_id=1, source_target_pairs={{0,16},{8,24},{16,0},{24,8},{1,17},{9,25},{17,1},{25,9},{2,18},{10... | collective-permute-start | bytes 393224 | tf_op jit(solution)/shard_map/ppermute | solution.py:199
  36.7 5.0 %collective-permute-start.11 = (bf16[256,256]{1,0:T(8,128)(2,1)S(1)}, bf16[256,256]{1,0:T(8,128)(2,1)S(1)}, u32[]{:S(2)}, u32[]{:S(2)}) collective-permute-start(bf16[256,256]{1,0:T(8,128)(2,1)S(1)} %collective-permute-done.7.refs_6_), channel_id=1, source_target_pairs={{0,16},{8,24},{16,0},{24,8},{1,17},{9,25},{17,1},{25,9},{2,18},{10... | collective-permute-start | bytes 393224 | tf_op jit(solution)/shard_map/ppermute | solution.py:199
  38.9 8.8 %collective-permute-start.12 = (bf16[256,256]{1,0:T(8,128)(2,1)}, bf16[256,256]{1,0:T(8,128)(2,1)S(1)}, u32[]{:S(2)}, u32[]{:S(2)}) collective-permute-start(bf16[256,256]{1,0:T(8,128)(2,1)} %collective-permute-done.10.refs_9_), channel_id=1, source_target_pairs={{0,8},{8,0},{16,24},{24,16},{1,9},{9,1},{17,25},{25,17},{2,10},{10... | collective-permute-start | bytes 393224 | tf_op jit(solution)/shard_map/ppermute | solution.py:199
  41.7 25.6 %collective-permute-start.22 = (bf16[256,512]{1,0:T(8,128)(2,1)S(1)}, bf16[256,512]{1,0:T(8,128)(2,1)S(1)}, u32[]{:S(2)}, u32[]{:S(2)}) collective-permute-start(bf16[256,512]{1,0:T(8,128)(2,1)S(1)} %copy-done.4), channel_id=1, source_target_pairs={{0,8},{8,0},{16,24},{24,16},{1,9},{9,1},{17,25},{25,17},{2,10},{10... | collective-permute-start | bytes 786440 | tf_op jit(solution)/shard_map/ppermute | solution.py:199
  46.1 22.8 %collective-permute-start.25 = (bf16[256,512]{1,0:T(8,128)(2,1)S(1)}, bf16[256,512]{1,0:T(8,128)(2,1)S(1)}, u32[]{:S(2)}, u32[]{:S(2)}) collective-permute-start(bf16[256,512]{1,0:T(8,128)(2,1)S(1)} %collective-permute-done.21.refs_5_), channel_id=1, source_target_pairs={{0,16},{8,24},{16,0},{24,8},{1,17},{9,25},{17,1},{25,9},{2,18},{10... | collective-permute-start | bytes 786440 | tf_op jit(solution)/shard_map/ppermute | solution.py:199
  53.4 17.0 %collective-permute-start.15 = (bf16[512,256]{1,0:T(8,128)(2,1)}, bf16[512,256]{1,0:T(8,128)(2,1)S(1)}, u32[]{:S(2)}, u32[]{:S(2)}) collective-permute-start(bf16[512,256]{1,0:T(8,128)(2,1)} %project_kv.1.refs_0_), channel_id=1, source_target_pairs={{0,4},{1,5},{2,6},{3,7},{4,0},{5,1},{6,2},{7,3},{8,12},{9,13},{10,... | collective-permute-start | bytes 786440 | tf_op jit(solution)/shard_map/ppermute | solution.py:202
  54.0 17.0 %collective-permute-start.16 = (bf16[512,256]{1,0:T(8,128)(2,1)}, bf16[512,256]{1,0:T(8,128)(2,1)S(1)}, u32[]{:S(2)}, u32[]{:S(2)}) collective-permute-start(bf16[512,256]{1,0:T(8,128)(2,1)} %project_kv.1.refs_0_), channel_id=1, source_target_pairs={{0,1},{1,0},{2,3},{3,2},{4,5},{5,4},{6,7},{7,6},{8,9},{9,8},{10,11... | collective-permute-start | bytes 786440 | tf_op jit(solution)/shard_map/ppermute | solution.py:196
  55.5 11.2 %collective-permute-start.28 = (s32[1,8]{1,0:T(1,128)S(1)}, s32[1,8]{1,0:T(1,128)S(1)}, u32[]{:S(2)}, u32[]{:S(2)}) collective-permute-start(s32[1,8]{1,0:T(1,128)S(1)} %copy-done.35), channel_id=1, source_target_pairs={{0,4},{1,5},{2,6},{3,7},{4,0},{5,1},{6,2},{7,3},{8,12},{9,13},{10,... | collective-permute-start | bytes 104 | tf_op jit(solution)/shard_map/ppermute | solution.py:202
  66.8 9.2 %collective-permute-start.24 = (bf16[256,512]{1,0:T(8,128)(2,1)S(1)}, bf16[256,512]{1,0:T(8,128)(2,1)S(1)}, u32[]{:S(2)}, u32[]{:S(2)}) collective-permute-start(bf16[256,512]{1,0:T(8,128)(2,1)S(1)} %copy-done.4), channel_id=1, source_target_pairs={{0,16},{8,24},{16,0},{24,8},{1,17},{9,25},{17,1},{25,9},{2,18},{10... | collective-permute-start | bytes 786440 | tf_op jit(solution)/shard_map/ppermute | solution.py:199
  67.3 9.3 %collective-permute-start.23 = (bf16[256,512]{1,0:T(8,128)(2,1)S(1)}, bf16[256,512]{1,0:T(8,128)(2,1)S(1)}, u32[]{:S(2)}, u32[]{:S(2)}) collective-permute-start(bf16[256,512]{1,0:T(8,128)(2,1)S(1)} %collective-permute-done.21.refs_5_), channel_id=1, source_target_pairs={{0,8},{8,0},{16,24},{24,16},{1,9},{9,1},{17,25},{25,17},{2,10},{10... | collective-permute-start | bytes 786440 | tf_op jit(solution)/shard_map/ppermute | solution.py:199
  68.9 11.7 %collective-permute-start.26 = (bf16[256,512]{1,0:T(8,128)(2,1)S(1)}, bf16[256,512]{1,0:T(8,128)(2,1)S(1)}, u32[]{:S(2)}, u32[]{:S(2)}) collective-permute-start(bf16[256,512]{1,0:T(8,128)(2,1)S(1)} %collective-permute-done.22.refs_6_), channel_id=1, source_target_pairs={{0,16},{8,24},{16,0},{24,8},{1,17},{9,25},{17,1},{25,9},{2,18},{10... | collective-permute-start | bytes 786440 | tf_op jit(solution)/shard_map/ppermute | solution.py:199
  70.4 10.4 %collective-permute-start.27 = (bf16[256,512]{1,0:T(8,128)(2,1)S(1)}, bf16[256,512]{1,0:T(8,128)(2,1)S(1)}, u32[]{:S(2)}, u32[]{:S(2)}) collective-permute-start(bf16[256,512]{1,0:T(8,128)(2,1)S(1)} %collective-permute-done.25.refs_9_), channel_id=1, source_target_pairs={{0,8},{8,0},{16,24},{24,16},{1,9},{9,1},{17,25},{25,17},{2,10},{10... | collective-permute-start | bytes 786440 | tf_op jit(solution)/shard_map/ppermute | solution.py:199
  76.0 29.9 %collective-permute-start.32 = (bf16[4,64,512]{2,1,0:T(8,128)(2,1)}, bf16[4,64,512]{2,1,0:T(8,128)(2,1)S(1)}, u32[]{:S(2)}, u32[]{:S(2)}) collective-permute-start(bf16[4,64,512]{2,1,0:T(8,128)(2,1)} %get-tuple-element.27), channel_id=1, source_target_pairs={{0,2},{1,3},{2,0},{3,1},{4,6},{5,7},{6,4},{7,5},{8,10},{9,11},{10,... | collective-permute-start | bytes 786440 | tf_op jit(solution)/shard_map/ppermute | solution.py:196
  92.1 7.1 %collective-permute-start.29 = (bf16[128,512]{1,0:T(8,128)(2,1)}, bf16[128,512]{1,0:T(8,128)(2,1)S(1)}, u32[]{:S(2)}, u32[]{:S(2)}) collective-permute-start(bf16[128,512]{1,0:T(8,128)(2,1)} %get-tuple-element.23), channel_id=1, source_target_pairs={{0,1},{1,0},{2,3},{3,2},{4,5},{5,4},{6,7},{7,6},{8,9},{9,8},{10,11... | collective-permute-start | bytes 393224 | tf_op jit(solution)/shard_map/ppermute | solution.py:196
  97.3 6.6 %collective-permute-start.30 = (bf16[128,512]{1,0:T(8,128)(2,1)}, bf16[128,512]{1,0:T(8,128)(2,1)S(1)}, u32[]{:S(2)}, u32[]{:S(2)}) collective-permute-start(bf16[128,512]{1,0:T(8,128)(2,1)} %get-tuple-element.24), channel_id=1, source_target_pairs={{0,2},{1,3},{2,0},{3,1},{4,6},{5,7},{6,4},{7,5},{8,10},{9,11},{10,... | collective-permute-start | bytes 393224 | tf_op jit(solution)/shard_map/ppermute | solution.py:196
  97.4 8.5 %collective-permute-start.31 = (bf16[128,512]{1,0:T(8,128)(2,1)}, bf16[128,512]{1,0:T(8,128)(2,1)S(1)}, u32[]{:S(2)}, u32[]{:S(2)}) collective-permute-start(bf16[128,512]{1,0:T(8,128)(2,1)} %get-tuple-element.25), channel_id=1, source_target_pairs={{0,3},{1,2},{2,1},{3,0},{4,7},{5,6},{6,5},{7,4},{8,11},{9,10},{10,... | collective-permute-start | bytes 393224 | tf_op jit(solution)/shard_map/ppermute | solution.py:196
  (37 other events, 199.3 us)

commit v2 on v1

v2 whole, which is shorter than its diff:
```python
import functools

import jax
import jax.numpy as jnp
from jax import lax
from jax.experimental import pallas as pl
from jax.experimental.pallas import tpu as pltpu
from jax.sharding import PartitionSpec as P

H = 8
KVH = 2
HD = 256
TEAM = 4
ROPE_BASE = 1000000.0
NORM_EPS = 1e-06
MIB = 1024 * 1024

ANY = pl.BlockSpec(memory_space=pl.ANY)
VMEM = pl.BlockSpec(memory_space=pltpu.VMEM)
SMEM = pl.BlockSpec(memory_space=pltpu.SMEM)


def params(mib):
    return pltpu.CompilerParams(vmem_limit_bytes=mib * MIB)


def place():
    blk = lax.axis_index("blk")
    return lax.axis_index("req"), (blk // 2) % 2, blk % 2


def run(copies):
    for copy in copies:
        copy.start()
    for copy in copies:
        copy.wait()


def aligned(index, size):
    return pl.ds(pl.multiple_of(index * size, size), size)


def project_kernel(steps, n_pieces, is_kv, *refs):
    tokens, refs = refs[: len(steps)], refs[len(steps) :]
    weights, refs = refs[:n_pieces], refs[n_pieces:]
    gain_ref, cos_ref, sin_ref, out, x_all, w_all, x_sem, w_sem = refs
    req, pair, core = place()
    member = pair * 2 + core
    rows = tokens[0].shape[0]
    copies = []
    for i, k in enumerate(steps):
        slot = member ^ k if is_kv else i
        copies.append(pltpu.make_async_copy(tokens[i], x_all.at[aligned(slot, rows), :], x_sem.at[i]))
    depth = weights[0].shape[0]
    n_req = w_all.shape[0] // depth
    for i in range(n_pieces):
        part = slice(i // n_req * HD, (i // n_req + 1) * HD)
        copies.append(
            pltpu.make_async_copy(
                weights[i], w_all.at[aligned(req ^ (i % n_req), depth), part], w_sem.at[i]
            )
        )
    run(copies)
    half = HD // 2
    gain = gain_ref[...]
    if is_kv:
        cosine, sine = cos_ref[...], sin_ref[...]
        is_key = core == 0
        cosine = jnp.where(is_key, cosine, 1.0)
        sine = jnp.where(is_key, sine, 0.0)
        gain = jnp.where(is_key, gain, 1.0)
    else:
        cosine = jnp.concatenate([cos_ref[aligned(member ^ k, rows), :] for k in steps], 0)
        sine = jnp.concatenate([sin_ref[aligned(member ^ k, rows), :] for k in steps], 0)
    product = jnp.dot(x_all[...], w_all[...], preferred_element_type=jnp.float32)
    for h in range(out.shape[1] // HD):
        head = product[:, h * HD : (h + 1) * HD]
        mean = jnp.mean(head * head, axis=-1, keepdims=True)
        head = head * lax.rsqrt(mean + NORM_EPS) * gain
        front, second = head[:, :half], head[:, half:]
        out[:, h * HD : h * HD + half] = (front * cosine - second * sine).astype(jnp.bfloat16)
        out[:, h * HD + half : (h + 1) * HD] = (second * cosine + front * sine).astype(jnp.bfloat16)


def load_kv(n_out, blk_rows, mine, other, ids_ref, store, sems, core):
    per_piece = mine[0].shape[0] // blk_rows
    copies = []
    for k in range(n_out):
        for j in range(per_piece):
            n = k * per_piece + j
            there = aligned(ids_ref[n], blk_rows)
            here = pl.ds(j * blk_rows, blk_rows)
            copies.append(pltpu.make_async_copy(mine[k].at[here, :], store.at[core, there, :], sems.at[0, n]))
            copies.append(pltpu.make_async_copy(other[k].at[here, :], store.at[1 - core, there, :], sems.at[1, n]))
    run(copies)


def attend_kernel(n_out, blk_rows, step, *refs):
    mine, other = refs[:n_out], refs[n_out : 2 * n_out]
    q_ref, near_ref, ids_ref, length_ref, out, store, sems = refs[2 * n_out :]
    _, pair, core = place()
    load_kv(n_out, blk_rows, mine, other, ids_ref, store, sems, core)
    length = length_ref[0]
    rows = out.shape[0]
    member = (pair * 2 + core) ^ step
    total = store.shape[1]
    quarter = total // 4
    heads = 2 * (out.shape[1] // (2 * HD))
    first = step // 2 * rows
    for j in range(rows // blk_rows):
        block = ids_ref[member * (rows // blk_rows) + j]
        here = slice(first + j * blk_rows, first + (j + 1) * blk_rows)
        there = slice(j * blk_rows, (j + 1) * blk_rows)
        for variant in range(4):
            seen = (variant + 1) * quarter

            @pl.when((block * blk_rows) // quarter == variant)
            def _():
                queries = jnp.concatenate(
                    [ref[here, h * HD : (h + 1) * HD] for ref in (q_ref, near_ref) for h in range(heads // 2)], 0
                )
                shape = (heads * blk_rows, 1)
                query_pos = block * blk_rows + lax.rem(lax.broadcasted_iota(jnp.int32, shape, 0), blk_rows)
                limit = jnp.minimum(query_pos, length - 1)
                key_pos = lax.broadcasted_iota(jnp.int32, (1, seen), 1)
                scores = lax.dot_general(
                    queries,
                    store[0, :seen, :],
                    (((1,), (1,)), ((), ())),
                    preferred_element_type=jnp.float32,
                )
                scores = jnp.where(key_pos <= limit, scores, jnp.finfo(jnp.float32).min)
                weights = jnp.exp(scores - jnp.max(scores, axis=-1, keepdims=True))
                row_sum = jnp.sum(weights, axis=-1, keepdims=True)
                summed = jnp.dot(
                    weights.astype(jnp.bfloat16), store[1, :seen, :], preferred_element_type=jnp.float32
                )
                result = jnp.where(query_pos < length, summed / row_sum, 0.0).astype(jnp.bfloat16)
                for n in range(heads):
                    side = core if n < heads // 2 else 1 - core
                    column = side * (heads // 2) + n % (heads // 2)
                    out[there, aligned(column, HD)] = result[n * blk_rows : (n + 1) * blk_rows]


def pages_kernel(n_out, blk_rows, *refs):
    mine, other = refs[:n_out], refs[n_out : 2 * n_out]
    ids_ref, info_ref, own, away, store, sems = refs[2 * n_out :]
    _, _, core = place()
    load_kv(n_out, blk_rows, mine, other, ids_ref, store, sems, core)
    slots = own.shape[0]
    row = lax.broadcasted_iota(jnp.int32, (blk_rows, HD), 0)
    for target, base in ((own, 0), (away, slots)):
        for i in range(slots):
            here = aligned(info_ref[1, base + i], blk_rows)
            live = row < info_ref[2, base + i]
            for half in range(2):
                page = store[half, here, :]
                target[i, :, half * HD : (half + 1) * HD] = jnp.where(live, page, jnp.zeros_like(page))


def finish_kernel(kept, from_far, own_pages, got_pages, info_ref, att_out, page_out, sems):
    _, pair, _ = place()
    width = kept.shape[1]
    copies = [
        pltpu.make_async_copy(kept, att_out.at[:, aligned(pair, width)], sems.at[0]),
        pltpu.make_async_copy(from_far, att_out.at[:, aligned(1 - pair, width)], sems.at[1]),
    ]
    for copy in copies:
        copy.start()
    for i in range(page_out.shape[0]):
        here = info_ref[0, i] == pair
        ours = pltpu.make_async_copy(own_pages.at[i], page_out.at[i], sems.at[2 + i])
        theirs = pltpu.make_async_copy(got_pages.at[i], page_out.at[i], sems.at[2 + i])
        copies.append(ours)

        @pl.when(here)
        def _():
            ours.start()

        @pl.when(jnp.logical_not(here))
        def _():
            theirs.start()

    for copy in copies:
        copy.wait()


def body(tokens, block_ids, lengths, page_table, qkv_weight, q_gain, k_gain):
    n_req, n_blk = lax.axis_size("req"), lax.axis_size("blk")
    n_out = n_blk // TEAM
    bf16 = jnp.bfloat16
    shape = jax.ShapeDtypeStruct
    blk = lax.axis_index("blk")
    member = blk % TEAM

    def in_team(array, k):
        return lax.ppermute(array, "blk", [(i, i ^ k) for i in range(n_blk)])

    def in_req(array, k):
        return lax.ppermute(array, "req", [(i, i ^ k) for i in range(n_req)])

    def across(array, k):
        return lax.ppermute(array, "blk", [(i, (i + TEAM * k) % n_blk) for i in range(n_blk)])

    blk_rows = tokens.shape[1] // block_ids.shape[1]

    def join(array, bit):
        got = in_team(array, bit)
        low = member & bit == 0
        return jnp.where(low, jnp.concatenate([array, got], 1), jnp.concatenate([got, array], 1))

    team_ids = join(join(block_ids, 1), 2)
    all_ids = jnp.concatenate([team_ids] + [across(team_ids, k) for k in range(1, n_out)], 1)[0]

    w_rows = qkv_weight.shape[0]
    q_part = qkv_weight[:, : H * HD].reshape(w_rows, 2, 2, 2, HD).transpose(3, 1, 2, 0, 4)
    kv_part = qkv_weight[:, H * HD :].reshape(w_rows, 2, 2, HD).transpose(2, 1, 0, 3)

    def to_columns(part):
        part = jnp.broadcast_to(part[None], (n_out,) + part.shape).reshape(n_blk * w_rows, HD)
        return lax.all_to_all(part, "blk", split_axis=0, concat_axis=0, tiled=True)

    def to_prompts(piece, share):
        rows = piece.shape[0]
        cut = rows * share // 4
        one, two = in_req(piece, 1), in_req(piece, 2)
        if cut == rows:
            return [piece, one, two, in_req(one, 2)]
        if cut == 0:
            return [piece, one, two, in_req(two, 1)]
        return [piece, one, two, jnp.concatenate([in_req(one[:cut], 2), in_req(two[cut:], 1)], 0)]

    kv_pieces = to_prompts(to_columns(kv_part), 4)
    q_pieces = to_prompts(to_columns(q_part[0]), 0) + to_prompts(to_columns(q_part[1]), 2)

    own = tokens[0]
    rows = own.shape[0]
    own, all_ids = lax.optimization_barrier((own, all_ids))
    far = in_team(own, 2)
    team_tokens = [own, in_team(own, 1), far, in_team(far, 1)]

    offsets = jnp.arange(blk_rows, dtype=jnp.int32)
    positions = (team_ids[0][:, None] * blk_rows + offsets[None, :]).reshape(-1, 1)
    inverse = jnp.power(jnp.float32(ROPE_BASE), -2.0 * jnp.arange(HD // 2).astype(jnp.float32) / HD)
    angles = positions.astype(jnp.float32) * inverse[None, :]
    cosine, sine = jnp.cos(angles), jnp.sin(angles)

    def project(steps, pieces, is_kv, gain):
        width = len(pieces) // n_req * HD
        depth = own.shape[1]
        return pl.pallas_call(
            functools.partial(project_kernel, steps, len(pieces), is_kv),
            out_shape=shape((len(steps) * rows, width), bf16),
            in_specs=[ANY] * (len(steps) + len(pieces)) + [VMEM] * 3,
            out_specs=VMEM,
            scratch_shapes=[
                pltpu.VMEM((len(steps) * rows, depth), bf16),
                pltpu.VMEM((depth, width), bf16),
                pltpu.SemaphoreType.DMA((len(steps),)),
                pltpu.SemaphoreType.DMA((len(pieces),)),
            ],
            cost_estimate=pl.CostEstimate(
                flops=2 * len(steps) * rows * depth * width, bytes_accessed=6 * MIB, transcendentals=0
            ),
            compiler_params=params(12),
            name="project_kv" if is_kv else "project_q",
        )(*[team_tokens[k] for k in steps], *pieces, gain[None, :], cosine, sine)

    made = project((0, 1, 2, 3), kv_pieces, True, k_gain)
    mine = [made] + [across(made, k) for k in range(1, n_out)]
    other = [in_team(part, 1) for part in mine]

    from_near = in_team(project((1, 3), q_pieces, False, q_gain), 1)
    queries = project((0, 2), q_pieces, False, q_gain)

    table = page_table[0].reshape(-1)
    per_head = page_table.shape[2]
    slot_count = page_table.shape[1] * per_head // n_blk
    wanted = jnp.concatenate(
        [b * slot_count + jnp.arange(slot_count, dtype=jnp.int32) for b in (blk, blk ^ 2)]
    )
    flat = jnp.sum(
        jnp.where(wanted[:, None] == table[None, :], jnp.arange(table.shape[0], dtype=jnp.int32)[None, :], 0), 1
    )
    block = flat % per_head
    info = jnp.stack([flat // per_head, block, lengths[0] - block * blk_rows])

    total = TEAM * rows * n_out
    store = [pltpu.VMEM((2, total, HD), bf16), pltpu.SemaphoreType.DMA((2, total // blk_rows))]
    store_mib = -(-2 * total * HD * 2 // MIB)
    page_shape = shape((slot_count, blk_rows, 2 * HD), bf16)
    own_pages, away_pages = pl.pallas_call(
        functools.partial(pages_kernel, n_out, blk_rows),
        out_shape=[page_shape, page_shape],
        in_specs=[ANY] * (2 * n_out) + [SMEM] * 2,
        out_specs=[VMEM, VMEM],
        scratch_shapes=store,
        cost_estimate=pl.CostEstimate(flops=0, bytes_accessed=4 * MIB, transcendentals=0),
        compiler_params=params(store_mib + 4),
        name="pages",
    )(*mine, *other, all_ids, info)
    got_pages = in_team(away_pages, 2)

    def attend(step):
        return pl.pallas_call(
            functools.partial(attend_kernel, n_out, blk_rows, step),
            out_shape=shape((rows, H // 2 * HD), bf16),
            in_specs=[ANY] * (2 * n_out) + [VMEM] * 2 + [SMEM] * 2,
            out_specs=VMEM,
            scratch_shapes=store,
            cost_estimate=pl.CostEstimate(
                flops=2 * H * HD * rows * total, bytes_accessed=4 * MIB, transcendentals=0
            ),
            compiler_params=params(store_mib + 4 + 4 * total // 1024),
            name="attend",
        )(*mine, *other, queries, from_near, all_ids, lengths)

    from_far = in_team(attend(2), 2)
    kept = attend(0)

    attended, pages = pl.pallas_call(
        finish_kernel,
        out_shape=[shape((rows, H * HD), bf16), page_shape],
        in_specs=[ANY] * 4 + [SMEM],
        out_specs=[ANY] * 2,
        scratch_shapes=[pltpu.SemaphoreType.DMA((2 + slot_count,))],
        compiler_params=params(1),
        name="finish",
    )(kept, from_far, own_pages, got_pages, info)
    return attended[None], pages[None]


def solution(mesh):
    in_specs = (
        P("req", "blk", None),
        P("req", "blk"),
        P("req"),
        P("req", None, None),
        P(("req", "blk"), None),
        P(),
        P(),
    )
    out_specs = (P("req", "blk", None), P("req", "blk", None, None))
    return jax.shard_map(body, mesh=mesh, in_specs=in_specs, out_specs=out_specs, check_vma=False)
```

time: 109 us -> 110 us (level)
  Pallas kernels: 30.5 us -> 16.6 us
  waiting for transfers between devices: 33.1 us -> 43.6 us
  starting transfers between devices: 32.3 us -> 40.3 us
  other arithmetic: 4.55 us -> 1.72 us
    all_to_all x0 -> x3, starting transfers between devices: none -> 14.8 us  [to_columns(): return lax.all_to_all(part, 'blk', split_axis=0, concat_axis=0, tiled=True)]
    pallas_call x7 -> x5, Pallas kernels: 25.5 us -> 12.6 us  [the longest x2 8 us: attend(): pl.pallas_call(functools.partial(attend_kernel, n_out, blk_rows, step), o...]
    all_to_all x0 -> x3, waiting for transfers between devices: none -> 9.61 us  [to_columns(): return lax.all_to_all(part, 'blk', split_axis=0, concat_axis=0, tiled=True)]
    ppermute x17 -> x10, starting transfers between devices: 10.5 us -> 5.58 us  [in_team(): return lax.ppermute(array, 'blk', [(i, i ^ k) for i in range(n_blk)])]
    unnamed x72 -> x15, local copies, waits for them, and re-layouts: 4.48 us -> 1.42 us
    ppermute x12 -> x10, waiting for transfers between devices: 7.2 us -> 10.2 us  [in_req(): return lax.ppermute(array, 'req', [(i, i ^ k) for i in range(n_req)])]
    ppermute x12 -> x10, starting transfers between devices: 15.9 us -> 13.3 us  [in_req(): return lax.ppermute(array, 'req', [(i, i ^ k) for i in range(n_req)])]
    broadcast_in_dim x0 -> x4, local copies, waits for them, and re-layouts: none -> 2.24 us  [to_columns(): jnp.broadcast_to(part[None], (n_out,) + part.shape)]
  transfers between devices with their start and end apart: 33 -> 25, of which waited for: 13 -> 14; matrix products, arithmetic and copies ran while one was open for 6% -> 4% of each run, Pallas kernels for 26% -> 10%
where the time goes in v2:
time: 110 us
  waiting for transfers between devices  43.6 us (40%)
  starting transfers between devices  40.3 us (37%)
  Pallas kernels  16.6 us (15%)
  local copies, waits for them, and re-layouts  5.82 us (5%)
  between operations  1.74 us (2%)
  other arithmetic  1.72 us (2%)
    all_to_all x3, starting transfers between devices, to_columns(): return lax.all_to_all(part, 'blk', split_axis=0, concat_axis=0, tiled=True)  14.8 us
    ppermute x10, starting transfers between devices, in_req(): return lax.ppermute(array, 'req', [(i, i ^ k) for i in range(n_req)])  13.3 us
    ppermute x10, waiting for transfers between devices, in_team(): return lax.ppermute(array, 'blk', [(i, i ^ k) for i in range(n_blk)])  13 us
    ppermute x2, waiting for transfers between devices, across(): lax.ppermute(array, 'blk', [(i, (i + TEAM * k) % n_blk) for i in range(n_...  10.9 us
    ppermute x10, waiting for transfers between devices, in_req(): return lax.ppermute(array, 'req', [(i, i ^ k) for i in range(n_req)])  10.2 us
    all_to_all x3, waiting for transfers between devices, to_columns(): return lax.all_to_all(part, 'blk', split_axis=0, concat_axis=0, tiled=True)  9.61 us
    pallas_call x2, Pallas kernels, attend(): pl.pallas_call(functools.partial(attend_kernel, n_out, blk_rows, step), o...  8 us
    ppermute x2, starting transfers between devices, across(): lax.ppermute(array, 'blk', [(i, (i + TEAM * k) % n_blk) for i in range(n_...  6.64 us
  transfers between devices with their start and end apart: 25, of which 14 were waited for; matrix products, arithmetic and copies ran while one was open for 4% of the time, Pallas kernels for 10%

profile of v2, /device:TPU:0, one launch (start us, length us, event | category | flops | bytes accessed | tf_op | source)
XLA Modules:
  0.0 109.8 jit_solution(11188762161618698321)
XLA Ops:
  2.4 6.3 %all-to-all-start = ((bf16[8,64,256]{2,1,0:T(8,128)(2,1)}), bf16[8,64,256]{2,1,0:T(8,128)(2,1)}, u32[]{:S(2)}, u32[]{:S(2)}) async-start(bf16[8,64,256]{2,1,0:T(8,128)(2,1)} %bitcast.6), calls=%async_computation | async-start | bytes 524288 | tf_op jit(solution)/shard_map/all_to_all | solution.py:221
  10.3 8.2 %all-to-all-done = bf16[8,64,256]{2,1,0:T(8,128)(2,1)} async-done(((bf16[8,64,256]{2,1,0:T(8,128)(2,1)}), bf16[8,64,256]{2,1,0:T(8,128)(2,1)}, u32[]{:S(2)}, u32[]{:S(2)}) %all-to-all-start) | async-done | bytes 262176 | tf_op jit(solution)/shard_map/all_to_all | solution.py:221
  19.3 3.5 %all-to-all-start.2 = ((bf16[8,64,256]{2,1,0:T(8,128)(2,1)}), bf16[8,64,256]{2,1,0:T(8,128)(2,1)S(1)}, u32[]{:S(2)}, u32[]{:S(2)}) async-start(bf16[8,64,256]{2,1,0:T(8,128)(2,1)} %bitcast.15), calls=%async_computation.2 | async-start | bytes 524288 | tf_op jit(solution)/shard_map/all_to_all | solution.py:221
  22.9 1.9 %collective-permute-start.1 = (s32[1,4]{1,0:T(1,128)S(1)}, s32[1,4]{1,0:T(1,128)S(1)}, u32[]{:S(2)}, u32[]{:S(2)}) collective-permute-start(s32[1,4]{1,0:T(1,128)S(1)} %broadcast_select_fusion.1), channel_id=1, source_target_pairs={{0,2},{1,3},{2,0},{3,1},{4,6},{5,7},{6,4},{7,5},{8,10},{9,11},{10,... | collective-permute-start | bytes 56 | tf_op jit(solution)/shard_map/ppermute | solution.py:197
  24.9 3.2 %collective-permute-done.1 = s32[1,4]{1,0:T(1,128)S(1)} collective-permute-done((s32[1,4]{1,0:T(1,128)S(1)}, s32[1,4]{1,0:T(1,128)S(1)}, u32[]{:S(2)}, u32[]{:S(2)}) %collective-permute-start.1) | collective-permute-done | bytes 48 | tf_op jit(solution)/shard_map/ppermute | solution.py:197
  28.2 4.4 %collective-permute-start.2 = (s32[1,8]{1,0:T(1,128)S(1)}, s32[1,8]{1,0:T(1,128)S(1)}, u32[]{:S(2)}, u32[]{:S(2)}) collective-permute-start(s32[1,8]{1,0:T(1,128)S(1)} %broadcast_select_fusion.3), channel_id=1, source_target_pairs={{0,4},{1,5},{2,6},{3,7},{4,0},{5,1},{6,2},{7,3},{8,12},{9,13},{10,... | collective-permute-start | bytes 104 | tf_op jit(solution)/shard_map/ppermute | solution.py:203
  32.7 1.5 %collective-permute-done.2 = s32[1,8]{1,0:T(1,128)S(1)} collective-permute-done((s32[1,8]{1,0:T(1,128)S(1)}, s32[1,8]{1,0:T(1,128)S(1)}, u32[]{:S(2)}, u32[]{:S(2)}) %collective-permute-start.2) | collective-permute-done | bytes 64 | tf_op jit(solution)/shard_map/ppermute | solution.py:203
  35.8 4.9 %all-to-all-start.1 = ((bf16[8,64,256]{2,1,0:T(8,128)(2,1)}), bf16[8,64,256]{2,1,0:T(8,128)(2,1)S(1)}, u32[]{:S(2)}, u32[]{:S(2)}) async-start(bf16[8,64,256]{2,1,0:T(8,128)(2,1)} %bitcast.12), calls=%async_computation.1 | async-start | bytes 524288 | tf_op jit(solution)/shard_map/all_to_all | solution.py:221
  40.8 1.6 %collective-permute-start.6 = (bf16[512,256]{1,0:T(8,128)(2,1)}, bf16[512,256]{1,0:T(8,128)(2,1)S(1)}, u32[]{:S(2)}, u32[]{:S(2)}) collective-permute-start(bf16[512,256]{1,0:T(8,128)(2,1)} %bitcast.7.refs_4_), channel_id=1, source_target_pairs={{0,8},{8,0},{16,24},{24,16},{1,9},{9,1},{17,25},{25,17},{2,10},{10... | collective-permute-start | bytes 786440 | tf_op jit(solution)/shard_map/ppermute | solution.py:200
  43.9 1.6 %collective-permute-start.16 = (bf16[512,256]{1,0:T(8,128)(2,1)S(1)}, bf16[512,256]{1,0:T(8,128)(2,1)S(1)}, u32[]{:S(2)}, u32[]{:S(2)}) collective-permute-start(bf16[512,256]{1,0:T(8,128)(2,1)S(1)} %bitcast.43), channel_id=1, source_target_pairs={{0,16},{8,24},{16,0},{24,8},{1,17},{9,25},{17,1},{25,9},{2,18},{10... | collective-permute-start | bytes 786440 | tf_op jit(solution)/shard_map/ppermute | solution.py:200
  45.5 4.0 %collective-permute-done.4.refs_2_.refs_1_ = bf16[128,2048]{1,0:T(8,128)(2,1)S(1)} collective-permute-done((bf16[128,2048]{1,0:T(8,128)(2,1)S(1)}, bf16[128,2048]{1,0:T(8,128)(2,1)S(1)}, u32[]{:S(2)}, u32[]{:S(2)}) %collective-permute-start.4) | collective-permute-done | bytes 524320 | tf_op jit(solution)/shard_map/ppermute | solution.py:197
  49.5 1.5 %collective-permute-start.7 = (bf16[512,256]{1,0:T(8,128)(2,1)}, bf16[512,256]{1,0:T(8,128)(2,1)}, u32[]{:S(2)}, u32[]{:S(2)}) collective-permute-start(bf16[512,256]{1,0:T(8,128)(2,1)} %bitcast.7.refs_4_), channel_id=1, source_target_pairs={{0,16},{8,24},{16,0},{24,8},{1,17},{9,25},{17,1},{25,9},{2,18},{10... | collective-permute-start | bytes 786440 | tf_op jit(solution)/shard_map/ppermute | solution.py:200
  51.0 1.4 %all-to-all-done.1 = bf16[8,64,256]{2,1,0:T(8,128)(2,1)S(1)} async-done(((bf16[8,64,256]{2,1,0:T(8,128)(2,1)}), bf16[8,64,256]{2,1,0:T(8,128)(2,1)S(1)}, u32[]{:S(2)}, u32[]{:S(2)}) %all-to-all-start.1) | async-done | bytes 262176 | tf_op jit(solution)/shard_map/all_to_all | solution.py:221
  53.1 1.5 %collective-permute-start.13 = (bf16[512,256]{1,0:T(8,128)(2,1)S(1)}, bf16[512,256]{1,0:T(8,128)(2,1)S(1)}, u32[]{:S(2)}, u32[]{:S(2)}) collective-permute-start(bf16[512,256]{1,0:T(8,128)(2,1)S(1)} %bitcast.46), channel_id=1, source_target_pairs={{0,16},{8,24},{16,0},{24,8},{1,17},{9,25},{17,1},{25,9},{2,18},{10... | collective-permute-start | bytes 786440 | tf_op jit(solution)/shard_map/ppermute | solution.py:200
  55.4 1.5 %collective-permute-start.8 = (bf16[512,256]{1,0:T(8,128)(2,1)}, bf16[512,256]{1,0:T(8,128)(2,1)}, u32[]{:S(2)}, u32[]{:S(2)}) collective-permute-start(bf16[512,256]{1,0:T(8,128)(2,1)} %copy-done.1), channel_id=1, source_target_pairs={{0,16},{8,24},{16,0},{24,8},{1,17},{9,25},{17,1},{25,9},{2,18},{10... | collective-permute-start | bytes 786440 | tf_op jit(solution)/shard_map/ppermute | solution.py:200
  57.7 1.0 multiply_sine_fusion
  58.9 1.5 %collective-permute-start.12 = (bf16[512,256]{1,0:T(8,128)(2,1)S(1)}, bf16[512,256]{1,0:T(8,128)(2,1)S(1)}, u32[]{:S(2)}, u32[]{:S(2)}) collective-permute-start(bf16[512,256]{1,0:T(8,128)(2,1)S(1)} %bitcast.47), channel_id=1, source_target_pairs={{0,8},{8,0},{16,24},{24,16},{1,9},{9,1},{17,25},{25,17},{2,10},{10... | collective-permute-start | bytes 786440 | tf_op jit(solution)/shard_map/ppermute | solution.py:200
  60.4 4.0 %collective-permute-done.13.refs_4_ = bf16[512,256]{1,0:T(8,128)(2,1)S(1)} collective-permute-done((bf16[512,256]{1,0:T(8,128)(2,1)S(1)}, bf16[512,256]{1,0:T(8,128)(2,1)S(1)}, u32[]{:S(2)}, u32[]{:S(2)}) %collective-permute-start.13) | collective-permute-done | bytes 262176 | tf_op jit(solution)/shard_map/ppermute | solution.py:200
  64.4 1.5 %collective-permute-start.18 = (bf16[256,256]{1,0:T(8,128)(2,1)S(1)}, bf16[256,256]{1,0:T(8,128)(2,1)S(1)}, u32[]{:S(2)}, u32[]{:S(2)}) collective-permute-start(bf16[256,256]{1,0:T(8,128)(2,1)S(1)} %slice.27), channel_id=1, source_target_pairs={{0,8},{8,0},{16,24},{24,16},{1,9},{9,1},{17,25},{25,17},{2,10},{10... | collective-permute-start | bytes 393224 | tf_op jit(solution)/shard_map/ppermute | solution.py:200
  65.9 4.2 %collective-permute-done.8.refs_7_ = bf16[512,256]{1,0:T(8,128)(2,1)} collective-permute-done((bf16[512,256]{1,0:T(8,128)(2,1)}, bf16[512,256]{1,0:T(8,128)(2,1)}, u32[]{:S(2)}, u32[]{:S(2)}) %collective-permute-start.8) | collective-permute-done | bytes 262176 | tf_op jit(solution)/shard_map/ppermute | solution.py:200
  70.2 1.5 %collective-permute-start.14 = (bf16[512,256]{1,0:T(8,128)(2,1)S(1)}, bf16[512,256]{1,0:T(8,128)(2,1)S(1)}, u32[]{:S(2)}, u32[]{:S(2)}) collective-permute-start(bf16[512,256]{1,0:T(8,128)(2,1)S(1)} %collective-permute-done.13.refs_4_), channel_id=1, source_target_pairs={{0,8},{8,0},{16,24},{24,16},{1,9},{9,1},{17,25},{25,17},{2,10},{10... | collective-permute-start | bytes 786440 | tf_op jit(solution)/shard_map/ppermute | solution.py:200
  72.3 2.1 %project_kv.1.refs_0_ = bf16[512,256]{1,0:T(8,128)(2,1)S(1)} custom-call(bf16[128,2048]{1,0:T(8,128)(2,1)S(1)} %bitcast.52, bf16[128,2048]{1,0:T(8,128)(2,1)S(1)} %collective-permute-done.3.refs_1_.refs_0_, bf16[128,2048]{1,0:T(8,128)(2,1)S(1)} %collective-permute-done.4.refs_2_.refs_1_, bf16[128,2048]{1,0:T(8,128)(2,1)S(1)} %collective-permute-done.5.refs_3_.refs_1_, ...), custom_call_target="tpu_custom_call" | custom-call | flops 536870912 | bytes 6291456 | tf_op jit(solution)/shard_map/project_kv/pallas_call | solution.py:251
  74.5 2.2 %collective-permute-start.9 = (bf16[512,256]{1,0:T(8,128)(2,1)S(1)}, bf16[512,256]{1,0:T(8,128)(2,1)S(1)}, u32[]{:S(2)}, u32[]{:S(2)}) collective-permute-start(bf16[512,256]{1,0:T(8,128)(2,1)S(1)} %project_kv.1.refs_0_), channel_id=1, source_target_pairs={{0,4},{1,5},{2,6},{3,7},{4,0},{5,1},{6,2},{7,3},{8,12},{9,13},{10,... | collective-permute-start | bytes 786440 | tf_op jit(solution)/shard_map/ppermute | solution.py:203
  77.7 1.2 %project_q.3 = bf16[256,512]{1,0:T(8,128)(2,1)S(1)} custom-call(bf16[128,2048]{1,0:T(8,128)(2,1)S(1)} %collective-permute-done.3.refs_1_.refs_0_, bf16[128,2048]{1,0:T(8,128)(2,1)S(1)} %collective-permute-done.5.refs_3_.refs_1_, bf16[512,256]{1,0:T(8,128)(2,1)S(1)} %bitcast.48, bf16[512,256]{1,0:T(8,128)(2,1)S(1)} %collective-permute-done.12.refs_3_, ...), custom_call_target="tpu_custom_call" | custom-call | flops 536870912 | bytes 6291456 | tf_op jit(solution)/shard_map/project_q/pallas_call | solution.py:251
  79.0 9.3 %collective-permute-done.9.refs_1_ = bf16[512,256]{1,0:T(8,128)(2,1)S(1)} collective-permute-done((bf16[512,256]{1,0:T(8,128)(2,1)S(1)}, bf16[512,256]{1,0:T(8,128)(2,1)S(1)}, u32[]{:S(2)}, u32[]{:S(2)}) %collective-permute-start.9) | collective-permute-done | bytes 262176 | tf_op jit(solution)/shard_map/ppermute | solution.py:203
  88.4 1.2 %project_q.2.refs_4_ = bf16[256,512]{1,0:T(8,128)(2,1)S(1)} custom-call(bf16[128,2048]{1,0:T(8,128)(2,1)S(1)} %bitcast.53, bf16[128,2048]{1,0:T(8,128)(2,1)S(1)} %collective-permute-done.4.refs_2_.refs_1_, bf16[512,256]{1,0:T(8,128)(2,1)S(1)} %bitcast.49, bf16[512,256]{1,0:T(8,128)(2,1)S(1)} %collective-permute-done.12.refs_3_, ...), custom_call_target="tpu_custom_call" | custom-call | flops 536870912 | bytes 6291456 | tf_op jit(solution)/shard_map/project_q/pallas_call | solution.py:251
  89.9 4.1 %attend.3 = bf16[128,1024]{1,0:T(8,128)(2,1)S(1)} custom-call(bf16[512,256]{1,0:T(8,128)(2,1)S(1)} %project_kv.1.refs_0_, bf16[512,256]{1,0:T(8,128)(2,1)S(1)} %collective-permute-done.9.refs_1_, bf16[512,256]{1,0:T(8,128)(2,1)S(1)} %collective-permute-done.10.refs_2_, bf16[512,256]{1,0:T(8,128)(2,1)S(1)} %collective-permute-done.11.refs_3_, ...), custom_call_target="tpu_custom_call" | custom-call | flops 536870912 | bytes 4194304 | tf_op jit(solution)/shard_map/attend/pallas_call | solution.py:305
  94.3 2.5 %pages.1 = (bf16[4,64,512]{2,1,0:T(8,128)(2,1)S(1)}, bf16[4,64,512]{2,1,0:T(8,128)(2,1)S(1)}) custom-call(bf16[512,256]{1,0:T(8,128)(2,1)S(1)} %project_kv.1.refs_0_, bf16[512,256]{1,0:T(8,128)(2,1)S(1)} %collective-permute-done.9.refs_1_, bf16[512,256]{1,0:T(8,128)(2,1)S(1)} %collective-permute-done.10.refs_2_, ...), custom_call_target="tpu_custom_call" | custom-call | bytes 4194304 | tf_op jit(solution)/shard_map/pages/pallas_call | solution.py:292
  96.8 1.9 %collective-permute-start.21 = (bf16[4,64,512]{2,1,0:T(8,128)(2,1)S(1)}, bf16[4,64,512]{2,1,0:T(8,128)(2,1)S(1)}, u32[]{:S(2)}, u32[]{:S(2)}) collective-permute-start(bf16[4,64,512]{2,1,0:T(8,128)(2,1)S(1)} %get-tuple-element.11), channel_id=1, source_target_pairs={{0,2},{1,3},{2,0},{3,1},{4,6},{5,7},{6,4},{7,5},{8,10},{9,11},{10,... | collective-permute-start | bytes 786440 | tf_op jit(solution)/shard_map/ppermute | solution.py:197
  98.7 3.9 %attend.2.kept = bf16[128,1024]{1,0:T(8,128)(2,1)S(1)} custom-call(bf16[512,256]{1,0:T(8,128)(2,1)S(1)} %project_kv.1.refs_0_, bf16[512,256]{1,0:T(8,128)(2,1)S(1)} %collective-permute-done.9.refs_1_, bf16[512,256]{1,0:T(8,128)(2,1)S(1)} %collective-permute-done.10.refs_2_, bf16[512,256]{1,0:T(8,128)(2,1)S(1)} %collective-permute-done.11.refs_3_, ...), custom_call_target="tpu_custom_call" | custom-call | flops 536870912 | bytes 4194304 | tf_op jit(solution)/shard_map/attend/pallas_call | solution.py:305
  103.2 4.9 %collective-permute-done.21.got_pages = bf16[4,64,512]{2,1,0:T(8,128)(2,1)S(1)} collective-permute-done((bf16[4,64,512]{2,1,0:T(8,128)(2,1)S(1)}, bf16[4,64,512]{2,1,0:T(8,128)(2,1)S(1)}, u32[]{:S(2)}, u32[]{:S(2)}) %collective-permute-start.21) | collective-permute-done | bytes 262176 | tf_op jit(solution)/shard_map/ppermute | solution.py:197
  108.1 1.5 %finish.1 = (bf16[128,2048]{1,0:T(8,128)(2,1)}, bf16[4,64,512]{2,1,0:T(8,128)(2,1)}) custom-call(bf16[128,1024]{1,0:T(8,128)(2,1)S(1)} %attend.2.kept, bf16[128,1024]{1,0:T(8,128)(2,1)S(1)} %collective-permute-done.20.from_far, bf16[4,64,512]{2,1,0:T(8,128)(2,1)S(1)} %get-tuple-element.10.own_pages, ...), custom_call_target="tpu_custom_call" | custom-call | tf_op jit(solution)/shard_map/finish/pallas_call | solution.py:321
  (70 shorter events, 12.2 us)
Async XLA Ops:
  0.6 0.9 slice-start
  0.6 22.2 %collective-permute-start = (s32[1,2]{1,0:T(1,128)}, s32[1,2]{1,0:T(1,128)S(1)}, u32[]{:S(2)}, u32[]{:S(2)}) collective-permute-start(s32[1,2]{1,0:T(1,128)} %param.8), channel_id=1, source_target_pairs={{0,1},{1,0},{2,3},{3,2},{4,5},{5,4},{6,7},{7,6},{8,9},{9,8},{10,11... | collective-permute-start | bytes 32 | tf_op jit(solution)/shard_map/ppermute | solution.py:197
  2.4 16.2 %all-to-all-start = ((bf16[8,64,256]{2,1,0:T(8,128)(2,1)}), bf16[8,64,256]{2,1,0:T(8,128)(2,1)}, u32[]{:S(2)}, u32[]{:S(2)}) async-start(bf16[8,64,256]{2,1,0:T(8,128)(2,1)} %bitcast.6), calls=%async_computation | async-start | bytes 524288 | tf_op jit(solution)/shard_map/all_to_all | solution.py:221
  8.7 0.9 slice-start.1
  10.3 24.0 %copy-start = (bf16[1,128,2048]{2,1,0:T(8,128)(2,1)S(1)}, bf16[1,128,2048]{2,1,0:T(8,128)(2,1)}, u32[]{:S(2)}) copy-start(bf16[1,128,2048]{2,1,0:T(8,128)(2,1)} %param.7) | copy-start | bytes 1572868
  19.3 3.6 %copy-start.5 = (s32[1,2]{1,0:T(1,128)S(1)}, s32[1,2]{1,0:T(1,128)}, u32[]{:S(2)}) copy-start(s32[1,2]{1,0:T(1,128)} %param.8) | copy-start | bytes 28
  19.3 15.8 %all-to-all-start.2 = ((bf16[8,64,256]{2,1,0:T(8,128)(2,1)}), bf16[8,64,256]{2,1,0:T(8,128)(2,1)S(1)}, u32[]{:S(2)}, u32[]{:S(2)}) async-start(bf16[8,64,256]{2,1,0:T(8,128)(2,1)} %bitcast.15), calls=%async_computation.2 | async-start | bytes 524288 | tf_op jit(solution)/shard_map/all_to_all | solution.py:221
  22.9 5.2 %collective-permute-start.1 = (s32[1,4]{1,0:T(1,128)S(1)}, s32[1,4]{1,0:T(1,128)S(1)}, u32[]{:S(2)}, u32[]{:S(2)}) collective-permute-start(s32[1,4]{1,0:T(1,128)S(1)} %broadcast_select_fusion.1), channel_id=1, source_target_pairs={{0,2},{1,3},{2,0},{3,1},{4,6},{5,7},{6,4},{7,5},{8,10},{9,11},{10,... | collective-permute-start | bytes 56 | tf_op jit(solution)/shard_map/ppermute | solution.py:197
  28.2 6.0 %collective-permute-start.2 = (s32[1,8]{1,0:T(1,128)S(1)}, s32[1,8]{1,0:T(1,128)S(1)}, u32[]{:S(2)}, u32[]{:S(2)}) collective-permute-start(s32[1,8]{1,0:T(1,128)S(1)} %broadcast_select_fusion.3), channel_id=1, source_target_pairs={{0,4},{1,5},{2,6},{3,7},{4,0},{5,1},{6,2},{7,3},{8,12},{9,13},{10,... | collective-permute-start | bytes 104 | tf_op jit(solution)/shard_map/ppermute | solution.py:203
  34.3 15.2 %collective-permute-start.4 = (bf16[128,2048]{1,0:T(8,128)(2,1)S(1)}, bf16[128,2048]{1,0:T(8,128)(2,1)S(1)}, u32[]{:S(2)}, u32[]{:S(2)}) collective-permute-start(bf16[128,2048]{1,0:T(8,128)(2,1)S(1)} %bitcast.50), channel_id=1, source_target_pairs={{0,2},{1,3},{2,0},{3,1},{4,6},{5,7},{6,4},{7,5},{8,10},{9,11},{10,... | collective-permute-start | bytes 1572872 | tf_op jit(solution)/shard_map/ppermute | solution.py:197
  35.1 14.4 %collective-permute-start.3 = (bf16[128,2048]{1,0:T(8,128)(2,1)S(1)}, bf16[128,2048]{1,0:T(8,128)(2,1)S(1)}, u32[]{:S(2)}, u32[]{:S(2)}) collective-permute-start(bf16[128,2048]{1,0:T(8,128)(2,1)S(1)} %bitcast.51), channel_id=1, source_target_pairs={{0,1},{1,0},{2,3},{3,2},{4,5},{5,4},{6,7},{7,6},{8,9},{9,8},{10,11... | collective-permute-start | bytes 1572872 | tf_op jit(solution)/shard_map/ppermute | solution.py:197
  35.8 16.6 %all-to-all-start.1 = ((bf16[8,64,256]{2,1,0:T(8,128)(2,1)}), bf16[8,64,256]{2,1,0:T(8,128)(2,1)S(1)}, u32[]{:S(2)}, u32[]{:S(2)}) async-start(bf16[8,64,256]{2,1,0:T(8,128)(2,1)} %bitcast.12), calls=%async_computation.1 | async-start | bytes 524288 | tf_op jit(solution)/shard_map/all_to_all | solution.py:221
  40.8 11.6 %collective-permute-start.6 = (bf16[512,256]{1,0:T(8,128)(2,1)}, bf16[512,256]{1,0:T(8,128)(2,1)S(1)}, u32[]{:S(2)}, u32[]{:S(2)}) collective-permute-start(bf16[512,256]{1,0:T(8,128)(2,1)} %bitcast.7.refs_4_), channel_id=1, source_target_pairs={{0,8},{8,0},{16,24},{24,16},{1,9},{9,1},{17,25},{25,17},{2,10},{10... | collective-permute-start | bytes 786440 | tf_op jit(solution)/shard_map/ppermute | solution.py:200
  42.3 13.1 %collective-permute-start.15 = (bf16[512,256]{1,0:T(8,128)(2,1)S(1)}, bf16[512,256]{1,0:T(8,128)(2,1)S(1)}, u32[]{:S(2)}, u32[]{:S(2)}) collective-permute-start(bf16[512,256]{1,0:T(8,128)(2,1)S(1)} %bitcast.42), channel_id=1, source_target_pairs={{0,8},{8,0},{16,24},{24,16},{1,9},{9,1},{17,25},{25,17},{2,10},{10... | collective-permute-start | bytes 786440 | tf_op jit(solution)/shard_map/ppermute | solution.py:200
  43.9 13.2 %collective-permute-start.16 = (bf16[512,256]{1,0:T(8,128)(2,1)S(1)}, bf16[512,256]{1,0:T(8,128)(2,1)S(1)}, u32[]{:S(2)}, u32[]{:S(2)}) collective-permute-start(bf16[512,256]{1,0:T(8,128)(2,1)S(1)} %bitcast.43), channel_id=1, source_target_pairs={{0,16},{8,24},{16,0},{24,8},{1,17},{9,25},{17,1},{25,9},{2,18},{10... | collective-permute-start | bytes 786440 | tf_op jit(solution)/shard_map/ppermute | solution.py:200
  49.4 22.2 %collective-permute-start.5 = (bf16[128,2048]{1,0:T(8,128)(2,1)S(1)}, bf16[128,2048]{1,0:T(8,128)(2,1)S(1)}, u32[]{:S(2)}, u32[]{:S(2)}) collective-permute-start(bf16[128,2048]{1,0:T(8,128)(2,1)S(1)} %collective-permute-done.4.refs_2_.refs_1_), channel_id=1, source_target_pairs={{0,1},{1,0},{2,3},{3,2},{4,5},{5,4},{6,7},{7,6},{8,9},{9,8},{10,11... | collective-permute-start | bytes 1572872 | tf_op jit(solution)/shard_map/ppermute | solution.py:197
  49.5 9.4 %collective-permute-start.7 = (bf16[512,256]{1,0:T(8,128)(2,1)}, bf16[512,256]{1,0:T(8,128)(2,1)}, u32[]{:S(2)}, u32[]{:S(2)}) collective-permute-start(bf16[512,256]{1,0:T(8,128)(2,1)} %bitcast.7.refs_4_), channel_id=1, source_target_pairs={{0,16},{8,24},{16,0},{24,8},{1,17},{9,25},{17,1},{25,9},{2,18},{10... | collective-permute-start | bytes 786440 | tf_op jit(solution)/shard_map/ppermute | solution.py:200
  52.4 0.7 copy-start.1
  53.1 11.3 %collective-permute-start.13 = (bf16[512,256]{1,0:T(8,128)(2,1)S(1)}, bf16[512,256]{1,0:T(8,128)(2,1)S(1)}, u32[]{:S(2)}, u32[]{:S(2)}) collective-permute-start(bf16[512,256]{1,0:T(8,128)(2,1)S(1)} %bitcast.46), channel_id=1, source_target_pairs={{0,16},{8,24},{16,0},{24,8},{1,17},{9,25},{17,1},{25,9},{2,18},{10... | collective-permute-start | bytes 786440 | tf_op jit(solution)/shard_map/ppermute | solution.py:200
  55.4 14.8 %collective-permute-start.8 = (bf16[512,256]{1,0:T(8,128)(2,1)}, bf16[512,256]{1,0:T(8,128)(2,1)}, u32[]{:S(2)}, u32[]{:S(2)}) collective-permute-start(bf16[512,256]{1,0:T(8,128)(2,1)} %copy-done.1), channel_id=1, source_target_pairs={{0,16},{8,24},{16,0},{24,8},{1,17},{9,25},{17,1},{25,9},{2,18},{10... | collective-permute-start | bytes 786440 | tf_op jit(solution)/shard_map/ppermute | solution.py:200
  57.1 19.6 %collective-permute-start.17 = (bf16[256,256]{1,0:T(8,128)(2,1)S(1)}, bf16[256,256]{1,0:T(8,128)(2,1)S(1)}, u32[]{:S(2)}, u32[]{:S(2)}) collective-permute-start(bf16[256,256]{1,0:T(8,128)(2,1)S(1)} %slice.26), channel_id=1, source_target_pairs={{0,16},{8,24},{16,0},{24,8},{1,17},{9,25},{17,1},{25,9},{2,18},{10... | collective-permute-start | bytes 393224 | tf_op jit(solution)/shard_map/ppermute | solution.py:200
  58.6 13.0 %copy-start.2 = (bf16[512,256]{1,0:T(8,128)(2,1)S(1)}, bf16[512,256]{1,0:T(8,128)(2,1)}, u32[]{:S(2)}) copy-start(bf16[512,256]{1,0:T(8,128)(2,1)} %copy-done.1) | copy-start | bytes 786436
  58.9 17.9 %collective-permute-start.12 = (bf16[512,256]{1,0:T(8,128)(2,1)S(1)}, bf16[512,256]{1,0:T(8,128)(2,1)S(1)}, u32[]{:S(2)}, u32[]{:S(2)}) collective-permute-start(bf16[512,256]{1,0:T(8,128)(2,1)S(1)} %bitcast.47), channel_id=1, source_target_pairs={{0,8},{8,0},{16,24},{24,16},{1,9},{9,1},{17,25},{25,17},{2,10},{10... | collective-permute-start | bytes 786440 | tf_op jit(solution)/shard_map/ppermute | solution.py:200
  64.4 12.3 %collective-permute-start.18 = (bf16[256,256]{1,0:T(8,128)(2,1)S(1)}, bf16[256,256]{1,0:T(8,128)(2,1)S(1)}, u32[]{:S(2)}, u32[]{:S(2)}) collective-permute-start(bf16[256,256]{1,0:T(8,128)(2,1)S(1)} %slice.27), channel_id=1, source_target_pairs={{0,8},{8,0},{16,24},{24,16},{1,9},{9,1},{17,25},{25,17},{2,10},{10... | collective-permute-start | bytes 393224 | tf_op jit(solution)/shard_map/ppermute | solution.py:200
  70.2 7.6 %collective-permute-start.14 = (bf16[512,256]{1,0:T(8,128)(2,1)S(1)}, bf16[512,256]{1,0:T(8,128)(2,1)S(1)}, u32[]{:S(2)}, u32[]{:S(2)}) collective-permute-start(bf16[512,256]{1,0:T(8,128)(2,1)S(1)} %collective-permute-done.13.refs_4_), channel_id=1, source_target_pairs={{0,8},{8,0},{16,24},{24,16},{1,9},{9,1},{17,25},{25,17},{2,10},{10... | collective-permute-start | bytes 786440 | tf_op jit(solution)/shard_map/ppermute | solution.py:200
  74.5 13.9 %collective-permute-start.9 = (bf16[512,256]{1,0:T(8,128)(2,1)S(1)}, bf16[512,256]{1,0:T(8,128)(2,1)S(1)}, u32[]{:S(2)}, u32[]{:S(2)}) collective-permute-start(bf16[512,256]{1,0:T(8,128)(2,1)S(1)} %project_kv.1.refs_0_), channel_id=1, source_target_pairs={{0,4},{1,5},{2,6},{3,7},{4,0},{5,1},{6,2},{7,3},{8,12},{9,13},{10,... | collective-permute-start | bytes 786440 | tf_op jit(solution)/shard_map/ppermute | solution.py:203
  76.7 1.0 copy-start.3
  76.8 12.9 %collective-permute-start.10 = (bf16[512,256]{1,0:T(8,128)(2,1)S(1)}, bf16[512,256]{1,0:T(8,128)(2,1)S(1)}, u32[]{:S(2)}, u32[]{:S(2)}) collective-permute-start(bf16[512,256]{1,0:T(8,128)(2,1)S(1)} %project_kv.1.refs_0_), channel_id=1, source_target_pairs={{0,1},{1,0},{2,3},{3,2},{4,5},{5,4},{6,7},{7,6},{8,9},{9,8},{10,11... | collective-permute-start | bytes 786440 | tf_op jit(solution)/shard_map/ppermute | solution.py:197
  78.9 10.7 %collective-permute-start.19 = (bf16[256,512]{1,0:T(8,128)(2,1)S(1)}, bf16[256,512]{1,0:T(8,128)(2,1)S(1)}, u32[]{:S(2)}, u32[]{:S(2)}) collective-permute-start(bf16[256,512]{1,0:T(8,128)(2,1)S(1)} %project_q.3), channel_id=1, source_target_pairs={{0,1},{1,0},{2,3},{3,2},{4,5},{5,4},{6,7},{7,6},{8,9},{9,8},{10,11... | collective-permute-start | bytes 786440 | tf_op jit(solution)/shard_map/ppermute | solution.py:197
  88.3 1.5 %collective-permute-start.11 = (bf16[512,256]{1,0:T(8,128)(2,1)S(1)}, bf16[512,256]{1,0:T(8,128)(2,1)S(1)}, u32[]{:S(2)}, u32[]{:S(2)}) collective-permute-start(bf16[512,256]{1,0:T(8,128)(2,1)S(1)} %collective-permute-done.9.refs_1_), channel_id=1, source_target_pairs={{0,1},{1,0},{2,3},{3,2},{4,5},{5,4},{6,7},{7,6},{8,9},{9,8},{10,11... | collective-permute-start | bytes 786440 | tf_op jit(solution)/shard_map/ppermute | solution.py:197
  94.0 9.2 %collective-permute-start.20 = (bf16[128,1024]{1,0:T(8,128)(2,1)S(1)}, bf16[128,1024]{1,0:T(8,128)(2,1)S(1)}, u32[]{:S(2)}, u32[]{:S(2)}) collective-permute-start(bf16[128,1024]{1,0:T(8,128)(2,1)S(1)} %attend.3), channel_id=1, source_target_pairs={{0,2},{1,3},{2,0},{3,1},{4,6},{5,7},{6,4},{7,5},{8,10},{9,11},{10,... | collective-permute-start | bytes 786440 | tf_op jit(solution)/shard_map/ppermute | solution.py:197
  96.8 11.3 %collective-permute-start.21 = (bf16[4,64,512]{2,1,0:T(8,128)(2,1)S(1)}, bf16[4,64,512]{2,1,0:T(8,128)(2,1)S(1)}, u32[]{:S(2)}, u32[]{:S(2)}) collective-permute-start(bf16[4,64,512]{2,1,0:T(8,128)(2,1)S(1)} %get-tuple-element.11), channel_id=1, source_target_pairs={{0,2},{1,3},{2,0},{3,1},{4,6},{5,7},{6,4},{7,5},{8,10},{9,11},{10,... | collective-permute-start | bytes 786440 | tf_op jit(solution)/shard_map/ppermute | solution.py:197
  (2 other events, 1.4 us)

commit v3 on v2

--- a/solution.py
+++ b/solution.py
@@ -40,26 +40,49 @@
     return pl.ds(pl.multiple_of(index * size, size), size)
 
 
-def project_kernel(steps, n_pieces, is_kv, *refs):
+def q_start(pair, core):
+    return pl.multiple_of((pair * 2 + core) * 2 * HD, 2 * HD)
+
+
+def kv_start(pair, core):
+    return pl.multiple_of(H * HD + core * KVH * HD + pair * HD, HD)
+
+
+def pack_kernel(w_ref, *refs):
+    outs, sems = refs[:-1], refs[-1]
+    _, pair, core = place()
+    copies = []
+    for k in range(1, TEAM):
+        to_pair, to_core = pair ^ (k // 2), core ^ (k % 2)
+        kv_part = w_ref.at[:, pl.ds(kv_start(to_pair, to_core), HD)]
+        q_part = w_ref.at[:, pl.ds(q_start(to_pair, to_core), 2 * HD)]
+        copies.append(pltpu.make_async_copy(kv_part, outs[k - 1], sems.at[k - 1]))
+        copies.append(pltpu.make_async_copy(q_part, outs[TEAM - 2 + k], sems.at[TEAM - 2 + k]))
+    run(copies)
+
+
+def team_kernel(is_kv, w_ref, *refs):
+    _, pair, core = place()
+    got, out, sems = refs[:-2], refs[-2], refs[-1]
+    rows, width = w_ref.shape[0], out.shape[1]
+    start = kv_start(pair, core) if is_kv else q_start(pair, core)
+    member = pair * 2 + core
+    copies = [pltpu.make_async_copy(w_ref.at[:, pl.ds(start, width)], out.at[aligned(member, rows), :], sems.at[0])]
+    for k in range(1, TEAM):
+        copies.append(pltpu.make_async_copy(got[k - 1], out.at[aligned(member ^ k, rows), :], sems.at[k]))
+    run(copies)
+
+
+def project_kernel(steps, is_kv, *refs):
     tokens, refs = refs[: len(steps)], refs[len(steps) :]
-    weights, refs = refs[:n_pieces], refs[n_pieces:]
-    gain_ref, cos_ref, sin_ref, out, x_all, w_all, x_sem, w_sem = refs
-    req, pair, core = place()
+    w_all, gain_ref, cos_ref, sin_ref, out, x_all, x_sem = refs
+    _, pair, core = place()
     member = pair * 2 + core
     rows = tokens[0].shape[0]
     copies = []
     for i, k in enumerate(steps):
         slot = member ^ k if is_kv else i
         copies.append(pltpu.make_async_copy(tokens[i], x_all.at[aligned(slot, rows), :], x_sem.at[i]))
-    depth = weights[0].shape[0]
-    n_req = w_all.shape[0] // depth
-    for i in range(n_pieces):
-        part = slice(i // n_req * HD, (i // n_req + 1) * HD)
-        copies.append(
-            pltpu.make_async_copy(
-                weights[i], w_all.at[aligned(req ^ (i % n_req), depth), part], w_sem.at[i]
-            )
-        )
     run(copies)
     half = HD // 2
     gain = gain_ref[...]
@@ -95,11 +118,8 @@
     run(copies)
 
 
-def attend_kernel(n_out, blk_rows, step, *refs):
-    mine, other = refs[:n_out], refs[n_out : 2 * n_out]
-    q_ref, near_ref, ids_ref, length_ref, out, store, sems = refs[2 * n_out :]
+def attend_kernel(blk_rows, step, store, q_ref, near_ref, ids_ref, length_ref, out):
     _, pair, core = place()
-    load_kv(n_out, blk_rows, mine, other, ids_ref, store, sems, core)
     length = length_ref[0]
     rows = out.shape[0]
     member = (pair * 2 + core) ^ step
@@ -213,25 +233,32 @@
     all_ids = jnp.concatenate([team_ids] + [across(team_ids, k) for k in range(1, n_out)], 1)[0]
 
     w_rows = qkv_weight.shape[0]
-    q_part = qkv_weight[:, : H * HD].reshape(w_rows, 2, 2, 2, HD).transpose(3, 1, 2, 0, 4)
-    kv_part = qkv_weight[:, H * HD :].reshape(w_rows, 2, 2, HD).transpose(2, 1, 0, 3)
-
-    def to_columns(part):
-        part = jnp.broadcast_to(part[None], (n_out,) + part.shape).reshape(n_blk * w_rows, HD)
-        return lax.all_to_all(part, "blk", split_axis=0, concat_axis=0, tiled=True)
-
-    def to_prompts(piece, share):
-        rows = piece.shape[0]
-        cut = rows * share // 4
-        one, two = in_req(piece, 1), in_req(piece, 2)
-        if cut == rows:
-            return [piece, one, two, in_req(one, 2)]
-        if cut == 0:
-            return [piece, one, two, in_req(two, 1)]
-        return [piece, one, two, jnp.concatenate([in_req(one[:cut], 2), in_req(two[cut:], 1)], 0)]
-
-    kv_pieces = to_prompts(to_columns(kv_part), 4)
-    q_pieces = to_prompts(to_columns(q_part[0]), 0) + to_prompts(to_columns(q_part[1]), 2)
+    packed = pl.pallas_call(
+        pack_kernel,
+        out_shape=[shape((w_rows, HD), bf16)] * 3 + [shape((w_rows, 2 * HD), bf16)] * 3,
+        in_specs=[ANY],
+        out_specs=[ANY] * 6,
+        scratch_shapes=[pltpu.SemaphoreType.DMA((6,))],
+        compiler_params=params(1),
+        name="pack",
+    )(qkv_weight)
+
+    def gather_weight(parts, is_kv):
+        got = [in_team(part, k + 1) for k, part in enumerate(parts)]
+        team = pl.pallas_call(
+            functools.partial(team_kernel, is_kv),
+            out_shape=shape((TEAM * w_rows, parts[0].shape[1]), bf16),
+            in_specs=[ANY] * TEAM,
+            out_specs=ANY,
+            scratch_shapes=[pltpu.SemaphoreType.DMA((TEAM,))],
+            compiler_params=params(1),
+            name="team",
+        )(qkv_weight, *got)
+        same = [[r * n_blk + o * TEAM + m for r in range(n_req) for o in range(n_out)] for m in range(TEAM)]
+        return lax.all_gather(team, ("req", "blk"), axis_index_groups=same, axis=0, tiled=True)
+
+    kv_weight = gather_weight(packed[:3], True)
+    q_weight = gather_weight(packed[3:], False)
 
     own = tokens[0]
     rows = own.shape[0]
@@ -245,33 +272,31 @@
     angles = positions.astype(jnp.float32) * inverse[None, :]
     cosine, sine = jnp.cos(angles), jnp.sin(angles)
 
-    def project(steps, pieces, is_kv, gain):
-        width = len(pieces) // n_req * HD
-        depth = own.shape[1]
+    def project(steps, weight, is_kv, gain):
+        depth, width = weight.shape
         return pl.pallas_call(
-            functools.partial(project_kernel, steps, len(pieces), is_kv),
+            functools.partial(project_kernel, steps, is_kv),
             out_shape=shape((len(steps) * rows, width), bf16),
-            in_specs=[ANY] * (len(steps) + len(pieces)) + [VMEM] * 3,
+            in_specs=[ANY] * len(steps) + [VMEM] * 4,
             out_specs=VMEM,
             scratch_shapes=[
                 pltpu.VMEM((len(steps) * rows, depth), bf16),
-                pltpu.VMEM((depth, width), bf16),
                 pltpu.SemaphoreType.DMA((len(steps),)),
-                pltpu.SemaphoreType.DMA((len(pieces),)),
             ],
             cost_estimate=pl.CostEstimate(
                 flops=2 * len(steps) * rows * depth * width, bytes_accessed=6 * MIB, transcendentals=0
             ),
             compiler_params=params(12),
             name="project_kv" if is_kv else "project_q",
-        )(*[team_tokens[k] for k in steps], *pieces, gain[None, :], cosine, sine)
-
-    made = project((0, 1, 2, 3), kv_pieces, True, k_gain)
+        )(*[team_tokens[k] for k in steps], weight, gain[None, :], cosine, sine)
+
+    made = project((0, 1, 2, 3), kv_weight, True, k_gain)
+    made, all_ids = lax.optimization_barrier((made, all_ids))
     mine = [made] + [across(made, k) for k in range(1, n_out)]
     other = [in_team(part, 1) for part in mine]
 
-    from_near = in_team(project((1, 3), q_pieces, False, q_gain), 1)
-    queries = project((0, 2), q_pieces, False, q_gain)
+    from_near = in_team(project((1, 3), q_weight, False, q_gain), 1)
+    queries = project((0, 2), q_weight, False, q_gain)
 
     table = page_table[0].reshape(-1)
     per_head = page_table.shape[2]
@@ -286,15 +311,14 @@
     info = jnp.stack([flat // per_head, block, lengths[0] - block * blk_rows])
 
     total = TEAM * rows * n_out
-    store = [pltpu.VMEM((2, total, HD), bf16), pltpu.SemaphoreType.DMA((2, total // blk_rows))]
     store_mib = -(-2 * total * HD * 2 // MIB)
     page_shape = shape((slot_count, blk_rows, 2 * HD), bf16)
-    own_pages, away_pages = pl.pallas_call(
+    own_pages, away_pages, store = pl.pallas_call(
         functools.partial(pages_kernel, n_out, blk_rows),
-        out_shape=[page_shape, page_shape],
+        out_shape=[page_shape, page_shape, shape((2, total, HD), bf16)],
         in_specs=[ANY] * (2 * n_out) + [SMEM] * 2,
-        out_specs=[VMEM, VMEM],
-        scratch_shapes=store,
+        out_specs=[VMEM] * 3,
+        scratch_shapes=[pltpu.SemaphoreType.DMA((2, total // blk_rows))],
         cost_estimate=pl.CostEstimate(flops=0, bytes_accessed=4 * MIB, transcendentals=0),
         compiler_params=params(store_mib + 4),
         name="pages",
@@ -303,17 +327,16 @@
 
     def attend(step):
         return pl.pallas_call(
-            functools.partial(attend_kernel, n_out, blk_rows, step),
+            functools.partial(attend_kernel, blk_rows, step),
             out_shape=shape((rows, H // 2 * HD), bf16),
-            in_specs=[ANY] * (2 * n_out) + [VMEM] * 2 + [SMEM] * 2,
+            in_specs=[VMEM] * 3 + [SMEM] * 2,
             out_specs=VMEM,
-            scratch_shapes=store,
             cost_estimate=pl.CostEstimate(
                 flops=2 * H * HD * rows * total, bytes_accessed=4 * MIB, transcendentals=0
             ),
             compiler_params=params(store_mib + 4 + 4 * total // 1024),
             name="attend",
-        )(*mine, *other, queries, from_near, all_ids, lengths)
+        )(store, queries, from_near, all_ids, lengths)
 
     from_far = in_team(attend(2), 2)
     kept = attend(0)

time: 110 us -> 144 us (1.31)
  waiting for transfers between devices: 43.6 us -> 95.3 us
  starting transfers between devices: 40.3 us -> 12.8 us
  between operations: 1.74 us -> 14.9 us
  Pallas kernels: 16.6 us -> 12.8 us
    all_gather x0 -> x2, waiting for transfers between devices: none -> 46.3 us  [gather_weight(): lax.all_gather(team, ('req', 'blk'), axis_index_groups=same, axis=0, tile...]
    ppermute x10 -> x16, waiting for transfers between devices: 13 us -> 31.1 us  [in_team(): return lax.ppermute(array, 'blk', [(i, i ^ k) for i in range(n_blk)])]
    all_to_all x3 -> x0, starting transfers between devices: 14.8 us -> none  [to_columns(): return lax.all_to_all(part, 'blk', split_axis=0, concat_axis=0, tiled=True)]
    ppermute x10 -> x0, starting transfers between devices: 13.3 us -> none  [in_req(): return lax.ppermute(array, 'req', [(i, i ^ k) for i in range(n_req)])]
    ppermute x10 -> x0, waiting for transfers between devices: 10.2 us -> none  [in_req(): return lax.ppermute(array, 'req', [(i, i ^ k) for i in range(n_req)])]
    all_to_all x3 -> x0, waiting for transfers between devices: 9.61 us -> none  [to_columns(): return lax.all_to_all(part, 'blk', split_axis=0, concat_axis=0, tiled=True)]
    ppermute x2, waiting for transfers between devices: 10.9 us -> 17.8 us  [across(): lax.ppermute(array, 'blk', [(i, (i + TEAM * k) % n_blk) for i in range(n_...]
    ppermute x10 -> x16, starting transfers between devices: 5.58 us -> 10.1 us  [in_team(): return lax.ppermute(array, 'blk', [(i, i ^ k) for i in range(n_blk)])]
  transfers between devices with their start and end apart: 25 -> 20, of which waited for: 14 -> 14; matrix products, arithmetic and copies ran while one was open for 4% -> 1% of each run, Pallas kernels for 10% -> 7%
where the time goes in v3:
time: 144 us
  waiting for transfers between devices  95.3 us (66%)
  between operations  14.9 us (10%)
  starting transfers between devices  12.8 us (9%)
  Pallas kernels  12.8 us (9%)
  local copies, waits for them, and re-layouts  5.98 us (4%)
  other arithmetic  1.73 us (1%)
    all_gather x2, waiting for transfers between devices, gather_weight(): lax.all_gather(team, ('req', 'blk'), axis_index_groups=same, axis=0, tile...  46.3 us
    ppermute x16, waiting for transfers between devices, in_team(): return lax.ppermute(array, 'blk', [(i, i ^ k) for i in range(n_blk)])  31.1 us
    ppermute x2, waiting for transfers between devices, across(): lax.ppermute(array, 'blk', [(i, (i + TEAM * k) % n_blk) for i in range(n_...  17.8 us
    ppermute x16, starting transfers between devices, in_team(): return lax.ppermute(array, 'blk', [(i, i ^ k) for i in range(n_blk)])  10.1 us
    unnamed x20, local copies, waits for them, and re-layouts  5.82 us
    pallas_call x2, Pallas kernels, attend(): pl.pallas_call(functools.partial(attend_kernel, blk_rows, step), out_shap...  3.95 us
    pallas_call x3, Pallas kernels, project(): pl.pallas_call(functools.partial(project_kernel, steps, is_kv), out_shape...  2.91 us
  transfers between devices with their start and end apart: 20, of which 14 were waited for; matrix products, arithmetic and copies ran while one was open for 1% of the time, Pallas kernels for 7%

profile of v3, /device:TPU:0, one launch (start us, length us, event | category | flops | bytes accessed | tf_op | source)
XLA Modules:
  0.0 143.5 jit_solution(17716659372325563318)
XLA Ops:
  7.2 1.0 copy-done.1
  8.9 2.6 %collective-permute-start.7 = (bf16[64,256]{1,0:T(8,128)(2,1)S(1)}, bf16[64,256]{1,0:T(8,128)(2,1)S(1)}, u32[]{:S(2)}, u32[]{:S(2)}) collective-permute-start(bf16[64,256]{1,0:T(8,128)(2,1)S(1)} %get-tuple-element.19), channel_id=1, source_target_pairs={{0,2},{1,3},{2,0},{3,1},{4,6},{5,7},{6,4},{7,5},{8,10},{9,11},{10,... | collective-permute-start | bytes 98312 | tf_op jit(solution)/shard_map/ppermute | solution.py:217
  11.6 1.9 %collective-permute-done.7.refs_1_ = bf16[64,256]{1,0:T(8,128)(2,1)S(1)} collective-permute-done((bf16[64,256]{1,0:T(8,128)(2,1)S(1)}, bf16[64,256]{1,0:T(8,128)(2,1)S(1)}, u32[]{:S(2)}, u32[]{:S(2)}) %collective-permute-start.7) | collective-permute-done | bytes 32800 | tf_op jit(solution)/shard_map/ppermute | solution.py:217
  13.5 1.4 collective-permute-done.8.refs_2_
  14.9 1.0 copy-done.2
  16.8 0.8 collective-permute-start.13
  17.6 0.9 collective-permute-start.14
  18.5 3.2 %collective-permute-done.13.refs_1_ = bf16[64,512]{1,0:T(8,128)(2,1)S(1)} collective-permute-done((bf16[64,512]{1,0:T(8,128)(2,1)S(1)}, bf16[64,512]{1,0:T(8,128)(2,1)S(1)}, u32[]{:S(2)}, u32[]{:S(2)}) %collective-permute-start.13) | collective-permute-done | bytes 65568 | tf_op jit(solution)/shard_map/ppermute | solution.py:217
  22.0 1.0 copy-done.3
  24.2 0.8 collective-permute-done
  25.1 1.1 collective-permute-start.1
  26.3 2.4 %collective-permute-done.1 = s32[1,4]{1,0:T(1,128)S(1)} collective-permute-done((s32[1,4]{1,0:T(1,128)S(1)}, s32[1,4]{1,0:T(1,128)S(1)}, u32[]{:S(2)}, u32[]{:S(2)}) %collective-permute-start.1) | collective-permute-done | bytes 48 | tf_op jit(solution)/shard_map/ppermute | solution.py:217
  28.8 2.6 %collective-permute-start.2 = (s32[1,8]{1,0:T(1,128)S(1)}, s32[1,8]{1,0:T(1,128)S(1)}, u32[]{:S(2)}, u32[]{:S(2)}) collective-permute-start(s32[1,8]{1,0:T(1,128)S(1)} %broadcast_select_fusion.3), channel_id=1, source_target_pairs={{0,4},{1,5},{2,6},{3,7},{4,0},{5,1},{6,2},{7,3},{8,12},{9,13},{10,... | collective-permute-start | bytes 104 | tf_op jit(solution)/shard_map/ppermute | solution.py:223
  31.4 1.9 %collective-permute-done.2 = s32[1,8]{1,0:T(1,128)S(1)} collective-permute-done((s32[1,8]{1,0:T(1,128)S(1)}, s32[1,8]{1,0:T(1,128)S(1)}, u32[]{:S(2)}, u32[]{:S(2)}) %collective-permute-start.2) | collective-permute-done | bytes 64 | tf_op jit(solution)/shard_map/ppermute | solution.py:223
  33.3 1.1 collective-permute-start.4
  34.4 13.2 %collective-permute-done.4.refs_2_.refs_1_ = bf16[128,2048]{1,0:T(8,128)(2,1)S(1)} collective-permute-done((bf16[128,2048]{1,0:T(8,128)(2,1)}, bf16[128,2048]{1,0:T(8,128)(2,1)S(1)}, u32[]{:S(2)}, u32[]{:S(2)}) %collective-permute-start.4) | collective-permute-done | bytes 524320 | tf_op jit(solution)/shard_map/ppermute | solution.py:217
  47.8 1.0 multiply_sine_fusion
  49.5 8.2 %all-gather.3.cloned.1.call-done.refs_4_ = bf16[2048,256]{1,0:T(8,128)(2,1)} async-done(((bf16[256,256]{1,0:T(8,128)(2,1)}), bf16[2048,256]{1,0:T(8,128)(2,1)}) %all-gather.3.cloned.1.call-update) | async-done | bytes 1048592 | tf_op jit(solution)/shard_map/all_gather | solution.py:258
  57.7 1.2 copy-done.5
  58.9 1.0 project_kv.1.refs_0_
  61.1 16.0 %collective-permute-done.9.refs_1_ = bf16[512,256]{1,0:T(8,128)(2,1)S(1)} collective-permute-done((bf16[512,256]{1,0:T(8,128)(2,1)S(1)}, bf16[512,256]{1,0:T(8,128)(2,1)S(1)}, u32[]{:S(2)}, u32[]{:S(2)}) %collective-permute-start.9) | collective-permute-done | bytes 262176 | tf_op jit(solution)/shard_map/ppermute | solution.py:223
  77.1 38.1 %all-gather.5.cloned.1.call-done.refs_2_ = bf16[2048,512]{1,0:T(8,128)(2,1)} async-done(((bf16[256,512]{1,0:T(8,128)(2,1)}), bf16[2048,512]{1,0:T(8,128)(2,1)}) %all-gather.5.cloned.1.call-update) | async-done | bytes 2097168 | tf_op jit(solution)/shard_map/all_gather | solution.py:258
  115.2 1.6 %copy-done = bf16[2048,512]{1,0:T(8,128)(2,1)S(1)} copy-done((bf16[2048,512]{1,0:T(8,128)(2,1)S(1)}, bf16[2048,512]{1,0:T(8,128)(2,1)}, u32[]{:S(2)}) %copy-start) | copy-done | bytes 2097176
  116.8 0.9 project_q.3
  117.9 2.9 %pages.1 = (bf16[4,64,512]{2,1,0:T(8,128)(2,1)S(1)}, bf16[4,64,512]{2,1,0:T(8,128)(2,1)S(1)}, bf16[2,1024,256]{2,1,0:T(8,128)(2,1)S(1)}) custom-call(bf16[512,256]{1,0:T(8,128)(2,1)S(1)} %project_kv.1.refs_0_, bf16[512,256]{1,0:T(8,128)(2,1)S(1)} %collective-permute-done.9.refs_1_, bf16[512,256]{1,0:T(8,128)(2,1)S(1)} %collective-permute-done.10.refs_2_, ...), custom_call_target="tpu_custom_call" | custom-call | bytes 4194304 | tf_op jit(solution)/shard_map/pages/pallas_call | solution.py:316
  120.9 1.0 project_q.2.q_ref
  121.8 2.0 %attend.3 = bf16[128,1024]{1,0:T(8,128)(2,1)S(1)} custom-call(bf16[2,1024,256]{2,1,0:T(8,128)(2,1)S(1)} %get-tuple-element.24.store, bf16[256,512]{1,0:T(8,128)(2,1)S(1)} %project_q.2.q_ref, bf16[256,512]{1,0:T(8,128)(2,1)S(1)} %collective-permute-done.15.near_ref, s32[16]{0:T(128)S(1)} %add_bitcast_fusion.refs_4_.ids_ref, s32[1]{0:T(128)} %copy.9.length_ref), custom_call_target="tpu_custom_call" | custom-call | flops 536870912 | bytes 4194304 | tf_op jit(solution)/shard_map/attend/pallas_call | solution.py:329
  123.8 2.1 %collective-permute-start.16 = (bf16[128,1024]{1,0:T(8,128)(2,1)S(1)}, bf16[128,1024]{1,0:T(8,128)(2,1)S(1)}, u32[]{:S(2)}, u32[]{:S(2)}) collective-permute-start(bf16[128,1024]{1,0:T(8,128)(2,1)S(1)} %attend.3), channel_id=1, source_target_pairs={{0,2},{1,3},{2,0},{3,1},{4,6},{5,7},{6,4},{7,5},{8,10},{9,11},{10,... | collective-permute-start | bytes 786440 | tf_op jit(solution)/shard_map/ppermute | solution.py:217
  125.9 2.0 %attend.2.kept = bf16[128,1024]{1,0:T(8,128)(2,1)S(1)} custom-call(bf16[2,1024,256]{2,1,0:T(8,128)(2,1)S(1)} %get-tuple-element.24.store, bf16[256,512]{1,0:T(8,128)(2,1)S(1)} %project_q.2.q_ref, bf16[256,512]{1,0:T(8,128)(2,1)S(1)} %collective-permute-done.15.near_ref, s32[16]{0:T(128)S(1)} %add_bitcast_fusion.refs_4_.ids_ref, s32[1]{0:T(128)} %copy.9.length_ref), custom_call_target="tpu_custom_call" | custom-call | flops 536870912 | bytes 4194304 | tf_op jit(solution)/shard_map/attend/pallas_call | solution.py:329
  127.9 2.1 %collective-permute-done.17.got_pages = bf16[4,64,512]{2,1,0:T(8,128)(2,1)S(1)} collective-permute-done((bf16[4,64,512]{2,1,0:T(8,128)(2,1)S(1)}, bf16[4,64,512]{2,1,0:T(8,128)(2,1)S(1)}, u32[]{:S(2)}, u32[]{:S(2)}) %collective-permute-start.17) | collective-permute-done | bytes 262176 | tf_op jit(solution)/shard_map/ppermute | solution.py:217
  129.9 5.2 %collective-permute-done.16.from_far = bf16[128,1024]{1,0:T(8,128)(2,1)S(1)} collective-permute-done((bf16[128,1024]{1,0:T(8,128)(2,1)S(1)}, bf16[128,1024]{1,0:T(8,128)(2,1)S(1)}, u32[]{:S(2)}, u32[]{:S(2)}) %collective-permute-start.16) | collective-permute-done | bytes 262176 | tf_op jit(solution)/shard_map/ppermute | solution.py:217
  135.2 1.5 %finish.1 = (bf16[128,2048]{1,0:T(8,128)(2,1)}, bf16[4,64,512]{2,1,0:T(8,128)(2,1)}) custom-call(bf16[128,1024]{1,0:T(8,128)(2,1)S(1)} %attend.2.kept, bf16[128,1024]{1,0:T(8,128)(2,1)S(1)} %collective-permute-done.16.from_far, bf16[4,64,512]{2,1,0:T(8,128)(2,1)S(1)} %get-tuple-element.28.own_pages, ...), custom_call_target="tpu_custom_call" | custom-call | tf_op jit(solution)/shard_map/finish/pallas_call | solution.py:344
  (55 shorter events, 5.1 us)
Async XLA Ops:
  7.2 50.5 %all-gather.3.cloned.1.call-start = ((), (), s32[]{:S(2)}) async-start(), calls=%async_computation | async-start | bytes 1179648 | tf_op jit(solution)/shard_map/all_gather | solution.py:258
  7.2 1.0 copy-start.1
  8.2 15.6 %copy-start.8 = (s32[1,2]{1,0:T(1,128)S(1)}, s32[1,2]{1,0:T(1,128)}, u32[]{:S(2)}) copy-start(s32[1,2]{1,0:T(1,128)} %param.8) | copy-start | bytes 28
  8.2 49.5 %copy-start.7 = (f32[256]{0:T(256)S(1)}, f32[256]{0:T(256)}, u32[]{:S(2)}) copy-start(f32[256]{0:T(256)} %param.13) | copy-start | bytes 3076
  8.3 3.2 %collective-permute-start.6 = (bf16[64,256]{1,0:T(8,128)(2,1)S(1)}, bf16[64,256]{1,0:T(8,128)(2,1)S(1)}, u32[]{:S(2)}, u32[]{:S(2)}) collective-permute-start(bf16[64,256]{1,0:T(8,128)(2,1)S(1)} %get-tuple-element.18), channel_id=1, source_target_pairs={{0,1},{1,0},{2,3},{3,2},{4,5},{5,4},{6,7},{7,6},{8,9},{9,8},{10,11... | collective-permute-start | bytes 98312 | tf_op jit(solution)/shard_map/ppermute | solution.py:217
  8.9 4.6 %collective-permute-start.7 = (bf16[64,256]{1,0:T(8,128)(2,1)S(1)}, bf16[64,256]{1,0:T(8,128)(2,1)S(1)}, u32[]{:S(2)}, u32[]{:S(2)}) collective-permute-start(bf16[64,256]{1,0:T(8,128)(2,1)S(1)} %get-tuple-element.19), channel_id=1, source_target_pairs={{0,2},{1,3},{2,0},{3,1},{4,6},{5,7},{6,4},{7,5},{8,10},{9,11},{10,... | collective-permute-start | bytes 98312 | tf_op jit(solution)/shard_map/ppermute | solution.py:217
  11.5 3.3 %collective-permute-start.8 = (bf16[64,256]{1,0:T(8,128)(2,1)S(1)}, bf16[64,256]{1,0:T(8,128)(2,1)S(1)}, u32[]{:S(2)}, u32[]{:S(2)}) collective-permute-start(bf16[64,256]{1,0:T(8,128)(2,1)S(1)} %get-tuple-element.20), channel_id=1, source_target_pairs={{0,3},{1,2},{2,1},{3,0},{4,7},{5,6},{6,5},{7,4},{8,11},{9,10},{10,... | collective-permute-start | bytes 98312 | tf_op jit(solution)/shard_map/ppermute | solution.py:217
  14.9 1.0 copy-start.2
  15.8 41.9 %copy-start.4 = (bf16[1,128,2048]{2,1,0:T(8,128)(2,1)S(1)}, bf16[1,128,2048]{2,1,0:T(8,128)(2,1)}, u32[]{:S(2)}) copy-start(bf16[1,128,2048]{2,1,0:T(8,128)(2,1)} %param.7) | copy-start | bytes 1572868
  16.6 98.6 %all-gather.5.cloned.1.call-start = ((), (), s32[]{:S(2)}) async-start(), calls=%async_computation.1 | async-start | bytes 2359296 | tf_op jit(solution)/shard_map/all_gather | solution.py:258
  16.6 1.9 %collective-permute-start.12 = (bf16[64,512]{1,0:T(8,128)(2,1)S(1)}, bf16[64,512]{1,0:T(8,128)(2,1)S(1)}, u32[]{:S(2)}, u32[]{:S(2)}) collective-permute-start(bf16[64,512]{1,0:T(8,128)(2,1)S(1)} %get-tuple-element.25), channel_id=1, source_target_pairs={{0,1},{1,0},{2,3},{3,2},{4,5},{5,4},{6,7},{7,6},{8,9},{9,8},{10,11... | collective-permute-start | bytes 196616 | tf_op jit(solution)/shard_map/ppermute | solution.py:217
  16.8 4.9 %collective-permute-start.13 = (bf16[64,512]{1,0:T(8,128)(2,1)S(1)}, bf16[64,512]{1,0:T(8,128)(2,1)S(1)}, u32[]{:S(2)}, u32[]{:S(2)}) collective-permute-start(bf16[64,512]{1,0:T(8,128)(2,1)S(1)} %get-tuple-element.26), channel_id=1, source_target_pairs={{0,2},{1,3},{2,0},{3,1},{4,6},{5,7},{6,4},{7,5},{8,10},{9,11},{10,... | collective-permute-start | bytes 196616 | tf_op jit(solution)/shard_map/ppermute | solution.py:217
  17.6 4.4 %collective-permute-start.14 = (bf16[64,512]{1,0:T(8,128)(2,1)S(1)}, bf16[64,512]{1,0:T(8,128)(2,1)S(1)}, u32[]{:S(2)}, u32[]{:S(2)}) collective-permute-start(bf16[64,512]{1,0:T(8,128)(2,1)S(1)} %get-tuple-element.27), channel_id=1, source_target_pairs={{0,3},{1,2},{2,1},{3,0},{4,7},{5,6},{6,5},{7,4},{8,11},{9,10},{10,... | collective-permute-start | bytes 196616 | tf_op jit(solution)/shard_map/ppermute | solution.py:217
  22.0 1.0 copy-start.3
  23.8 1.3 collective-permute-start
  25.1 3.5 %collective-permute-start.1 = (s32[1,4]{1,0:T(1,128)S(1)}, s32[1,4]{1,0:T(1,128)S(1)}, u32[]{:S(2)}, u32[]{:S(2)}) collective-permute-start(s32[1,4]{1,0:T(1,128)S(1)} %broadcast_select_fusion.1), channel_id=1, source_target_pairs={{0,2},{1,3},{2,0},{3,1},{4,6},{5,7},{6,4},{7,5},{8,10},{9,11},{10,... | collective-permute-start | bytes 56 | tf_op jit(solution)/shard_map/ppermute | solution.py:217
  28.8 4.4 %collective-permute-start.2 = (s32[1,8]{1,0:T(1,128)S(1)}, s32[1,8]{1,0:T(1,128)S(1)}, u32[]{:S(2)}, u32[]{:S(2)}) collective-permute-start(s32[1,8]{1,0:T(1,128)S(1)} %broadcast_select_fusion.3), channel_id=1, source_target_pairs={{0,4},{1,5},{2,6},{3,7},{4,0},{5,1},{6,2},{7,3},{8,12},{9,13},{10,... | collective-permute-start | bytes 104 | tf_op jit(solution)/shard_map/ppermute | solution.py:223
  33.3 14.3 %collective-permute-start.4 = (bf16[128,2048]{1,0:T(8,128)(2,1)}, bf16[128,2048]{1,0:T(8,128)(2,1)S(1)}, u32[]{:S(2)}, u32[]{:S(2)}) collective-permute-start(bf16[128,2048]{1,0:T(8,128)(2,1)} %bitcast.30), channel_id=1, source_target_pairs={{0,2},{1,3},{2,0},{3,1},{4,6},{5,7},{6,4},{7,5},{8,10},{9,11},{10,... | collective-permute-start | bytes 1572872 | tf_op jit(solution)/shard_map/ppermute | solution.py:217
  34.3 14.5 %collective-permute-start.3 = (bf16[128,2048]{1,0:T(8,128)(2,1)}, bf16[128,2048]{1,0:T(8,128)(2,1)S(1)}, u32[]{:S(2)}, u32[]{:S(2)}) collective-permute-start(bf16[128,2048]{1,0:T(8,128)(2,1)} %bitcast.31), channel_id=1, source_target_pairs={{0,1},{1,0},{2,3},{3,2},{4,5},{5,4},{6,7},{7,6},{8,9},{9,8},{10,11... | collective-permute-start | bytes 1572872 | tf_op jit(solution)/shard_map/ppermute | solution.py:217
  47.6 1.9 %collective-permute-start.5 = (bf16[128,2048]{1,0:T(8,128)(2,1)S(1)}, bf16[128,2048]{1,0:T(8,128)(2,1)S(1)}, u32[]{:S(2)}, u32[]{:S(2)}) collective-permute-start(bf16[128,2048]{1,0:T(8,128)(2,1)S(1)} %collective-permute-done.4.refs_2_.refs_1_), channel_id=1, source_target_pairs={{0,1},{1,0},{2,3},{3,2},{4,5},{5,4},{6,7},{7,6},{8,9},{9,8},{10,11... | collective-permute-start | bytes 1572872 | tf_op jit(solution)/shard_map/ppermute | solution.py:217
  48.8 11.9 %copy-start.9 = (s32[1,2,16]{2,1,0:T(2,128)S(1)}, s32[1,2,16]{2,1,0:T(2,128)}, u32[]{:S(2)}) copy-start(s32[1,2,16]{2,1,0:T(2,128)} %param.10) | copy-start | bytes 388
  48.8 66.4 %copy-start.6 = (f32[256]{0:T(256)S(1)}, f32[256]{0:T(256)}, u32[]{:S(2)}) copy-start(f32[256]{0:T(256)} %param.12) | copy-start | bytes 3076
  57.7 1.2 copy-start.5
  59.9 17.1 %collective-permute-start.9 = (bf16[512,256]{1,0:T(8,128)(2,1)S(1)}, bf16[512,256]{1,0:T(8,128)(2,1)S(1)}, u32[]{:S(2)}, u32[]{:S(2)}) collective-permute-start(bf16[512,256]{1,0:T(8,128)(2,1)S(1)} %project_kv.1.refs_0_), channel_id=1, source_target_pairs={{0,4},{1,5},{2,6},{3,7},{4,0},{5,1},{6,2},{7,3},{8,12},{9,13},{10,... | collective-permute-start | bytes 786440 | tf_op jit(solution)/shard_map/ppermute | solution.py:223
  61.0 56.8 %collective-permute-start.10 = (bf16[512,256]{1,0:T(8,128)(2,1)S(1)}, bf16[512,256]{1,0:T(8,128)(2,1)S(1)}, u32[]{:S(2)}, u32[]{:S(2)}) collective-permute-start(bf16[512,256]{1,0:T(8,128)(2,1)S(1)} %project_kv.1.refs_0_), channel_id=1, source_target_pairs={{0,1},{1,0},{2,3},{3,2},{4,5},{5,4},{6,7},{7,6},{8,9},{9,8},{10,11... | collective-permute-start | bytes 786440 | tf_op jit(solution)/shard_map/ppermute | solution.py:217
  77.1 40.8 %collective-permute-start.11 = (bf16[512,256]{1,0:T(8,128)(2,1)S(1)}, bf16[512,256]{1,0:T(8,128)(2,1)}, u32[]{:S(2)}, u32[]{:S(2)}) collective-permute-start(bf16[512,256]{1,0:T(8,128)(2,1)S(1)} %collective-permute-done.9.refs_1_), channel_id=1, source_target_pairs={{0,1},{1,0},{2,3},{3,2},{4,5},{5,4},{6,7},{7,6},{8,9},{9,8},{10,11... | collective-permute-start | bytes 786440 | tf_op jit(solution)/shard_map/ppermute | solution.py:217
  115.2 1.6 %copy-start = (bf16[2048,512]{1,0:T(8,128)(2,1)S(1)}, bf16[2048,512]{1,0:T(8,128)(2,1)}, u32[]{:S(2)}) copy-start(bf16[2048,512]{1,0:T(8,128)(2,1)} %all-gather.5.cloned.1.call-done.refs_2_) | copy-start | bytes 6291460
  117.8 4.1 %collective-permute-start.15 = (bf16[256,512]{1,0:T(8,128)(2,1)S(1)}, bf16[256,512]{1,0:T(8,128)(2,1)S(1)}, u32[]{:S(2)}, u32[]{:S(2)}) collective-permute-start(bf16[256,512]{1,0:T(8,128)(2,1)S(1)} %project_q.3), channel_id=1, source_target_pairs={{0,1},{1,0},{2,3},{3,2},{4,5},{5,4},{6,7},{7,6},{8,9},{9,8},{10,11... | collective-permute-start | bytes 786440 | tf_op jit(solution)/shard_map/ppermute | solution.py:217
  120.8 9.2 %collective-permute-start.17 = (bf16[4,64,512]{2,1,0:T(8,128)(2,1)S(1)}, bf16[4,64,512]{2,1,0:T(8,128)(2,1)S(1)}, u32[]{:S(2)}, u32[]{:S(2)}) collective-permute-start(bf16[4,64,512]{2,1,0:T(8,128)(2,1)S(1)} %get-tuple-element.29), channel_id=1, source_target_pairs={{0,2},{1,3},{2,0},{3,1},{4,6},{5,7},{6,4},{7,5},{8,10},{9,11},{10,... | collective-permute-start | bytes 786440 | tf_op jit(solution)/shard_map/ppermute | solution.py:217
  123.8 11.3 %collective-permute-start.16 = (bf16[128,1024]{1,0:T(8,128)(2,1)S(1)}, bf16[128,1024]{1,0:T(8,128)(2,1)S(1)}, u32[]{:S(2)}, u32[]{:S(2)}) collective-permute-start(bf16[128,1024]{1,0:T(8,128)(2,1)S(1)} %attend.3), channel_id=1, source_target_pairs={{0,2},{1,3},{2,0},{3,1},{4,6},{5,7},{6,4},{7,5},{8,10},{9,11},{10,... | collective-permute-start | bytes 786440 | tf_op jit(solution)/shard_map/ppermute | solution.py:217
Sparse Core Ops, SparseCore 0:
  16.7 40.9 all-gather.2
  60.5 54.6 all-gather.4

commit v4 on v3

--- a/solution.py
+++ b/solution.py
@@ -11,6 +11,7 @@
 KVH = 2
 HD = 256
 TEAM = 4
+ID_ROWS = 16
 ROPE_BASE = 1000000.0
 NORM_EPS = 1e-06
 MIB = 1024 * 1024
@@ -48,54 +49,78 @@
     return pl.multiple_of(H * HD + core * KVH * HD + pair * HD, HD)
 
 
-def pack_kernel(w_ref, *refs):
-    outs, sems = refs[:-1], refs[-1]
+def pack_kernel(w_ref, ids_ref, *outs):
     _, pair, core = place()
-    copies = []
-    for k in range(1, TEAM):
+    rows = w_ref.shape[0]
+    for k in range(TEAM):
         to_pair, to_core = pair ^ (k // 2), core ^ (k % 2)
-        kv_part = w_ref.at[:, pl.ds(kv_start(to_pair, to_core), HD)]
-        q_part = w_ref.at[:, pl.ds(q_start(to_pair, to_core), 2 * HD)]
-        copies.append(pltpu.make_async_copy(kv_part, outs[k - 1], sems.at[k - 1]))
-        copies.append(pltpu.make_async_copy(q_part, outs[TEAM - 2 + k], sems.at[TEAM - 2 + k]))
-    run(copies)
-
-
-def team_kernel(is_kv, w_ref, *refs):
+        outs[k][:rows, :] = w_ref[:, pl.ds(kv_start(to_pair, to_core), HD)]
+        outs[k][rows:, :] = ids_ref[...]
+        outs[TEAM + k][...] = w_ref[:, pl.ds(q_start(to_pair, to_core), 2 * HD)]
+
+
+def team_kernel(rows, *refs):
     _, pair, core = place()
-    got, out, sems = refs[:-2], refs[-2], refs[-1]
-    rows, width = w_ref.shape[0], out.shape[1]
-    start = kv_start(pair, core) if is_kv else q_start(pair, core)
+    parts, outs = refs[:TEAM], refs[TEAM:]
     member = pair * 2 + core
-    copies = [pltpu.make_async_copy(w_ref.at[:, pl.ds(start, width)], out.at[aligned(member, rows), :], sems.at[0])]
-    for k in range(1, TEAM):
-        copies.append(pltpu.make_async_copy(got[k - 1], out.at[aligned(member ^ k, rows), :], sems.at[k]))
-    run(copies)
-
-
-def project_kernel(steps, is_kv, *refs):
-    tokens, refs = refs[: len(steps)], refs[len(steps) :]
-    w_all, gain_ref, cos_ref, sin_ref, out, x_all, x_sem = refs
+    for n, out in enumerate(outs):
+        cols = slice(n * HD, (n + 1) * HD)
+        for k in range(TEAM):
+            out[aligned(member ^ k, rows), :] = parts[k][:rows, cols]
+        if parts[0].shape[0] > rows:
+            below = [part[rows:, cols].astype(jnp.float32) for part in parts]
+            out[TEAM * rows :, :] = sum(below[1:], below[0]).astype(out.dtype)
+
+
+def stack_kernel(*refs):
+    _, pair, core = place()
+    tokens, out, sems = refs[:TEAM], refs[TEAM], refs[TEAM + 1]
+    rows = tokens[0].shape[0]
+    member = pair * 2 + core
+    run([
+        pltpu.make_async_copy(tokens[k], out.at[aligned(member ^ k, rows), :], sems.at[k]) for k in range(TEAM)
+    ])
+
+
+def project_kernel(steps, n_out, depth, is_kv, x_ref, *refs):
+    gain_ref, cos_ref, sin_ref, out, w_all, sems = refs[-6:]
+    weights = refs[:-6]
+    req = lax.axis_index("req")
+    outer = lax.axis_index("blk") // TEAM
     _, pair, core = place()
     member = pair * 2 + core
-    rows = tokens[0].shape[0]
+    rows = x_ref.shape[0] // TEAM
     copies = []
-    for i, k in enumerate(steps):
-        slot = member ^ k if is_kv else i
-        copies.append(pltpu.make_async_copy(tokens[i], x_all.at[aligned(slot, rows), :], x_sem.at[i]))
+    per_chunk = 2 * (w_all.shape[0] // (depth * n_out))
+    for at, piece in enumerate(weights):
+        i = at % per_chunk
+        cols = slice(at // per_chunk * HD, (at // per_chunk + 1) * HD)
+        from_req = req ^ (i // 2)
+        tall = piece.shape[0] // (n_out - 1 if i % 2 else 1)
+        for n in range(n_out - 1 if i % 2 else 1):
+            from_outer = lax.rem(outer + n_out - n - i % 2, n_out)
+            copies.append(
+                pltpu.make_async_copy(
+                    piece.at[pl.ds(n * tall, depth), :],
+                    w_all.at[aligned(from_req * n_out + from_outer, depth), cols],
+                    sems.at[len(copies)],
+                )
+            )
     run(copies)
     half = HD // 2
     gain = gain_ref[...]
     if is_kv:
-        cosine, sine = cos_ref[...], sin_ref[...]
+        x, cosine, sine = x_ref[...], cos_ref[...], sin_ref[...]
         is_key = core == 0
         cosine = jnp.where(is_key, cosine, 1.0)
         sine = jnp.where(is_key, sine, 0.0)
         gain = jnp.where(is_key, gain, 1.0)
     else:
-        cosine = jnp.concatenate([cos_ref[aligned(member ^ k, rows), :] for k in steps], 0)
-        sine = jnp.concatenate([sin_ref[aligned(member ^ k, rows), :] for k in steps], 0)
-    product = jnp.dot(x_all[...], w_all[...], preferred_element_type=jnp.float32)
+        x, cosine, sine = (
+            jnp.concatenate([ref[aligned(member ^ k, rows), :] for k in steps], 0)
+            for ref in (x_ref, cos_ref, sin_ref)
+        )
+    product = jnp.dot(x, w_all[...], preferred_element_type=jnp.float32)
     for h in range(out.shape[1] // HD):
         head = product[:, h * HD : (h + 1) * HD]
         mean = jnp.mean(head * head, axis=-1, keepdims=True)
@@ -222,49 +247,82 @@
     def across(array, k):
         return lax.ppermute(array, "blk", [(i, (i + TEAM * k) % n_blk) for i in range(n_blk)])
 
-    blk_rows = tokens.shape[1] // block_ids.shape[1]
-
-    def join(array, bit):
-        got = in_team(array, bit)
-        low = member & bit == 0
-        return jnp.where(low, jnp.concatenate([array, got], 1), jnp.concatenate([got, array], 1))
-
-    team_ids = join(join(block_ids, 1), 2)
-    all_ids = jnp.concatenate([team_ids] + [across(team_ids, k) for k in range(1, n_out)], 1)[0]
+    def sync(*arrays):
+        return lax.optimization_barrier(arrays)
 
     w_rows = qkv_weight.shape[0]
+    per_device = block_ids.shape[1]
+    lane = jnp.arange(HD, dtype=jnp.int32) - member * per_device
+    ids_row = jnp.zeros((HD,), jnp.int32)
+    for j in range(per_device):
+        ids_row = jnp.where(lane == j, block_ids[0, j], ids_row)
+    ids_rows = jnp.broadcast_to(ids_row.astype(bf16)[None, :], (ID_ROWS, HD))
     packed = pl.pallas_call(
         pack_kernel,
-        out_shape=[shape((w_rows, HD), bf16)] * 3 + [shape((w_rows, 2 * HD), bf16)] * 3,
-        in_specs=[ANY],
-        out_specs=[ANY] * 6,
-        scratch_shapes=[pltpu.SemaphoreType.DMA((6,))],
-        compiler_params=params(1),
+        out_shape=[shape((w_rows + ID_ROWS, HD), bf16)] * TEAM + [shape((w_rows, 2 * HD), bf16)] * TEAM,
+        in_specs=[VMEM] * 2,
+        out_specs=[VMEM] * (2 * TEAM),
+        compiler_params=params(2),
         name="pack",
-    )(qkv_weight)
-
-    def gather_weight(parts, is_kv):
-        got = [in_team(part, k + 1) for k, part in enumerate(parts)]
-        team = pl.pallas_call(
-            functools.partial(team_kernel, is_kv),
-            out_shape=shape((TEAM * w_rows, parts[0].shape[1]), bf16),
-            in_specs=[ANY] * TEAM,
-            out_specs=ANY,
-            scratch_shapes=[pltpu.SemaphoreType.DMA((TEAM,))],
-            compiler_params=params(1),
+    )(qkv_weight, ids_rows)
+
+    def exchange(parts):
+        return [parts[0]] + [in_team(part, k) for k, part in enumerate(parts) if k]
+
+    def assemble(parts):
+        below = parts[0].shape[0] - w_rows
+        return pl.pallas_call(
+            functools.partial(team_kernel, w_rows),
+            out_shape=[shape((TEAM * w_rows + below, HD), bf16)] * (parts[0].shape[1] // HD),
+            in_specs=[VMEM] * TEAM,
+            out_specs=[VMEM] * (parts[0].shape[1] // HD),
+            compiler_params=params(2),
             name="team",
-        )(qkv_weight, *got)
-        same = [[r * n_blk + o * TEAM + m for r in range(n_req) for o in range(n_out)] for m in range(TEAM)]
-        return lax.all_gather(team, ("req", "blk"), axis_index_groups=same, axis=0, tiled=True)
-
-    kv_weight = gather_weight(packed[:3], True)
-    q_weight = gather_weight(packed[3:], False)
+        )(*parts)
+
+    def from_others(piece):
+        got = [across(piece, k) for k in range(1, n_out)]
+        return got[0] if len(got) == 1 else jnp.concatenate(got, 0)
 
     own = tokens[0]
     rows = own.shape[0]
-    own, all_ids = lax.optimization_barrier((own, all_ids))
-    far = in_team(own, 2)
-    team_tokens = [own, in_team(own, 1), far, in_team(far, 1)]
+    own_near = in_team(own, 1)
+    (kv,) = assemble(exchange(packed[:TEAM]))
+    kv, own, *q_parts = sync(kv, own, *packed[TEAM:])
+    kv_o, kv_x, kv_y = from_others(kv), in_req(kv, 1), in_req(kv, 2)
+    qa, qb = assemble(exchange(q_parts))
+    far_a = in_team(own[: rows // 2], 2)
+    kv, kv_o, kv_x, kv_y, qa, qb, far_a, own, own_near = sync(kv, kv_o, kv_x, kv_y, qa, qb, far_a, own, own_near)
+    kv_ox, kv_oy, kv_d = in_req(kv_o, 1), in_req(kv_o, 2), in_req(kv_x, 2)
+    qa_o, qa_x = from_others(qa), in_req(qa, 1)
+    far_b = in_team(own[rows // 2 :], 2)
+    kv_ox, kv_oy, kv_d, qa, qa_o, qa_x, qb, far_a, far_b = sync(kv_ox, kv_oy, kv_d, qa, qa_o, qa_x, qb, far_a, far_b)
+    kv_od = in_req(kv_oy, 1)
+    qb_o, qa_y, qa_ox, qa_oy = from_others(qb), in_req(qa, 2), in_req(qa_o, 1), in_req(qa_o, 2)
+    far = jnp.concatenate([far_a, far_b], 0)
+    far_near = in_team(far, 1)
+    stacked = pl.pallas_call(
+        stack_kernel,
+        out_shape=shape((TEAM * rows, own.shape[1]), bf16),
+        in_specs=[ANY] * TEAM,
+        out_specs=VMEM,
+        scratch_shapes=[pltpu.SemaphoreType.DMA((TEAM,))],
+        compiler_params=params(4),
+        name="stack",
+    )(own, own_near, far, far_near)
+    kv_od, qa_y, qa_ox, qa_oy, qb, qb_o, stacked = sync(kv_od, qa_y, qa_ox, qa_oy, qb, qb_o, stacked)
+    kv_weight = [kv, kv_o, kv_x, kv_ox, kv_y, kv_oy, kv_d, kv_od]
+    qb_x, qb_y, qb_ox, qb_oy = in_req(qb, 1), in_req(qb, 2), in_req(qb_o, 1), in_req(qb_o, 2)
+    qa_x, qa_oy, qb_x, qb_y, qb_ox, qb_oy = sync(qa_x, qa_oy, qb_x, qb_y, qb_ox, qb_oy)
+    qa_od, qb_od, qa_d, qb_d = in_req(qa_oy, 1), in_req(qb_oy, 1), in_req(qa_x, 2), in_req(qb_x, 2)
+    q_weight = [qa, qa_o, qa_x, qa_ox, qa_y, qa_oy, qa_d, qa_od]
+    q_weight += [qb, qb_o, qb_x, qb_ox, qb_y, qb_oy, qb_d, qb_od]
+
+    blk_rows = rows // per_device
+    tall = kv.shape[0]
+    team_ids = kv[tall - ID_ROWS, : TEAM * per_device][None].astype(jnp.int32)
+    other_ids = kv_o.reshape(n_out - 1, tall, HD)[:, tall - ID_ROWS, : TEAM * per_device].astype(jnp.int32)
+    all_ids = jnp.concatenate([team_ids, other_ids], 0).reshape(-1)
 
     offsets = jnp.arange(blk_rows, dtype=jnp.int32)
     positions = (team_ids[0][:, None] * blk_rows + offsets[None, :]).reshape(-1, 1)
@@ -273,25 +331,25 @@
     cosine, sine = jnp.cos(angles), jnp.sin(angles)
 
     def project(steps, weight, is_kv, gain):
-        depth, width = weight.shape
+        width = len(weight) // (2 * n_req) * HD
+        depth = own.shape[1]
         return pl.pallas_call(
-            functools.partial(project_kernel, steps, is_kv),
+            functools.partial(project_kernel, steps, n_out, TEAM * w_rows, is_kv),
             out_shape=shape((len(steps) * rows, width), bf16),
-            in_specs=[ANY] * len(steps) + [VMEM] * 4,
+            in_specs=[VMEM] + [ANY] * len(weight) + [VMEM] * 3,
             out_specs=VMEM,
             scratch_shapes=[
-                pltpu.VMEM((len(steps) * rows, depth), bf16),
-                pltpu.SemaphoreType.DMA((len(steps),)),
+                pltpu.VMEM((depth, width), bf16),
+                pltpu.SemaphoreType.DMA((n_req * n_out * width // HD,)),
             ],
             cost_estimate=pl.CostEstimate(
                 flops=2 * len(steps) * rows * depth * width, bytes_accessed=6 * MIB, transcendentals=0
             ),
             compiler_params=params(12),
             name="project_kv" if is_kv else "project_q",
-        )(*[team_tokens[k] for k in steps], weight, gain[None, :], cosine, sine)
+        )(stacked, *weight, gain[None, :], cosine, sine)
 
     made = project((0, 1, 2, 3), kv_weight, True, k_gain)
-    made, all_ids = lax.optimization_barrier((made, all_ids))
     mine = [made] + [across(made, k) for k in range(1, n_out)]
     other = [in_team(part, 1) for part in mine]
 

time: 144 us -> 111 us (0.77)
  waiting for transfers between devices: 95.3 us -> 33.8 us
  starting transfers between devices: 12.8 us -> 36.2 us
  between operations: 14.9 us -> 1.94 us
  local copies, waits for them, and re-layouts: 5.98 us -> 17.9 us
  Pallas kernels: 12.8 us -> 17.1 us
  other arithmetic: 1.73 us -> 3.19 us
    all_gather x2 -> x0, waiting for transfers between devices: 46.3 us -> none  [gather_weight(): lax.all_gather(team, ('req', 'blk'), axis_index_groups=same, axis=0, tile...]
    ppermute x0 -> x18, starting transfers between devices: none -> 19.7 us  [in_req(): return lax.ppermute(array, 'req', [(i, i ^ k) for i in range(n_req)])]
    ppermute x16 -> x15, waiting for transfers between devices: 31.1 us -> 19.8 us  [in_team(): return lax.ppermute(array, 'blk', [(i, i ^ k) for i in range(n_blk)])]
    ppermute x2 -> x4, waiting for transfers between devices: 17.8 us -> 8.02 us  [across(): lax.ppermute(array, 'blk', [(i, (i + TEAM * k) % n_blk) for i in range(n_...]
    unnamed x20 -> x71, local copies, waits for them, and re-layouts: 5.82 us -> 13.7 us
    ppermute x0 -> x18, waiting for transfers between devices: none -> 5.98 us  [in_req(): return lax.ppermute(array, 'req', [(i, i ^ k) for i in range(n_req)])]
    ppermute x2 -> x4, starting transfers between devices: 2.66 us -> 8.03 us  [across(): lax.ppermute(array, 'blk', [(i, (i + TEAM * k) % n_blk) for i in range(n_...]
    pallas_call x6 -> x7, Pallas kernels: 4.43 us -> 8.27 us  [the longest x3 7.96 us: project(): pl.pallas_call(functools.partial(project_kernel, steps, n_out, TEAM * w_r...]
  transfers between devices with their start and end apart: 20 -> 37, of which waited for: 14 -> 14; matrix products, arithmetic and copies ran while one was open for 1% -> 7% of each run, Pallas kernels for 7% -> 12%
where the time goes in v4:
time: 111 us; the launch traced here: 110 us
  starting transfers between devices  36.2 us (33%)
  waiting for transfers between devices  33.8 us (30%)
  local copies, waits for them, and re-layouts  17.9 us (16%)
  Pallas kernels  17.1 us (15%)
  other arithmetic  3.19 us (3%)
  between operations  1.94 us (2%)
    ppermute x15, waiting for transfers between devices, in_team(): return lax.ppermute(array, 'blk', [(i, i ^ k) for i in range(n_blk)])  19.8 us
    ppermute x18, starting transfers between devices, in_req(): return lax.ppermute(array, 'req', [(i, i ^ k) for i in range(n_req)])  19.7 us
    unnamed x71, local copies, waits for them, and re-layouts  13.7 us
    ppermute x15, starting transfers between devices, in_team(): return lax.ppermute(array, 'blk', [(i, i ^ k) for i in range(n_blk)])  8.53 us
    ppermute x4, starting transfers between devices, across(): lax.ppermute(array, 'blk', [(i, (i + TEAM * k) % n_blk) for i in range(n_...  8.03 us
    ppermute x4, waiting for transfers between devices, across(): lax.ppermute(array, 'blk', [(i, (i + TEAM * k) % n_blk) for i in range(n_...  8.02 us
    pallas_call x3, Pallas kernels, project(): pl.pallas_call(functools.partial(project_kernel, steps, n_out, TEAM * w_r...  7.96 us
    ppermute x18, waiting for transfers between devices, in_req(): return lax.ppermute(array, 'req', [(i, i ^ k) for i in range(n_req)])  5.98 us
  transfers between devices with their start and end apart: 37, of which 14 were waited for; matrix products, arithmetic and copies ran while one was open for 7% of the time, Pallas kernels for 12%

profile of v4, /device:TPU:0, one launch (start us, length us, event | category | flops | bytes accessed | tf_op | source)
XLA Modules:
  0.0 110.2 jit_solution(3217324095406299002)
XLA Ops:
  1.2 1.3 %fusion.2 = (s32[1,1]{1,0:T(1,128)}, s32[1,1]{1,0:T(1,128)}) fusion(s32[1,2]{1,0:T(1,128)} %param.8), kind=kLoop, calls=%fused_computation.26 | loop fusion | bytes 16 | tf_op jit(solution)/shard_map/slice | solution.py:258
  2.5 1.3 %fusion = bf16[256]{0:T(256)(128)(2,1)S(1)} fusion(s32[]{:T(128)} %bitcast.1, s32[]{:T(128)} %bitcast, s32[]{:T(128)S(6)} %mul.46), kind=kLoop, calls=%fused_computation.14 | loop fusion | flops 1536 | bytes 524 | tf_op jit(solution)/shard_map/convert_element_type | solution.py:259
  5.0 3.0 %collective-permute-start.1 = (bf16[80,256]{1,0:T(8,128)(2,1)S(1)}, bf16[80,256]{1,0:T(8,128)(2,1)S(1)}, u32[]{:S(2)}, u32[]{:S(2)}) collective-permute-start(bf16[80,256]{1,0:T(8,128)(2,1)S(1)} %get-tuple-element.56), channel_id=1, source_target_pairs={{0,2},{1,3},{2,0},{3,1},{4,6},{5,7},{6,4},{7,5},{8,10},{9,11},{10,... | collective-permute-start | bytes 122888 | tf_op jit(solution)/shard_map/ppermute | solution.py:242
  8.0 2.0 %collective-permute-done.1.refs_2_ = bf16[80,256]{1,0:T(8,128)(2,1)S(1)} collective-permute-done((bf16[80,256]{1,0:T(8,128)(2,1)S(1)}, bf16[80,256]{1,0:T(8,128)(2,1)S(1)}, u32[]{:S(2)}, u32[]{:S(2)}) %collective-permute-start.1) | collective-permute-done | bytes 40992 | tf_op jit(solution)/shard_map/ppermute | solution.py:242
  10.0 1.9 %collective-permute-done.2.refs_3_ = bf16[80,256]{1,0:T(8,128)(2,1)S(1)} collective-permute-done((bf16[80,256]{1,0:T(8,128)(2,1)S(1)}, bf16[80,256]{1,0:T(8,128)(2,1)S(1)}, u32[]{:S(2)}, u32[]{:S(2)}) %collective-permute-start.2) | collective-permute-done | bytes 40992 | tf_op jit(solution)/shard_map/ppermute | solution.py:242
  13.1 1.9 %collective-permute-start.7 = (bf16[64,512]{1,0:T(8,128)(2,1)S(1)}, bf16[64,512]{1,0:T(8,128)(2,1)S(1)}, u32[]{:S(2)}, u32[]{:S(2)}) collective-permute-start(bf16[64,512]{1,0:T(8,128)(2,1)S(1)} %get-tuple-element.65), channel_id=1, source_target_pairs={{0,2},{1,3},{2,0},{3,1},{4,6},{5,7},{6,4},{7,5},{8,10},{9,11},{10,... | collective-permute-start | bytes 196616 | tf_op jit(solution)/shard_map/ppermute | solution.py:242
  15.1 1.7 %collective-permute-start.5 = (bf16[272,256]{1,0:T(8,128)(2,1)S(1)}, bf16[272,256]{1,0:T(8,128)(2,1)S(1)}, u32[]{:S(2)}, u32[]{:S(2)}) collective-permute-start(bf16[272,256]{1,0:T(8,128)(2,1)S(1)} %team.2.refs_0_), channel_id=1, source_target_pairs={{0,16},{8,24},{16,0},{24,8},{1,17},{9,25},{17,1},{25,9},{2,18},{10... | collective-permute-start | bytes 417800 | tf_op jit(solution)/shard_map/ppermute | solution.py:245
  16.8 6.5 %collective-permute-done.7.refs_2_ = bf16[64,512]{1,0:T(8,128)(2,1)S(1)} collective-permute-done((bf16[64,512]{1,0:T(8,128)(2,1)S(1)}, bf16[64,512]{1,0:T(8,128)(2,1)S(1)}, u32[]{:S(2)}, u32[]{:S(2)}) %collective-permute-start.7) | collective-permute-done | bytes 65568 | tf_op jit(solution)/shard_map/ppermute | solution.py:242
  23.3 1.5 %collective-permute-start.4 = (bf16[272,256]{1,0:T(8,128)(2,1)S(1)}, bf16[272,256]{1,0:T(8,128)(2,1)S(1)}, u32[]{:S(2)}, u32[]{:S(2)}) collective-permute-start(bf16[272,256]{1,0:T(8,128)(2,1)S(1)} %team.2.refs_0_), channel_id=1, source_target_pairs={{0,8},{8,0},{16,24},{24,16},{1,9},{9,1},{17,25},{25,17},{2,10},{10... | collective-permute-start | bytes 417800 | tf_op jit(solution)/shard_map/ppermute | solution.py:245
  24.8 2.6 %collective-permute-start.3 = (bf16[272,256]{1,0:T(8,128)(2,1)S(1)}, bf16[272,256]{1,0:T(8,128)(2,1)S(1)}, u32[]{:S(2)}, u32[]{:S(2)}) collective-permute-start(bf16[272,256]{1,0:T(8,128)(2,1)S(1)} %team.2.refs_0_), channel_id=1, source_target_pairs={{0,4},{1,5},{2,6},{3,7},{4,0},{5,1},{6,2},{7,3},{8,12},{9,13},{10,... | collective-permute-start | bytes 417800 | tf_op jit(solution)/shard_map/ppermute | solution.py:248
  28.4 4.9 %collective-permute-done.3.refs_1_ = bf16[272,256]{1,0:T(8,128)(2,1)S(1)} collective-permute-done((bf16[272,256]{1,0:T(8,128)(2,1)S(1)}, bf16[272,256]{1,0:T(8,128)(2,1)S(1)}, u32[]{:S(2)}, u32[]{:S(2)}) %collective-permute-start.3) | collective-permute-done | bytes 139296 | tf_op jit(solution)/shard_map/ppermute | solution.py:248
  34.1 1.5 %collective-permute-start.15 = (bf16[256,256]{1,0:T(8,128)(2,1)S(1)}, bf16[256,256]{1,0:T(8,128)(2,1)S(1)}, u32[]{:S(2)}, u32[]{:S(2)}) collective-permute-start(bf16[256,256]{1,0:T(8,128)(2,1)S(1)} %get-tuple-element.77.refs_0_), channel_id=1, source_target_pairs={{0,8},{8,0},{16,24},{24,16},{1,9},{9,1},{17,25},{25,17},{2,10},{10... | collective-permute-start | bytes 393224 | tf_op jit(solution)/shard_map/ppermute | solution.py:245
  37.2 3.2 %collective-permute-start.14 = (bf16[256,256]{1,0:T(8,128)(2,1)S(1)}, bf16[256,256]{1,0:T(8,128)(2,1)}, u32[]{:S(2)}, u32[]{:S(2)}) collective-permute-start(bf16[256,256]{1,0:T(8,128)(2,1)S(1)} %get-tuple-element.77.refs_0_), channel_id=1, source_target_pairs={{0,4},{1,5},{2,6},{3,7},{4,0},{5,1},{6,2},{7,3},{8,12},{9,13},{10,... | collective-permute-start | bytes 393224 | tf_op jit(solution)/shard_map/ppermute | solution.py:248
  40.4 1.5 %collective-permute-start.12 = (bf16[272,256]{1,0:T(8,128)(2,1)S(1)}, bf16[272,256]{1,0:T(8,128)(2,1)}, u32[]{:S(2)}, u32[]{:S(2)}) collective-permute-start(bf16[272,256]{1,0:T(8,128)(2,1)S(1)} %collective-permute-done.3.refs_1_), channel_id=1, source_target_pairs={{0,16},{8,24},{16,0},{24,8},{1,17},{9,25},{17,1},{25,9},{2,18},{10... | collective-permute-start | bytes 417800 | tf_op jit(solution)/shard_map/ppermute | solution.py:245
  45.9 2.2 %collective-permute-done.13.refs_6_ = bf16[272,256]{1,0:T(8,128)(2,1)S(1)} collective-permute-done((bf16[272,256]{1,0:T(8,128)(2,1)S(1)}, bf16[272,256]{1,0:T(8,128)(2,1)S(1)}, u32[]{:S(2)}, u32[]{:S(2)}) %collective-permute-start.13) | collective-permute-done | bytes 139296 | tf_op jit(solution)/shard_map/ppermute | solution.py:245
  49.7 1.3 %collective-permute-start.19 = (bf16[256,256]{1,0:T(8,128)(2,1)}, bf16[256,256]{1,0:T(8,128)(2,1)}, u32[]{:S(2)}, u32[]{:S(2)}) collective-permute-start(bf16[256,256]{1,0:T(8,128)(2,1)} %collective-permute-done.14.refs_1_), channel_id=1, source_target_pairs={{0,8},{8,0},{16,24},{24,16},{1,9},{9,1},{17,25},{25,17},{2,10},{10... | collective-permute-start | bytes 393224 | tf_op jit(solution)/shard_map/ppermute | solution.py:245
  56.9 2.9 %collective-permute-done.21.refs_9_ = bf16[256,256]{1,0:T(8,128)(2,1)} collective-permute-done((bf16[256,256]{1,0:T(8,128)(2,1)S(1)}, bf16[256,256]{1,0:T(8,128)(2,1)}, u32[]{:S(2)}, u32[]{:S(2)}) %collective-permute-start.21) | collective-permute-done | bytes 131104 | tf_op jit(solution)/shard_map/ppermute | solution.py:248
  59.8 1.5 %collective-permute-start.27 = (bf16[256,256]{1,0:T(8,128)(2,1)S(1)}, bf16[256,256]{1,0:T(8,128)(2,1)S(1)}, u32[]{:S(2)}, u32[]{:S(2)}) collective-permute-start(bf16[256,256]{1,0:T(8,128)(2,1)S(1)} %get-tuple-element.92.refs_8_), channel_id=1, source_target_pairs={{0,16},{8,24},{16,0},{24,8},{1,17},{9,25},{17,1},{25,9},{2,18},{10... | collective-permute-start | bytes 393224 | tf_op jit(solution)/shard_map/ppermute | solution.py:245
  61.8 1.2 %collective-permute-start.29 = (bf16[256,256]{1,0:T(8,128)(2,1)}, bf16[256,256]{1,0:T(8,128)(2,1)S(1)}, u32[]{:S(2)}, u32[]{:S(2)}) collective-permute-start(bf16[256,256]{1,0:T(8,128)(2,1)} %collective-permute-done.21.refs_9_), channel_id=1, source_target_pairs={{0,16},{8,24},{16,0},{24,8},{1,17},{9,25},{17,1},{25,9},{2,18},{10... | collective-permute-start | bytes 393224 | tf_op jit(solution)/shard_map/ppermute | solution.py:245
  65.0 2.9 %project_kv.1.refs_0_ = bf16[512,256]{1,0:T(8,128)(2,1)S(1)} custom-call(bf16[512,2048]{1,0:T(8,128)(2,1)S(1)} %stack.8.x_ref, bf16[272,256]{1,0:T(8,128)(2,1)S(1)} %team.2.refs_0_, bf16[272,256]{1,0:T(8,128)(2,1)S(1)} %copy-done.23, bf16[272,256]{1,0:T(8,128)(2,1)S(1)} %copy-done.27, bf16[272,256]{1,0:T(8,128)(2,1)S(1)} %copy-done.29, ...), custom_call_target="tpu_custom_call" | custom-call | flops 536870912 | bytes 6291456 | tf_op jit(solution)/shard_map/project_kv/pallas_call | solution.py:336
  67.8 1.9 %collective-permute-start.23 = (bf16[512,256]{1,0:T(8,128)(2,1)S(1)}, bf16[512,256]{1,0:T(8,128)(2,1)}, u32[]{:S(2)}, u32[]{:S(2)}) collective-permute-start(bf16[512,256]{1,0:T(8,128)(2,1)S(1)} %project_kv.1.refs_0_), channel_id=1, source_target_pairs={{0,4},{1,5},{2,6},{3,7},{4,0},{5,1},{6,2},{7,3},{8,12},{9,13},{10,... | collective-permute-start | bytes 786440 | tf_op jit(solution)/shard_map/ppermute | solution.py:248
  71.1 1.4 %collective-permute-start.32 = (bf16[256,256]{1,0:T(8,128)(2,1)S(1)}, bf16[256,256]{1,0:T(8,128)(2,1)S(1)}, u32[]{:S(2)}, u32[]{:S(2)}) collective-permute-start(bf16[256,256]{1,0:T(8,128)(2,1)S(1)} %collective-permute-done.26.refs_10_), channel_id=1, source_target_pairs={{0,16},{8,24},{16,0},{24,8},{1,17},{9,25},{17,1},{25,9},{2,18},{10... | collective-permute-start | bytes 393224 | tf_op jit(solution)/shard_map/ppermute | solution.py:245
  72.4 1.5 %collective-permute-start.33 = (bf16[256,256]{1,0:T(8,128)(2,1)S(1)}, bf16[256,256]{1,0:T(8,128)(2,1)S(1)}, u32[]{:S(2)}, u32[]{:S(2)}) collective-permute-start(bf16[256,256]{1,0:T(8,128)(2,1)S(1)} %collective-permute-done.29.refs_13_), channel_id=1, source_target_pairs={{0,8},{8,0},{16,24},{24,16},{1,9},{9,1},{17,25},{25,17},{2,10},{10... | collective-permute-start | bytes 393224 | tf_op jit(solution)/shard_map/ppermute | solution.py:245
  77.4 2.9 %project_q.3 = bf16[256,512]{1,0:T(8,128)(2,1)} custom-call(bf16[512,2048]{1,0:T(8,128)(2,1)S(1)} %stack.8.x_ref, bf16[256,256]{1,0:T(8,128)(2,1)S(1)} %get-tuple-element.77.refs_0_, bf16[256,256]{1,0:T(8,128)(2,1)} %collective-permute-done.14.refs_1_, bf16[256,256]{1,0:T(8,128)(2,1)S(1)} %copy-done.2, bf16[256,256]{1,0:T(8,128)(2,1)} %collective-permute-done.19.refs_3_, ...), custom_call_target="tpu_custom_call" | custom-call | flops 536870912 | bytes 6291456 | tf_op jit(solution)/shard_map/project_q/pallas_call | solution.py:336
  87.4 2.2 %project_q.2.q_ref = bf16[256,512]{1,0:T(8,128)(2,1)S(1)} custom-call(bf16[512,2048]{1,0:T(8,128)(2,1)S(1)} %stack.8.x_ref, bf16[256,256]{1,0:T(8,128)(2,1)S(1)} %get-tuple-element.77.refs_0_, bf16[256,256]{1,0:T(8,128)(2,1)} %collective-permute-done.14.refs_1_, bf16[256,256]{1,0:T(8,128)(2,1)S(1)} %copy-done.2, ...), custom_call_target="tpu_custom_call" | custom-call | flops 536870912 | bytes 6291456 | tf_op jit(solution)/shard_map/project_q/pallas_call | solution.py:336
  89.6 2.3 %pages.1 = (bf16[4,64,512]{2,1,0:T(8,128)(2,1)S(1)}, bf16[4,64,512]{2,1,0:T(8,128)(2,1)S(1)}, bf16[2,1024,256]{2,1,0:T(8,128)(2,1)S(1)}) custom-call(bf16[512,256]{1,0:T(8,128)(2,1)S(1)} %project_kv.1.refs_0_, bf16[512,256]{1,0:T(8,128)(2,1)} %collective-permute-done.23.refs_1_, bf16[512,256]{1,0:T(8,128)(2,1)} %collective-permute-done.24.refs_2_, ...), custom_call_target="tpu_custom_call" | custom-call | bytes 4194304 | tf_op jit(solution)/shard_map/pages/pallas_call | solution.py:374
  91.9 2.4 %attend.3 = bf16[128,1024]{1,0:T(8,128)(2,1)S(1)} custom-call(bf16[2,1024,256]{2,1,0:T(8,128)(2,1)S(1)} %get-tuple-element.89.store, bf16[256,512]{1,0:T(8,128)(2,1)S(1)} %project_q.2.q_ref, bf16[256,512]{1,0:T(8,128)(2,1)} %collective-permute-done.34.near_ref, s32[16]{0:T(128)S(1)} %reshape.150.refs_4_.ids_ref, s32[1]{0:T(128)} %copy.10.length_ref), custom_call_target="tpu_custom_call" | custom-call | flops 536870912 | bytes 4194304 | tf_op jit(solution)/shard_map/attend/pallas_call | solution.py:387
  94.4 1.4 %collective-permute-start.35 = (bf16[128,1024]{1,0:T(8,128)(2,1)S(1)}, bf16[128,1024]{1,0:T(8,128)(2,1)S(1)}, u32[]{:S(2)}, u32[]{:S(2)}) collective-permute-start(bf16[128,1024]{1,0:T(8,128)(2,1)S(1)} %attend.3), channel_id=1, source_target_pairs={{0,2},{1,3},{2,0},{3,1},{4,6},{5,7},{6,4},{7,5},{8,10},{9,11},{10,... | collective-permute-start | bytes 786440 | tf_op jit(solution)/shard_map/ppermute | solution.py:242
  96.5 2.6 %attend.2.kept = bf16[128,1024]{1,0:T(8,128)(2,1)S(1)} custom-call(bf16[2,1024,256]{2,1,0:T(8,128)(2,1)S(1)} %get-tuple-element.89.store, bf16[256,512]{1,0:T(8,128)(2,1)S(1)} %project_q.2.q_ref, bf16[256,512]{1,0:T(8,128)(2,1)} %collective-permute-done.34.near_ref, s32[16]{0:T(128)S(1)} %reshape.150.refs_4_.ids_ref, s32[1]{0:T(128)} %copy.10.length_ref), custom_call_target="tpu_custom_call" | custom-call | flops 536870912 | bytes 4194304 | tf_op jit(solution)/shard_map/attend/pallas_call | solution.py:387
  99.1 4.5 %collective-permute-done.35.from_far = bf16[128,1024]{1,0:T(8,128)(2,1)S(1)} collective-permute-done((bf16[128,1024]{1,0:T(8,128)(2,1)S(1)}, bf16[128,1024]{1,0:T(8,128)(2,1)S(1)}, u32[]{:S(2)}, u32[]{:S(2)}) %collective-permute-start.35) | collective-permute-done | bytes 262176 | tf_op jit(solution)/shard_map/ppermute | solution.py:242
  103.6 4.9 %collective-permute-done.36.got_pages = bf16[4,64,512]{2,1,0:T(8,128)(2,1)S(1)} collective-permute-done((bf16[4,64,512]{2,1,0:T(8,128)(2,1)S(1)}, bf16[4,64,512]{2,1,0:T(8,128)(2,1)S(1)}, u32[]{:S(2)}, u32[]{:S(2)}) %collective-permute-start.36) | collective-permute-done | bytes 262176 | tf_op jit(solution)/shard_map/ppermute | solution.py:242
  108.5 1.5 %finish.1 = (bf16[128,2048]{1,0:T(8,128)(2,1)}, bf16[4,64,512]{2,1,0:T(8,128)(2,1)}) custom-call(bf16[128,1024]{1,0:T(8,128)(2,1)S(1)} %attend.2.kept, bf16[128,1024]{1,0:T(8,128)(2,1)S(1)} %collective-permute-done.35.from_far, bf16[4,64,512]{2,1,0:T(8,128)(2,1)S(1)} %get-tuple-element.102.own_pages, ...), custom_call_target="tpu_custom_call" | custom-call | tf_op jit(solution)/shard_map/finish/pallas_call | solution.py:402
  (145 shorter events, 32.0 us)
Async XLA Ops:
  0.6 32.7 %collective-permute-start.10 = (bf16[128,2048]{1,0:T(8,128)(2,1)}, bf16[128,2048]{1,0:T(8,128)(2,1)S(1)}, u32[]{:S(2)}, u32[]{:S(2)}) collective-permute-start(bf16[128,2048]{1,0:T(8,128)(2,1)} %bitcast.34), channel_id=1, source_target_pairs={{0,1},{1,0},{2,3},{3,2},{4,5},{5,4},{6,7},{7,6},{8,9},{9,8},{10,11... | collective-permute-start | bytes 1572872 | tf_op jit(solution)/shard_map/ppermute | solution.py:242
  5.0 5.0 %collective-permute-start.1 = (bf16[80,256]{1,0:T(8,128)(2,1)S(1)}, bf16[80,256]{1,0:T(8,128)(2,1)S(1)}, u32[]{:S(2)}, u32[]{:S(2)}) collective-permute-start(bf16[80,256]{1,0:T(8,128)(2,1)S(1)} %get-tuple-element.56), channel_id=1, source_target_pairs={{0,2},{1,3},{2,0},{3,1},{4,6},{5,7},{6,4},{7,5},{8,10},{9,11},{10,... | collective-permute-start | bytes 122888 | tf_op jit(solution)/shard_map/ppermute | solution.py:242
  12.8 20.5 %collective-permute-start.9 = (bf16[64,2048]{1,0:T(8,128)(2,1)S(1)}, bf16[64,2048]{1,0:T(8,128)(2,1)S(1)}, u32[]{:S(2)}, u32[]{:S(2)}) collective-permute-start(bf16[64,2048]{1,0:T(8,128)(2,1)S(1)} %slice.20), channel_id=1, source_target_pairs={{0,2},{1,3},{2,0},{3,1},{4,6},{5,7},{6,4},{7,5},{8,10},{9,11},{10,... | collective-permute-start | bytes 786440 | tf_op jit(solution)/shard_map/ppermute | solution.py:242
  13.1 10.2 %collective-permute-start.7 = (bf16[64,512]{1,0:T(8,128)(2,1)S(1)}, bf16[64,512]{1,0:T(8,128)(2,1)S(1)}, u32[]{:S(2)}, u32[]{:S(2)}) collective-permute-start(bf16[64,512]{1,0:T(8,128)(2,1)S(1)} %get-tuple-element.65), channel_id=1, source_target_pairs={{0,2},{1,3},{2,0},{3,1},{4,6},{5,7},{6,4},{7,5},{8,10},{9,11},{10,... | collective-permute-start | bytes 196616 | tf_op jit(solution)/shard_map/ppermute | solution.py:242
  14.9 9.9 %collective-permute-start.8 = (bf16[64,512]{1,0:T(8,128)(2,1)S(1)}, bf16[64,512]{1,0:T(8,128)(2,1)S(1)}, u32[]{:S(2)}, u32[]{:S(2)}) collective-permute-start(bf16[64,512]{1,0:T(8,128)(2,1)S(1)} %get-tuple-element.66), channel_id=1, source_target_pairs={{0,3},{1,2},{2,1},{3,0},{4,7},{5,6},{6,5},{7,4},{8,11},{9,10},{10,... | collective-permute-start | bytes 196616 | tf_op jit(solution)/shard_map/ppermute | solution.py:242
  15.1 12.4 %collective-permute-start.5 = (bf16[272,256]{1,0:T(8,128)(2,1)S(1)}, bf16[272,256]{1,0:T(8,128)(2,1)S(1)}, u32[]{:S(2)}, u32[]{:S(2)}) collective-permute-start(bf16[272,256]{1,0:T(8,128)(2,1)S(1)} %team.2.refs_0_), channel_id=1, source_target_pairs={{0,16},{8,24},{16,0},{24,8},{1,17},{9,25},{17,1},{25,9},{2,18},{10... | collective-permute-start | bytes 417800 | tf_op jit(solution)/shard_map/ppermute | solution.py:245
  23.3 5.1 %collective-permute-start.4 = (bf16[272,256]{1,0:T(8,128)(2,1)S(1)}, bf16[272,256]{1,0:T(8,128)(2,1)S(1)}, u32[]{:S(2)}, u32[]{:S(2)}) collective-permute-start(bf16[272,256]{1,0:T(8,128)(2,1)S(1)} %team.2.refs_0_), channel_id=1, source_target_pairs={{0,8},{8,0},{16,24},{24,16},{1,9},{9,1},{17,25},{25,17},{2,10},{10... | collective-permute-start | bytes 417800 | tf_op jit(solution)/shard_map/ppermute | solution.py:245
  24.8 8.5 %collective-permute-start.3 = (bf16[272,256]{1,0:T(8,128)(2,1)S(1)}, bf16[272,256]{1,0:T(8,128)(2,1)S(1)}, u32[]{:S(2)}, u32[]{:S(2)}) collective-permute-start(bf16[272,256]{1,0:T(8,128)(2,1)S(1)} %team.2.refs_0_), channel_id=1, source_target_pairs={{0,4},{1,5},{2,6},{3,7},{4,0},{5,1},{6,2},{7,3},{8,12},{9,13},{10,... | collective-permute-start | bytes 417800 | tf_op jit(solution)/shard_map/ppermute | solution.py:248
  34.1 9.0 %collective-permute-start.15 = (bf16[256,256]{1,0:T(8,128)(2,1)S(1)}, bf16[256,256]{1,0:T(8,128)(2,1)S(1)}, u32[]{:S(2)}, u32[]{:S(2)}) collective-permute-start(bf16[256,256]{1,0:T(8,128)(2,1)S(1)} %get-tuple-element.77.refs_0_), channel_id=1, source_target_pairs={{0,8},{8,0},{16,24},{24,16},{1,9},{9,1},{17,25},{25,17},{2,10},{10... | collective-permute-start | bytes 393224 | tf_op jit(solution)/shard_map/ppermute | solution.py:245
  36.6 12.3 %collective-permute-start.16 = (bf16[64,2048]{1,0:T(8,128)(2,1)S(1)}, bf16[64,2048]{1,0:T(8,128)(2,1)S(1)}, u32[]{:S(2)}, u32[]{:S(2)}) collective-permute-start(bf16[64,2048]{1,0:T(8,128)(2,1)S(1)} %slice.21), channel_id=1, source_target_pairs={{0,2},{1,3},{2,0},{3,1},{4,6},{5,7},{6,4},{7,5},{8,10},{9,11},{10,... | collective-permute-start | bytes 786440 | tf_op jit(solution)/shard_map/ppermute | solution.py:242
  37.2 8.8 %collective-permute-start.14 = (bf16[256,256]{1,0:T(8,128)(2,1)S(1)}, bf16[256,256]{1,0:T(8,128)(2,1)}, u32[]{:S(2)}, u32[]{:S(2)}) collective-permute-start(bf16[256,256]{1,0:T(8,128)(2,1)S(1)} %get-tuple-element.77.refs_0_), channel_id=1, source_target_pairs={{0,4},{1,5},{2,6},{3,7},{4,0},{5,1},{6,2},{7,3},{8,12},{9,13},{10,... | collective-permute-start | bytes 393224 | tf_op jit(solution)/shard_map/ppermute | solution.py:248
  40.4 8.4 %collective-permute-start.12 = (bf16[272,256]{1,0:T(8,128)(2,1)S(1)}, bf16[272,256]{1,0:T(8,128)(2,1)}, u32[]{:S(2)}, u32[]{:S(2)}) collective-permute-start(bf16[272,256]{1,0:T(8,128)(2,1)S(1)} %collective-permute-done.3.refs_1_), channel_id=1, source_target_pairs={{0,16},{8,24},{16,0},{24,8},{1,17},{9,25},{17,1},{25,9},{2,18},{10... | collective-permute-start | bytes 417800 | tf_op jit(solution)/shard_map/ppermute | solution.py:245
  41.9 6.9 %collective-permute-start.11 = (bf16[272,256]{1,0:T(8,128)(2,1)S(1)}, bf16[272,256]{1,0:T(8,128)(2,1)S(1)}, u32[]{:S(2)}, u32[]{:S(2)}) collective-permute-start(bf16[272,256]{1,0:T(8,128)(2,1)S(1)} %collective-permute-done.3.refs_1_), channel_id=1, source_target_pairs={{0,8},{8,0},{16,24},{24,16},{1,9},{9,1},{17,25},{25,17},{2,10},{10... | collective-permute-start | bytes 417800 | tf_op jit(solution)/shard_map/ppermute | solution.py:245
  43.1 5.1 %collective-permute-start.13 = (bf16[272,256]{1,0:T(8,128)(2,1)S(1)}, bf16[272,256]{1,0:T(8,128)(2,1)S(1)}, u32[]{:S(2)}, u32[]{:S(2)}) collective-permute-start(bf16[272,256]{1,0:T(8,128)(2,1)S(1)} %collective-permute-done.4.refs_2_), channel_id=1, source_target_pairs={{0,16},{8,24},{16,0},{24,8},{1,17},{9,25},{17,1},{25,9},{2,18},{10... | collective-permute-start | bytes 417800 | tf_op jit(solution)/shard_map/ppermute | solution.py:245
  49.0 10.8 %collective-permute-start.20 = (bf16[256,256]{1,0:T(8,128)(2,1)}, bf16[256,256]{1,0:T(8,128)(2,1)}, u32[]{:S(2)}, u32[]{:S(2)}) collective-permute-start(bf16[256,256]{1,0:T(8,128)(2,1)} %collective-permute-done.14.refs_1_), channel_id=1, source_target_pairs={{0,16},{8,24},{16,0},{24,8},{1,17},{9,25},{17,1},{25,9},{2,18},{10... | collective-permute-start | bytes 393224 | tf_op jit(solution)/shard_map/ppermute | solution.py:245
  49.7 10.0 %collective-permute-start.19 = (bf16[256,256]{1,0:T(8,128)(2,1)}, bf16[256,256]{1,0:T(8,128)(2,1)}, u32[]{:S(2)}, u32[]{:S(2)}) collective-permute-start(bf16[256,256]{1,0:T(8,128)(2,1)} %collective-permute-done.14.refs_1_), channel_id=1, source_target_pairs={{0,8},{8,0},{16,24},{24,16},{1,9},{9,1},{17,25},{25,17},{2,10},{10... | collective-permute-start | bytes 393224 | tf_op jit(solution)/shard_map/ppermute | solution.py:245
  51.1 8.7 %collective-permute-start.21 = (bf16[256,256]{1,0:T(8,128)(2,1)S(1)}, bf16[256,256]{1,0:T(8,128)(2,1)}, u32[]{:S(2)}, u32[]{:S(2)}) collective-permute-start(bf16[256,256]{1,0:T(8,128)(2,1)S(1)} %get-tuple-element.92.refs_8_), channel_id=1, source_target_pairs={{0,4},{1,5},{2,6},{3,7},{4,0},{5,1},{6,2},{7,3},{8,12},{9,13},{10,... | collective-permute-start | bytes 393224 | tf_op jit(solution)/shard_map/ppermute | solution.py:248
  51.4 8.4 %collective-permute-start.18 = (bf16[256,256]{1,0:T(8,128)(2,1)S(1)}, bf16[256,256]{1,0:T(8,128)(2,1)}, u32[]{:S(2)}, u32[]{:S(2)}) collective-permute-start(bf16[256,256]{1,0:T(8,128)(2,1)S(1)} %get-tuple-element.77.refs_0_), channel_id=1, source_target_pairs={{0,16},{8,24},{16,0},{24,8},{1,17},{9,25},{17,1},{25,9},{2,18},{10... | collective-permute-start | bytes 393224 | tf_op jit(solution)/shard_map/ppermute | solution.py:245
  53.4 6.4 %collective-permute-start.17 = (bf16[272,256]{1,0:T(8,128)(2,1)}, bf16[272,256]{1,0:T(8,128)(2,1)}, u32[]{:S(2)}, u32[]{:S(2)}) collective-permute-start(bf16[272,256]{1,0:T(8,128)(2,1)} %collective-permute-done.12.refs_5_), channel_id=1, source_target_pairs={{0,8},{8,0},{16,24},{24,16},{1,9},{9,1},{17,25},{25,17},{2,10},{10... | collective-permute-start | bytes 417800 | tf_op jit(solution)/shard_map/ppermute | solution.py:245
  59.8 10.0 %collective-permute-start.27 = (bf16[256,256]{1,0:T(8,128)(2,1)S(1)}, bf16[256,256]{1,0:T(8,128)(2,1)S(1)}, u32[]{:S(2)}, u32[]{:S(2)}) collective-permute-start(bf16[256,256]{1,0:T(8,128)(2,1)S(1)} %get-tuple-element.92.refs_8_), channel_id=1, source_target_pairs={{0,16},{8,24},{16,0},{24,8},{1,17},{9,25},{17,1},{25,9},{2,18},{10... | collective-permute-start | bytes 393224 | tf_op jit(solution)/shard_map/ppermute | solution.py:245
  61.3 8.5 %collective-permute-start.26 = (bf16[256,256]{1,0:T(8,128)(2,1)S(1)}, bf16[256,256]{1,0:T(8,128)(2,1)S(1)}, u32[]{:S(2)}, u32[]{:S(2)}) collective-permute-start(bf16[256,256]{1,0:T(8,128)(2,1)S(1)} %get-tuple-element.92.refs_8_), channel_id=1, source_target_pairs={{0,8},{8,0},{16,24},{24,16},{1,9},{9,1},{17,25},{25,17},{2,10},{10... | collective-permute-start | bytes 393224 | tf_op jit(solution)/shard_map/ppermute | solution.py:245
  61.8 7.9 %collective-permute-start.29 = (bf16[256,256]{1,0:T(8,128)(2,1)}, bf16[256,256]{1,0:T(8,128)(2,1)S(1)}, u32[]{:S(2)}, u32[]{:S(2)}) collective-permute-start(bf16[256,256]{1,0:T(8,128)(2,1)} %collective-permute-done.21.refs_9_), channel_id=1, source_target_pairs={{0,16},{8,24},{16,0},{24,8},{1,17},{9,25},{17,1},{25,9},{2,18},{10... | collective-permute-start | bytes 393224 | tf_op jit(solution)/shard_map/ppermute | solution.py:245
  63.0 6.7 %collective-permute-start.28 = (bf16[256,256]{1,0:T(8,128)(2,1)}, bf16[256,256]{1,0:T(8,128)(2,1)S(1)}, u32[]{:S(2)}, u32[]{:S(2)}) collective-permute-start(bf16[256,256]{1,0:T(8,128)(2,1)} %collective-permute-done.21.refs_9_), channel_id=1, source_target_pairs={{0,8},{8,0},{16,24},{24,16},{1,9},{9,1},{17,25},{25,17},{2,10},{10... | collective-permute-start | bytes 393224 | tf_op jit(solution)/shard_map/ppermute | solution.py:245
  67.8 12.8 %collective-permute-start.23 = (bf16[512,256]{1,0:T(8,128)(2,1)S(1)}, bf16[512,256]{1,0:T(8,128)(2,1)}, u32[]{:S(2)}, u32[]{:S(2)}) collective-permute-start(bf16[512,256]{1,0:T(8,128)(2,1)S(1)} %project_kv.1.refs_0_), channel_id=1, source_target_pairs={{0,4},{1,5},{2,6},{3,7},{4,0},{5,1},{6,2},{7,3},{8,12},{9,13},{10,... | collective-permute-start | bytes 786440 | tf_op jit(solution)/shard_map/ppermute | solution.py:248
  69.8 5.1 %collective-permute-start.30 = (bf16[256,256]{1,0:T(8,128)(2,1)S(1)}, bf16[256,256]{1,0:T(8,128)(2,1)S(1)}, u32[]{:S(2)}, u32[]{:S(2)}) collective-permute-start(bf16[256,256]{1,0:T(8,128)(2,1)S(1)} %copy-done.2), channel_id=1, source_target_pairs={{0,16},{8,24},{16,0},{24,8},{1,17},{9,25},{17,1},{25,9},{2,18},{10... | collective-permute-start | bytes 393224 | tf_op jit(solution)/shard_map/ppermute | solution.py:245
  70.4 5.2 %collective-permute-start.31 = (bf16[256,256]{1,0:T(8,128)(2,1)}, bf16[256,256]{1,0:T(8,128)(2,1)S(1)}, u32[]{:S(2)}, u32[]{:S(2)}) collective-permute-start(bf16[256,256]{1,0:T(8,128)(2,1)} %collective-permute-done.20.refs_5_), channel_id=1, source_target_pairs={{0,8},{8,0},{16,24},{24,16},{1,9},{9,1},{17,25},{25,17},{2,10},{10... | collective-permute-start | bytes 393224 | tf_op jit(solution)/shard_map/ppermute | solution.py:245
  71.1 5.2 %collective-permute-start.32 = (bf16[256,256]{1,0:T(8,128)(2,1)S(1)}, bf16[256,256]{1,0:T(8,128)(2,1)S(1)}, u32[]{:S(2)}, u32[]{:S(2)}) collective-permute-start(bf16[256,256]{1,0:T(8,128)(2,1)S(1)} %collective-permute-done.26.refs_10_), channel_id=1, source_target_pairs={{0,16},{8,24},{16,0},{24,8},{1,17},{9,25},{17,1},{25,9},{2,18},{10... | collective-permute-start | bytes 393224 | tf_op jit(solution)/shard_map/ppermute | solution.py:245
  74.9 14.7 %collective-permute-start.24 = (bf16[512,256]{1,0:T(8,128)(2,1)S(1)}, bf16[512,256]{1,0:T(8,128)(2,1)}, u32[]{:S(2)}, u32[]{:S(2)}) collective-permute-start(bf16[512,256]{1,0:T(8,128)(2,1)S(1)} %project_kv.1.refs_0_), channel_id=1, source_target_pairs={{0,1},{1,0},{2,3},{3,2},{4,5},{5,4},{6,7},{7,6},{8,9},{9,8},{10,11... | collective-permute-start | bytes 786440 | tf_op jit(solution)/shard_map/ppermute | solution.py:242
  80.4 11.5 %collective-permute-start.34 = (bf16[256,512]{1,0:T(8,128)(2,1)}, bf16[256,512]{1,0:T(8,128)(2,1)}, u32[]{:S(2)}, u32[]{:S(2)}) collective-permute-start(bf16[256,512]{1,0:T(8,128)(2,1)} %project_q.3), channel_id=1, source_target_pairs={{0,1},{1,0},{2,3},{3,2},{4,5},{5,4},{6,7},{7,6},{8,9},{9,8},{10,11... | collective-permute-start | bytes 786440 | tf_op jit(solution)/shard_map/ppermute | solution.py:242
  80.7 9.0 %collective-permute-start.25 = (bf16[512,256]{1,0:T(8,128)(2,1)}, bf16[512,256]{1,0:T(8,128)(2,1)}, u32[]{:S(2)}, u32[]{:S(2)}) collective-permute-start(bf16[512,256]{1,0:T(8,128)(2,1)} %collective-permute-done.23.refs_1_), channel_id=1, source_target_pairs={{0,1},{1,0},{2,3},{3,2},{4,5},{5,4},{6,7},{7,6},{8,9},{9,8},{10,11... | collective-permute-start | bytes 786440 | tf_op jit(solution)/shard_map/ppermute | solution.py:242
  94.4 9.2 %collective-permute-start.35 = (bf16[128,1024]{1,0:T(8,128)(2,1)S(1)}, bf16[128,1024]{1,0:T(8,128)(2,1)S(1)}, u32[]{:S(2)}, u32[]{:S(2)}) collective-permute-start(bf16[128,1024]{1,0:T(8,128)(2,1)S(1)} %attend.3), channel_id=1, source_target_pairs={{0,2},{1,3},{2,0},{3,1},{4,6},{5,7},{6,4},{7,5},{8,10},{9,11},{10,... | collective-permute-start | bytes 786440 | tf_op jit(solution)/shard_map/ppermute | solution.py:242
  95.7 12.8 %collective-permute-start.36 = (bf16[4,64,512]{2,1,0:T(8,128)(2,1)S(1)}, bf16[4,64,512]{2,1,0:T(8,128)(2,1)S(1)}, u32[]{:S(2)}, u32[]{:S(2)}) collective-permute-start(bf16[4,64,512]{2,1,0:T(8,128)(2,1)S(1)} %get-tuple-element.103), channel_id=1, source_target_pairs={{0,2},{1,3},{2,0},{3,1},{4,6},{5,7},{6,4},{7,5},{8,10},{9,11},{10,... | collective-permute-start | bytes 786440 | tf_op jit(solution)/shard_map/ppermute | solution.py:242
  (40 other events, 220.3 us)

commit v5 on v4

--- a/solution.py
+++ b/solution.py
@@ -51,25 +51,33 @@
 
 def pack_kernel(w_ref, ids_ref, *outs):
     _, pair, core = place()
+    member = pair * 2 + core
     rows = w_ref.shape[0]
+    per_device = ids_ref.shape[1]
+    lane = lax.broadcasted_iota(jnp.int32, (ID_ROWS, HD), 1) - member * per_device
+    ids = jnp.zeros((ID_ROWS, HD), jnp.int32)
+    for j in range(per_device):
+        ids = jnp.where(lane == j, ids_ref[0, j], ids)
+    ids = ids.astype(jnp.float32).astype(jnp.bfloat16)
     for k in range(TEAM):
         to_pair, to_core = pair ^ (k // 2), core ^ (k % 2)
-        outs[k][:rows, :] = w_ref[:, pl.ds(kv_start(to_pair, to_core), HD)]
-        outs[k][rows:, :] = ids_ref[...]
-        outs[TEAM + k][...] = w_ref[:, pl.ds(q_start(to_pair, to_core), 2 * HD)]
-
-
-def team_kernel(rows, *refs):
+        outs[k][:rows, :HD] = w_ref[:, pl.ds(kv_start(to_pair, to_core), HD)]
+        outs[k][:rows, HD:] = w_ref[:, pl.ds(q_start(to_pair, to_core), 2 * HD)]
+        outs[k][rows:, :HD] = ids
+        outs[k][rows:, HD:] = jnp.zeros((ID_ROWS, 2 * HD), jnp.bfloat16)
+
+
+def team_kernel(*refs):
     _, pair, core = place()
-    parts, outs = refs[:TEAM], refs[TEAM:]
+    parts, kv_out, q_out = refs[:TEAM], refs[TEAM], refs[TEAM + 1]
+    rows = q_out.shape[0] // TEAM
     member = pair * 2 + core
-    for n, out in enumerate(outs):
-        cols = slice(n * HD, (n + 1) * HD)
-        for k in range(TEAM):
-            out[aligned(member ^ k, rows), :] = parts[k][:rows, cols]
-        if parts[0].shape[0] > rows:
-            below = [part[rows:, cols].astype(jnp.float32) for part in parts]
-            out[TEAM * rows :, :] = sum(below[1:], below[0]).astype(out.dtype)
+    for k in range(TEAM):
+        here = aligned(member ^ k, rows)
+        kv_out[here, :] = parts[k][:rows, :HD]
+        q_out[here, :] = parts[k][:rows, HD:]
+    below = [part[rows:, :HD].astype(jnp.float32) for part in parts]
+    kv_out[TEAM * rows :, :] = sum(below[1:], below[0]).astype(jnp.bfloat16)
 
 
 def stack_kernel(*refs):
@@ -82,19 +90,17 @@
     ])
 
 
-def project_kernel(steps, n_out, depth, is_kv, x_ref, *refs):
-    gain_ref, cos_ref, sin_ref, out, w_all, sems = refs[-6:]
-    weights = refs[:-6]
+def project_kernel(n_out, depth, is_kv, x_ref, *refs):
+    n_outs = 1 if is_kv else 2
+    weights, (gain_ref, cos_ref, sin_ref) = refs[: -5 - n_outs], refs[-5 - n_outs : -2 - n_outs]
+    outs, (w_all, sems) = refs[-2 - n_outs : -2], refs[-2:]
     req = lax.axis_index("req")
     outer = lax.axis_index("blk") // TEAM
     _, pair, core = place()
     member = pair * 2 + core
     rows = x_ref.shape[0] // TEAM
     copies = []
-    per_chunk = 2 * (w_all.shape[0] // (depth * n_out))
-    for at, piece in enumerate(weights):
-        i = at % per_chunk
-        cols = slice(at // per_chunk * HD, (at // per_chunk + 1) * HD)
+    for i, piece in enumerate(weights):
         from_req = req ^ (i // 2)
         tall = piece.shape[0] // (n_out - 1 if i % 2 else 1)
         for n in range(n_out - 1 if i % 2 else 1):
@@ -102,7 +108,7 @@
             copies.append(
                 pltpu.make_async_copy(
                     piece.at[pl.ds(n * tall, depth), :],
-                    w_all.at[aligned(from_req * n_out + from_outer, depth), cols],
+                    w_all.at[aligned(from_req * n_out + from_outer, depth), :],
                     sems.at[len(copies)],
                 )
             )
@@ -110,24 +116,25 @@
     half = HD // 2
     gain = gain_ref[...]
     if is_kv:
-        x, cosine, sine = x_ref[...], cos_ref[...], sin_ref[...]
-        is_key = core == 0
-        cosine = jnp.where(is_key, cosine, 1.0)
-        sine = jnp.where(is_key, sine, 0.0)
-        gain = jnp.where(is_key, gain, 1.0)
-    else:
-        x, cosine, sine = (
-            jnp.concatenate([ref[aligned(member ^ k, rows), :] for k in steps], 0)
-            for ref in (x_ref, cos_ref, sin_ref)
-        )
-    product = jnp.dot(x, w_all[...], preferred_element_type=jnp.float32)
-    for h in range(out.shape[1] // HD):
-        head = product[:, h * HD : (h + 1) * HD]
-        mean = jnp.mean(head * head, axis=-1, keepdims=True)
-        head = head * lax.rsqrt(mean + NORM_EPS) * gain
-        front, second = head[:, :half], head[:, half:]
-        out[:, h * HD : h * HD + half] = (front * cosine - second * sine).astype(jnp.bfloat16)
-        out[:, h * HD + half : (h + 1) * HD] = (second * cosine + front * sine).astype(jnp.bfloat16)
+        gain = jnp.where(core == 0, gain, 1.0)
+    for out, steps in zip(outs, [(0, 1, 2, 3)] if is_kv else [(1, 3), (0, 2)]):
+        if is_kv:
+            x, cosine, sine = x_ref[...], cos_ref[...], sin_ref[...]
+            cosine = jnp.where(core == 0, cosine, 1.0)
+            sine = jnp.where(core == 0, sine, 0.0)
+        else:
+            x, cosine, sine = (
+                jnp.concatenate([ref[aligned(member ^ k, rows), :] for k in steps], 0)
+                for ref in (x_ref, cos_ref, sin_ref)
+            )
+        product = jnp.dot(x, w_all[...], preferred_element_type=jnp.float32)
+        for h in range(out.shape[1] // HD):
+            head = product[:, h * HD : (h + 1) * HD]
+            mean = jnp.mean(head * head, axis=-1, keepdims=True)
+            head = head * lax.rsqrt(mean + NORM_EPS) * gain
+            front, second = head[:, :half], head[:, half:]
+            out[:, h * HD : h * HD + half] = (front * cosine - second * sine).astype(jnp.bfloat16)
+            out[:, h * HD + half : (h + 1) * HD] = (second * cosine + front * sine).astype(jnp.bfloat16)
 
 
 def load_kv(n_out, blk_rows, mine, other, ids_ref, store, sems, core):
@@ -252,55 +259,44 @@
 
     w_rows = qkv_weight.shape[0]
     per_device = block_ids.shape[1]
-    lane = jnp.arange(HD, dtype=jnp.int32) - member * per_device
-    ids_row = jnp.zeros((HD,), jnp.int32)
-    for j in range(per_device):
-        ids_row = jnp.where(lane == j, block_ids[0, j], ids_row)
-    ids_rows = jnp.broadcast_to(ids_row.astype(bf16)[None, :], (ID_ROWS, HD))
-    packed = pl.pallas_call(
+    parts = pl.pallas_call(
         pack_kernel,
-        out_shape=[shape((w_rows + ID_ROWS, HD), bf16)] * TEAM + [shape((w_rows, 2 * HD), bf16)] * TEAM,
-        in_specs=[VMEM] * 2,
-        out_specs=[VMEM] * (2 * TEAM),
+        out_shape=[shape((w_rows + ID_ROWS, 3 * HD), bf16)] * TEAM,
+        in_specs=[VMEM, SMEM],
+        out_specs=[VMEM] * TEAM,
         compiler_params=params(2),
         name="pack",
-    )(qkv_weight, ids_rows)
-
-    def exchange(parts):
-        return [parts[0]] + [in_team(part, k) for k, part in enumerate(parts) if k]
-
-    def assemble(parts):
-        below = parts[0].shape[0] - w_rows
-        return pl.pallas_call(
-            functools.partial(team_kernel, w_rows),
-            out_shape=[shape((TEAM * w_rows + below, HD), bf16)] * (parts[0].shape[1] // HD),
-            in_specs=[VMEM] * TEAM,
-            out_specs=[VMEM] * (parts[0].shape[1] // HD),
-            compiler_params=params(2),
-            name="team",
-        )(*parts)
+    )(qkv_weight, block_ids)
+    own = tokens[0]
+    rows = own.shape[0]
+    own_near = in_team(own, 1)
+    kv, q = pl.pallas_call(
+        team_kernel,
+        out_shape=[shape((TEAM * w_rows + ID_ROWS, HD), bf16), shape((TEAM * w_rows, 2 * HD), bf16)],
+        in_specs=[VMEM] * TEAM,
+        out_specs=[VMEM] * 2,
+        compiler_params=params(2),
+        name="team",
+    )(parts[0], *[in_team(parts[k], k) for k in range(1, TEAM)])
 
     def from_others(piece):
         got = [across(piece, k) for k in range(1, n_out)]
         return got[0] if len(got) == 1 else jnp.concatenate(got, 0)
 
-    own = tokens[0]
-    rows = own.shape[0]
-    own_near = in_team(own, 1)
-    (kv,) = assemble(exchange(packed[:TEAM]))
-    kv, own, *q_parts = sync(kv, own, *packed[TEAM:])
+    kv, q, own, own_near = sync(kv, q, own, own_near)
     kv_o, kv_x, kv_y = from_others(kv), in_req(kv, 1), in_req(kv, 2)
-    qa, qb = assemble(exchange(q_parts))
-    far_a = in_team(own[: rows // 2], 2)
-    kv, kv_o, kv_x, kv_y, qa, qb, far_a, own, own_near = sync(kv, kv_o, kv_x, kv_y, qa, qb, far_a, own, own_near)
-    kv_ox, kv_oy, kv_d = in_req(kv_o, 1), in_req(kv_o, 2), in_req(kv_x, 2)
-    qa_o, qa_x = from_others(qa), in_req(qa, 1)
-    far_b = in_team(own[rows // 2 :], 2)
-    kv_ox, kv_oy, kv_d, qa, qa_o, qa_x, qb, far_a, far_b = sync(kv_ox, kv_oy, kv_d, qa, qa_o, qa_x, qb, far_a, far_b)
-    kv_od = in_req(kv_oy, 1)
-    qb_o, qa_y, qa_ox, qa_oy = from_others(qb), in_req(qa, 2), in_req(qa_o, 1), in_req(qa_o, 2)
-    far = jnp.concatenate([far_a, far_b], 0)
-    far_near = in_team(far, 1)
+    far = in_team(own, 2)
+    kv_x, kv_y, q = sync(kv_x, kv_y, q)
+    q_x, q_y, kv_d = in_req(q, 1), in_req(q, 2), in_req(kv_x, 2)
+    kv_o, kv_d, q = sync(kv_o, kv_d, q)
+    q_o, kv_ox, kv_oy = from_others(q), in_req(kv_o, 1), in_req(kv_o, 2)
+    q_x, q_y, kv_ox, kv_oy, far = sync(q_x, q_y, kv_ox, kv_oy, far)
+    kv_od, q_d, far_near = in_req(kv_oy, 1), in_req(q_x, 2), in_team(far, 1)
+    kv_weight = [kv, kv_o, kv_x, kv_ox, kv_y, kv_oy, kv_d, kv_od]
+    q_o, q_d, kv_od = sync(q_o, q_d, kv_od)
+    q_ox, q_oy = in_req(q_o, 1), in_req(q_o, 2)
+    q_od = in_req(q_oy, 1)
+    q_weight = [q, q_o, q_x, q_ox, q_y, q_oy, q_d, q_od]
     stacked = pl.pallas_call(
         stack_kernel,
         out_shape=shape((TEAM * rows, own.shape[1]), bf16),
@@ -310,13 +306,6 @@
         compiler_params=params(4),
         name="stack",
     )(own, own_near, far, far_near)
-    kv_od, qa_y, qa_ox, qa_oy, qb, qb_o, stacked = sync(kv_od, qa_y, qa_ox, qa_oy, qb, qb_o, stacked)
-    kv_weight = [kv, kv_o, kv_x, kv_ox, kv_y, kv_oy, kv_d, kv_od]
-    qb_x, qb_y, qb_ox, qb_oy = in_req(qb, 1), in_req(qb, 2), in_req(qb_o, 1), in_req(qb_o, 2)
-    qa_x, qa_oy, qb_x, qb_y, qb_ox, qb_oy = sync(qa_x, qa_oy, qb_x, qb_y, qb_ox, qb_oy)
-    qa_od, qb_od, qa_d, qb_d = in_req(qa_oy, 1), in_req(qb_oy, 1), in_req(qa_x, 2), in_req(qb_x, 2)
-    q_weight = [qa, qa_o, qa_x, qa_ox, qa_y, qa_oy, qa_d, qa_od]
-    q_weight += [qb, qb_o, qb_x, qb_ox, qb_y, qb_oy, qb_d, qb_od]
 
     blk_rows = rows // per_device
     tall = kv.shape[0]
@@ -330,31 +319,32 @@
     angles = positions.astype(jnp.float32) * inverse[None, :]
     cosine, sine = jnp.cos(angles), jnp.sin(angles)
 
-    def project(steps, weight, is_kv, gain):
-        width = len(weight) // (2 * n_req) * HD
+    def project(weight, is_kv, gain):
+        width = weight[0].shape[1]
         depth = own.shape[1]
+        n_outs = 1 if is_kv else 2
         return pl.pallas_call(
-            functools.partial(project_kernel, steps, n_out, TEAM * w_rows, is_kv),
-            out_shape=shape((len(steps) * rows, width), bf16),
+            functools.partial(project_kernel, n_out, TEAM * w_rows, is_kv),
+            out_shape=[shape((TEAM * rows // n_outs, width), bf16)] * n_outs,
             in_specs=[VMEM] + [ANY] * len(weight) + [VMEM] * 3,
-            out_specs=VMEM,
+            out_specs=[VMEM] * n_outs,
             scratch_shapes=[
                 pltpu.VMEM((depth, width), bf16),
-                pltpu.SemaphoreType.DMA((n_req * n_out * width // HD,)),
+                pltpu.SemaphoreType.DMA((n_req * n_out,)),
             ],
             cost_estimate=pl.CostEstimate(
-                flops=2 * len(steps) * rows * depth * width, bytes_accessed=6 * MIB, transcendentals=0
+                flops=2 * TEAM * rows * depth * width, bytes_accessed=6 * MIB, transcendentals=0
             ),
             compiler_params=params(12),
             name="project_kv" if is_kv else "project_q",
         )(stacked, *weight, gain[None, :], cosine, sine)
 
-    made = project((0, 1, 2, 3), kv_weight, True, k_gain)
+    (made,) = project(kv_weight, True, k_gain)
     mine = [made] + [across(made, k) for k in range(1, n_out)]
     other = [in_team(part, 1) for part in mine]
 
-    from_near = in_team(project((1, 3), q_weight, False, q_gain), 1)
-    queries = project((0, 2), q_weight, False, q_gain)
+    to_near, queries = project(q_weight, False, q_gain)
+    from_near = in_team(to_near, 1)
 
     table = page_table[0].reshape(-1)
     per_head = page_table.shape[2]

time: 111 us -> 85.2 us (0.77)
  local copies, waits for them, and re-layouts: 17.9 us -> 4.95 us
  starting transfers between devices: 36.2 us -> 25.4 us
  waiting for transfers between devices: 33.8 us -> 37.9 us
  Pallas kernels: 17.1 us -> 13.7 us
  other arithmetic: 3.19 us -> 1.37 us
    ppermute x4 -> x3, waiting for transfers between devices: 8.02 us -> 18.6 us  [across(): lax.ppermute(array, 'blk', [(i, (i + TEAM * k) % n_blk) for i in range(n_...]
    unnamed x71 -> x18, local copies, waits for them, and re-layouts: 13.7 us -> 4.03 us
    ppermute x18 -> x12, starting transfers between devices: 19.7 us -> 10.3 us  [in_req(): return lax.ppermute(array, 'req', [(i, i ^ k) for i in range(n_req)])]
    ppermute x15 -> x11, waiting for transfers between devices: 19.8 us -> 13.7 us  [in_team(): return lax.ppermute(array, 'blk', [(i, i ^ k) for i in range(n_blk)])]
    slice x3 -> x0, local copies, waits for them, and re-layouts: 3.25 us -> none  [the longest x1 1.31 us: body(): ids_row = jnp.where(lane == j, block_ids[0, j], ids_row)]
    pallas_call x6 -> x4, Pallas kernels: 8.05 us -> 5.31 us  [the longest x2 4.67 us: project(): pl.pallas_call(functools.partial(project_kernel, n_out, TEAM * w_rows, is...]
    convert_element_type x1 -> x0, other arithmetic: 1.3 us -> none  [body(): ids_rows = jnp.broadcast_to(ids_row.astype(bf16)[None, :], (ID_ROWS, HD))]
    ppermute x4 -> x3, starting transfers between devices: 8.03 us -> 7.17 us  [across(): lax.ppermute(array, 'blk', [(i, (i + TEAM * k) % n_blk) for i in range(n_...]
  transfers between devices with their start and end apart: 37 -> 26, of which waited for: 14 -> 12; matrix products, arithmetic and copies ran while one was open for 7% -> 3% of each run, Pallas kernels for 12% -> 14%
where the time goes in v5:
time: 85.2 us; the launch traced here: 85 us
  waiting for transfers between devices  37.9 us (44%)
  starting transfers between devices  25.4 us (30%)
  Pallas kernels  13.7 us (16%)
  local copies, waits for them, and re-layouts  4.95 us (6%)
  between operations  1.64 us (2%)
  other arithmetic  1.37 us (2%)
    ppermute x3, waiting for transfers between devices, across(): lax.ppermute(array, 'blk', [(i, (i + TEAM * k) % n_blk) for i in range(n_...  18.6 us
    ppermute x11, waiting for transfers between devices, in_team(): return lax.ppermute(array, 'blk', [(i, i ^ k) for i in range(n_blk)])  13.7 us
    ppermute x12, starting transfers between devices, in_req(): return lax.ppermute(array, 'req', [(i, i ^ k) for i in range(n_req)])  10.3 us
    ppermute x11, starting transfers between devices, in_team(): return lax.ppermute(array, 'blk', [(i, i ^ k) for i in range(n_blk)])  7.92 us
    ppermute x3, starting transfers between devices, across(): lax.ppermute(array, 'blk', [(i, (i + TEAM * k) % n_blk) for i in range(n_...  7.17 us
    ppermute x12, waiting for transfers between devices, in_req(): return lax.ppermute(array, 'req', [(i, i ^ k) for i in range(n_req)])  5.51 us
    pallas_call x2, Pallas kernels, project(): pl.pallas_call(functools.partial(project_kernel, n_out, TEAM * w_rows, is...  4.67 us
    pallas_call x2, Pallas kernels, attend(): pl.pallas_call(functools.partial(attend_kernel, blk_rows, step), out_shap...  4.19 us
  transfers between devices with their start and end apart: 26, of which 12 were waited for; matrix products, arithmetic and copies ran while one was open for 3% of the time, Pallas kernels for 14%

profile of v5, /device:TPU:0, one launch (start us, length us, event | category | flops | bytes accessed | tf_op | source)
XLA Modules:
  0.0 85.0 jit_solution(16688998035727566367)
XLA Ops:
  1.1 1.0 %copy-done.1 = bf16[64,3072]{1,0:T(8,128)(2,1)S(1)} copy-done((bf16[64,3072]{1,0:T(8,128)(2,1)S(1)}, bf16[64,3072]{1,0:T(8,128)(2,1)}, u32[]{:S(2)}) %copy-start.1) | copy-done | bytes 393240
  3.5 3.0 %collective-permute-start.1 = (bf16[80,768]{1,0:T(8,128)(2,1)S(1)}, bf16[80,768]{1,0:T(8,128)(2,1)S(1)}, u32[]{:S(2)}, u32[]{:S(2)}) collective-permute-start(bf16[80,768]{1,0:T(8,128)(2,1)S(1)} %get-tuple-element.34), channel_id=1, source_target_pairs={{0,2},{1,3},{2,0},{3,1},{4,6},{5,7},{6,4},{7,5},{8,10},{9,11},{10,... | collective-permute-start | bytes 368648 | tf_op jit(solution)/shard_map/ppermute | solution.py:249
  6.6 4.1 %collective-permute-done.1.refs_2_ = bf16[80,768]{1,0:T(8,128)(2,1)S(1)} collective-permute-done((bf16[80,768]{1,0:T(8,128)(2,1)S(1)}, bf16[80,768]{1,0:T(8,128)(2,1)S(1)}, u32[]{:S(2)}, u32[]{:S(2)}) %collective-permute-start.1) | collective-permute-done | bytes 122912 | tf_op jit(solution)/shard_map/ppermute | solution.py:249
  10.7 1.5 %collective-permute-done.2.refs_3_ = bf16[80,768]{1,0:T(8,128)(2,1)S(1)} collective-permute-done((bf16[80,768]{1,0:T(8,128)(2,1)S(1)}, bf16[80,768]{1,0:T(8,128)(2,1)S(1)}, u32[]{:S(2)}, u32[]{:S(2)}) %collective-permute-start.2) | collective-permute-done | bytes 122912 | tf_op jit(solution)/shard_map/ppermute | solution.py:249
  12.3 1.5 %collective-permute-start.4 = (bf16[272,256]{1,0:T(8,128)(2,1)S(1)}, bf16[272,256]{1,0:T(8,128)(2,1)S(1)}, u32[]{:S(2)}, u32[]{:S(2)}) collective-permute-start(bf16[272,256]{1,0:T(8,128)(2,1)S(1)} %get-tuple-element.40.refs_0_), channel_id=1, source_target_pairs={{0,8},{8,0},{16,24},{24,16},{1,9},{9,1},{17,25},{25,17},{2,10},{10... | collective-permute-start | bytes 417800 | tf_op jit(solution)/shard_map/ppermute | solution.py:252
  13.8 1.5 %collective-permute-start.5 = (bf16[272,256]{1,0:T(8,128)(2,1)S(1)}, bf16[272,256]{1,0:T(8,128)(2,1)S(1)}, u32[]{:S(2)}, u32[]{:S(2)}) collective-permute-start(bf16[272,256]{1,0:T(8,128)(2,1)S(1)} %get-tuple-element.40.refs_0_), channel_id=1, source_target_pairs={{0,16},{8,24},{16,0},{24,8},{1,17},{9,25},{17,1},{25,9},{2,18},{10... | collective-permute-start | bytes 417800 | tf_op jit(solution)/shard_map/ppermute | solution.py:252
  15.3 2.6 %collective-permute-start.8 = (bf16[272,256]{1,0:T(8,128)(2,1)S(1)}, bf16[272,256]{1,0:T(8,128)(2,1)S(1)}, u32[]{:S(2)}, u32[]{:S(2)}) collective-permute-start(bf16[272,256]{1,0:T(8,128)(2,1)S(1)} %get-tuple-element.40.refs_0_), channel_id=1, source_target_pairs={{0,4},{1,5},{2,6},{3,7},{4,0},{5,1},{6,2},{7,3},{8,12},{9,13},{10,... | collective-permute-start | bytes 417800 | tf_op jit(solution)/shard_map/ppermute | solution.py:255
  17.9 1.4 %collective-permute-start.12 = (bf16[128,2048]{1,0:T(8,128)(2,1)}, bf16[128,2048]{1,0:T(8,128)(2,1)S(1)}, u32[]{:S(2)}, u32[]{:S(2)}) collective-permute-start(bf16[128,2048]{1,0:T(8,128)(2,1)} %bitcast.33), channel_id=1, source_target_pairs={{0,2},{1,3},{2,0},{3,1},{4,6},{5,7},{6,4},{7,5},{8,10},{9,11},{10,... | collective-permute-start | bytes 1572872 | tf_op jit(solution)/shard_map/ppermute | solution.py:249
  19.6 1.5 %collective-permute-start.9 = (bf16[272,256]{1,0:T(8,128)(2,1)S(1)}, bf16[272,256]{1,0:T(8,128)(2,1)S(1)}, u32[]{:S(2)}, u32[]{:S(2)}) collective-permute-start(bf16[272,256]{1,0:T(8,128)(2,1)S(1)} %collective-permute-done.4.refs_2_), channel_id=1, source_target_pairs={{0,16},{8,24},{16,0},{24,8},{1,17},{9,25},{17,1},{25,9},{2,18},{10... | collective-permute-start | bytes 417800 | tf_op jit(solution)/shard_map/ppermute | solution.py:252
  21.2 0.8 eq.18
  23.8 1.1 %collective-permute-done.8.refs_1_ = bf16[272,256]{1,0:T(8,128)(2,1)S(1)} collective-permute-done((bf16[272,256]{1,0:T(8,128)(2,1)S(1)}, bf16[272,256]{1,0:T(8,128)(2,1)S(1)}, u32[]{:S(2)}, u32[]{:S(2)}) %collective-permute-start.8) | collective-permute-done | bytes 139296 | tf_op jit(solution)/shard_map/ppermute | solution.py:255
  24.9 0.7 copy-done.2
  26.1 1.5 %collective-permute-start.11 = (bf16[272,256]{1,0:T(8,128)(2,1)S(1)}, bf16[272,256]{1,0:T(8,128)(2,1)}, u32[]{:S(2)}, u32[]{:S(2)}) collective-permute-start(bf16[272,256]{1,0:T(8,128)(2,1)S(1)} %collective-permute-done.8.refs_1_), channel_id=1, source_target_pairs={{0,16},{8,24},{16,0},{24,8},{1,17},{9,25},{17,1},{25,9},{2,18},{10... | collective-permute-start | bytes 417800 | tf_op jit(solution)/shard_map/ppermute | solution.py:252
  27.7 4.1 %collective-permute-done.6.refs_2_ = bf16[256,512]{1,0:T(8,128)(2,1)S(1)} collective-permute-done((bf16[256,512]{1,0:T(8,128)(2,1)S(1)}, bf16[256,512]{1,0:T(8,128)(2,1)S(1)}, u32[]{:S(2)}, u32[]{:S(2)}) %collective-permute-start.6) | collective-permute-done | bytes 262176 | tf_op jit(solution)/shard_map/ppermute | solution.py:252
  31.8 2.6 %collective-permute-start.18 = (bf16[256,512]{1,0:T(8,128)(2,1)S(1)}, bf16[256,512]{1,0:T(8,128)(2,1)S(1)}, u32[]{:S(2)}, u32[]{:S(2)}) collective-permute-start(bf16[256,512]{1,0:T(8,128)(2,1)S(1)} %get-tuple-element.51.refs_0_), channel_id=1, source_target_pairs={{0,4},{1,5},{2,6},{3,7},{4,0},{5,1},{6,2},{7,3},{8,12},{9,13},{10,... | collective-permute-start | bytes 786440 | tf_op jit(solution)/shard_map/ppermute | solution.py:255
  34.4 0.7 copy-done.4
  36.5 6.9 %collective-permute-done.18.refs_1_ = bf16[256,512]{1,0:T(8,128)(2,1)S(1)} collective-permute-done((bf16[256,512]{1,0:T(8,128)(2,1)S(1)}, bf16[256,512]{1,0:T(8,128)(2,1)S(1)}, u32[]{:S(2)}, u32[]{:S(2)}) %collective-permute-start.18) | collective-permute-done | bytes 262176 | tf_op jit(solution)/shard_map/ppermute | solution.py:255
  43.3 1.0 %collective-permute-done.19.refs_6_ = bf16[256,512]{1,0:T(8,128)(2,1)S(1)} collective-permute-done((bf16[256,512]{1,0:T(8,128)(2,1)S(1)}, bf16[256,512]{1,0:T(8,128)(2,1)S(1)}, u32[]{:S(2)}, u32[]{:S(2)}) %collective-permute-start.19) | collective-permute-done | bytes 262176 | tf_op jit(solution)/shard_map/ppermute | solution.py:252
  44.9 1.0 %multiply_sine_fusion = (f32[512,128]{1,0:T(8,128)S(1)}, f32[512,128]{1,0:T(8,128)S(1)}) fusion(f32[128]{0:T(128)S(1)} %multiply_power_fusion, f32[512]{0:T(512)S(1)} %convert_element_type.37), kind=kLoop, calls=%fused_computation | loop fusion | flops 65536 | bytes 526848 | tf_op jit(solution)/shard_map/sin | solution.py:320
  46.1 1.0 %copy-done = bf16[1,128,2048]{2,1,0:T(8,128)(2,1)S(1)} copy-done((bf16[1,128,2048]{2,1,0:T(8,128)(2,1)S(1)}, bf16[1,128,2048]{2,1,0:T(8,128)(2,1)}, u32[]{:S(2)}) %copy-start) | copy-done | bytes 524312
  47.4 2.9 %project_kv.1.refs_0_ = bf16[512,256]{1,0:T(8,128)(2,1)S(1)} custom-call(bf16[512,2048]{1,0:T(8,128)(2,1)S(1)} %stack.8.x_ref, bf16[272,256]{1,0:T(8,128)(2,1)S(1)} %get-tuple-element.40.refs_0_, bf16[272,256]{1,0:T(8,128)(2,1)S(1)} %collective-permute-done.8.refs_1_, bf16[272,256]{1,0:T(8,128)(2,1)S(1)} %collective-permute-done.4.refs_2_, ...), custom_call_target="tpu_custom_call" | custom-call | flops 536870912 | bytes 6291456 | tf_op jit(solution)/shard_map/project_kv/pallas_call | solution.py:326
  50.2 2.0 %collective-permute-start.15 = (bf16[512,256]{1,0:T(8,128)(2,1)S(1)}, bf16[512,256]{1,0:T(8,128)(2,1)S(1)}, u32[]{:S(2)}, u32[]{:S(2)}) collective-permute-start(bf16[512,256]{1,0:T(8,128)(2,1)S(1)} %project_kv.1.refs_0_), channel_id=1, source_target_pairs={{0,4},{1,5},{2,6},{3,7},{4,0},{5,1},{6,2},{7,3},{8,12},{9,13},{10,... | collective-permute-start | bytes 786440 | tf_op jit(solution)/shard_map/ppermute | solution.py:255
  52.3 1.3 %collective-permute-start.22 = (bf16[256,512]{1,0:T(8,128)(2,1)S(1)}, bf16[256,512]{1,0:T(8,128)(2,1)S(1)}, u32[]{:S(2)}, u32[]{:S(2)}) collective-permute-start(bf16[256,512]{1,0:T(8,128)(2,1)S(1)} %collective-permute-done.21.refs_5_), channel_id=1, source_target_pairs={{0,8},{8,0},{16,24},{24,16},{1,9},{9,1},{17,25},{25,17},{2,10},{10... | collective-permute-start | bytes 786440 | tf_op jit(solution)/shard_map/ppermute | solution.py:252
  53.6 10.7 %collective-permute-done.15.refs_1_ = bf16[512,256]{1,0:T(8,128)(2,1)S(1)} collective-permute-done((bf16[512,256]{1,0:T(8,128)(2,1)S(1)}, bf16[512,256]{1,0:T(8,128)(2,1)S(1)}, u32[]{:S(2)}, u32[]{:S(2)}) %collective-permute-start.15) | collective-permute-done | bytes 262176 | tf_op jit(solution)/shard_map/ppermute | solution.py:255
  64.3 1.8 %project_q.1 = (bf16[256,512]{1,0:T(8,128)(2,1)S(1)}, bf16[256,512]{1,0:T(8,128)(2,1)S(1)}) custom-call(bf16[512,2048]{1,0:T(8,128)(2,1)S(1)} %stack.8.x_ref, bf16[256,512]{1,0:T(8,128)(2,1)S(1)} %get-tuple-element.51.refs_0_, bf16[256,512]{1,0:T(8,128)(2,1)S(1)} %collective-permute-done.18.refs_1_, bf16[256,512]{1,0:T(8,128)(2,1)S(1)} %collective-permute-done.6.refs_2_, ...), custom_call_target="tpu_custom_call" | custom-call | flops 1073741824 | bytes 6291456 | tf_op jit(solution)/shard_map/project_q/pallas_call | solution.py:326
  66.8 2.5 %pages.1 = (bf16[4,64,512]{2,1,0:T(8,128)(2,1)S(1)}, bf16[4,64,512]{2,1,0:T(8,128)(2,1)S(1)}, bf16[2,1024,256]{2,1,0:T(8,128)(2,1)S(1)}) custom-call(bf16[512,256]{1,0:T(8,128)(2,1)S(1)} %project_kv.1.refs_0_, bf16[512,256]{1,0:T(8,128)(2,1)S(1)} %collective-permute-done.15.refs_1_, bf16[512,256]{1,0:T(8,128)(2,1)S(1)} %collective-permute-done.16.refs_2_, ...), custom_call_target="tpu_custom_call" | custom-call | bytes 4194304 | tf_op jit(solution)/shard_map/pages/pallas_call | solution.py:364
  69.5 2.0 %attend.3 = bf16[128,1024]{1,0:T(8,128)(2,1)S(1)} custom-call(bf16[2,1024,256]{2,1,0:T(8,128)(2,1)S(1)} %get-tuple-element.50.store, bf16[256,512]{1,0:T(8,128)(2,1)S(1)} %get-tuple-element.56.q_ref, bf16[256,512]{1,0:T(8,128)(2,1)S(1)} %collective-permute-done.23.near_ref, s32[16]{0:T(128)S(1)} %reshape.141.refs_4_.ids_ref, s32[1]{0:T(128)} %copy.9.length_ref), custom_call_target="tpu_custom_call" | custom-call | flops 536870912 | bytes 4194304 | tf_op jit(solution)/shard_map/attend/pallas_call | solution.py:377
  71.5 2.1 %collective-permute-start.24 = (bf16[128,1024]{1,0:T(8,128)(2,1)S(1)}, bf16[128,1024]{1,0:T(8,128)(2,1)S(1)}, u32[]{:S(2)}, u32[]{:S(2)}) collective-permute-start(bf16[128,1024]{1,0:T(8,128)(2,1)S(1)} %attend.3), channel_id=1, source_target_pairs={{0,2},{1,3},{2,0},{3,1},{4,6},{5,7},{6,4},{7,5},{8,10},{9,11},{10,... | collective-permute-start | bytes 786440 | tf_op jit(solution)/shard_map/ppermute | solution.py:249
  73.6 2.2 %attend.2.kept = bf16[128,1024]{1,0:T(8,128)(2,1)S(1)} custom-call(bf16[2,1024,256]{2,1,0:T(8,128)(2,1)S(1)} %get-tuple-element.50.store, bf16[256,512]{1,0:T(8,128)(2,1)S(1)} %get-tuple-element.56.q_ref, bf16[256,512]{1,0:T(8,128)(2,1)S(1)} %collective-permute-done.23.near_ref, s32[16]{0:T(128)S(1)} %reshape.141.refs_4_.ids_ref, s32[1]{0:T(128)} %copy.9.length_ref), custom_call_target="tpu_custom_call" | custom-call | flops 536870912 | bytes 4194304 | tf_op jit(solution)/shard_map/attend/pallas_call | solution.py:377
  75.8 2.8 %collective-permute-done.25.got_pages = bf16[4,64,512]{2,1,0:T(8,128)(2,1)S(1)} collective-permute-done((bf16[4,64,512]{2,1,0:T(8,128)(2,1)S(1)}, bf16[4,64,512]{2,1,0:T(8,128)(2,1)S(1)}, u32[]{:S(2)}, u32[]{:S(2)}) %collective-permute-start.25) | collective-permute-done | bytes 262176 | tf_op jit(solution)/shard_map/ppermute | solution.py:249
  78.6 4.7 %collective-permute-done.24.from_far = bf16[128,1024]{1,0:T(8,128)(2,1)S(1)} collective-permute-done((bf16[128,1024]{1,0:T(8,128)(2,1)S(1)}, bf16[128,1024]{1,0:T(8,128)(2,1)S(1)}, u32[]{:S(2)}, u32[]{:S(2)}) %collective-permute-start.24) | collective-permute-done | bytes 262176 | tf_op jit(solution)/shard_map/ppermute | solution.py:249
  83.3 1.5 %finish.1 = (bf16[128,2048]{1,0:T(8,128)(2,1)}, bf16[4,64,512]{2,1,0:T(8,128)(2,1)}) custom-call(bf16[128,1024]{1,0:T(8,128)(2,1)S(1)} %attend.2.kept, bf16[128,1024]{1,0:T(8,128)(2,1)S(1)} %collective-permute-done.24.from_far, bf16[4,64,512]{2,1,0:T(8,128)(2,1)S(1)} %get-tuple-element.58.own_pages, ...), custom_call_target="tpu_custom_call" | custom-call | tf_op jit(solution)/shard_map/finish/pallas_call | solution.py:392
  (62 shorter events, 7.3 us)
Async XLA Ops:
  0.6 11.6 %collective-permute-start.3 = (bf16[128,2048]{1,0:T(8,128)(2,1)}, bf16[128,2048]{1,0:T(8,128)(2,1)S(1)}, u32[]{:S(2)}, u32[]{:S(2)}) collective-permute-start(bf16[128,2048]{1,0:T(8,128)(2,1)} %bitcast.32), channel_id=1, source_target_pairs={{0,1},{1,0},{2,3},{3,2},{4,5},{5,4},{6,7},{7,6},{8,9},{9,8},{10,11... | collective-permute-start | bytes 1572872 | tf_op jit(solution)/shard_map/ppermute | solution.py:249
  1.1 1.0 %copy-start.1 = (bf16[64,3072]{1,0:T(8,128)(2,1)S(1)}, bf16[64,3072]{1,0:T(8,128)(2,1)}, u32[]{:S(2)}) copy-start(bf16[64,3072]{1,0:T(8,128)(2,1)} %w_ref.1) | copy-start | bytes 1179652
  3.4 3.2 %collective-permute-start = (bf16[80,768]{1,0:T(8,128)(2,1)S(1)}, bf16[80,768]{1,0:T(8,128)(2,1)S(1)}, u32[]{:S(2)}, u32[]{:S(2)}) collective-permute-start(bf16[80,768]{1,0:T(8,128)(2,1)S(1)} %get-tuple-element.33), channel_id=1, source_target_pairs={{0,1},{1,0},{2,3},{3,2},{4,5},{5,4},{6,7},{7,6},{8,9},{9,8},{10,11... | collective-permute-start | bytes 368648 | tf_op jit(solution)/shard_map/ppermute | solution.py:249
  3.5 7.1 %collective-permute-start.1 = (bf16[80,768]{1,0:T(8,128)(2,1)S(1)}, bf16[80,768]{1,0:T(8,128)(2,1)S(1)}, u32[]{:S(2)}, u32[]{:S(2)}) collective-permute-start(bf16[80,768]{1,0:T(8,128)(2,1)S(1)} %get-tuple-element.34), channel_id=1, source_target_pairs={{0,2},{1,3},{2,0},{3,1},{4,6},{5,7},{6,4},{7,5},{8,10},{9,11},{10,... | collective-permute-start | bytes 368648 | tf_op jit(solution)/shard_map/ppermute | solution.py:249
  6.5 5.6 %collective-permute-start.2 = (bf16[80,768]{1,0:T(8,128)(2,1)S(1)}, bf16[80,768]{1,0:T(8,128)(2,1)S(1)}, u32[]{:S(2)}, u32[]{:S(2)}) collective-permute-start(bf16[80,768]{1,0:T(8,128)(2,1)S(1)} %get-tuple-element.35), channel_id=1, source_target_pairs={{0,3},{1,2},{2,1},{3,0},{4,7},{5,6},{6,5},{7,4},{8,11},{9,10},{10,... | collective-permute-start | bytes 368648 | tf_op jit(solution)/shard_map/ppermute | solution.py:249
  12.3 7.1 %collective-permute-start.4 = (bf16[272,256]{1,0:T(8,128)(2,1)S(1)}, bf16[272,256]{1,0:T(8,128)(2,1)S(1)}, u32[]{:S(2)}, u32[]{:S(2)}) collective-permute-start(bf16[272,256]{1,0:T(8,128)(2,1)S(1)} %get-tuple-element.40.refs_0_), channel_id=1, source_target_pairs={{0,8},{8,0},{16,24},{24,16},{1,9},{9,1},{17,25},{25,17},{2,10},{10... | collective-permute-start | bytes 417800 | tf_op jit(solution)/shard_map/ppermute | solution.py:252
  13.8 5.9 %collective-permute-start.5 = (bf16[272,256]{1,0:T(8,128)(2,1)S(1)}, bf16[272,256]{1,0:T(8,128)(2,1)S(1)}, u32[]{:S(2)}, u32[]{:S(2)}) collective-permute-start(bf16[272,256]{1,0:T(8,128)(2,1)S(1)} %get-tuple-element.40.refs_0_), channel_id=1, source_target_pairs={{0,16},{8,24},{16,0},{24,8},{1,17},{9,25},{17,1},{25,9},{2,18},{10... | collective-permute-start | bytes 417800 | tf_op jit(solution)/shard_map/ppermute | solution.py:252
  15.3 9.6 %collective-permute-start.8 = (bf16[272,256]{1,0:T(8,128)(2,1)S(1)}, bf16[272,256]{1,0:T(8,128)(2,1)S(1)}, u32[]{:S(2)}, u32[]{:S(2)}) collective-permute-start(bf16[272,256]{1,0:T(8,128)(2,1)S(1)} %get-tuple-element.40.refs_0_), channel_id=1, source_target_pairs={{0,4},{1,5},{2,6},{3,7},{4,0},{5,1},{6,2},{7,3},{8,12},{9,13},{10,... | collective-permute-start | bytes 417800 | tf_op jit(solution)/shard_map/ppermute | solution.py:255
  17.9 17.7 %collective-permute-start.12 = (bf16[128,2048]{1,0:T(8,128)(2,1)}, bf16[128,2048]{1,0:T(8,128)(2,1)S(1)}, u32[]{:S(2)}, u32[]{:S(2)}) collective-permute-start(bf16[128,2048]{1,0:T(8,128)(2,1)} %bitcast.33), channel_id=1, source_target_pairs={{0,2},{1,3},{2,0},{3,1},{4,6},{5,7},{6,4},{7,5},{8,10},{9,11},{10,... | collective-permute-start | bytes 1572872 | tf_op jit(solution)/shard_map/ppermute | solution.py:249
  19.6 5.2 %collective-permute-start.9 = (bf16[272,256]{1,0:T(8,128)(2,1)S(1)}, bf16[272,256]{1,0:T(8,128)(2,1)S(1)}, u32[]{:S(2)}, u32[]{:S(2)}) collective-permute-start(bf16[272,256]{1,0:T(8,128)(2,1)S(1)} %collective-permute-done.4.refs_2_), channel_id=1, source_target_pairs={{0,16},{8,24},{16,0},{24,8},{1,17},{9,25},{17,1},{25,9},{2,18},{10... | collective-permute-start | bytes 417800 | tf_op jit(solution)/shard_map/ppermute | solution.py:252
  22.8 8.9 %collective-permute-start.6 = (bf16[256,512]{1,0:T(8,128)(2,1)S(1)}, bf16[256,512]{1,0:T(8,128)(2,1)S(1)}, u32[]{:S(2)}, u32[]{:S(2)}) collective-permute-start(bf16[256,512]{1,0:T(8,128)(2,1)S(1)} %get-tuple-element.51.refs_0_), channel_id=1, source_target_pairs={{0,8},{8,0},{16,24},{24,16},{1,9},{9,1},{17,25},{25,17},{2,10},{10... | collective-permute-start | bytes 786440 | tf_op jit(solution)/shard_map/ppermute | solution.py:252
  23.4 10.9 %collective-permute-start.7 = (bf16[256,512]{1,0:T(8,128)(2,1)S(1)}, bf16[256,512]{1,0:T(8,128)(2,1)S(1)}, u32[]{:S(2)}, u32[]{:S(2)}) collective-permute-start(bf16[256,512]{1,0:T(8,128)(2,1)S(1)} %get-tuple-element.51.refs_0_), channel_id=1, source_target_pairs={{0,16},{8,24},{16,0},{24,8},{1,17},{9,25},{17,1},{25,9},{2,18},{10... | collective-permute-start | bytes 786440 | tf_op jit(solution)/shard_map/ppermute | solution.py:252
  25.5 8.8 %collective-permute-start.10 = (bf16[272,256]{1,0:T(8,128)(2,1)S(1)}, bf16[272,256]{1,0:T(8,128)(2,1)S(1)}, u32[]{:S(2)}, u32[]{:S(2)}) collective-permute-start(bf16[272,256]{1,0:T(8,128)(2,1)S(1)} %collective-permute-done.8.refs_1_), channel_id=1, source_target_pairs={{0,8},{8,0},{16,24},{24,16},{1,9},{9,1},{17,25},{25,17},{2,10},{10... | collective-permute-start | bytes 417800 | tf_op jit(solution)/shard_map/ppermute | solution.py:252
  26.1 8.9 %collective-permute-start.11 = (bf16[272,256]{1,0:T(8,128)(2,1)S(1)}, bf16[272,256]{1,0:T(8,128)(2,1)}, u32[]{:S(2)}, u32[]{:S(2)}) collective-permute-start(bf16[272,256]{1,0:T(8,128)(2,1)S(1)} %collective-permute-done.8.refs_1_), channel_id=1, source_target_pairs={{0,16},{8,24},{16,0},{24,8},{1,17},{9,25},{17,1},{25,9},{2,18},{10... | collective-permute-start | bytes 417800 | tf_op jit(solution)/shard_map/ppermute | solution.py:252
  31.8 11.5 %collective-permute-start.18 = (bf16[256,512]{1,0:T(8,128)(2,1)S(1)}, bf16[256,512]{1,0:T(8,128)(2,1)S(1)}, u32[]{:S(2)}, u32[]{:S(2)}) collective-permute-start(bf16[256,512]{1,0:T(8,128)(2,1)S(1)} %get-tuple-element.51.refs_0_), channel_id=1, source_target_pairs={{0,4},{1,5},{2,6},{3,7},{4,0},{5,1},{6,2},{7,3},{8,12},{9,13},{10,... | collective-permute-start | bytes 786440 | tf_op jit(solution)/shard_map/ppermute | solution.py:255
  35.6 10.5 %collective-permute-start.13 = (bf16[128,2048]{1,0:T(8,128)(2,1)S(1)}, bf16[128,2048]{1,0:T(8,128)(2,1)S(1)}, u32[]{:S(2)}, u32[]{:S(2)}) collective-permute-start(bf16[128,2048]{1,0:T(8,128)(2,1)S(1)} %collective-permute-done.12.refs_2_), channel_id=1, source_target_pairs={{0,1},{1,0},{2,3},{3,2},{4,5},{5,4},{6,7},{7,6},{8,9},{9,8},{10,11... | collective-permute-start | bytes 1572872 | tf_op jit(solution)/shard_map/ppermute | solution.py:249
  35.6 8.7 %collective-permute-start.19 = (bf16[256,512]{1,0:T(8,128)(2,1)S(1)}, bf16[256,512]{1,0:T(8,128)(2,1)S(1)}, u32[]{:S(2)}, u32[]{:S(2)}) collective-permute-start(bf16[256,512]{1,0:T(8,128)(2,1)S(1)} %collective-permute-done.6.refs_2_), channel_id=1, source_target_pairs={{0,16},{8,24},{16,0},{24,8},{1,17},{9,25},{17,1},{25,9},{2,18},{10... | collective-permute-start | bytes 786440 | tf_op jit(solution)/shard_map/ppermute | solution.py:252
  36.1 7.2 %collective-permute-start.14 = (bf16[272,256]{1,0:T(8,128)(2,1)}, bf16[272,256]{1,0:T(8,128)(2,1)}, u32[]{:S(2)}, u32[]{:S(2)}) collective-permute-start(bf16[272,256]{1,0:T(8,128)(2,1)} %collective-permute-done.11.refs_5_), channel_id=1, source_target_pairs={{0,8},{8,0},{16,24},{24,16},{1,9},{9,1},{17,25},{25,17},{2,10},{10... | collective-permute-start | bytes 417800 | tf_op jit(solution)/shard_map/ppermute | solution.py:252
  44.3 7.9 %collective-permute-start.21 = (bf16[256,512]{1,0:T(8,128)(2,1)S(1)}, bf16[256,512]{1,0:T(8,128)(2,1)S(1)}, u32[]{:S(2)}, u32[]{:S(2)}) collective-permute-start(bf16[256,512]{1,0:T(8,128)(2,1)S(1)} %collective-permute-done.18.refs_1_), channel_id=1, source_target_pairs={{0,16},{8,24},{16,0},{24,8},{1,17},{9,25},{17,1},{25,9},{2,18},{10... | collective-permute-start | bytes 786440 | tf_op jit(solution)/shard_map/ppermute | solution.py:252
  44.8 2.5 %copy-start.3 = (bf16[272,256]{1,0:T(8,128)(2,1)S(1)}, bf16[272,256]{1,0:T(8,128)(2,1)}, u32[]{:S(2)}) copy-start(bf16[272,256]{1,0:T(8,128)(2,1)} %copy-done.2) | copy-start | bytes 417796
  44.8 2.5 %copy-start.5 = (bf16[272,256]{1,0:T(8,128)(2,1)S(1)}, bf16[272,256]{1,0:T(8,128)(2,1)}, u32[]{:S(2)}) copy-start(bf16[272,256]{1,0:T(8,128)(2,1)} %copy-done.4) | copy-start | bytes 417796
  44.9 2.5 %copy-start.6 = (f32[256]{0:T(256)S(1)}, f32[256]{0:T(256)}, u32[]{:S(2)}) copy-start(f32[256]{0:T(256)} %param.13) | copy-start | bytes 3076
  45.8 18.5 %collective-permute-start.20 = (bf16[256,512]{1,0:T(8,128)(2,1)S(1)}, bf16[256,512]{1,0:T(8,128)(2,1)S(1)}, u32[]{:S(2)}, u32[]{:S(2)}) collective-permute-start(bf16[256,512]{1,0:T(8,128)(2,1)S(1)} %collective-permute-done.18.refs_1_), channel_id=1, source_target_pairs={{0,8},{8,0},{16,24},{24,16},{1,9},{9,1},{17,25},{25,17},{2,10},{10... | collective-permute-start | bytes 786440 | tf_op jit(solution)/shard_map/ppermute | solution.py:252
  46.1 1.0 %copy-start = (bf16[1,128,2048]{2,1,0:T(8,128)(2,1)S(1)}, bf16[1,128,2048]{2,1,0:T(8,128)(2,1)}, u32[]{:S(2)}) copy-start(bf16[1,128,2048]{2,1,0:T(8,128)(2,1)} %param.7) | copy-start | bytes 1572868
  47.3 17.0 %copy-start.7 = (f32[256]{0:T(256)S(1)}, f32[256]{0:T(256)}, u32[]{:S(2)}) copy-start(f32[256]{0:T(256)} %param.12) | copy-start | bytes 3076
  50.2 14.1 %collective-permute-start.15 = (bf16[512,256]{1,0:T(8,128)(2,1)S(1)}, bf16[512,256]{1,0:T(8,128)(2,1)S(1)}, u32[]{:S(2)}, u32[]{:S(2)}) collective-permute-start(bf16[512,256]{1,0:T(8,128)(2,1)S(1)} %project_kv.1.refs_0_), channel_id=1, source_target_pairs={{0,4},{1,5},{2,6},{3,7},{4,0},{5,1},{6,2},{7,3},{8,12},{9,13},{10,... | collective-permute-start | bytes 786440 | tf_op jit(solution)/shard_map/ppermute | solution.py:255
  52.3 12.0 %collective-permute-start.22 = (bf16[256,512]{1,0:T(8,128)(2,1)S(1)}, bf16[256,512]{1,0:T(8,128)(2,1)S(1)}, u32[]{:S(2)}, u32[]{:S(2)}) collective-permute-start(bf16[256,512]{1,0:T(8,128)(2,1)S(1)} %collective-permute-done.21.refs_5_), channel_id=1, source_target_pairs={{0,8},{8,0},{16,24},{24,16},{1,9},{9,1},{17,25},{25,17},{2,10},{10... | collective-permute-start | bytes 786440 | tf_op jit(solution)/shard_map/ppermute | solution.py:252
  53.6 13.3 %collective-permute-start.16 = (bf16[512,256]{1,0:T(8,128)(2,1)S(1)}, bf16[512,256]{1,0:T(8,128)(2,1)S(1)}, u32[]{:S(2)}, u32[]{:S(2)}) collective-permute-start(bf16[512,256]{1,0:T(8,128)(2,1)S(1)} %project_kv.1.refs_0_), channel_id=1, source_target_pairs={{0,1},{1,0},{2,3},{3,2},{4,5},{5,4},{6,7},{7,6},{8,9},{9,8},{10,11... | collective-permute-start | bytes 786440 | tf_op jit(solution)/shard_map/ppermute | solution.py:249
  64.3 2.5 %collective-permute-start.17 = (bf16[512,256]{1,0:T(8,128)(2,1)S(1)}, bf16[512,256]{1,0:T(8,128)(2,1)S(1)}, u32[]{:S(2)}, u32[]{:S(2)}) collective-permute-start(bf16[512,256]{1,0:T(8,128)(2,1)S(1)} %collective-permute-done.15.refs_1_), channel_id=1, source_target_pairs={{0,1},{1,0},{2,3},{3,2},{4,5},{5,4},{6,7},{7,6},{8,9},{9,8},{10,11... | collective-permute-start | bytes 786440 | tf_op jit(solution)/shard_map/ppermute | solution.py:249
  66.2 3.3 %collective-permute-start.23 = (bf16[256,512]{1,0:T(8,128)(2,1)S(1)}, bf16[256,512]{1,0:T(8,128)(2,1)S(1)}, u32[]{:S(2)}, u32[]{:S(2)}) collective-permute-start(bf16[256,512]{1,0:T(8,128)(2,1)S(1)} %get-tuple-element.57), channel_id=1, source_target_pairs={{0,1},{1,0},{2,3},{3,2},{4,5},{5,4},{6,7},{7,6},{8,9},{9,8},{10,11... | collective-permute-start | bytes 786440 | tf_op jit(solution)/shard_map/ppermute | solution.py:249
  69.4 9.2 %collective-permute-start.25 = (bf16[4,64,512]{2,1,0:T(8,128)(2,1)S(1)}, bf16[4,64,512]{2,1,0:T(8,128)(2,1)S(1)}, u32[]{:S(2)}, u32[]{:S(2)}) collective-permute-start(bf16[4,64,512]{2,1,0:T(8,128)(2,1)S(1)} %get-tuple-element.59), channel_id=1, source_target_pairs={{0,2},{1,3},{2,0},{3,1},{4,6},{5,7},{6,4},{7,5},{8,10},{9,11},{10,... | collective-permute-start | bytes 786440 | tf_op jit(solution)/shard_map/ppermute | solution.py:249
  71.5 11.8 %collective-permute-start.24 = (bf16[128,1024]{1,0:T(8,128)(2,1)S(1)}, bf16[128,1024]{1,0:T(8,128)(2,1)S(1)}, u32[]{:S(2)}, u32[]{:S(2)}) collective-permute-start(bf16[128,1024]{1,0:T(8,128)(2,1)S(1)} %attend.3), channel_id=1, source_target_pairs={{0,2},{1,3},{2,0},{3,1},{4,6},{5,7},{6,4},{7,5},{8,10},{9,11},{10,... | collective-permute-start | bytes 786440 | tf_op jit(solution)/shard_map/ppermute | solution.py:249
  (3 other events, 2.0 us)

commit v6 on v5

--- a/solution.py
+++ b/solution.py
@@ -12,6 +12,7 @@
 HD = 256
 TEAM = 4
 ID_ROWS = 16
+LANES = 128
 ROPE_BASE = 1000000.0
 NORM_EPS = 1e-06
 MIB = 1024 * 1024
@@ -49,35 +50,53 @@
     return pl.multiple_of(H * HD + core * KVH * HD + pair * HD, HD)
 
 
-def pack_kernel(w_ref, ids_ref, *outs):
+def pack_kernel(w_hbm, ids_hbm, *refs):
+    outs, (w_ref, ids_ref, sems) = refs[:TEAM], refs[TEAM:]
+    run([pltpu.make_async_copy(w_hbm, w_ref, sems.at[0]), pltpu.make_async_copy(ids_hbm, ids_ref, sems.at[1])])
     _, pair, core = place()
     member = pair * 2 + core
     rows = w_ref.shape[0]
     per_device = ids_ref.shape[1]
-    lane = lax.broadcasted_iota(jnp.int32, (ID_ROWS, HD), 1) - member * per_device
-    ids = jnp.zeros((ID_ROWS, HD), jnp.int32)
+    lane = lax.broadcasted_iota(jnp.int32, (ID_ROWS, LANES), 1) - member * per_device
+    ids = jnp.zeros((ID_ROWS, LANES), jnp.int32)
     for j in range(per_device):
         ids = jnp.where(lane == j, ids_ref[0, j], ids)
     ids = ids.astype(jnp.float32).astype(jnp.bfloat16)
     for k in range(TEAM):
         to_pair, to_core = pair ^ (k // 2), core ^ (k % 2)
-        outs[k][:rows, :HD] = w_ref[:, pl.ds(kv_start(to_pair, to_core), HD)]
-        outs[k][:rows, HD:] = w_ref[:, pl.ds(q_start(to_pair, to_core), 2 * HD)]
-        outs[k][rows:, :HD] = ids
-        outs[k][rows:, HD:] = jnp.zeros((ID_ROWS, 2 * HD), jnp.bfloat16)
+        for n in range(3 * HD // LANES):
+            if n < HD // LANES:
+                start = pl.multiple_of(kv_start(to_pair, to_core) + n * LANES, LANES)
+            else:
+                start = pl.multiple_of(q_start(to_pair, to_core) + n * LANES - HD, LANES)
+            outs[k][n * rows : (n + 1) * rows, :] = w_ref[:, pl.ds(start, LANES)]
+        outs[k][3 * HD // LANES * rows :, :] = ids
 
 
 def team_kernel(*refs):
     _, pair, core = place()
-    parts, kv_out, q_out = refs[:TEAM], refs[TEAM], refs[TEAM + 1]
+    parts, (kv_out, q_out, *q_halves) = refs[:TEAM], refs[TEAM:]
     rows = q_out.shape[0] // TEAM
     member = pair * 2 + core
     for k in range(TEAM):
         here = aligned(member ^ k, rows)
-        kv_out[here, :] = parts[k][:rows, :HD]
-        q_out[here, :] = parts[k][:rows, HD:]
-    below = [part[rows:, :HD].astype(jnp.float32) for part in parts]
-    kv_out[TEAM * rows :, :] = sum(below[1:], below[0]).astype(jnp.bfloat16)
+        for n in range(3 * HD // LANES):
+            out = kv_out if n < HD // LANES else q_out
+            first = n * LANES if n < HD // LANES else n * LANES - HD
+            part = parts[k][n * rows : (n + 1) * rows, :]
+            out[here, first : first + LANES] = part
+            if out is q_out:
+                q_halves[first // HD][here, first % HD : first % HD + LANES] = part
+    below = [part[3 * HD // LANES * rows :, :].astype(jnp.float32) for part in parts]
+    ids = sum(below[1:], below[0]).astype(jnp.bfloat16)
+    kv_out[TEAM * rows :, :] = jnp.concatenate([ids] * (HD // LANES), 1)
+
+
+def join_kernel(*refs):
+    out = refs[-1]
+    for n, ref in enumerate(refs[:-1]):
+        width = ref.shape[1]
+        out[:, n * width : (n + 1) * width] = ref[...]
 
 
 def stack_kernel(*refs):
@@ -99,35 +118,39 @@
     _, pair, core = place()
     member = pair * 2 + core
     rows = x_ref.shape[0] // TEAM
-    copies = []
+    direct = depth % LANES == 0
+    places = []
     for i, piece in enumerate(weights):
         from_req = req ^ (i // 2)
         tall = piece.shape[0] // (n_out - 1 if i % 2 else 1)
         for n in range(n_out - 1 if i % 2 else 1):
             from_outer = lax.rem(outer + n_out - n - i % 2, n_out)
-            copies.append(
-                pltpu.make_async_copy(
-                    piece.at[pl.ds(n * tall, depth), :],
-                    w_all.at[aligned(from_req * n_out + from_outer, depth), :],
-                    sems.at[len(copies)],
-                )
-            )
-    run(copies)
+            places.append((piece.at[pl.ds(n * tall, depth), :], aligned(from_req * n_out + from_outer, depth)))
+    if not direct:
+        run([
+            pltpu.make_async_copy(piece, w_all.at[there, :], sems.at[n]) for n, (piece, there) in enumerate(places)
+        ])
     half = HD // 2
     gain = gain_ref[...]
     if is_kv:
         gain = jnp.where(core == 0, gain, 1.0)
     for out, steps in zip(outs, [(0, 1, 2, 3)] if is_kv else [(1, 3), (0, 2)]):
+        def team_rows(ref, cols):
+            if is_kv:
+                return ref[:, cols]
+            return jnp.concatenate([ref[aligned(member ^ k, rows), cols] for k in steps], 0)
+
+        every = slice(None)
+        cosine, sine = team_rows(cos_ref, every), team_rows(sin_ref, every)
         if is_kv:
-            x, cosine, sine = x_ref[...], cos_ref[...], sin_ref[...]
             cosine = jnp.where(core == 0, cosine, 1.0)
             sine = jnp.where(core == 0, sine, 0.0)
+        if direct:
+            product = 0.0
+            for piece, there in places:
+                product += jnp.dot(team_rows(x_ref, there), piece[...], preferred_element_type=jnp.float32)
         else:
-            x, cosine, sine = (
-                jnp.concatenate([ref[aligned(member ^ k, rows), :] for k in steps], 0)
-                for ref in (x_ref, cos_ref, sin_ref)
-            )
-        product = jnp.dot(x, w_all[...], preferred_element_type=jnp.float32)
+            product = jnp.dot(team_rows(x_ref, every), w_all[...], preferred_element_type=jnp.float32)
         for h in range(out.shape[1] // HD):
             head = product[:, h * HD : (h + 1) * HD]
             mean = jnp.mean(head * head, axis=-1, keepdims=True)
@@ -135,19 +158,6 @@
             front, second = head[:, :half], head[:, half:]
             out[:, h * HD : h * HD + half] = (front * cosine - second * sine).astype(jnp.bfloat16)
             out[:, h * HD + half : (h + 1) * HD] = (second * cosine + front * sine).astype(jnp.bfloat16)
-
-
-def load_kv(n_out, blk_rows, mine, other, ids_ref, store, sems, core):
-    per_piece = mine[0].shape[0] // blk_rows
-    copies = []
-    for k in range(n_out):
-        for j in range(per_piece):
-            n = k * per_piece + j
-            there = aligned(ids_ref[n], blk_rows)
-            here = pl.ds(j * blk_rows, blk_rows)
-            copies.append(pltpu.make_async_copy(mine[k].at[here, :], store.at[core, there, :], sems.at[0, n]))
-            copies.append(pltpu.make_async_copy(other[k].at[here, :], store.at[1 - core, there, :], sems.at[1, n]))
-    run(copies)
 
 
 def attend_kernel(blk_rows, step, store, q_ref, near_ref, ids_ref, length_ref, out):
@@ -196,12 +206,18 @@
 
 def pages_kernel(n_out, blk_rows, *refs):
     mine, other = refs[:n_out], refs[n_out : 2 * n_out]
-    ids_ref, info_ref, own, away, store, sems = refs[2 * n_out :]
+    ids_ref, info_ref, own, away, store = refs[2 * n_out :]
     _, _, core = place()
-    load_kv(n_out, blk_rows, mine, other, ids_ref, store, sems, core)
+    per_piece = mine[0].shape[0] // blk_rows
+    for k in range(n_out):
+        for j in range(per_piece):
+            there = aligned(ids_ref[k * per_piece + j], blk_rows)
+            here = slice(j * blk_rows, (j + 1) * blk_rows)
+            store[core, there, :] = mine[k][here, :]
+            store[1 - core, there, :] = other[k][here, :]
     slots = own.shape[0]
     row = lax.broadcasted_iota(jnp.int32, (blk_rows, HD), 0)
-    for target, base in ((own, 0), (away, slots)):
+    for target, base in ((away, slots), (own, 0)):
         for i in range(slots):
             here = aligned(info_ref[1, base + i], blk_rows)
             live = row < info_ref[2, base + i]
@@ -259,22 +275,27 @@
 
     w_rows = qkv_weight.shape[0]
     per_device = block_ids.shape[1]
+    own = tokens[0]
+    rows = own.shape[0]
     parts = pl.pallas_call(
         pack_kernel,
-        out_shape=[shape((w_rows + ID_ROWS, 3 * HD), bf16)] * TEAM,
-        in_specs=[VMEM, SMEM],
+        out_shape=[shape((3 * HD // LANES * w_rows + ID_ROWS, LANES), bf16)] * TEAM,
+        in_specs=[ANY] * 2,
         out_specs=[VMEM] * TEAM,
-        compiler_params=params(2),
+        scratch_shapes=[
+            pltpu.VMEM(qkv_weight.shape, bf16),
+            pltpu.SMEM(block_ids.shape, jnp.int32),
+            pltpu.SemaphoreType.DMA((2,)),
+        ],
+        compiler_params=params(4),
         name="pack",
     )(qkv_weight, block_ids)
-    own = tokens[0]
-    rows = own.shape[0]
-    own_near = in_team(own, 1)
-    kv, q = pl.pallas_call(
+    head_rows = shape((TEAM * w_rows, HD), bf16)
+    kv, q, qa, qb = pl.pallas_call(
         team_kernel,
-        out_shape=[shape((TEAM * w_rows + ID_ROWS, HD), bf16), shape((TEAM * w_rows, 2 * HD), bf16)],
+        out_shape=[shape((TEAM * w_rows + ID_ROWS, HD), bf16), shape((TEAM * w_rows, 2 * HD), bf16), head_rows, head_rows],
         in_specs=[VMEM] * TEAM,
-        out_specs=[VMEM] * 2,
+        out_specs=[VMEM] * 4,
         compiler_params=params(2),
         name="team",
     )(parts[0], *[in_team(parts[k], k) for k in range(1, TEAM)])
@@ -283,20 +304,17 @@
         got = [across(piece, k) for k in range(1, n_out)]
         return got[0] if len(got) == 1 else jnp.concatenate(got, 0)
 
-    kv, q, own, own_near = sync(kv, q, own, own_near)
+    kv, q, own = sync(kv, q, own)
     kv_o, kv_x, kv_y = from_others(kv), in_req(kv, 1), in_req(kv, 2)
-    far = in_team(own, 2)
-    kv_x, kv_y, q = sync(kv_x, kv_y, q)
-    q_x, q_y, kv_d = in_req(q, 1), in_req(q, 2), in_req(kv_x, 2)
-    kv_o, kv_d, q = sync(kv_o, kv_d, q)
-    q_o, kv_ox, kv_oy = from_others(q), in_req(kv_o, 1), in_req(kv_o, 2)
-    q_x, q_y, kv_ox, kv_oy, far = sync(q_x, q_y, kv_ox, kv_oy, far)
-    kv_od, q_d, far_near = in_req(kv_oy, 1), in_req(q_x, 2), in_team(far, 1)
+    far, own_near = in_team(own, 2), in_team(own, 1)
+    kv_x, kv_y, q, own_near = sync(kv_x, kv_y, q, own_near)
+    kv_d, q_x = in_req(kv_x, 2), in_req(q, 1)
+    kv_o, kv_d, qa = sync(kv_o, kv_d, qa)
+    qa_o, kv_ox, kv_oy = from_others(qa), in_req(kv_o, 1), in_req(kv_o, 2)
+    kv_ox, kv_oy, q_x, q, qa_o, qb, far = sync(kv_ox, kv_oy, q_x, q, qa_o, qb, far)
+    kv_od, q_y, qb_o, far_near = in_req(kv_oy, 1), in_req(q, 2), from_others(qb), in_team(far, 1)
+    kv_od, q_y, qb_o, far_near = sync(kv_od, q_y, qb_o, far_near)
     kv_weight = [kv, kv_o, kv_x, kv_ox, kv_y, kv_oy, kv_d, kv_od]
-    q_o, q_d, kv_od = sync(q_o, q_d, kv_od)
-    q_ox, q_oy = in_req(q_o, 1), in_req(q_o, 2)
-    q_od = in_req(q_oy, 1)
-    q_weight = [q, q_o, q_x, q_ox, q_y, q_oy, q_d, q_od]
     stacked = pl.pallas_call(
         stack_kernel,
         out_shape=shape((TEAM * rows, own.shape[1]), bf16),
@@ -326,10 +344,10 @@
         return pl.pallas_call(
             functools.partial(project_kernel, n_out, TEAM * w_rows, is_kv),
             out_shape=[shape((TEAM * rows // n_outs, width), bf16)] * n_outs,
-            in_specs=[VMEM] + [ANY] * len(weight) + [VMEM] * 3,
+            in_specs=[VMEM] * (4 + len(weight)),
             out_specs=[VMEM] * n_outs,
             scratch_shapes=[
-                pltpu.VMEM((depth, width), bf16),
+                pltpu.VMEM((depth, width) if w_rows * TEAM % LANES else (ID_ROWS, LANES), bf16),
                 pltpu.SemaphoreType.DMA((n_req * n_out,)),
             ],
             cost_estimate=pl.CostEstimate(
@@ -340,6 +358,18 @@
         )(stacked, *weight, gain[None, :], cosine, sine)
 
     (made,) = project(kv_weight, True, k_gain)
+    q_o = pl.pallas_call(
+        join_kernel,
+        out_shape=shape((qa_o.shape[0], 2 * HD), bf16),
+        in_specs=[VMEM] * 2,
+        out_specs=VMEM,
+        compiler_params=params(2 + 2 * n_out // 8),
+        name="join",
+    )(qa_o, qb_o)
+    q_ox, q_oy = in_req(q_o, 1), in_req(q_o, 2)
+    q_ox, q_oy, q_y = sync(q_ox, q_oy, q_y)
+    q_d, q_od = in_req(q_y, 1), in_req(q_ox, 2)
+    q_weight = [q, q_o, q_x, q_ox, q_y, q_oy, q_d, q_od]
     mine = [made] + [across(made, k) for k in range(1, n_out)]
     other = [in_team(part, 1) for part in mine]
 
@@ -364,11 +394,10 @@
     own_pages, away_pages, store = pl.pallas_call(
         functools.partial(pages_kernel, n_out, blk_rows),
         out_shape=[page_shape, page_shape, shape((2, total, HD), bf16)],
-        in_specs=[ANY] * (2 * n_out) + [SMEM] * 2,
+        in_specs=[VMEM] * (2 * n_out) + [SMEM] * 2,
         out_specs=[VMEM] * 3,
-        scratch_shapes=[pltpu.SemaphoreType.DMA((2, total // blk_rows))],
         cost_estimate=pl.CostEstimate(flops=0, bytes_accessed=4 * MIB, transcendentals=0),
-        compiler_params=params(store_mib + 4),
+        compiler_params=params(2 * store_mib + 4),
         name="pages",
     )(*mine, *other, all_ids, info)
     got_pages = in_team(away_pages, 2)

time: 85.2 us -> 93.3 us (1.095)
  waiting for transfers between devices: 37.9 us -> 43.6 us
  starting transfers between devices: 25.4 us -> 27.8 us
  local copies, waits for them, and re-layouts: 4.95 us -> 6.87 us
  Pallas kernels: 13.7 us -> 11.8 us
    ppermute x3 -> x4, waiting for transfers between devices: 18.6 us -> 27.9 us  [across(): lax.ppermute(array, 'blk', [(i, (i + TEAM * k) % n_blk) for i in range(n_...]
    ppermute x12, waiting for transfers between devices: 5.51 us -> 2.37 us  [in_req(): return lax.ppermute(array, 'req', [(i, i ^ k) for i in range(n_req)])]
    ppermute x12, starting transfers between devices: 10.3 us -> 12.3 us  [in_req(): return lax.ppermute(array, 'req', [(i, i ^ k) for i in range(n_req)])]
    unnamed x18 -> x24, local copies, waits for them, and re-layouts: 4.03 us -> 5.95 us
    pallas_call x1, Pallas kernels: 2.54 us -> 0.71 us  [body(): pl.pallas_call(functools.partial(pages_kernel, n_out, blk_rows), out_shap...]
    pallas_call x2, Pallas kernels: 4.67 us -> 3.47 us  [project(): pl.pallas_call(functools.partial(project_kernel, n_out, TEAM * w_rows, is...]
    pallas_call x1 -> x2, Pallas kernels: 0.59 us -> 1.78 us  [the longest x1 0.92 us: body(): pl.pallas_call(join_kernel, out_shape=shape((qa_o.shape[0], 2 * HD), bf16...]
    ppermute x3 -> x4, starting transfers between devices: 7.17 us -> 8.1 us  [across(): lax.ppermute(array, 'blk', [(i, (i + TEAM * k) % n_blk) for i in range(n_...]
  transfers between devices with their start and end apart: 26 -> 27, of which waited for: 12 -> 11; matrix products, arithmetic and copies ran while one was open for 3% -> 2% of each run, Pallas kernels for 14% -> 9%
where the time goes in v6:
time: 93.3 us; the launch traced here: 93 us
  waiting for transfers between devices  43.6 us (47%)
  starting transfers between devices  27.8 us (30%)
  Pallas kernels  11.8 us (13%)
  local copies, waits for them, and re-layouts  6.87 us (7%)
  between operations  1.52 us (2%)
  other arithmetic  1.36 us (1%)
    ppermute x4, waiting for transfers between devices, across(): lax.ppermute(array, 'blk', [(i, (i + TEAM * k) % n_blk) for i in range(n_...  27.9 us
    ppermute x11, waiting for transfers between devices, in_team(): return lax.ppermute(array, 'blk', [(i, i ^ k) for i in range(n_blk)])  13.3 us
    ppermute x12, starting transfers between devices, in_req(): return lax.ppermute(array, 'req', [(i, i ^ k) for i in range(n_req)])  12.3 us
    ppermute x4, starting transfers between devices, across(): lax.ppermute(array, 'blk', [(i, (i + TEAM * k) % n_blk) for i in range(n_...  8.1 us
    ppermute x11, starting transfers between devices, in_team(): return lax.ppermute(array, 'blk', [(i, i ^ k) for i in range(n_blk)])  7.46 us
    unnamed x24, local copies, waits for them, and re-layouts  5.95 us
    pallas_call x2, Pallas kernels, attend(): pl.pallas_call(functools.partial(attend_kernel, blk_rows, step), out_shap...  4.03 us
    pallas_call x2, Pallas kernels, project(): pl.pallas_call(functools.partial(project_kernel, n_out, TEAM * w_rows, is...  3.47 us
  transfers between devices with their start and end apart: 27, of which 11 were waited for; matrix products, arithmetic and copies ran while one was open for 2% of the time, Pallas kernels for 9%

profile of v6, /device:TPU:0, one launch (start us, length us, event | category | flops | bytes accessed | tf_op | source)
XLA Modules:
  0.0 93.0 jit_solution(3983189945676140650)
XLA Ops:
  0.7 1.0 %copy-done.1 = bf16[64,3072]{1,0:T(8,128)(2,1)S(1)} copy-done((bf16[64,3072]{1,0:T(8,128)(2,1)S(1)}, bf16[64,3072]{1,0:T(8,128)(2,1)}, u32[]{:S(2)}) %copy-start.1) | copy-done | bytes 393240
  2.4 0.9 pack.1
  3.7 2.6 %collective-permute-start.1 = (bf16[400,128]{1,0:T(8,128)(2,1)S(1)}, bf16[400,128]{1,0:T(8,128)(2,1)S(1)}, u32[]{:S(2)}, u32[]{:S(2)}) collective-permute-start(bf16[400,128]{1,0:T(8,128)(2,1)S(1)} %get-tuple-element.43), channel_id=1, source_target_pairs={{0,2},{1,3},{2,0},{3,1},{4,6},{5,7},{6,4},{7,5},{8,10},{9,11},{10,... | collective-permute-start | bytes 307208 | tf_op jit(solution)/shard_map/ppermute | solution.py:265
  6.5 3.7 %collective-permute-done.1.refs_2_ = bf16[400,128]{1,0:T(8,128)(2,1)S(1)} collective-permute-done((bf16[400,128]{1,0:T(8,128)(2,1)S(1)}, bf16[400,128]{1,0:T(8,128)(2,1)S(1)}, u32[]{:S(2)}, u32[]{:S(2)}) %collective-permute-start.1) | collective-permute-done | bytes 102432 | tf_op jit(solution)/shard_map/ppermute | solution.py:265
  10.1 1.7 %collective-permute-done.2.refs_3_ = bf16[400,128]{1,0:T(8,128)(2,1)S(1)} collective-permute-done((bf16[400,128]{1,0:T(8,128)(2,1)S(1)}, bf16[400,128]{1,0:T(8,128)(2,1)S(1)}, u32[]{:S(2)}, u32[]{:S(2)}) %collective-permute-start.2) | collective-permute-done | bytes 102432 | tf_op jit(solution)/shard_map/ppermute | solution.py:265
  12.7 1.6 %collective-permute-start.3 = (bf16[272,256]{1,0:T(8,128)(2,1)S(1)}, bf16[272,256]{1,0:T(8,128)(2,1)S(1)}, u32[]{:S(2)}, u32[]{:S(2)}) collective-permute-start(bf16[272,256]{1,0:T(8,128)(2,1)S(1)} %get-tuple-element.48.refs_0_), channel_id=1, source_target_pairs={{0,8},{8,0},{16,24},{24,16},{1,9},{9,1},{17,25},{25,17},{2,10},{10... | collective-permute-start | bytes 417800 | tf_op jit(solution)/shard_map/ppermute | solution.py:268
  14.3 1.5 %collective-permute-start.4 = (bf16[272,256]{1,0:T(8,128)(2,1)S(1)}, bf16[272,256]{1,0:T(8,128)(2,1)S(1)}, u32[]{:S(2)}, u32[]{:S(2)}) collective-permute-start(bf16[272,256]{1,0:T(8,128)(2,1)S(1)} %get-tuple-element.48.refs_0_), channel_id=1, source_target_pairs={{0,16},{8,24},{16,0},{24,8},{1,17},{9,25},{17,1},{25,9},{2,18},{10... | collective-permute-start | bytes 417800 | tf_op jit(solution)/shard_map/ppermute | solution.py:268
  15.8 1.6 %collective-permute-start.12 = (bf16[128,2048]{1,0:T(8,128)(2,1)}, bf16[128,2048]{1,0:T(8,128)(2,1)S(1)}, u32[]{:S(2)}, u32[]{:S(2)}) collective-permute-start(bf16[128,2048]{1,0:T(8,128)(2,1)} %bitcast.33), channel_id=1, source_target_pairs={{0,2},{1,3},{2,0},{3,1},{4,6},{5,7},{6,4},{7,5},{8,10},{9,11},{10,... | collective-permute-start | bytes 1572872 | tf_op jit(solution)/shard_map/ppermute | solution.py:265
  17.4 2.6 %collective-permute-start.6 = (bf16[272,256]{1,0:T(8,128)(2,1)S(1)}, bf16[272,256]{1,0:T(8,128)(2,1)S(1)}, u32[]{:S(2)}, u32[]{:S(2)}) collective-permute-start(bf16[272,256]{1,0:T(8,128)(2,1)S(1)} %get-tuple-element.48.refs_0_), channel_id=1, source_target_pairs={{0,4},{1,5},{2,6},{3,7},{4,0},{5,1},{6,2},{7,3},{8,12},{9,13},{10,... | collective-permute-start | bytes 417800 | tf_op jit(solution)/shard_map/ppermute | solution.py:271
  20.0 1.4 %collective-permute-start.7 = (bf16[272,256]{1,0:T(8,128)(2,1)S(1)}, bf16[272,256]{1,0:T(8,128)(2,1)S(1)}, u32[]{:S(2)}, u32[]{:S(2)}) collective-permute-start(bf16[272,256]{1,0:T(8,128)(2,1)S(1)} %collective-permute-done.3.refs_2_), channel_id=1, source_target_pairs={{0,16},{8,24},{16,0},{24,8},{1,17},{9,25},{17,1},{25,9},{2,18},{10... | collective-permute-start | bytes 417800 | tf_op jit(solution)/shard_map/ppermute | solution.py:268
  21.4 0.8 eq.18
  23.6 8.1 %collective-permute-done.6.refs_1_ = bf16[272,256]{1,0:T(8,128)(2,1)S(1)} collective-permute-done((bf16[272,256]{1,0:T(8,128)(2,1)S(1)}, bf16[272,256]{1,0:T(8,128)(2,1)S(1)}, u32[]{:S(2)}, u32[]{:S(2)}) %collective-permute-start.6) | collective-permute-done | bytes 139296 | tf_op jit(solution)/shard_map/ppermute | solution.py:271
  33.3 3.4 %collective-permute-start.11 = (bf16[256,256]{1,0:T(8,128)(2,1)S(1)}, bf16[256,256]{1,0:T(8,128)(2,1)S(1)}, u32[]{:S(2)}, u32[]{:S(2)}) collective-permute-start(bf16[256,256]{1,0:T(8,128)(2,1)S(1)} %get-tuple-element.55), channel_id=1, source_target_pairs={{0,4},{1,5},{2,6},{3,7},{4,0},{5,1},{6,2},{7,3},{8,12},{9,13},{10,... | collective-permute-start | bytes 393224 | tf_op jit(solution)/shard_map/ppermute | solution.py:271
  36.7 4.0 %collective-permute-done.11.refs_0_ = bf16[256,256]{1,0:T(8,128)(2,1)S(1)} collective-permute-done((bf16[256,256]{1,0:T(8,128)(2,1)S(1)}, bf16[256,256]{1,0:T(8,128)(2,1)S(1)}, u32[]{:S(2)}, u32[]{:S(2)}) %collective-permute-start.11) | collective-permute-done | bytes 131104 | tf_op jit(solution)/shard_map/ppermute | solution.py:271
  42.1 1.6 %collective-permute-start.14 = (bf16[256,512]{1,0:T(8,128)(2,1)S(1)}, bf16[256,512]{1,0:T(8,128)(2,1)S(1)}, u32[]{:S(2)}, u32[]{:S(2)}) collective-permute-start(bf16[256,512]{1,0:T(8,128)(2,1)S(1)} %get-tuple-element.59.refs_0_), channel_id=1, source_target_pairs={{0,16},{8,24},{16,0},{24,8},{1,17},{9,25},{17,1},{25,9},{2,18},{10... | collective-permute-start | bytes 786440 | tf_op jit(solution)/shard_map/ppermute | solution.py:268
  43.7 1.5 %collective-permute-start.13 = (bf16[272,256]{1,0:T(8,128)(2,1)}, bf16[272,256]{1,0:T(8,128)(2,1)}, u32[]{:S(2)}, u32[]{:S(2)}) collective-permute-start(bf16[272,256]{1,0:T(8,128)(2,1)} %collective-permute-done.9.refs_5_), channel_id=1, source_target_pairs={{0,8},{8,0},{16,24},{24,16},{1,9},{9,1},{17,25},{25,17},{2,10},{10... | collective-permute-start | bytes 417800 | tf_op jit(solution)/shard_map/ppermute | solution.py:268
  45.2 1.9 %collective-permute-start.15 = (bf16[256,256]{1,0:T(8,128)(2,1)}, bf16[256,256]{1,0:T(8,128)(2,1)}, u32[]{:S(2)}, u32[]{:S(2)}) collective-permute-start(bf16[256,256]{1,0:T(8,128)(2,1)} %copy-done.11), channel_id=1, source_target_pairs={{0,4},{1,5},{2,6},{3,7},{4,0},{5,1},{6,2},{7,3},{8,12},{9,13},{10,... | collective-permute-start | bytes 393224 | tf_op jit(solution)/shard_map/ppermute | solution.py:271
  47.3 7.3 %collective-permute-done.15.refs_1_ = bf16[256,256]{1,0:T(8,128)(2,1)} collective-permute-done((bf16[256,256]{1,0:T(8,128)(2,1)}, bf16[256,256]{1,0:T(8,128)(2,1)}, u32[]{:S(2)}, u32[]{:S(2)}) %collective-permute-start.15) | collective-permute-done | bytes 131104 | tf_op jit(solution)/shard_map/ppermute | solution.py:271
  54.5 0.9 copy-done.7
  55.4 0.9 join.1.refs_1_
  57.5 1.0 %multiply_sine_fusion = (f32[512,128]{1,0:T(8,128)S(1)}, f32[512,128]{1,0:T(8,128)S(1)}) fusion(f32[128]{0:T(128)S(1)} %multiply_power_fusion, f32[512]{0:T(512)S(1)} %convert_element_type.37), kind=kLoop, calls=%fused_computation | loop fusion | flops 65536 | bytes 526848 | tf_op jit(solution)/shard_map/sin | solution.py:338
  59.4 1.9 %project_kv.1.refs_0_ = bf16[512,256]{1,0:T(8,128)(2,1)S(1)} custom-call(bf16[512,2048]{1,0:T(8,128)(2,1)S(1)} %stack.8.x_ref, bf16[272,256]{1,0:T(8,128)(2,1)S(1)} %get-tuple-element.48.refs_0_, bf16[272,256]{1,0:T(8,128)(2,1)S(1)} %collective-permute-done.6.refs_1_, bf16[272,256]{1,0:T(8,128)(2,1)S(1)} %collective-permute-done.3.refs_2_, ...), custom_call_target="tpu_custom_call" | custom-call | flops 536870912 | bytes 6291456 | tf_op jit(solution)/shard_map/project_kv/pallas_call | solution.py:344
  61.6 2.1 %collective-permute-done.20.refs_3_ = bf16[256,512]{1,0:T(8,128)(2,1)S(1)} collective-permute-done((bf16[256,512]{1,0:T(8,128)(2,1)S(1)}, bf16[256,512]{1,0:T(8,128)(2,1)S(1)}, u32[]{:S(2)}, u32[]{:S(2)}) %collective-permute-start.20) | collective-permute-done | bytes 262176 | tf_op jit(solution)/shard_map/ppermute | solution.py:268
  63.9 1.5 %collective-permute-start.22 = (bf16[256,512]{1,0:T(8,128)(2,1)S(1)}, bf16[256,512]{1,0:T(8,128)(2,1)S(1)}, u32[]{:S(2)}, u32[]{:S(2)}) collective-permute-start(bf16[256,512]{1,0:T(8,128)(2,1)S(1)} %collective-permute-done.14.refs_4_), channel_id=1, source_target_pairs={{0,8},{8,0},{16,24},{24,16},{1,9},{9,1},{17,25},{25,17},{2,10},{10... | collective-permute-start | bytes 786440 | tf_op jit(solution)/shard_map/ppermute | solution.py:268
  66.0 8.6 %collective-permute-done.17.refs_1_ = bf16[512,256]{1,0:T(8,128)(2,1)S(1)} collective-permute-done((bf16[512,256]{1,0:T(8,128)(2,1)S(1)}, bf16[512,256]{1,0:T(8,128)(2,1)S(1)}, u32[]{:S(2)}, u32[]{:S(2)}) %collective-permute-start.17) | collective-permute-done | bytes 262176 | tf_op jit(solution)/shard_map/ppermute | solution.py:271
  74.6 1.6 %project_q.1 = (bf16[256,512]{1,0:T(8,128)(2,1)S(1)}, bf16[256,512]{1,0:T(8,128)(2,1)S(1)}) custom-call(bf16[512,2048]{1,0:T(8,128)(2,1)S(1)} %stack.8.x_ref, bf16[256,512]{1,0:T(8,128)(2,1)S(1)} %get-tuple-element.59.refs_0_, bf16[256,512]{1,0:T(8,128)(2,1)S(1)} %join.1.refs_1_, bf16[256,512]{1,0:T(8,128)(2,1)S(1)} %collective-permute-done.10.refs_2_, ...), custom_call_target="tpu_custom_call" | custom-call | flops 1073741824 | bytes 6291456 | tf_op jit(solution)/shard_map/project_q/pallas_call | solution.py:344
  77.9 2.0 %attend.3 = bf16[128,1024]{1,0:T(8,128)(2,1)S(1)} custom-call(bf16[2,1024,256]{2,1,0:T(8,128)(2,1)S(1)} %get-tuple-element.66.store, bf16[256,512]{1,0:T(8,128)(2,1)S(1)} %get-tuple-element.74.q_ref, bf16[256,512]{1,0:T(8,128)(2,1)S(1)} %collective-permute-done.24.near_ref, s32[16]{0:T(128)S(1)} %reshape.141.refs_4_.ids_ref, s32[1]{0:T(128)} %copy.9.length_ref), custom_call_target="tpu_custom_call" | custom-call | flops 536870912 | bytes 4194304 | tf_op jit(solution)/shard_map/attend/pallas_call | solution.py:406
  80.0 1.8 %collective-permute-start.25 = (bf16[128,1024]{1,0:T(8,128)(2,1)S(1)}, bf16[128,1024]{1,0:T(8,128)(2,1)S(1)}, u32[]{:S(2)}, u32[]{:S(2)}) collective-permute-start(bf16[128,1024]{1,0:T(8,128)(2,1)S(1)} %attend.3), channel_id=1, source_target_pairs={{0,2},{1,3},{2,0},{3,1},{4,6},{5,7},{6,4},{7,5},{8,10},{9,11},{10,... | collective-permute-start | bytes 786440 | tf_op jit(solution)/shard_map/ppermute | solution.py:265
  81.8 2.0 %attend.2.kept = bf16[128,1024]{1,0:T(8,128)(2,1)S(1)} custom-call(bf16[2,1024,256]{2,1,0:T(8,128)(2,1)S(1)} %get-tuple-element.66.store, bf16[256,512]{1,0:T(8,128)(2,1)S(1)} %get-tuple-element.74.q_ref, bf16[256,512]{1,0:T(8,128)(2,1)S(1)} %collective-permute-done.24.near_ref, s32[16]{0:T(128)S(1)} %reshape.141.refs_4_.ids_ref, s32[1]{0:T(128)} %copy.9.length_ref), custom_call_target="tpu_custom_call" | custom-call | flops 536870912 | bytes 4194304 | tf_op jit(solution)/shard_map/attend/pallas_call | solution.py:406
  83.8 3.0 %collective-permute-done.26.got_pages = bf16[4,64,512]{2,1,0:T(8,128)(2,1)S(1)} collective-permute-done((bf16[4,64,512]{2,1,0:T(8,128)(2,1)S(1)}, bf16[4,64,512]{2,1,0:T(8,128)(2,1)S(1)}, u32[]{:S(2)}, u32[]{:S(2)}) %collective-permute-start.26) | collective-permute-done | bytes 262176 | tf_op jit(solution)/shard_map/ppermute | solution.py:265
  86.8 4.7 %collective-permute-done.25.from_far = bf16[128,1024]{1,0:T(8,128)(2,1)S(1)} collective-permute-done((bf16[128,1024]{1,0:T(8,128)(2,1)S(1)}, bf16[128,1024]{1,0:T(8,128)(2,1)S(1)}, u32[]{:S(2)}, u32[]{:S(2)}) %collective-permute-start.25) | collective-permute-done | bytes 262176 | tf_op jit(solution)/shard_map/ppermute | solution.py:265
  91.5 1.5 %finish.1 = (bf16[128,2048]{1,0:T(8,128)(2,1)}, bf16[4,64,512]{2,1,0:T(8,128)(2,1)}) custom-call(bf16[128,1024]{1,0:T(8,128)(2,1)S(1)} %attend.2.kept, bf16[128,1024]{1,0:T(8,128)(2,1)S(1)} %collective-permute-done.25.from_far, bf16[4,64,512]{2,1,0:T(8,128)(2,1)S(1)} %get-tuple-element.76.own_pages, ...), custom_call_target="tpu_custom_call" | custom-call | tf_op jit(solution)/shard_map/finish/pallas_call | solution.py:421
  (71 shorter events, 11.0 us)
Async XLA Ops:
  0.6 57.8 %copy-start = (bf16[1,128,2048]{2,1,0:T(8,128)(2,1)S(1)}, bf16[1,128,2048]{2,1,0:T(8,128)(2,1)}, u32[]{:S(2)}) copy-start(bf16[1,128,2048]{2,1,0:T(8,128)(2,1)} %param.7) | copy-start | bytes 1572868
  0.6 1.1 %copy-start.1 = (bf16[64,3072]{1,0:T(8,128)(2,1)S(1)}, bf16[64,3072]{1,0:T(8,128)(2,1)}, u32[]{:S(2)}) copy-start(bf16[64,3072]{1,0:T(8,128)(2,1)} %w_hbm.1) | copy-start | bytes 1179652
  3.2 3.2 %collective-permute-start = (bf16[400,128]{1,0:T(8,128)(2,1)S(1)}, bf16[400,128]{1,0:T(8,128)(2,1)S(1)}, u32[]{:S(2)}, u32[]{:S(2)}) collective-permute-start(bf16[400,128]{1,0:T(8,128)(2,1)S(1)} %get-tuple-element.42), channel_id=1, source_target_pairs={{0,1},{1,0},{2,3},{3,2},{4,5},{5,4},{6,7},{7,6},{8,9},{9,8},{10,11... | collective-permute-start | bytes 307208 | tf_op jit(solution)/shard_map/ppermute | solution.py:265
  3.7 6.4 %collective-permute-start.1 = (bf16[400,128]{1,0:T(8,128)(2,1)S(1)}, bf16[400,128]{1,0:T(8,128)(2,1)S(1)}, u32[]{:S(2)}, u32[]{:S(2)}) collective-permute-start(bf16[400,128]{1,0:T(8,128)(2,1)S(1)} %get-tuple-element.43), channel_id=1, source_target_pairs={{0,2},{1,3},{2,0},{3,1},{4,6},{5,7},{6,4},{7,5},{8,10},{9,11},{10,... | collective-permute-start | bytes 307208 | tf_op jit(solution)/shard_map/ppermute | solution.py:265
  6.4 5.4 %collective-permute-start.2 = (bf16[400,128]{1,0:T(8,128)(2,1)S(1)}, bf16[400,128]{1,0:T(8,128)(2,1)S(1)}, u32[]{:S(2)}, u32[]{:S(2)}) collective-permute-start(bf16[400,128]{1,0:T(8,128)(2,1)S(1)} %get-tuple-element.44), channel_id=1, source_target_pairs={{0,3},{1,2},{2,1},{3,0},{4,7},{5,6},{6,5},{7,4},{8,11},{9,10},{10,... | collective-permute-start | bytes 307208 | tf_op jit(solution)/shard_map/ppermute | solution.py:265
  12.6 7.5 %collective-permute-start.5 = (bf16[128,2048]{1,0:T(8,128)(2,1)}, bf16[128,2048]{1,0:T(8,128)(2,1)S(1)}, u32[]{:S(2)}, u32[]{:S(2)}) collective-permute-start(bf16[128,2048]{1,0:T(8,128)(2,1)} %bitcast.32), channel_id=1, source_target_pairs={{0,1},{1,0},{2,3},{3,2},{4,5},{5,4},{6,7},{7,6},{8,9},{9,8},{10,11... | collective-permute-start | bytes 1572872 | tf_op jit(solution)/shard_map/ppermute | solution.py:265
  12.7 7.3 %collective-permute-start.3 = (bf16[272,256]{1,0:T(8,128)(2,1)S(1)}, bf16[272,256]{1,0:T(8,128)(2,1)S(1)}, u32[]{:S(2)}, u32[]{:S(2)}) collective-permute-start(bf16[272,256]{1,0:T(8,128)(2,1)S(1)} %get-tuple-element.48.refs_0_), channel_id=1, source_target_pairs={{0,8},{8,0},{16,24},{24,16},{1,9},{9,1},{17,25},{25,17},{2,10},{10... | collective-permute-start | bytes 417800 | tf_op jit(solution)/shard_map/ppermute | solution.py:268
  14.3 5.7 %collective-permute-start.4 = (bf16[272,256]{1,0:T(8,128)(2,1)S(1)}, bf16[272,256]{1,0:T(8,128)(2,1)S(1)}, u32[]{:S(2)}, u32[]{:S(2)}) collective-permute-start(bf16[272,256]{1,0:T(8,128)(2,1)S(1)} %get-tuple-element.48.refs_0_), channel_id=1, source_target_pairs={{0,16},{8,24},{16,0},{24,8},{1,17},{9,25},{17,1},{25,9},{2,18},{10... | collective-permute-start | bytes 417800 | tf_op jit(solution)/shard_map/ppermute | solution.py:268
  15.8 20.9 %collective-permute-start.12 = (bf16[128,2048]{1,0:T(8,128)(2,1)}, bf16[128,2048]{1,0:T(8,128)(2,1)S(1)}, u32[]{:S(2)}, u32[]{:S(2)}) collective-permute-start(bf16[128,2048]{1,0:T(8,128)(2,1)} %bitcast.33), channel_id=1, source_target_pairs={{0,2},{1,3},{2,0},{3,1},{4,6},{5,7},{6,4},{7,5},{8,10},{9,11},{10,... | collective-permute-start | bytes 1572872 | tf_op jit(solution)/shard_map/ppermute | solution.py:265
  17.4 14.2 %collective-permute-start.6 = (bf16[272,256]{1,0:T(8,128)(2,1)S(1)}, bf16[272,256]{1,0:T(8,128)(2,1)S(1)}, u32[]{:S(2)}, u32[]{:S(2)}) collective-permute-start(bf16[272,256]{1,0:T(8,128)(2,1)S(1)} %get-tuple-element.48.refs_0_), channel_id=1, source_target_pairs={{0,4},{1,5},{2,6},{3,7},{4,0},{5,1},{6,2},{7,3},{8,12},{9,13},{10,... | collective-permute-start | bytes 417800 | tf_op jit(solution)/shard_map/ppermute | solution.py:271
  20.0 11.6 %collective-permute-start.7 = (bf16[272,256]{1,0:T(8,128)(2,1)S(1)}, bf16[272,256]{1,0:T(8,128)(2,1)S(1)}, u32[]{:S(2)}, u32[]{:S(2)}) collective-permute-start(bf16[272,256]{1,0:T(8,128)(2,1)S(1)} %collective-permute-done.3.refs_2_), channel_id=1, source_target_pairs={{0,16},{8,24},{16,0},{24,8},{1,17},{9,25},{17,1},{25,9},{2,18},{10... | collective-permute-start | bytes 417800 | tf_op jit(solution)/shard_map/ppermute | solution.py:268
  22.2 14.5 %collective-permute-start.10 = (bf16[256,512]{1,0:T(8,128)(2,1)S(1)}, bf16[256,512]{1,0:T(8,128)(2,1)S(1)}, u32[]{:S(2)}, u32[]{:S(2)}) collective-permute-start(bf16[256,512]{1,0:T(8,128)(2,1)S(1)} %get-tuple-element.59.refs_0_), channel_id=1, source_target_pairs={{0,8},{8,0},{16,24},{24,16},{1,9},{9,1},{17,25},{25,17},{2,10},{10... | collective-permute-start | bytes 786440 | tf_op jit(solution)/shard_map/ppermute | solution.py:268
  32.3 9.2 %collective-permute-start.8 = (bf16[272,256]{1,0:T(8,128)(2,1)S(1)}, bf16[272,256]{1,0:T(8,128)(2,1)S(1)}, u32[]{:S(2)}, u32[]{:S(2)}) collective-permute-start(bf16[272,256]{1,0:T(8,128)(2,1)S(1)} %collective-permute-done.6.refs_1_), channel_id=1, source_target_pairs={{0,8},{8,0},{16,24},{24,16},{1,9},{9,1},{17,25},{25,17},{2,10},{10... | collective-permute-start | bytes 417800 | tf_op jit(solution)/shard_map/ppermute | solution.py:268
  32.8 9.3 %collective-permute-start.9 = (bf16[272,256]{1,0:T(8,128)(2,1)S(1)}, bf16[272,256]{1,0:T(8,128)(2,1)}, u32[]{:S(2)}, u32[]{:S(2)}) collective-permute-start(bf16[272,256]{1,0:T(8,128)(2,1)S(1)} %collective-permute-done.6.refs_1_), channel_id=1, source_target_pairs={{0,16},{8,24},{16,0},{24,8},{1,17},{9,25},{17,1},{25,9},{2,18},{10... | collective-permute-start | bytes 417800 | tf_op jit(solution)/shard_map/ppermute | solution.py:268
  33.3 7.5 %collective-permute-start.11 = (bf16[256,256]{1,0:T(8,128)(2,1)S(1)}, bf16[256,256]{1,0:T(8,128)(2,1)S(1)}, u32[]{:S(2)}, u32[]{:S(2)}) collective-permute-start(bf16[256,256]{1,0:T(8,128)(2,1)S(1)} %get-tuple-element.55), channel_id=1, source_target_pairs={{0,4},{1,5},{2,6},{3,7},{4,0},{5,1},{6,2},{7,3},{8,12},{9,13},{10,... | collective-permute-start | bytes 393224 | tf_op jit(solution)/shard_map/ppermute | solution.py:271
  42.1 12.4 %collective-permute-start.16 = (bf16[128,2048]{1,0:T(8,128)(2,1)S(1)}, bf16[128,2048]{1,0:T(8,128)(2,1)S(1)}, u32[]{:S(2)}, u32[]{:S(2)}) collective-permute-start(bf16[128,2048]{1,0:T(8,128)(2,1)S(1)} %collective-permute-done.12.refs_2_), channel_id=1, source_target_pairs={{0,1},{1,0},{2,3},{3,2},{4,5},{5,4},{6,7},{7,6},{8,9},{9,8},{10,11... | collective-permute-start | bytes 1572872 | tf_op jit(solution)/shard_map/ppermute | solution.py:265
  42.1 12.4 %collective-permute-start.14 = (bf16[256,512]{1,0:T(8,128)(2,1)S(1)}, bf16[256,512]{1,0:T(8,128)(2,1)S(1)}, u32[]{:S(2)}, u32[]{:S(2)}) collective-permute-start(bf16[256,512]{1,0:T(8,128)(2,1)S(1)} %get-tuple-element.59.refs_0_), channel_id=1, source_target_pairs={{0,16},{8,24},{16,0},{24,8},{1,17},{9,25},{17,1},{25,9},{2,18},{10... | collective-permute-start | bytes 786440 | tf_op jit(solution)/shard_map/ppermute | solution.py:268
  43.7 10.8 %collective-permute-start.13 = (bf16[272,256]{1,0:T(8,128)(2,1)}, bf16[272,256]{1,0:T(8,128)(2,1)}, u32[]{:S(2)}, u32[]{:S(2)}) collective-permute-start(bf16[272,256]{1,0:T(8,128)(2,1)} %collective-permute-done.9.refs_5_), channel_id=1, source_target_pairs={{0,8},{8,0},{16,24},{24,16},{1,9},{9,1},{17,25},{25,17},{2,10},{10... | collective-permute-start | bytes 417800 | tf_op jit(solution)/shard_map/ppermute | solution.py:268
  45.2 9.3 %collective-permute-start.15 = (bf16[256,256]{1,0:T(8,128)(2,1)}, bf16[256,256]{1,0:T(8,128)(2,1)}, u32[]{:S(2)}, u32[]{:S(2)}) collective-permute-start(bf16[256,256]{1,0:T(8,128)(2,1)} %copy-done.11), channel_id=1, source_target_pairs={{0,4},{1,5},{2,6},{3,7},{4,0},{5,1},{6,2},{7,3},{8,12},{9,13},{10,... | collective-permute-start | bytes 393224 | tf_op jit(solution)/shard_map/ppermute | solution.py:271
  56.4 7.3 %collective-permute-start.20 = (bf16[256,512]{1,0:T(8,128)(2,1)S(1)}, bf16[256,512]{1,0:T(8,128)(2,1)S(1)}, u32[]{:S(2)}, u32[]{:S(2)}) collective-permute-start(bf16[256,512]{1,0:T(8,128)(2,1)S(1)} %join.1.refs_1_), channel_id=1, source_target_pairs={{0,8},{8,0},{16,24},{24,16},{1,9},{9,1},{17,25},{25,17},{2,10},{10... | collective-permute-start | bytes 786440 | tf_op jit(solution)/shard_map/ppermute | solution.py:268
  57.0 6.9 %collective-permute-start.21 = (bf16[256,512]{1,0:T(8,128)(2,1)S(1)}, bf16[256,512]{1,0:T(8,128)(2,1)S(1)}, u32[]{:S(2)}, u32[]{:S(2)}) collective-permute-start(bf16[256,512]{1,0:T(8,128)(2,1)S(1)} %join.1.refs_1_), channel_id=1, source_target_pairs={{0,16},{8,24},{16,0},{24,8},{1,17},{9,25},{17,1},{25,9},{2,18},{10... | collective-permute-start | bytes 786440 | tf_op jit(solution)/shard_map/ppermute | solution.py:268
  58.5 1.0 %copy-start.5 = (bf16[272,256]{1,0:T(8,128)(2,1)S(1)}, bf16[272,256]{1,0:T(8,128)(2,1)}, u32[]{:S(2)}) copy-start(bf16[272,256]{1,0:T(8,128)(2,1)} %copy-done.4) | copy-start | bytes 417796
  58.5 1.0 %copy-start.8 = (f32[256]{0:T(256)S(1)}, f32[256]{0:T(256)}, u32[]{:S(2)}) copy-start(f32[256]{0:T(256)} %param.13) | copy-start | bytes 3076
  58.7 15.9 %copy-start.9 = (f32[256]{0:T(256)S(1)}, f32[256]{0:T(256)}, u32[]{:S(2)}) copy-start(f32[256]{0:T(256)} %param.12) | copy-start | bytes 3076
  61.3 13.2 %collective-permute-start.17 = (bf16[512,256]{1,0:T(8,128)(2,1)S(1)}, bf16[512,256]{1,0:T(8,128)(2,1)S(1)}, u32[]{:S(2)}, u32[]{:S(2)}) collective-permute-start(bf16[512,256]{1,0:T(8,128)(2,1)S(1)} %project_kv.1.refs_0_), channel_id=1, source_target_pairs={{0,4},{1,5},{2,6},{3,7},{4,0},{5,1},{6,2},{7,3},{8,12},{9,13},{10,... | collective-permute-start | bytes 786440 | tf_op jit(solution)/shard_map/ppermute | solution.py:271
  63.9 10.7 %collective-permute-start.22 = (bf16[256,512]{1,0:T(8,128)(2,1)S(1)}, bf16[256,512]{1,0:T(8,128)(2,1)S(1)}, u32[]{:S(2)}, u32[]{:S(2)}) collective-permute-start(bf16[256,512]{1,0:T(8,128)(2,1)S(1)} %collective-permute-done.14.refs_4_), channel_id=1, source_target_pairs={{0,8},{8,0},{16,24},{24,16},{1,9},{9,1},{17,25},{25,17},{2,10},{10... | collective-permute-start | bytes 786440 | tf_op jit(solution)/shard_map/ppermute | solution.py:268
  65.4 9.2 %collective-permute-start.23 = (bf16[256,512]{1,0:T(8,128)(2,1)S(1)}, bf16[256,512]{1,0:T(8,128)(2,1)S(1)}, u32[]{:S(2)}, u32[]{:S(2)}) collective-permute-start(bf16[256,512]{1,0:T(8,128)(2,1)S(1)} %collective-permute-done.20.refs_3_), channel_id=1, source_target_pairs={{0,16},{8,24},{16,0},{24,8},{1,17},{9,25},{17,1},{25,9},{2,18},{10... | collective-permute-start | bytes 786440 | tf_op jit(solution)/shard_map/ppermute | solution.py:268
  65.9 10.9 %collective-permute-start.18 = (bf16[512,256]{1,0:T(8,128)(2,1)S(1)}, bf16[512,256]{1,0:T(8,128)(2,1)S(1)}, u32[]{:S(2)}, u32[]{:S(2)}) collective-permute-start(bf16[512,256]{1,0:T(8,128)(2,1)S(1)} %project_kv.1.refs_0_), channel_id=1, source_target_pairs={{0,1},{1,0},{2,3},{3,2},{4,5},{5,4},{6,7},{7,6},{8,9},{9,8},{10,11... | collective-permute-start | bytes 786440 | tf_op jit(solution)/shard_map/ppermute | solution.py:265
  74.6 2.3 %collective-permute-start.19 = (bf16[512,256]{1,0:T(8,128)(2,1)S(1)}, bf16[512,256]{1,0:T(8,128)(2,1)S(1)}, u32[]{:S(2)}, u32[]{:S(2)}) collective-permute-start(bf16[512,256]{1,0:T(8,128)(2,1)S(1)} %collective-permute-done.17.refs_1_), channel_id=1, source_target_pairs={{0,1},{1,0},{2,3},{3,2},{4,5},{5,4},{6,7},{7,6},{8,9},{9,8},{10,11... | collective-permute-start | bytes 786440 | tf_op jit(solution)/shard_map/ppermute | solution.py:265
  76.2 1.7 %collective-permute-start.24 = (bf16[256,512]{1,0:T(8,128)(2,1)S(1)}, bf16[256,512]{1,0:T(8,128)(2,1)S(1)}, u32[]{:S(2)}, u32[]{:S(2)}) collective-permute-start(bf16[256,512]{1,0:T(8,128)(2,1)S(1)} %get-tuple-element.75), channel_id=1, source_target_pairs={{0,1},{1,0},{2,3},{3,2},{4,5},{5,4},{6,7},{7,6},{8,9},{9,8},{10,11... | collective-permute-start | bytes 786440 | tf_op jit(solution)/shard_map/ppermute | solution.py:265
  77.6 9.2 %collective-permute-start.26 = (bf16[4,64,512]{2,1,0:T(8,128)(2,1)S(1)}, bf16[4,64,512]{2,1,0:T(8,128)(2,1)S(1)}, u32[]{:S(2)}, u32[]{:S(2)}) collective-permute-start(bf16[4,64,512]{2,1,0:T(8,128)(2,1)S(1)} %get-tuple-element.77), channel_id=1, source_target_pairs={{0,2},{1,3},{2,0},{3,1},{4,6},{5,7},{6,4},{7,5},{8,10},{9,11},{10,... | collective-permute-start | bytes 786440 | tf_op jit(solution)/shard_map/ppermute | solution.py:265
  80.0 11.6 %collective-permute-start.25 = (bf16[128,1024]{1,0:T(8,128)(2,1)S(1)}, bf16[128,1024]{1,0:T(8,128)(2,1)S(1)}, u32[]{:S(2)}, u32[]{:S(2)}) collective-permute-start(bf16[128,1024]{1,0:T(8,128)(2,1)S(1)} %attend.3), channel_id=1, source_target_pairs={{0,2},{1,3},{2,0},{3,1},{4,6},{5,7},{6,4},{7,5},{8,10},{9,11},{10,... | collective-permute-start | bytes 786440 | tf_op jit(solution)/shard_map/ppermute | solution.py:265
  (7 other events, 5.1 us)

commit v7 on v6

--- a/solution.py
+++ b/solution.py
@@ -50,9 +50,12 @@
     return pl.multiple_of(H * HD + core * KVH * HD + pair * HD, HD)
 
 
-def pack_kernel(w_hbm, ids_hbm, *refs):
-    outs, (w_ref, ids_ref, sems) = refs[:TEAM], refs[TEAM:]
-    run([pltpu.make_async_copy(w_hbm, w_ref, sems.at[0]), pltpu.make_async_copy(ids_hbm, ids_ref, sems.at[1])])
+def pack_kernel(w_hbm, ids_hbm, tokens_hbm, *refs):
+    outs, (w_ref, ids_ref, tokens_ref, sems) = refs[:TEAM], refs[TEAM:]
+    run([
+        pltpu.make_async_copy(source, there, sems.at[n])
+        for n, (source, there) in enumerate(((w_hbm, w_ref), (ids_hbm, ids_ref), (tokens_hbm, tokens_ref)))
+    ])
     _, pair, core = place()
     member = pair * 2 + core
     rows = w_ref.shape[0]
@@ -62,20 +65,25 @@
     for j in range(per_device):
         ids = jnp.where(lane == j, ids_ref[0, j], ids)
     ids = ids.astype(jnp.float32).astype(jnp.bfloat16)
+    blocks = 3 * HD // LANES
     for k in range(TEAM):
         to_pair, to_core = pair ^ (k // 2), core ^ (k % 2)
-        for n in range(3 * HD // LANES):
+        for n in range(blocks):
             if n < HD // LANES:
                 start = pl.multiple_of(kv_start(to_pair, to_core) + n * LANES, LANES)
             else:
                 start = pl.multiple_of(q_start(to_pair, to_core) + n * LANES - HD, LANES)
             outs[k][n * rows : (n + 1) * rows, :] = w_ref[:, pl.ds(start, LANES)]
-        outs[k][3 * HD // LANES * rows :, :] = ids
+        outs[k][blocks * rows : blocks * rows + ID_ROWS, :] = ids
+    token_rows = tokens_ref.shape[0]
+    for n in range(tokens_ref.shape[1] // LANES):
+        first = blocks * rows + ID_ROWS + n * token_rows
+        outs[1][first : first + token_rows, :] = tokens_ref[:, n * LANES : (n + 1) * LANES]
 
 
 def team_kernel(*refs):
     _, pair, core = place()
-    parts, (kv_out, q_out, *q_halves) = refs[:TEAM], refs[TEAM:]
+    parts, (kv_out, q_out, whole) = refs[:TEAM], refs[TEAM:]
     rows = q_out.shape[0] // TEAM
     member = pair * 2 + core
     for k in range(TEAM):
@@ -85,28 +93,23 @@
             first = n * LANES if n < HD // LANES else n * LANES - HD
             part = parts[k][n * rows : (n + 1) * rows, :]
             out[here, first : first + LANES] = part
-            if out is q_out:
-                q_halves[first // HD][here, first % HD : first % HD + LANES] = part
-    below = [part[3 * HD // LANES * rows :, :].astype(jnp.float32) for part in parts]
+            whole[here, n * LANES : (n + 1) * LANES] = part
+    first = 3 * HD // LANES * rows
+    below = [part[first : first + ID_ROWS, :].astype(jnp.float32) for part in parts]
     ids = sum(below[1:], below[0]).astype(jnp.bfloat16)
     kv_out[TEAM * rows :, :] = jnp.concatenate([ids] * (HD // LANES), 1)
 
 
-def join_kernel(*refs):
-    out = refs[-1]
-    for n, ref in enumerate(refs[:-1]):
-        width = ref.shape[1]
-        out[:, n * width : (n + 1) * width] = ref[...]
-
-
-def stack_kernel(*refs):
+def stack_kernel(first_row, own, near, far, far_near, out):
     _, pair, core = place()
-    tokens, out, sems = refs[:TEAM], refs[TEAM], refs[TEAM + 1]
-    rows = tokens[0].shape[0]
+    rows = own.shape[0]
     member = pair * 2 + core
-    run([
-        pltpu.make_async_copy(tokens[k], out.at[aligned(member ^ k, rows), :], sems.at[k]) for k in range(TEAM)
-    ])
+    for k, ref in ((0, own), (2, far), (3, far_near)):
+        out[aligned(member ^ k, rows), :] = ref[...]
+    here = aligned(member ^ 1, rows)
+    for n in range(out.shape[1] // LANES):
+        first = first_row + n * rows
+        out[here, n * LANES : (n + 1) * LANES] = near[first : first + rows, :]
 
 
 def project_kernel(n_out, depth, is_kv, x_ref, *refs):
@@ -118,6 +121,7 @@
     _, pair, core = place()
     member = pair * 2 + core
     rows = x_ref.shape[0] // TEAM
+    width = outs[0].shape[1]
     direct = depth % LANES == 0
     places = []
     for i, piece in enumerate(weights):
@@ -125,7 +129,8 @@
         tall = piece.shape[0] // (n_out - 1 if i % 2 else 1)
         for n in range(n_out - 1 if i % 2 else 1):
             from_outer = lax.rem(outer + n_out - n - i % 2, n_out)
-            places.append((piece.at[pl.ds(n * tall, depth), :], aligned(from_req * n_out + from_outer, depth)))
+            cols = slice(None) if piece.shape[1] == width else slice(*((0, HD) if is_kv else (HD, 3 * HD)))
+            places.append((piece.at[pl.ds(n * tall, depth), cols], aligned(from_req * n_out + from_outer, depth)))
     if not direct:
         run([
             pltpu.make_async_copy(piece, w_all.at[there, :], sems.at[n]) for n, (piece, there) in enumerate(places)
@@ -277,53 +282,61 @@
     per_device = block_ids.shape[1]
     own = tokens[0]
     rows = own.shape[0]
+    packed_rows = 3 * HD // LANES * w_rows + ID_ROWS
     parts = pl.pallas_call(
         pack_kernel,
-        out_shape=[shape((3 * HD // LANES * w_rows + ID_ROWS, LANES), bf16)] * TEAM,
-        in_specs=[ANY] * 2,
+        out_shape=[
+            shape((packed_rows + (own.size // LANES if k == 1 else 0), LANES), bf16) for k in range(TEAM)
+        ],
+        in_specs=[pl.BlockSpec(memory_space=pltpu.HBM)] * 3,
         out_specs=[VMEM] * TEAM,
         scratch_shapes=[
             pltpu.VMEM(qkv_weight.shape, bf16),
             pltpu.SMEM(block_ids.shape, jnp.int32),
-            pltpu.SemaphoreType.DMA((2,)),
+            pltpu.VMEM(own.shape, bf16),
+            pltpu.SemaphoreType.DMA((3,)),
         ],
         compiler_params=params(4),
         name="pack",
-    )(qkv_weight, block_ids)
-    head_rows = shape((TEAM * w_rows, HD), bf16)
-    kv, q, qa, qb = pl.pallas_call(
+    )(qkv_weight, block_ids, own)
+    got = [parts[0]] + [in_team(parts[k], k) for k in range(1, TEAM)]
+    kv, q, w = pl.pallas_call(
         team_kernel,
-        out_shape=[shape((TEAM * w_rows + ID_ROWS, HD), bf16), shape((TEAM * w_rows, 2 * HD), bf16), head_rows, head_rows],
+        out_shape=[
+            shape((TEAM * w_rows + ID_ROWS, HD), bf16),
+            shape((TEAM * w_rows, 2 * HD), bf16),
+            shape((TEAM * w_rows, 3 * HD), bf16),
+        ],
         in_specs=[VMEM] * TEAM,
-        out_specs=[VMEM] * 4,
+        out_specs=[VMEM] * 3,
         compiler_params=params(2),
         name="team",
-    )(parts[0], *[in_team(parts[k], k) for k in range(1, TEAM)])
+    )(*got)
 
     def from_others(piece):
         got = [across(piece, k) for k in range(1, n_out)]
         return got[0] if len(got) == 1 else jnp.concatenate(got, 0)
 
-    kv, q, own = sync(kv, q, own)
-    kv_o, kv_x, kv_y = from_others(kv), in_req(kv, 1), in_req(kv, 2)
-    far, own_near = in_team(own, 2), in_team(own, 1)
-    kv_x, kv_y, q, own_near = sync(kv_x, kv_y, q, own_near)
-    kv_d, q_x = in_req(kv_x, 2), in_req(q, 1)
-    kv_o, kv_d, qa = sync(kv_o, kv_d, qa)
-    qa_o, kv_ox, kv_oy = from_others(qa), in_req(kv_o, 1), in_req(kv_o, 2)
-    kv_ox, kv_oy, q_x, q, qa_o, qb, far = sync(kv_ox, kv_oy, q_x, q, qa_o, qb, far)
-    kv_od, q_y, qb_o, far_near = in_req(kv_oy, 1), in_req(q, 2), from_others(qb), in_team(far, 1)
-    kv_od, q_y, qb_o, far_near = sync(kv_od, q_y, qb_o, far_near)
-    kv_weight = [kv, kv_o, kv_x, kv_ox, kv_y, kv_oy, kv_d, kv_od]
+    kv, q, w, own = sync(kv, q, w, own)
+    kv_o, w_x, w_y = from_others(kv), in_req(w, 1), in_req(w, 2)
+    q_o, far = from_others(q), in_team(own, 2)
+    kv_o, w_x, w_y = sync(kv_o, w_x, w_y)
+    kv_ox, kv_oy, w_d = in_req(kv_o, 1), in_req(kv_o, 2), in_req(w_x, 2)
+    kv_ox, kv_oy = sync(kv_ox, kv_oy)
+    kv_od = in_req(kv_oy, 1)
+    kv_od, w_d, q_o, far = sync(kv_od, w_d, q_o, far)
+    far_near = in_team(far, 1)
+    q_o, far_near = sync(q_o, far_near)
+    q_ox, q_oy = in_req(q_o, 1), in_req(q_o, 2)
+    kv_weight = [w, kv_o, w_x, kv_ox, w_y, kv_oy, w_d, kv_od]
     stacked = pl.pallas_call(
-        stack_kernel,
+        functools.partial(stack_kernel, packed_rows),
         out_shape=shape((TEAM * rows, own.shape[1]), bf16),
-        in_specs=[ANY] * TEAM,
+        in_specs=[VMEM] * TEAM,
         out_specs=VMEM,
-        scratch_shapes=[pltpu.SemaphoreType.DMA((TEAM,))],
-        compiler_params=params(4),
+        compiler_params=params(2),
         name="stack",
-    )(own, own_near, far, far_near)
+    )(own, got[1], far, far_near)
 
     blk_rows = rows // per_device
     tall = kv.shape[0]
@@ -338,7 +351,7 @@
     cosine, sine = jnp.cos(angles), jnp.sin(angles)
 
     def project(weight, is_kv, gain):
-        width = weight[0].shape[1]
+        width = weight[1].shape[1]
         depth = own.shape[1]
         n_outs = 1 if is_kv else 2
         return pl.pallas_call(
@@ -353,23 +366,14 @@
             cost_estimate=pl.CostEstimate(
                 flops=2 * TEAM * rows * depth * width, bytes_accessed=6 * MIB, transcendentals=0
             ),
-            compiler_params=params(12),
+            compiler_params=params(4 if w_rows * TEAM % LANES == 0 else 12),
             name="project_kv" if is_kv else "project_q",
         )(stacked, *weight, gain[None, :], cosine, sine)
 
     (made,) = project(kv_weight, True, k_gain)
-    q_o = pl.pallas_call(
-        join_kernel,
-        out_shape=shape((qa_o.shape[0], 2 * HD), bf16),
-        in_specs=[VMEM] * 2,
-        out_specs=VMEM,
-        compiler_params=params(2 + 2 * n_out // 8),
-        name="join",
-    )(qa_o, qb_o)
-    q_ox, q_oy = in_req(q_o, 1), in_req(q_o, 2)
-    q_ox, q_oy, q_y = sync(q_ox, q_oy, q_y)
-    q_d, q_od = in_req(q_y, 1), in_req(q_ox, 2)
-    q_weight = [q, q_o, q_x, q_ox, q_y, q_oy, q_d, q_od]
+    q_ox, q_oy = sync(q_ox, q_oy)
+    q_od = in_req(q_oy, 1)
+    q_weight = [w, q_o, w_x, q_ox, w_y, q_oy, w_d, q_od]
     mine = [made] + [across(made, k) for k in range(1, n_out)]
     other = [in_team(part, 1) for part in mine]
 
@@ -397,7 +401,7 @@
         in_specs=[VMEM] * (2 * n_out) + [SMEM] * 2,
         out_specs=[VMEM] * 3,
         cost_estimate=pl.CostEstimate(flops=0, bytes_accessed=4 * MIB, transcendentals=0),
-        compiler_params=params(2 * store_mib + 4),
+        compiler_params=params(store_mib + 1),
         name="pages",
     )(*mine, *other, all_ids, info)
     got_pages = in_team(away_pages, 2)
@@ -411,7 +415,7 @@
             cost_estimate=pl.CostEstimate(
                 flops=2 * H * HD * rows * total, bytes_accessed=4 * MIB, transcendentals=0
             ),
-            compiler_params=params(store_mib + 4 + 4 * total // 1024),
+            compiler_params=params(store_mib + 2 + 3 * total // 1024),
             name="attend",
         )(store, queries, from_near, all_ids, lengths)
 

time: 93.3 us -> 87.4 us (0.937)
  starting transfers between devices: 27.8 us -> 23.2 us
  waiting for transfers between devices: 43.6 us -> 41.2 us
  other arithmetic: 1.36 us -> 3.41 us
  local copies, waits for them, and re-layouts: 6.87 us -> 4.99 us
  Pallas kernels: 11.8 us -> 12.8 us
    ppermute x4 -> x3, waiting for transfers between devices: 27.9 us -> 23.9 us  [across(): lax.ppermute(array, 'blk', [(i, (i + TEAM * k) % n_blk) for i in range(n_...]
    ppermute x4 -> x3, starting transfers between devices: 8.1 us -> 5.14 us  [across(): lax.ppermute(array, 'blk', [(i, (i + TEAM * k) % n_blk) for i in range(n_...]
    unnamed x24 -> x18, local copies, waits for them, and re-layouts: 5.95 us -> 4.07 us
    ppermute x12 -> x9, starting transfers between devices: 12.3 us -> 10.5 us  [in_req(): return lax.ppermute(array, 'req', [(i, i ^ k) for i in range(n_req)])]
    ppermute x11 -> x10, waiting for transfers between devices: 13.3 us -> 14.2 us  [in_team(): return lax.ppermute(array, 'blk', [(i, i ^ k) for i in range(n_blk)])]
    ppermute x12 -> x9, waiting for transfers between devices: 2.37 us -> 3 us  [in_req(): return lax.ppermute(array, 'req', [(i, i ^ k) for i in range(n_req)])]
    pallas_call x3 -> x2, Pallas kernels: 1.99 us -> 2.24 us  [the longest x1 1.31 us: body(): pl.pallas_call(functools.partial(stack_kernel, packed_rows), out_shape=sh...]
    ppermute x11 -> x10, starting transfers between devices: 7.46 us -> 7.59 us  [in_team(): return lax.ppermute(array, 'blk', [(i, i ^ k) for i in range(n_blk)])]
  transfers between devices with their start and end apart: 27 -> 22, of which waited for: 11 -> 11; matrix products, arithmetic and copies ran while one was open for 2% -> 5% of each run, Pallas kernels for 9% -> 11%
where the time goes in v7:
time: 87.4 us; the launch traced here: 87 us
  waiting for transfers between devices  41.2 us (47%)
  starting transfers between devices  23.2 us (27%)
  Pallas kernels  12.8 us (15%)
  local copies, waits for them, and re-layouts  4.99 us (6%)
  other arithmetic  3.41 us (4%)
  between operations  1.48 us (2%)
    ppermute x3, waiting for transfers between devices, across(): lax.ppermute(array, 'blk', [(i, (i + TEAM * k) % n_blk) for i in range(n_...  23.9 us
    ppermute x10, waiting for transfers between devices, in_team(): return lax.ppermute(array, 'blk', [(i, i ^ k) for i in range(n_blk)])  14.2 us
    ppermute x9, starting transfers between devices, in_req(): return lax.ppermute(array, 'req', [(i, i ^ k) for i in range(n_req)])  10.5 us
    ppermute x10, starting transfers between devices, in_team(): return lax.ppermute(array, 'blk', [(i, i ^ k) for i in range(n_blk)])  7.59 us
    ppermute x3, starting transfers between devices, across(): lax.ppermute(array, 'blk', [(i, (i + TEAM * k) % n_blk) for i in range(n_...  5.14 us
    unnamed x18, local copies, waits for them, and re-layouts  4.07 us
    pallas_call x2, Pallas kernels, attend(): pl.pallas_call(functools.partial(attend_kernel, blk_rows, step), out_shap...  4.01 us
    pallas_call x2, Pallas kernels, project(): pl.pallas_call(functools.partial(project_kernel, n_out, TEAM * w_rows, is...  3.55 us
  transfers between devices with their start and end apart: 22, of which 11 were waited for; matrix products, arithmetic and copies ran while one was open for 5% of the time, Pallas kernels for 11%

profile of v7, /device:TPU:0, one launch (start us, length us, event | category | flops | bytes accessed | tf_op | source)
XLA Modules:
  0.0 87.0 jit_solution(12761467604014476697)
XLA Ops:
  0.6 1.0 %copy-done = bf16[1,128,2048]{2,1,0:T(8,128)(2,1)S(1)} copy-done((bf16[1,128,2048]{2,1,0:T(8,128)(2,1)S(1)}, bf16[1,128,2048]{2,1,0:T(8,128)(2,1)}, u32[]{:S(2)}) %copy-start) | copy-done | bytes 524312
  1.7 1.0 %copy-done.2 = bf16[64,3072]{1,0:T(8,128)(2,1)S(1)} copy-done((bf16[64,3072]{1,0:T(8,128)(2,1)S(1)}, bf16[64,3072]{1,0:T(8,128)(2,1)}, u32[]{:S(2)}) %copy-start.2) | copy-done | bytes 393240
  3.3 0.9 %pack.1 = (bf16[400,128]{1,0:T(8,128)(2,1)S(1)}, bf16[2448,128]{1,0:T(8,128)(2,1)S(1)}, bf16[400,128]{1,0:T(8,128)(2,1)S(1)}, bf16[400,128]{1,0:T(8,128)(2,1)S(1)}) custom-call(bf16[64,3072]{1,0:T(8,128)(2,1)S(1)} %copy-done.2, s32[1,2]{1,0:T(1,128)S(1)} %copy-done.7, bf16[128,2048]{1,0:T(8,128)(2,1)S(1)} %bitcast.33), custom_call_target="tpu_custom_call" | custom-call | tf_op jit(solution)/shard_map/pack/pallas_call | solution.py:286
  4.8 2.6 %collective-permute-start.1 = (bf16[400,128]{1,0:T(8,128)(2,1)S(1)}, bf16[400,128]{1,0:T(8,128)(2,1)S(1)}, u32[]{:S(2)}, u32[]{:S(2)}) collective-permute-start(bf16[400,128]{1,0:T(8,128)(2,1)S(1)} %get-tuple-element.35), channel_id=1, source_target_pairs={{0,2},{1,3},{2,0},{3,1},{4,6},{5,7},{6,4},{7,5},{8,10},{9,11},{10,... | collective-permute-start | bytes 307208 | tf_op jit(solution)/shard_map/ppermute | solution.py:270
  7.5 3.7 %collective-permute-done.1.refs_2_ = bf16[400,128]{1,0:T(8,128)(2,1)S(1)} collective-permute-done((bf16[400,128]{1,0:T(8,128)(2,1)S(1)}, bf16[400,128]{1,0:T(8,128)(2,1)S(1)}, u32[]{:S(2)}, u32[]{:S(2)}) %collective-permute-start.1) | collective-permute-done | bytes 102432 | tf_op jit(solution)/shard_map/ppermute | solution.py:270
  11.2 1.7 %collective-permute-done.2.refs_3_ = bf16[400,128]{1,0:T(8,128)(2,1)S(1)} collective-permute-done((bf16[400,128]{1,0:T(8,128)(2,1)S(1)}, bf16[400,128]{1,0:T(8,128)(2,1)S(1)}, u32[]{:S(2)}, u32[]{:S(2)}) %collective-permute-start.2) | collective-permute-done | bytes 102432 | tf_op jit(solution)/shard_map/ppermute | solution.py:270
  12.8 0.8 team.1
  14.3 1.5 %collective-permute-start.4 = (bf16[256,768]{1,0:T(8,128)(2,1)S(1)}, bf16[256,768]{1,0:T(8,128)(2,1)S(1)}, u32[]{:S(2)}, u32[]{:S(2)}) collective-permute-start(bf16[256,768]{1,0:T(8,128)(2,1)S(1)} %get-tuple-element.42.refs_0_), channel_id=1, source_target_pairs={{0,8},{8,0},{16,24},{24,16},{1,9},{9,1},{17,25},{25,17},{2,10},{10... | collective-permute-start | bytes 1179656 | tf_op jit(solution)/shard_map/ppermute | solution.py:273
  15.8 1.5 %collective-permute-start.5 = (bf16[256,768]{1,0:T(8,128)(2,1)S(1)}, bf16[256,768]{1,0:T(8,128)(2,1)S(1)}, u32[]{:S(2)}, u32[]{:S(2)}) collective-permute-start(bf16[256,768]{1,0:T(8,128)(2,1)S(1)} %get-tuple-element.42.refs_0_), channel_id=1, source_target_pairs={{0,16},{8,24},{16,0},{24,8},{1,17},{9,25},{17,1},{25,9},{2,18},{10... | collective-permute-start | bytes 1179656 | tf_op jit(solution)/shard_map/ppermute | solution.py:273
  17.3 2.6 %collective-permute-start.3 = (bf16[272,256]{1,0:T(8,128)(2,1)}, bf16[272,256]{1,0:T(8,128)(2,1)}, u32[]{:S(2)}, u32[]{:S(2)}) collective-permute-start(bf16[272,256]{1,0:T(8,128)(2,1)} %get-tuple-element.41), channel_id=1, source_target_pairs={{0,4},{1,5},{2,6},{3,7},{4,0},{5,1},{6,2},{7,3},{8,12},{9,13},{10,... | collective-permute-start | bytes 417800 | tf_op jit(solution)/shard_map/ppermute | solution.py:276
  19.9 1.6 %collective-permute-start.11 = (bf16[128,2048]{1,0:T(8,128)(2,1)}, bf16[128,2048]{1,0:T(8,128)(2,1)S(1)}, u32[]{:S(2)}, u32[]{:S(2)}) collective-permute-start(bf16[128,2048]{1,0:T(8,128)(2,1)} %bitcast.32), channel_id=1, source_target_pairs={{0,2},{1,3},{2,0},{3,1},{4,6},{5,7},{6,4},{7,5},{8,10},{9,11},{10,... | collective-permute-start | bytes 1572872 | tf_op jit(solution)/shard_map/ppermute | solution.py:270
  21.5 5.4 %collective-permute-done.3.refs_1_ = bf16[272,256]{1,0:T(8,128)(2,1)} collective-permute-done((bf16[272,256]{1,0:T(8,128)(2,1)}, bf16[272,256]{1,0:T(8,128)(2,1)}, u32[]{:S(2)}, u32[]{:S(2)}) %collective-permute-start.3) | collective-permute-done | bytes 139296 | tf_op jit(solution)/shard_map/ppermute | solution.py:276
  27.5 1.4 %collective-permute-start.7 = (bf16[272,256]{1,0:T(8,128)(2,1)}, bf16[272,256]{1,0:T(8,128)(2,1)}, u32[]{:S(2)}, u32[]{:S(2)}) collective-permute-start(bf16[272,256]{1,0:T(8,128)(2,1)} %collective-permute-done.3.refs_1_), channel_id=1, source_target_pairs={{0,16},{8,24},{16,0},{24,8},{1,17},{9,25},{17,1},{25,9},{2,18},{10... | collective-permute-start | bytes 417800 | tf_op jit(solution)/shard_map/ppermute | solution.py:273
  30.3 2.5 %collective-permute-start.10 = (bf16[256,512]{1,0:T(8,128)(2,1)}, bf16[256,512]{1,0:T(8,128)(2,1)S(1)}, u32[]{:S(2)}, u32[]{:S(2)}) collective-permute-start(bf16[256,512]{1,0:T(8,128)(2,1)} %copy-done.8), channel_id=1, source_target_pairs={{0,4},{1,5},{2,6},{3,7},{4,0},{5,1},{6,2},{7,3},{8,12},{9,13},{10,... | collective-permute-start | bytes 786440 | tf_op jit(solution)/shard_map/ppermute | solution.py:276
  34.4 1.5 %collective-permute-start.8 = (bf16[272,256]{1,0:T(8,128)(2,1)}, bf16[272,256]{1,0:T(8,128)(2,1)S(1)}, u32[]{:S(2)}, u32[]{:S(2)}) collective-permute-start(bf16[272,256]{1,0:T(8,128)(2,1)} %collective-permute-done.7.refs_5_), channel_id=1, source_target_pairs={{0,8},{8,0},{16,24},{24,16},{1,9},{9,1},{17,25},{25,17},{2,10},{10... | collective-permute-start | bytes 417800 | tf_op jit(solution)/shard_map/ppermute | solution.py:273
  35.9 7.8 %collective-permute-done.10.refs_1_ = bf16[256,512]{1,0:T(8,128)(2,1)S(1)} collective-permute-done((bf16[256,512]{1,0:T(8,128)(2,1)}, bf16[256,512]{1,0:T(8,128)(2,1)S(1)}, u32[]{:S(2)}, u32[]{:S(2)}) %collective-permute-start.10) | collective-permute-done | bytes 262176 | tf_op jit(solution)/shard_map/ppermute | solution.py:276
  45.2 1.2 %collective-permute-done.12.far_near = bf16[128,2048]{1,0:T(8,128)(2,1)} collective-permute-done((bf16[128,2048]{1,0:T(8,128)(2,1)S(1)}, bf16[128,2048]{1,0:T(8,128)(2,1)}, u32[]{:S(2)}, u32[]{:S(2)}) %collective-permute-start.12) | collective-permute-done | bytes 524320 | tf_op jit(solution)/shard_map/ppermute | solution.py:270
  46.4 1.4 %collective-permute-start.16 = (bf16[256,512]{1,0:T(8,128)(2,1)S(1)}, bf16[256,512]{1,0:T(8,128)(2,1)S(1)}, u32[]{:S(2)}, u32[]{:S(2)}) collective-permute-start(bf16[256,512]{1,0:T(8,128)(2,1)S(1)} %collective-permute-done.10.refs_1_), channel_id=1, source_target_pairs={{0,8},{8,0},{16,24},{24,16},{1,9},{9,1},{17,25},{25,17},{2,10},{10... | collective-permute-start | bytes 786440 | tf_op jit(solution)/shard_map/ppermute | solution.py:273
  47.8 1.4 %collective-permute-start.17 = (bf16[256,512]{1,0:T(8,128)(2,1)S(1)}, bf16[256,512]{1,0:T(8,128)(2,1)S(1)}, u32[]{:S(2)}, u32[]{:S(2)}) collective-permute-start(bf16[256,512]{1,0:T(8,128)(2,1)S(1)} %collective-permute-done.10.refs_1_), channel_id=1, source_target_pairs={{0,16},{8,24},{16,0},{24,8},{1,17},{9,25},{17,1},{25,9},{2,18},{10... | collective-permute-start | bytes 786440 | tf_op jit(solution)/shard_map/ppermute | solution.py:273
  49.2 1.0 %multiply_sine_fusion = (f32[512,128]{1,0:T(8,128)S(1)}, f32[512,128]{1,0:T(8,128)S(1)}) fusion(f32[128]{0:T(128)S(1)} %multiply_power_fusion, f32[512]{0:T(512)S(1)} %convert_element_type.37), kind=kLoop, calls=%fused_computation | loop fusion | flops 65536 | bytes 526848 | tf_op jit(solution)/shard_map/sin | solution.py:351
  50.3 1.3 %stack.8.x_ref = bf16[512,2048]{1,0:T(8,128)(2,1)S(1)} custom-call(bf16[128,2048]{1,0:T(8,128)(2,1)S(1)} %bitcast.34, bf16[2448,128]{1,0:T(8,128)(2,1)S(1)} %collective-permute-done.refs_1_.near, bf16[128,2048]{1,0:T(8,128)(2,1)S(1)} %collective-permute-done.11.far, bf16[128,2048]{1,0:T(8,128)(2,1)} %collective-permute-done.12.far_near), custom_call_target="tpu_custom_call" | custom-call | tf_op jit(solution)/shard_map/stack/pallas_call | solution.py:332
  51.6 1.9 %project_kv.1.refs_0_ = bf16[512,256]{1,0:T(8,128)(2,1)S(1)} custom-call(bf16[512,2048]{1,0:T(8,128)(2,1)S(1)} %stack.8.x_ref, bf16[256,768]{1,0:T(8,128)(2,1)S(1)} %get-tuple-element.42.refs_0_, bf16[272,256]{1,0:T(8,128)(2,1)} %collective-permute-done.3.refs_1_, bf16[256,768]{1,0:T(8,128)(2,1)S(1)} %collective-permute-done.4.refs_2_, ...), custom_call_target="tpu_custom_call" | custom-call | flops 536870912 | bytes 6291456 | tf_op jit(solution)/shard_map/project_kv/pallas_call | solution.py:357
  53.6 1.1 %collective-permute-done.16.refs_3_ = bf16[256,512]{1,0:T(8,128)(2,1)S(1)} collective-permute-done((bf16[256,512]{1,0:T(8,128)(2,1)S(1)}, bf16[256,512]{1,0:T(8,128)(2,1)S(1)}, u32[]{:S(2)}, u32[]{:S(2)}) %collective-permute-start.16) | collective-permute-done | bytes 262176 | tf_op jit(solution)/shard_map/ppermute | solution.py:273
  54.7 1.1 %collective-permute-done.17.refs_5_ = bf16[256,512]{1,0:T(8,128)(2,1)S(1)} collective-permute-done((bf16[256,512]{1,0:T(8,128)(2,1)S(1)}, bf16[256,512]{1,0:T(8,128)(2,1)S(1)}, u32[]{:S(2)}, u32[]{:S(2)}) %collective-permute-start.17) | collective-permute-done | bytes 262176 | tf_op jit(solution)/shard_map/ppermute | solution.py:273
  57.2 10.7 %collective-permute-done.13.refs_1_ = bf16[512,256]{1,0:T(8,128)(2,1)S(1)} collective-permute-done((bf16[512,256]{1,0:T(8,128)(2,1)S(1)}, bf16[512,256]{1,0:T(8,128)(2,1)S(1)}, u32[]{:S(2)}, u32[]{:S(2)}) %collective-permute-start.13) | collective-permute-done | bytes 262176 | tf_op jit(solution)/shard_map/ppermute | solution.py:276
  67.9 1.6 %project_q.1 = (bf16[256,512]{1,0:T(8,128)(2,1)S(1)}, bf16[256,512]{1,0:T(8,128)(2,1)S(1)}) custom-call(bf16[512,2048]{1,0:T(8,128)(2,1)S(1)} %stack.8.x_ref, bf16[256,768]{1,0:T(8,128)(2,1)S(1)} %get-tuple-element.42.refs_0_, bf16[256,512]{1,0:T(8,128)(2,1)S(1)} %collective-permute-done.10.refs_1_, bf16[256,768]{1,0:T(8,128)(2,1)S(1)} %collective-permute-done.4.refs_2_, ...), custom_call_target="tpu_custom_call" | custom-call | flops 1073741824 | bytes 6291456 | tf_op jit(solution)/shard_map/project_q/pallas_call | solution.py:357
  71.7 2.0 %attend.3 = bf16[128,1024]{1,0:T(8,128)(2,1)S(1)} custom-call(bf16[2,1024,256]{2,1,0:T(8,128)(2,1)S(1)} %get-tuple-element.54.store, bf16[256,512]{1,0:T(8,128)(2,1)S(1)} %get-tuple-element.58.q_ref, bf16[256,512]{1,0:T(8,128)(2,1)S(1)} %collective-permute-done.19.near_ref, s32[16]{0:T(128)S(1)} %reshape.141.refs_4_.ids_ref, s32[1]{0:T(128)} %copy.9.length_ref), custom_call_target="tpu_custom_call" | custom-call | flops 536870912 | bytes 4194304 | tf_op jit(solution)/shard_map/attend/pallas_call | solution.py:410
  73.7 2.1 %collective-permute-start.20 = (bf16[128,1024]{1,0:T(8,128)(2,1)S(1)}, bf16[128,1024]{1,0:T(8,128)(2,1)S(1)}, u32[]{:S(2)}, u32[]{:S(2)}) collective-permute-start(bf16[128,1024]{1,0:T(8,128)(2,1)S(1)} %attend.3), channel_id=1, source_target_pairs={{0,2},{1,3},{2,0},{3,1},{4,6},{5,7},{6,4},{7,5},{8,10},{9,11},{10,... | collective-permute-start | bytes 786440 | tf_op jit(solution)/shard_map/ppermute | solution.py:270
  75.8 2.0 %attend.2.kept = bf16[128,1024]{1,0:T(8,128)(2,1)S(1)} custom-call(bf16[2,1024,256]{2,1,0:T(8,128)(2,1)S(1)} %get-tuple-element.54.store, bf16[256,512]{1,0:T(8,128)(2,1)S(1)} %get-tuple-element.58.q_ref, bf16[256,512]{1,0:T(8,128)(2,1)S(1)} %collective-permute-done.19.near_ref, s32[16]{0:T(128)S(1)} %reshape.141.refs_4_.ids_ref, s32[1]{0:T(128)} %copy.9.length_ref), custom_call_target="tpu_custom_call" | custom-call | flops 536870912 | bytes 4194304 | tf_op jit(solution)/shard_map/attend/pallas_call | solution.py:410
  77.9 3.0 %collective-permute-done.21.got_pages = bf16[4,64,512]{2,1,0:T(8,128)(2,1)S(1)} collective-permute-done((bf16[4,64,512]{2,1,0:T(8,128)(2,1)S(1)}, bf16[4,64,512]{2,1,0:T(8,128)(2,1)S(1)}, u32[]{:S(2)}, u32[]{:S(2)}) %collective-permute-start.21) | collective-permute-done | bytes 262176 | tf_op jit(solution)/shard_map/ppermute | solution.py:270
  80.9 4.7 %collective-permute-done.20.from_far = bf16[128,1024]{1,0:T(8,128)(2,1)S(1)} collective-permute-done((bf16[128,1024]{1,0:T(8,128)(2,1)S(1)}, bf16[128,1024]{1,0:T(8,128)(2,1)S(1)}, u32[]{:S(2)}, u32[]{:S(2)}) %collective-permute-start.20) | collective-permute-done | bytes 262176 | tf_op jit(solution)/shard_map/ppermute | solution.py:270
  85.5 1.5 %finish.1 = (bf16[128,2048]{1,0:T(8,128)(2,1)}, bf16[4,64,512]{2,1,0:T(8,128)(2,1)}) custom-call(bf16[128,1024]{1,0:T(8,128)(2,1)S(1)} %attend.2.kept, bf16[128,1024]{1,0:T(8,128)(2,1)S(1)} %collective-permute-done.20.from_far, bf16[4,64,512]{2,1,0:T(8,128)(2,1)S(1)} %get-tuple-element.60.own_pages, ...), custom_call_target="tpu_custom_call" | custom-call | tf_op jit(solution)/shard_map/finish/pallas_call | solution.py:425
  (54 shorter events, 10.0 us)
Async XLA Ops:
  0.6 1.0 %copy-start = (bf16[1,128,2048]{2,1,0:T(8,128)(2,1)S(1)}, bf16[1,128,2048]{2,1,0:T(8,128)(2,1)}, u32[]{:S(2)}) copy-start(bf16[1,128,2048]{2,1,0:T(8,128)(2,1)} %param.7) | copy-start | bytes 1572868
  1.7 1.0 %copy-start.2 = (bf16[64,3072]{1,0:T(8,128)(2,1)S(1)}, bf16[64,3072]{1,0:T(8,128)(2,1)}, u32[]{:S(2)}) copy-start(bf16[64,3072]{1,0:T(8,128)(2,1)} %w_hbm.1) | copy-start | bytes 1179652
  2.7 0.7 copy-start.7
  3.3 46.9 %copy-start.1 = (bf16[1,128,2048]{2,1,0:T(8,128)(2,1)S(1)}, bf16[1,128,2048]{2,1,0:T(8,128)(2,1)}, u32[]{:S(2)}) copy-start(bf16[1,128,2048]{2,1,0:T(8,128)(2,1)} %param.7) | copy-start | bytes 1572868
  4.3 8.6 %collective-permute-start = (bf16[2448,128]{1,0:T(8,128)(2,1)S(1)}, bf16[2448,128]{1,0:T(8,128)(2,1)S(1)}, u32[]{:S(2)}, u32[]{:S(2)}) collective-permute-start(bf16[2448,128]{1,0:T(8,128)(2,1)S(1)} %get-tuple-element.34), channel_id=1, source_target_pairs={{0,1},{1,0},{2,3},{3,2},{4,5},{5,4},{6,7},{7,6},{8,9},{9,8},{10,11... | collective-permute-start | bytes 1880072 | tf_op jit(solution)/shard_map/ppermute | solution.py:270
  4.8 6.4 %collective-permute-start.1 = (bf16[400,128]{1,0:T(8,128)(2,1)S(1)}, bf16[400,128]{1,0:T(8,128)(2,1)S(1)}, u32[]{:S(2)}, u32[]{:S(2)}) collective-permute-start(bf16[400,128]{1,0:T(8,128)(2,1)S(1)} %get-tuple-element.35), channel_id=1, source_target_pairs={{0,2},{1,3},{2,0},{3,1},{4,6},{5,7},{6,4},{7,5},{8,10},{9,11},{10,... | collective-permute-start | bytes 307208 | tf_op jit(solution)/shard_map/ppermute | solution.py:270
  7.4 5.4 %collective-permute-start.2 = (bf16[400,128]{1,0:T(8,128)(2,1)S(1)}, bf16[400,128]{1,0:T(8,128)(2,1)S(1)}, u32[]{:S(2)}, u32[]{:S(2)}) collective-permute-start(bf16[400,128]{1,0:T(8,128)(2,1)S(1)} %get-tuple-element.36), channel_id=1, source_target_pairs={{0,3},{1,2},{2,1},{3,0},{4,7},{5,6},{6,5},{7,4},{8,11},{9,10},{10,... | collective-permute-start | bytes 307208 | tf_op jit(solution)/shard_map/ppermute | solution.py:270
  13.6 0.7 copy-start.8
  14.3 12.6 %collective-permute-start.4 = (bf16[256,768]{1,0:T(8,128)(2,1)S(1)}, bf16[256,768]{1,0:T(8,128)(2,1)S(1)}, u32[]{:S(2)}, u32[]{:S(2)}) collective-permute-start(bf16[256,768]{1,0:T(8,128)(2,1)S(1)} %get-tuple-element.42.refs_0_), channel_id=1, source_target_pairs={{0,8},{8,0},{16,24},{24,16},{1,9},{9,1},{17,25},{25,17},{2,10},{10... | collective-permute-start | bytes 1179656 | tf_op jit(solution)/shard_map/ppermute | solution.py:273
  15.8 11.1 %collective-permute-start.5 = (bf16[256,768]{1,0:T(8,128)(2,1)S(1)}, bf16[256,768]{1,0:T(8,128)(2,1)S(1)}, u32[]{:S(2)}, u32[]{:S(2)}) collective-permute-start(bf16[256,768]{1,0:T(8,128)(2,1)S(1)} %get-tuple-element.42.refs_0_), channel_id=1, source_target_pairs={{0,16},{8,24},{16,0},{24,8},{1,17},{9,25},{17,1},{25,9},{2,18},{10... | collective-permute-start | bytes 1179656 | tf_op jit(solution)/shard_map/ppermute | solution.py:273
  17.3 9.6 %collective-permute-start.3 = (bf16[272,256]{1,0:T(8,128)(2,1)}, bf16[272,256]{1,0:T(8,128)(2,1)}, u32[]{:S(2)}, u32[]{:S(2)}) collective-permute-start(bf16[272,256]{1,0:T(8,128)(2,1)} %get-tuple-element.41), channel_id=1, source_target_pairs={{0,4},{1,5},{2,6},{3,7},{4,0},{5,1},{6,2},{7,3},{8,12},{9,13},{10,... | collective-permute-start | bytes 417800 | tf_op jit(solution)/shard_map/ppermute | solution.py:276
  19.9 23.8 %collective-permute-start.11 = (bf16[128,2048]{1,0:T(8,128)(2,1)}, bf16[128,2048]{1,0:T(8,128)(2,1)S(1)}, u32[]{:S(2)}, u32[]{:S(2)}) collective-permute-start(bf16[128,2048]{1,0:T(8,128)(2,1)} %bitcast.32), channel_id=1, source_target_pairs={{0,2},{1,3},{2,0},{3,1},{4,6},{5,7},{6,4},{7,5},{8,10},{9,11},{10,... | collective-permute-start | bytes 1572872 | tf_op jit(solution)/shard_map/ppermute | solution.py:270
  26.9 6.7 %collective-permute-start.6 = (bf16[272,256]{1,0:T(8,128)(2,1)}, bf16[272,256]{1,0:T(8,128)(2,1)}, u32[]{:S(2)}, u32[]{:S(2)}) collective-permute-start(bf16[272,256]{1,0:T(8,128)(2,1)} %collective-permute-done.3.refs_1_), channel_id=1, source_target_pairs={{0,8},{8,0},{16,24},{24,16},{1,9},{9,1},{17,25},{25,17},{2,10},{10... | collective-permute-start | bytes 417800 | tf_op jit(solution)/shard_map/ppermute | solution.py:273
  27.5 6.9 %collective-permute-start.7 = (bf16[272,256]{1,0:T(8,128)(2,1)}, bf16[272,256]{1,0:T(8,128)(2,1)}, u32[]{:S(2)}, u32[]{:S(2)}) collective-permute-start(bf16[272,256]{1,0:T(8,128)(2,1)} %collective-permute-done.3.refs_1_), channel_id=1, source_target_pairs={{0,16},{8,24},{16,0},{24,8},{1,17},{9,25},{17,1},{25,9},{2,18},{10... | collective-permute-start | bytes 417800 | tf_op jit(solution)/shard_map/ppermute | solution.py:273
  28.9 15.5 %collective-permute-start.9 = (bf16[256,768]{1,0:T(8,128)(2,1)S(1)}, bf16[256,768]{1,0:T(8,128)(2,1)S(1)}, u32[]{:S(2)}, u32[]{:S(2)}) collective-permute-start(bf16[256,768]{1,0:T(8,128)(2,1)S(1)} %collective-permute-done.4.refs_2_), channel_id=1, source_target_pairs={{0,16},{8,24},{16,0},{24,8},{1,17},{9,25},{17,1},{25,9},{2,18},{10... | collective-permute-start | bytes 1179656 | tf_op jit(solution)/shard_map/ppermute | solution.py:273
  30.3 13.4 %collective-permute-start.10 = (bf16[256,512]{1,0:T(8,128)(2,1)}, bf16[256,512]{1,0:T(8,128)(2,1)S(1)}, u32[]{:S(2)}, u32[]{:S(2)}) collective-permute-start(bf16[256,512]{1,0:T(8,128)(2,1)} %copy-done.8), channel_id=1, source_target_pairs={{0,4},{1,5},{2,6},{3,7},{4,0},{5,1},{6,2},{7,3},{8,12},{9,13},{10,... | collective-permute-start | bytes 786440 | tf_op jit(solution)/shard_map/ppermute | solution.py:276
  34.4 9.3 %collective-permute-start.8 = (bf16[272,256]{1,0:T(8,128)(2,1)}, bf16[272,256]{1,0:T(8,128)(2,1)S(1)}, u32[]{:S(2)}, u32[]{:S(2)}) collective-permute-start(bf16[272,256]{1,0:T(8,128)(2,1)} %collective-permute-done.7.refs_5_), channel_id=1, source_target_pairs={{0,8},{8,0},{16,24},{24,16},{1,9},{9,1},{17,25},{25,17},{2,10},{10... | collective-permute-start | bytes 417800 | tf_op jit(solution)/shard_map/ppermute | solution.py:273
  43.7 0.7 copy-start.3
  44.4 2.0 %collective-permute-start.12 = (bf16[128,2048]{1,0:T(8,128)(2,1)S(1)}, bf16[128,2048]{1,0:T(8,128)(2,1)}, u32[]{:S(2)}, u32[]{:S(2)}) collective-permute-start(bf16[128,2048]{1,0:T(8,128)(2,1)S(1)} %collective-permute-done.11.far), channel_id=1, source_target_pairs={{0,1},{1,0},{2,3},{3,2},{4,5},{5,4},{6,7},{7,6},{8,9},{9,8},{10,11... | collective-permute-start | bytes 1572872 | tf_op jit(solution)/shard_map/ppermute | solution.py:270
  46.4 8.3 %collective-permute-start.16 = (bf16[256,512]{1,0:T(8,128)(2,1)S(1)}, bf16[256,512]{1,0:T(8,128)(2,1)S(1)}, u32[]{:S(2)}, u32[]{:S(2)}) collective-permute-start(bf16[256,512]{1,0:T(8,128)(2,1)S(1)} %collective-permute-done.10.refs_1_), channel_id=1, source_target_pairs={{0,8},{8,0},{16,24},{24,16},{1,9},{9,1},{17,25},{25,17},{2,10},{10... | collective-permute-start | bytes 786440 | tf_op jit(solution)/shard_map/ppermute | solution.py:273
  47.8 8.1 %collective-permute-start.17 = (bf16[256,512]{1,0:T(8,128)(2,1)S(1)}, bf16[256,512]{1,0:T(8,128)(2,1)S(1)}, u32[]{:S(2)}, u32[]{:S(2)}) collective-permute-start(bf16[256,512]{1,0:T(8,128)(2,1)S(1)} %collective-permute-done.10.refs_1_), channel_id=1, source_target_pairs={{0,16},{8,24},{16,0},{24,8},{1,17},{9,25},{17,1},{25,9},{2,18},{10... | collective-permute-start | bytes 786440 | tf_op jit(solution)/shard_map/ppermute | solution.py:273
  50.2 1.3 %copy-start.4 = (bf16[272,256]{1,0:T(8,128)(2,1)S(1)}, bf16[272,256]{1,0:T(8,128)(2,1)}, u32[]{:S(2)}) copy-start(bf16[272,256]{1,0:T(8,128)(2,1)} %copy-done.3) | copy-start | bytes 417796
  50.2 1.3 %copy-start.5 = (f32[256]{0:T(256)S(1)}, f32[256]{0:T(256)}, u32[]{:S(2)}) copy-start(f32[256]{0:T(256)} %param.13) | copy-start | bytes 3076
  51.6 16.3 %copy-start.6 = (f32[256]{0:T(256)S(1)}, f32[256]{0:T(256)}, u32[]{:S(2)}) copy-start(f32[256]{0:T(256)} %param.12) | copy-start | bytes 3076
  53.6 14.4 %collective-permute-start.13 = (bf16[512,256]{1,0:T(8,128)(2,1)S(1)}, bf16[512,256]{1,0:T(8,128)(2,1)S(1)}, u32[]{:S(2)}, u32[]{:S(2)}) collective-permute-start(bf16[512,256]{1,0:T(8,128)(2,1)S(1)} %project_kv.1.refs_0_), channel_id=1, source_target_pairs={{0,4},{1,5},{2,6},{3,7},{4,0},{5,1},{6,2},{7,3},{8,12},{9,13},{10,... | collective-permute-start | bytes 786440 | tf_op jit(solution)/shard_map/ppermute | solution.py:276
  55.9 12.0 %collective-permute-start.18 = (bf16[256,512]{1,0:T(8,128)(2,1)S(1)}, bf16[256,512]{1,0:T(8,128)(2,1)S(1)}, u32[]{:S(2)}, u32[]{:S(2)}) collective-permute-start(bf16[256,512]{1,0:T(8,128)(2,1)S(1)} %collective-permute-done.17.refs_5_), channel_id=1, source_target_pairs={{0,8},{8,0},{16,24},{24,16},{1,9},{9,1},{17,25},{25,17},{2,10},{10... | collective-permute-start | bytes 786440 | tf_op jit(solution)/shard_map/ppermute | solution.py:273
  57.2 13.7 %collective-permute-start.14 = (bf16[512,256]{1,0:T(8,128)(2,1)S(1)}, bf16[512,256]{1,0:T(8,128)(2,1)S(1)}, u32[]{:S(2)}, u32[]{:S(2)}) collective-permute-start(bf16[512,256]{1,0:T(8,128)(2,1)S(1)} %project_kv.1.refs_0_), channel_id=1, source_target_pairs={{0,1},{1,0},{2,3},{3,2},{4,5},{5,4},{6,7},{7,6},{8,9},{9,8},{10,11... | collective-permute-start | bytes 786440 | tf_op jit(solution)/shard_map/ppermute | solution.py:270
  67.9 3.0 %collective-permute-start.15 = (bf16[512,256]{1,0:T(8,128)(2,1)S(1)}, bf16[512,256]{1,0:T(8,128)(2,1)S(1)}, u32[]{:S(2)}, u32[]{:S(2)}) collective-permute-start(bf16[512,256]{1,0:T(8,128)(2,1)S(1)} %collective-permute-done.13.refs_1_), channel_id=1, source_target_pairs={{0,1},{1,0},{2,3},{3,2},{4,5},{5,4},{6,7},{7,6},{8,9},{9,8},{10,11... | collective-permute-start | bytes 786440 | tf_op jit(solution)/shard_map/ppermute | solution.py:270
  69.6 2.2 %collective-permute-start.19 = (bf16[256,512]{1,0:T(8,128)(2,1)S(1)}, bf16[256,512]{1,0:T(8,128)(2,1)S(1)}, u32[]{:S(2)}, u32[]{:S(2)}) collective-permute-start(bf16[256,512]{1,0:T(8,128)(2,1)S(1)} %get-tuple-element.59), channel_id=1, source_target_pairs={{0,1},{1,0},{2,3},{3,2},{4,5},{5,4},{6,7},{7,6},{8,9},{9,8},{10,11... | collective-permute-start | bytes 786440 | tf_op jit(solution)/shard_map/ppermute | solution.py:270
  71.6 9.2 %collective-permute-start.21 = (bf16[4,64,512]{2,1,0:T(8,128)(2,1)S(1)}, bf16[4,64,512]{2,1,0:T(8,128)(2,1)S(1)}, u32[]{:S(2)}, u32[]{:S(2)}) collective-permute-start(bf16[4,64,512]{2,1,0:T(8,128)(2,1)S(1)} %get-tuple-element.61), channel_id=1, source_target_pairs={{0,2},{1,3},{2,0},{3,1},{4,6},{5,7},{6,4},{7,5},{8,10},{9,11},{10,... | collective-permute-start | bytes 786440 | tf_op jit(solution)/shard_map/ppermute | solution.py:270
  73.7 11.8 %collective-permute-start.20 = (bf16[128,1024]{1,0:T(8,128)(2,1)S(1)}, bf16[128,1024]{1,0:T(8,128)(2,1)S(1)}, u32[]{:S(2)}, u32[]{:S(2)}) collective-permute-start(bf16[128,1024]{1,0:T(8,128)(2,1)S(1)} %attend.3), channel_id=1, source_target_pairs={{0,2},{1,3},{2,0},{3,1},{4,6},{5,7},{6,4},{7,5},{8,10},{9,11},{10,... | collective-permute-start | bytes 786440 | tf_op jit(solution)/shard_map/ppermute | solution.py:270

commit v8 on v7

--- a/solution.py
+++ b/solution.py
@@ -100,19 +100,12 @@
     kv_out[TEAM * rows :, :] = jnp.concatenate([ids] * (HD // LANES), 1)
 
 
-def stack_kernel(first_row, own, near, far, far_near, out):
-    _, pair, core = place()
-    rows = own.shape[0]
-    member = pair * 2 + core
-    for k, ref in ((0, own), (2, far), (3, far_near)):
-        out[aligned(member ^ k, rows), :] = ref[...]
-    here = aligned(member ^ 1, rows)
-    for n in range(out.shape[1] // LANES):
-        first = first_row + n * rows
-        out[here, n * LANES : (n + 1) * LANES] = near[first : first + rows, :]
-
-
-def project_kernel(n_out, depth, is_kv, x_ref, *refs):
+def cut_kernel(whole, kv_out, q_out):
+    kv_out[...] = whole[:, :HD]
+    q_out[...] = whole[:, HD:]
+
+
+def project_kernel(n_out, depth, first_row, is_kv, own, near, far, far_near, *refs):
     n_outs = 1 if is_kv else 2
     weights, (gain_ref, cos_ref, sin_ref) = refs[: -5 - n_outs], refs[-5 - n_outs : -2 - n_outs]
     outs, (w_all, sems) = refs[-2 - n_outs : -2], refs[-2:]
@@ -120,7 +113,7 @@
     outer = lax.axis_index("blk") // TEAM
     _, pair, core = place()
     member = pair * 2 + core
-    rows = x_ref.shape[0] // TEAM
+    rows = own.shape[0]
     width = outs[0].shape[1]
     direct = depth % LANES == 0
     places = []
@@ -130,39 +123,53 @@
         for n in range(n_out - 1 if i % 2 else 1):
             from_outer = lax.rem(outer + n_out - n - i % 2, n_out)
             cols = slice(None) if piece.shape[1] == width else slice(*((0, HD) if is_kv else (HD, 3 * HD)))
-            places.append((piece.at[pl.ds(n * tall, depth), cols], aligned(from_req * n_out + from_outer, depth)))
+            places.append((piece.at[pl.ds(n * tall, depth), cols], from_req * n_out + from_outer))
     if not direct:
         run([
-            pltpu.make_async_copy(piece, w_all.at[there, :], sems.at[n]) for n, (piece, there) in enumerate(places)
+            pltpu.make_async_copy(piece, w_all.at[aligned(index, depth), :], sems.at[n])
+            for n, (piece, index) in enumerate(places)
         ])
     half = HD // 2
     gain = gain_ref[...]
     if is_kv:
         gain = jnp.where(core == 0, gain, 1.0)
     for out, steps in zip(outs, [(0, 1, 2, 3)] if is_kv else [(1, 3), (0, 2)]):
-        def team_rows(ref, cols):
-            if is_kv:
-                return ref[:, cols]
-            return jnp.concatenate([ref[aligned(member ^ k, rows), cols] for k in steps], 0)
-
-        every = slice(None)
-        cosine, sine = team_rows(cos_ref, every), team_rows(sin_ref, every)
+
+        def token_rows(k, start, size):
+            if k != 1:
+                return (own, None, far, far_near)[k][:, pl.ds(start, size)]
+            blocks = []
+            for n in range(size // LANES):
+                first = pl.multiple_of(first_row + (start // LANES + n) * rows, 16)
+                blocks.append(near[pl.ds(first, rows), :])
+            return jnp.concatenate(blocks, 1)
+
+        def team_rows(start, size):
+            return jnp.concatenate([token_rows(k, start, size) for k in steps], 0)
+
+        cosine, sine = (
+            jnp.concatenate([ref[aligned(member ^ k, rows), :] for k in steps], 0) for ref in (cos_ref, sin_ref)
+        )
         if is_kv:
             cosine = jnp.where(core == 0, cosine, 1.0)
             sine = jnp.where(core == 0, sine, 0.0)
         if direct:
             product = 0.0
-            for piece, there in places:
-                product += jnp.dot(team_rows(x_ref, there), piece[...], preferred_element_type=jnp.float32)
+            for piece, index in places:
+                x = team_rows(pl.multiple_of(index * depth, depth), depth)
+                product += jnp.dot(x, piece[...], preferred_element_type=jnp.float32)
         else:
-            product = jnp.dot(team_rows(x_ref, every), w_all[...], preferred_element_type=jnp.float32)
+            product = jnp.dot(team_rows(0, w_all.shape[0]), w_all[...], preferred_element_type=jnp.float32)
         for h in range(out.shape[1] // HD):
             head = product[:, h * HD : (h + 1) * HD]
             mean = jnp.mean(head * head, axis=-1, keepdims=True)
             head = head * lax.rsqrt(mean + NORM_EPS) * gain
             front, second = head[:, :half], head[:, half:]
-            out[:, h * HD : h * HD + half] = (front * cosine - second * sine).astype(jnp.bfloat16)
-            out[:, h * HD + half : (h + 1) * HD] = (second * cosine + front * sine).astype(jnp.bfloat16)
+            turned = jnp.concatenate([front * cosine - second * sine, second * cosine + front * sine], 1)
+            turned = turned.astype(jnp.bfloat16)
+            for n, k in enumerate(steps):
+                there = aligned(member ^ k if is_kv else n, rows)
+                out[there, h * HD : (h + 1) * HD] = turned[n * rows : (n + 1) * rows]
 
 
 def attend_kernel(blk_rows, step, store, q_ref, near_ref, ids_ref, length_ref, out):
@@ -296,7 +303,7 @@
             pltpu.VMEM(own.shape, bf16),
             pltpu.SemaphoreType.DMA((3,)),
         ],
-        compiler_params=params(4),
+        compiler_params=params(56),
         name="pack",
     )(qkv_weight, block_ids, own)
     got = [parts[0]] + [in_team(parts[k], k) for k in range(1, TEAM)]
@@ -320,23 +327,6 @@
     kv, q, w, own = sync(kv, q, w, own)
     kv_o, w_x, w_y = from_others(kv), in_req(w, 1), in_req(w, 2)
     q_o, far = from_others(q), in_team(own, 2)
-    kv_o, w_x, w_y = sync(kv_o, w_x, w_y)
-    kv_ox, kv_oy, w_d = in_req(kv_o, 1), in_req(kv_o, 2), in_req(w_x, 2)
-    kv_ox, kv_oy = sync(kv_ox, kv_oy)
-    kv_od = in_req(kv_oy, 1)
-    kv_od, w_d, q_o, far = sync(kv_od, w_d, q_o, far)
-    far_near = in_team(far, 1)
-    q_o, far_near = sync(q_o, far_near)
-    q_ox, q_oy = in_req(q_o, 1), in_req(q_o, 2)
-    kv_weight = [w, kv_o, w_x, kv_ox, w_y, kv_oy, w_d, kv_od]
-    stacked = pl.pallas_call(
-        functools.partial(stack_kernel, packed_rows),
-        out_shape=shape((TEAM * rows, own.shape[1]), bf16),
-        in_specs=[VMEM] * TEAM,
-        out_specs=VMEM,
-        compiler_params=params(2),
-        name="stack",
-    )(own, got[1], far, far_near)
 
     blk_rows = rows // per_device
     tall = kv.shape[0]
@@ -349,36 +339,6 @@
     inverse = jnp.power(jnp.float32(ROPE_BASE), -2.0 * jnp.arange(HD // 2).astype(jnp.float32) / HD)
     angles = positions.astype(jnp.float32) * inverse[None, :]
     cosine, sine = jnp.cos(angles), jnp.sin(angles)
-
-    def project(weight, is_kv, gain):
-        width = weight[1].shape[1]
-        depth = own.shape[1]
-        n_outs = 1 if is_kv else 2
-        return pl.pallas_call(
-            functools.partial(project_kernel, n_out, TEAM * w_rows, is_kv),
-            out_shape=[shape((TEAM * rows // n_outs, width), bf16)] * n_outs,
-            in_specs=[VMEM] * (4 + len(weight)),
-            out_specs=[VMEM] * n_outs,
-            scratch_shapes=[
-                pltpu.VMEM((depth, width) if w_rows * TEAM % LANES else (ID_ROWS, LANES), bf16),
-                pltpu.SemaphoreType.DMA((n_req * n_out,)),
-            ],
-            cost_estimate=pl.CostEstimate(
-                flops=2 * TEAM * rows * depth * width, bytes_accessed=6 * MIB, transcendentals=0
-            ),
-            compiler_params=params(4 if w_rows * TEAM % LANES == 0 else 12),
-            name="project_kv" if is_kv else "project_q",
-        )(stacked, *weight, gain[None, :], cosine, sine)
-
-    (made,) = project(kv_weight, True, k_gain)
-    q_ox, q_oy = sync(q_ox, q_oy)
-    q_od = in_req(q_oy, 1)
-    q_weight = [w, q_o, w_x, q_ox, w_y, q_oy, w_d, q_od]
-    mine = [made] + [across(made, k) for k in range(1, n_out)]
-    other = [in_team(part, 1) for part in mine]
-
-    to_near, queries = project(q_weight, False, q_gain)
-    from_near = in_team(to_near, 1)
 
     table = page_table[0].reshape(-1)
     per_head = page_table.shape[2]
@@ -391,6 +351,54 @@
     )
     block = flat % per_head
     info = jnp.stack([flat // per_head, block, lengths[0] - block * blk_rows])
+
+    kv_o, w_x, w_y = sync(kv_o, w_x, w_y)
+    kv_x, q_x = pl.pallas_call(
+        cut_kernel,
+        out_shape=[shape((w_x.shape[0], HD), bf16), shape((w_x.shape[0], 2 * HD), bf16)],
+        in_specs=[VMEM],
+        out_specs=[VMEM] * 2,
+        compiler_params=params(1),
+        name="cut",
+    )(w_x)
+    kv_ox, kv_oy, kv_d = in_req(kv_o, 1), in_req(kv_o, 2), in_req(kv_x, 2)
+    kv_ox, kv_oy, kv_d, q_o, far, cosine, sine, all_ids, info = sync(
+        kv_ox, kv_oy, kv_d, q_o, far, cosine, sine, all_ids, info
+    )
+    kv_od, far_near = in_req(kv_oy, 1), in_team(far, 1)
+    kv_od, far_near, q_o = sync(kv_od, far_near, q_o)
+    q_ox, q_oy = in_req(q_o, 1), in_req(q_o, 2)
+    kv_weight = [kv, kv_o, w_x, kv_ox, w_y, kv_oy, kv_d, kv_od]
+
+    def project(weight, is_kv, gain):
+        width = weight[1].shape[1]
+        depth = own.shape[1]
+        n_outs = 1 if is_kv else 2
+        return pl.pallas_call(
+            functools.partial(project_kernel, n_out, TEAM * w_rows, packed_rows, is_kv),
+            out_shape=[shape((TEAM * rows // n_outs, width), bf16)] * n_outs,
+            in_specs=[VMEM] * (7 + len(weight)),
+            out_specs=[VMEM] * n_outs,
+            scratch_shapes=[
+                pltpu.VMEM((depth, width) if w_rows * TEAM % LANES else (ID_ROWS, LANES), bf16),
+                pltpu.SemaphoreType.DMA((n_req * n_out,)),
+            ],
+            cost_estimate=pl.CostEstimate(
+                flops=2 * TEAM * rows * depth * width, bytes_accessed=6 * MIB, transcendentals=0
+            ),
+            compiler_params=params(4 if w_rows * TEAM % LANES == 0 else 12),
+            name="project_kv" if is_kv else "project_q",
+        )(own, got[1], far, far_near, *weight, gain[None, :], cosine, sine)
+
+    (made,) = project(kv_weight, True, k_gain)
+    q_ox, q_oy, q_x = sync(q_ox, q_oy, q_x)
+    q_od, q_d = in_req(q_oy, 1), in_req(q_x, 2)
+    q_weight = [q, q_o, w_x, q_ox, w_y, q_oy, q_d, q_od]
+    mine = [made] + [across(made, k) for k in range(1, n_out)]
+    other = [in_team(part, 1) for part in mine]
+
+    to_near, queries = project(q_weight, False, q_gain)
+    from_near = in_team(to_near, 1)
 
     total = TEAM * rows * n_out
     store_mib = -(-2 * total * HD * 2 // MIB)

time: 87.4 us -> 82.8 us (0.947)
  local copies, waits for them, and re-layouts: 4.99 us -> 1.86 us
  starting transfers between devices: 23.2 us -> 21.2 us
  Pallas kernels: 12.8 us -> 13.8 us
    ppermute x3, waiting for transfers between devices: 23.9 us -> 17.6 us  [across(): lax.ppermute(array, 'blk', [(i, (i + TEAM * k) % n_blk) for i in range(n_...]
    ppermute x9 -> x10, waiting for transfers between devices: 3 us -> 8.92 us  [in_req(): return lax.ppermute(array, 'req', [(i, i ^ k) for i in range(n_req)])]
    unnamed x18 -> x14, local copies, waits for them, and re-layouts: 4.07 us -> 1.62 us
    pallas_call x1, Pallas kernels: 0.92 us -> 2.29 us  [body(): pl.pallas_call(pack_kernel, out_shape=[shape((packed_rows + (own.size //...]
    ppermute x9 -> x10, starting transfers between devices: 10.5 us -> 9.15 us  [in_req(): return lax.ppermute(array, 'req', [(i, i ^ k) for i in range(n_req)])]
  transfers between devices with their start and end apart: 22 -> 23, of which waited for: 11 -> 12; matrix products, arithmetic and copies ran while one was open for 5% -> 4% of each run, Pallas kernels for 11% -> 11%
where the time goes in v8:
time: 82.8 us; the launch traced here: 82.5 us
  waiting for transfers between devices  40.8 us (49%)
  starting transfers between devices  21.2 us (26%)
  Pallas kernels  13.8 us (17%)
  other arithmetic  3.44 us (4%)
  local copies, waits for them, and re-layouts  1.86 us (2%)
  between operations  1.44 us (2%)
    ppermute x3, waiting for transfers between devices, across(): lax.ppermute(array, 'blk', [(i, (i + TEAM * k) % n_blk) for i in range(n_...  17.6 us
    ppermute x10, waiting for transfers between devices, in_team(): return lax.ppermute(array, 'blk', [(i, i ^ k) for i in range(n_blk)])  14.3 us
    ppermute x10, starting transfers between devices, in_req(): return lax.ppermute(array, 'req', [(i, i ^ k) for i in range(n_req)])  9.15 us
    ppermute x10, waiting for transfers between devices, in_req(): return lax.ppermute(array, 'req', [(i, i ^ k) for i in range(n_req)])  8.92 us
    ppermute x10, starting transfers between devices, in_team(): return lax.ppermute(array, 'blk', [(i, i ^ k) for i in range(n_blk)])  7.27 us
    ppermute x3, starting transfers between devices, across(): lax.ppermute(array, 'blk', [(i, (i + TEAM * k) % n_blk) for i in range(n_...  4.73 us
    pallas_call x2, Pallas kernels, attend(): pl.pallas_call(functools.partial(attend_kernel, blk_rows, step), out_shap...  3.99 us
    pallas_call x2, Pallas kernels, project(): pl.pallas_call(functools.partial(project_kernel, n_out, TEAM * w_rows, pa...  3.69 us
  transfers between devices with their start and end apart: 23, of which 12 were waited for; matrix products, arithmetic and copies ran while one was open for 4% of the time, Pallas kernels for 11%

profile of v8, /device:TPU:0, one launch (start us, length us, event | category | flops | bytes accessed | tf_op | source)
XLA Modules:
  0.0 82.5 jit_solution(16077420610902991411)
XLA Ops:
  0.6 2.3 %pack.1 = (bf16[400,128]{1,0:T(8,128)(2,1)}, bf16[2448,128]{1,0:T(8,128)(2,1)}, bf16[400,128]{1,0:T(8,128)(2,1)}, bf16[400,128]{1,0:T(8,128)(2,1)}) custom-call(bf16[64,3072]{1,0:T(8,128)(2,1)} %w_hbm.1, s32[1,2]{1,0:T(1,128)} %ids_hbm.1, bf16[128,2048]{1,0:T(8,128)(2,1)} %bitcast.32), custom_call_target="tpu_custom_call" | custom-call | tf_op jit(solution)/shard_map/pack/pallas_call | solution.py:293
  3.5 2.7 %collective-permute-start.1 = (bf16[400,128]{1,0:T(8,128)(2,1)}, bf16[400,128]{1,0:T(8,128)(2,1)S(1)}, u32[]{:S(2)}, u32[]{:S(2)}) collective-permute-start(bf16[400,128]{1,0:T(8,128)(2,1)} %get-tuple-element.42), channel_id=1, source_target_pairs={{0,2},{1,3},{2,0},{3,1},{4,6},{5,7},{6,4},{7,5},{8,10},{9,11},{10,... | collective-permute-start | bytes 307208 | tf_op jit(solution)/shard_map/ppermute | solution.py:277
  7.2 2.8 %collective-permute-done.1.refs_2_ = bf16[400,128]{1,0:T(8,128)(2,1)S(1)} collective-permute-done((bf16[400,128]{1,0:T(8,128)(2,1)}, bf16[400,128]{1,0:T(8,128)(2,1)S(1)}, u32[]{:S(2)}, u32[]{:S(2)}) %collective-permute-start.1) | collective-permute-done | bytes 102432 | tf_op jit(solution)/shard_map/ppermute | solution.py:277
  10.1 1.7 %collective-permute-done.2.refs_3_ = bf16[400,128]{1,0:T(8,128)(2,1)S(1)} collective-permute-done((bf16[400,128]{1,0:T(8,128)(2,1)}, bf16[400,128]{1,0:T(8,128)(2,1)S(1)}, u32[]{:S(2)}, u32[]{:S(2)}) %collective-permute-start.2) | collective-permute-done | bytes 102432 | tf_op jit(solution)/shard_map/ppermute | solution.py:277
  11.7 0.9 %copy-done.1 = bf16[400,128]{1,0:T(8,128)(2,1)S(1)} copy-done((bf16[400,128]{1,0:T(8,128)(2,1)S(1)}, bf16[400,128]{1,0:T(8,128)(2,1)}, u32[]{:S(2)}) %copy-start.1) | copy-done | bytes 102424
  12.6 0.9 %team.1 = (bf16[272,256]{1,0:T(8,128)(2,1)}, bf16[256,512]{1,0:T(8,128)(2,1)S(1)}, bf16[256,768]{1,0:T(8,128)(2,1)}) custom-call(bf16[400,128]{1,0:T(8,128)(2,1)S(1)} %copy-done.1, bf16[2448,128]{1,0:T(8,128)(2,1)S(1)} %collective-permute-done.refs_1_.near, bf16[400,128]{1,0:T(8,128)(2,1)S(1)} %collective-permute-done.1.refs_2_, ...), custom_call_target="tpu_custom_call" | custom-call | tf_op jit(solution)/shard_map/team/pallas_call | solution.py:310
  13.6 1.5 %collective-permute-start.4 = (bf16[256,768]{1,0:T(8,128)(2,1)}, bf16[256,768]{1,0:T(8,128)(2,1)S(1)}, u32[]{:S(2)}, u32[]{:S(2)}) collective-permute-start(bf16[256,768]{1,0:T(8,128)(2,1)} %get-tuple-element.49), channel_id=1, source_target_pairs={{0,8},{8,0},{16,24},{24,16},{1,9},{9,1},{17,25},{25,17},{2,10},{10... | collective-permute-start | bytes 1179656 | tf_op jit(solution)/shard_map/ppermute | solution.py:280
  15.0 1.5 %collective-permute-start.5 = (bf16[256,768]{1,0:T(8,128)(2,1)}, bf16[256,768]{1,0:T(8,128)(2,1)S(1)}, u32[]{:S(2)}, u32[]{:S(2)}) collective-permute-start(bf16[256,768]{1,0:T(8,128)(2,1)} %get-tuple-element.49), channel_id=1, source_target_pairs={{0,16},{8,24},{16,0},{24,8},{1,17},{9,25},{17,1},{25,9},{2,18},{10... | collective-permute-start | bytes 1179656 | tf_op jit(solution)/shard_map/ppermute | solution.py:280
  16.6 2.6 %collective-permute-start.3 = (bf16[272,256]{1,0:T(8,128)(2,1)}, bf16[272,256]{1,0:T(8,128)(2,1)}, u32[]{:S(2)}, u32[]{:S(2)}) collective-permute-start(bf16[272,256]{1,0:T(8,128)(2,1)} %get-tuple-element.48.refs_0_), channel_id=1, source_target_pairs={{0,4},{1,5},{2,6},{3,7},{4,0},{5,1},{6,2},{7,3},{8,12},{9,13},{10,... | collective-permute-start | bytes 417800 | tf_op jit(solution)/shard_map/ppermute | solution.py:283
  19.1 0.7 multiply_bitcast_fusion
  20.0 1.6 %collective-permute-start.10 = (bf16[128,2048]{1,0:T(8,128)(2,1)S(1)}, bf16[128,2048]{1,0:T(8,128)(2,1)S(1)}, u32[]{:S(2)}, u32[]{:S(2)}) collective-permute-start(bf16[128,2048]{1,0:T(8,128)(2,1)S(1)} %bitcast.33), channel_id=1, source_target_pairs={{0,2},{1,3},{2,0},{3,1},{4,6},{5,7},{6,4},{7,5},{8,10},{9,11},{10,... | collective-permute-start | bytes 1572872 | tf_op jit(solution)/shard_map/ppermute | solution.py:277
  21.9 1.0 %multiply_sine_fusion = (f32[512,128]{1,0:T(8,128)S(1)}, f32[512,128]{1,0:T(8,128)S(1)}) fusion(f32[128]{0:T(128)S(1)} %multiply_power_fusion, f32[512]{0:T(512)S(1)} %convert_element_type.37), kind=kLoop, calls=%fused_computation | loop fusion | flops 65536 | bytes 526848 | tf_op jit(solution)/shard_map/sin | solution.py:341
  23.6 3.7 %collective-permute-done.3.refs_1_ = bf16[272,256]{1,0:T(8,128)(2,1)} collective-permute-done((bf16[272,256]{1,0:T(8,128)(2,1)}, bf16[272,256]{1,0:T(8,128)(2,1)}, u32[]{:S(2)}, u32[]{:S(2)}) %collective-permute-start.3) | collective-permute-done | bytes 139296 | tf_op jit(solution)/shard_map/ppermute | solution.py:283
  29.0 0.7 copy-done.4
  29.7 1.5 %collective-permute-start.8 = (bf16[256,256]{1,0:T(8,128)(2,1)}, bf16[256,256]{1,0:T(8,128)(2,1)}, u32[]{:S(2)}, u32[]{:S(2)}) collective-permute-start(bf16[256,256]{1,0:T(8,128)(2,1)} %get-tuple-element.52), channel_id=1, source_target_pairs={{0,16},{8,24},{16,0},{24,8},{1,17},{9,25},{17,1},{25,9},{2,18},{10... | collective-permute-start | bytes 393224 | tf_op jit(solution)/shard_map/ppermute | solution.py:280
  31.2 0.7 fusion
  32.0 7.0 %collective-permute-done.9.refs_1_ = bf16[256,512]{1,0:T(8,128)(2,1)S(1)} collective-permute-done((bf16[256,512]{1,0:T(8,128)(2,1)S(1)}, bf16[256,512]{1,0:T(8,128)(2,1)S(1)}, u32[]{:S(2)}, u32[]{:S(2)}) %collective-permute-start.9) | collective-permute-done | bytes 262176 | tf_op jit(solution)/shard_map/ppermute | solution.py:283
  39.1 1.7 %collective-permute-done.10.far = bf16[128,2048]{1,0:T(8,128)(2,1)S(1)} collective-permute-done((bf16[128,2048]{1,0:T(8,128)(2,1)S(1)}, bf16[128,2048]{1,0:T(8,128)(2,1)S(1)}, u32[]{:S(2)}, u32[]{:S(2)}) %collective-permute-start.10) | collective-permute-done | bytes 524320 | tf_op jit(solution)/shard_map/ppermute | solution.py:277
  41.5 5.7 %collective-permute-done.11.refs_7_ = bf16[272,256]{1,0:T(8,128)(2,1)S(1)} collective-permute-done((bf16[272,256]{1,0:T(8,128)(2,1)}, bf16[272,256]{1,0:T(8,128)(2,1)S(1)}, u32[]{:S(2)}, u32[]{:S(2)}) %collective-permute-start.11) | collective-permute-done | bytes 139296 | tf_op jit(solution)/shard_map/ppermute | solution.py:280
  48.2 2.1 %project_kv.1.refs_0_ = bf16[512,256]{1,0:T(8,128)(2,1)S(1)} custom-call(bf16[128,2048]{1,0:T(8,128)(2,1)S(1)} %bitcast.34, bf16[2448,128]{1,0:T(8,128)(2,1)S(1)} %collective-permute-done.refs_1_.near, bf16[128,2048]{1,0:T(8,128)(2,1)S(1)} %collective-permute-done.10.far, bf16[128,2048]{1,0:T(8,128)(2,1)S(1)} %collective-permute-done.12.far_near, ...), custom_call_target="tpu_custom_call" | custom-call | flops 536870912 | bytes 6291456 | tf_op jit(solution)/shard_map/project_kv/pallas_call | solution.py:377
  50.3 1.8 %collective-permute-start.13 = (bf16[512,256]{1,0:T(8,128)(2,1)S(1)}, bf16[512,256]{1,0:T(8,128)(2,1)S(1)}, u32[]{:S(2)}, u32[]{:S(2)}) collective-permute-start(bf16[512,256]{1,0:T(8,128)(2,1)S(1)} %project_kv.1.refs_0_), channel_id=1, source_target_pairs={{0,4},{1,5},{2,6},{3,7},{4,0},{5,1},{6,2},{7,3},{8,12},{9,13},{10,... | collective-permute-start | bytes 786440 | tf_op jit(solution)/shard_map/ppermute | solution.py:283
  52.1 2.9 %collective-permute-done.16.refs_3_ = bf16[256,512]{1,0:T(8,128)(2,1)S(1)} collective-permute-done((bf16[256,512]{1,0:T(8,128)(2,1)S(1)}, bf16[256,512]{1,0:T(8,128)(2,1)S(1)}, u32[]{:S(2)}, u32[]{:S(2)}) %collective-permute-start.16) | collective-permute-done | bytes 262176 | tf_op jit(solution)/shard_map/ppermute | solution.py:280
  55.8 1.5 %collective-permute-start.19 = (bf16[256,512]{1,0:T(8,128)(2,1)S(1)}, bf16[256,512]{1,0:T(8,128)(2,1)S(1)}, u32[]{:S(2)}, u32[]{:S(2)}) collective-permute-start(bf16[256,512]{1,0:T(8,128)(2,1)S(1)} %collective-permute-done.17.refs_5_), channel_id=1, source_target_pairs={{0,8},{8,0},{16,24},{24,16},{1,9},{9,1},{17,25},{25,17},{2,10},{10... | collective-permute-start | bytes 786440 | tf_op jit(solution)/shard_map/ppermute | solution.py:280
  57.3 6.9 %collective-permute-done.13.refs_1_ = bf16[512,256]{1,0:T(8,128)(2,1)S(1)} collective-permute-done((bf16[512,256]{1,0:T(8,128)(2,1)S(1)}, bf16[512,256]{1,0:T(8,128)(2,1)S(1)}, u32[]{:S(2)}, u32[]{:S(2)}) %collective-permute-start.13) | collective-permute-done | bytes 262176 | tf_op jit(solution)/shard_map/ppermute | solution.py:283
  64.2 1.6 %project_q.1 = (bf16[256,512]{1,0:T(8,128)(2,1)S(1)}, bf16[256,512]{1,0:T(8,128)(2,1)S(1)}) custom-call(bf16[128,2048]{1,0:T(8,128)(2,1)S(1)} %bitcast.35, bf16[2448,128]{1,0:T(8,128)(2,1)S(1)} %collective-permute-done.refs_1_.near, bf16[128,2048]{1,0:T(8,128)(2,1)S(1)} %collective-permute-done.10.far, ...), custom_call_target="tpu_custom_call" | custom-call | flops 1073741824 | bytes 6291456 | tf_op jit(solution)/shard_map/project_q/pallas_call | solution.py:377
  66.3 0.7 pages.1
  67.5 2.0 %attend.3 = bf16[128,1024]{1,0:T(8,128)(2,1)S(1)} custom-call(bf16[2,1024,256]{2,1,0:T(8,128)(2,1)S(1)} %get-tuple-element.66.store, bf16[256,512]{1,0:T(8,128)(2,1)S(1)} %get-tuple-element.72.q_ref, bf16[256,512]{1,0:T(8,128)(2,1)S(1)} %collective-permute-done.20.near_ref, s32[16]{0:T(128)S(1)} %reshape.141.refs_4_.ids_ref, s32[1]{0:T(128)} %copy.9.length_ref), custom_call_target="tpu_custom_call" | custom-call | flops 536870912 | bytes 4194304 | tf_op jit(solution)/shard_map/attend/pallas_call | solution.py:418
  69.5 1.8 %collective-permute-start.21 = (bf16[128,1024]{1,0:T(8,128)(2,1)S(1)}, bf16[128,1024]{1,0:T(8,128)(2,1)S(1)}, u32[]{:S(2)}, u32[]{:S(2)}) collective-permute-start(bf16[128,1024]{1,0:T(8,128)(2,1)S(1)} %attend.3), channel_id=1, source_target_pairs={{0,2},{1,3},{2,0},{3,1},{4,6},{5,7},{6,4},{7,5},{8,10},{9,11},{10,... | collective-permute-start | bytes 786440 | tf_op jit(solution)/shard_map/ppermute | solution.py:277
  71.2 2.0 %attend.2.kept = bf16[128,1024]{1,0:T(8,128)(2,1)S(1)} custom-call(bf16[2,1024,256]{2,1,0:T(8,128)(2,1)S(1)} %get-tuple-element.66.store, bf16[256,512]{1,0:T(8,128)(2,1)S(1)} %get-tuple-element.72.q_ref, bf16[256,512]{1,0:T(8,128)(2,1)S(1)} %collective-permute-done.20.near_ref, s32[16]{0:T(128)S(1)} %reshape.141.refs_4_.ids_ref, s32[1]{0:T(128)} %copy.9.length_ref), custom_call_target="tpu_custom_call" | custom-call | flops 536870912 | bytes 4194304 | tf_op jit(solution)/shard_map/attend/pallas_call | solution.py:418
  73.3 3.0 %collective-permute-done.22.got_pages = bf16[4,64,512]{2,1,0:T(8,128)(2,1)S(1)} collective-permute-done((bf16[4,64,512]{2,1,0:T(8,128)(2,1)S(1)}, bf16[4,64,512]{2,1,0:T(8,128)(2,1)S(1)}, u32[]{:S(2)}, u32[]{:S(2)}) %collective-permute-start.22) | collective-permute-done | bytes 262176 | tf_op jit(solution)/shard_map/ppermute | solution.py:277
  76.3 4.7 %collective-permute-done.21.from_far = bf16[128,1024]{1,0:T(8,128)(2,1)S(1)} collective-permute-done((bf16[128,1024]{1,0:T(8,128)(2,1)S(1)}, bf16[128,1024]{1,0:T(8,128)(2,1)S(1)}, u32[]{:S(2)}, u32[]{:S(2)}) %collective-permute-start.21) | collective-permute-done | bytes 262176 | tf_op jit(solution)/shard_map/ppermute | solution.py:277
  81.0 1.5 %finish.1 = (bf16[128,2048]{1,0:T(8,128)(2,1)}, bf16[4,64,512]{2,1,0:T(8,128)(2,1)}) custom-call(bf16[128,1024]{1,0:T(8,128)(2,1)S(1)} %attend.2.kept, bf16[128,1024]{1,0:T(8,128)(2,1)S(1)} %collective-permute-done.21.from_far, bf16[4,64,512]{2,1,0:T(8,128)(2,1)S(1)} %get-tuple-element.74.own_pages, ...), custom_call_target="tpu_custom_call" | custom-call | tf_op jit(solution)/shard_map/finish/pallas_call | solution.py:433
  (52 shorter events, 7.4 us)
Async XLA Ops:
  0.6 5.6 %copy-start.6 = (s32[1,2,16]{2,1,0:T(2,128)S(1)}, s32[1,2,16]{2,1,0:T(2,128)}, u32[]{:S(2)}) copy-start(s32[1,2,16]{2,1,0:T(2,128)} %param.10) | copy-start | bytes 388
  2.9 17.1 %copy-start = (bf16[1,128,2048]{2,1,0:T(8,128)(2,1)S(1)}, bf16[1,128,2048]{2,1,0:T(8,128)(2,1)}, u32[]{:S(2)}) copy-start(bf16[1,128,2048]{2,1,0:T(8,128)(2,1)} %param.7) | copy-start | bytes 1572868
  3.0 8.8 %collective-permute-start = (bf16[2448,128]{1,0:T(8,128)(2,1)}, bf16[2448,128]{1,0:T(8,128)(2,1)S(1)}, u32[]{:S(2)}, u32[]{:S(2)}) collective-permute-start(bf16[2448,128]{1,0:T(8,128)(2,1)} %get-tuple-element.41), channel_id=1, source_target_pairs={{0,1},{1,0},{2,3},{3,2},{4,5},{5,4},{6,7},{7,6},{8,9},{9,8},{10,11... | collective-permute-start | bytes 1880072 | tf_op jit(solution)/shard_map/ppermute | solution.py:277
  3.5 6.6 %collective-permute-start.1 = (bf16[400,128]{1,0:T(8,128)(2,1)}, bf16[400,128]{1,0:T(8,128)(2,1)S(1)}, u32[]{:S(2)}, u32[]{:S(2)}) collective-permute-start(bf16[400,128]{1,0:T(8,128)(2,1)} %get-tuple-element.42), channel_id=1, source_target_pairs={{0,2},{1,3},{2,0},{3,1},{4,6},{5,7},{6,4},{7,5},{8,10},{9,11},{10,... | collective-permute-start | bytes 307208 | tf_op jit(solution)/shard_map/ppermute | solution.py:277
  6.1 5.6 %collective-permute-start.2 = (bf16[400,128]{1,0:T(8,128)(2,1)}, bf16[400,128]{1,0:T(8,128)(2,1)S(1)}, u32[]{:S(2)}, u32[]{:S(2)}) collective-permute-start(bf16[400,128]{1,0:T(8,128)(2,1)} %get-tuple-element.43), channel_id=1, source_target_pairs={{0,3},{1,2},{2,1},{3,0},{4,7},{5,6},{6,5},{7,4},{8,11},{9,10},{10,... | collective-permute-start | bytes 307208 | tf_op jit(solution)/shard_map/ppermute | solution.py:277
  11.7 0.9 %copy-start.1 = (bf16[400,128]{1,0:T(8,128)(2,1)S(1)}, bf16[400,128]{1,0:T(8,128)(2,1)}, u32[]{:S(2)}) copy-start(bf16[400,128]{1,0:T(8,128)(2,1)} %get-tuple-element.40.refs_0_) | copy-start | bytes 307204
  13.6 13.7 %collective-permute-start.4 = (bf16[256,768]{1,0:T(8,128)(2,1)}, bf16[256,768]{1,0:T(8,128)(2,1)S(1)}, u32[]{:S(2)}, u32[]{:S(2)}) collective-permute-start(bf16[256,768]{1,0:T(8,128)(2,1)} %get-tuple-element.49), channel_id=1, source_target_pairs={{0,8},{8,0},{16,24},{24,16},{1,9},{9,1},{17,25},{25,17},{2,10},{10... | collective-permute-start | bytes 1179656 | tf_op jit(solution)/shard_map/ppermute | solution.py:280
  15.0 12.3 %collective-permute-start.5 = (bf16[256,768]{1,0:T(8,128)(2,1)}, bf16[256,768]{1,0:T(8,128)(2,1)S(1)}, u32[]{:S(2)}, u32[]{:S(2)}) collective-permute-start(bf16[256,768]{1,0:T(8,128)(2,1)} %get-tuple-element.49), channel_id=1, source_target_pairs={{0,16},{8,24},{16,0},{24,8},{1,17},{9,25},{17,1},{25,9},{2,18},{10... | collective-permute-start | bytes 1179656 | tf_op jit(solution)/shard_map/ppermute | solution.py:280
  16.6 10.7 %collective-permute-start.3 = (bf16[272,256]{1,0:T(8,128)(2,1)}, bf16[272,256]{1,0:T(8,128)(2,1)}, u32[]{:S(2)}, u32[]{:S(2)}) collective-permute-start(bf16[272,256]{1,0:T(8,128)(2,1)} %get-tuple-element.48.refs_0_), channel_id=1, source_target_pairs={{0,4},{1,5},{2,6},{3,7},{4,0},{5,1},{6,2},{7,3},{8,12},{9,13},{10,... | collective-permute-start | bytes 417800 | tf_op jit(solution)/shard_map/ppermute | solution.py:283
  20.0 20.8 %collective-permute-start.10 = (bf16[128,2048]{1,0:T(8,128)(2,1)S(1)}, bf16[128,2048]{1,0:T(8,128)(2,1)S(1)}, u32[]{:S(2)}, u32[]{:S(2)}) collective-permute-start(bf16[128,2048]{1,0:T(8,128)(2,1)S(1)} %bitcast.33), channel_id=1, source_target_pairs={{0,2},{1,3},{2,0},{3,1},{4,6},{5,7},{6,4},{7,5},{8,10},{9,11},{10,... | collective-permute-start | bytes 1572872 | tf_op jit(solution)/shard_map/ppermute | solution.py:277
  21.6 17.5 %collective-permute-start.9 = (bf16[256,512]{1,0:T(8,128)(2,1)S(1)}, bf16[256,512]{1,0:T(8,128)(2,1)S(1)}, u32[]{:S(2)}, u32[]{:S(2)}) collective-permute-start(bf16[256,512]{1,0:T(8,128)(2,1)S(1)} %get-tuple-element.53.refs_0_), channel_id=1, source_target_pairs={{0,4},{1,5},{2,6},{3,7},{4,0},{5,1},{6,2},{7,3},{8,12},{9,13},{10,... | collective-permute-start | bytes 786440 | tf_op jit(solution)/shard_map/ppermute | solution.py:283
  27.3 13.5 %collective-permute-start.6 = (bf16[272,256]{1,0:T(8,128)(2,1)}, bf16[272,256]{1,0:T(8,128)(2,1)}, u32[]{:S(2)}, u32[]{:S(2)}) collective-permute-start(bf16[272,256]{1,0:T(8,128)(2,1)} %collective-permute-done.3.refs_1_), channel_id=1, source_target_pairs={{0,8},{8,0},{16,24},{24,16},{1,9},{9,1},{17,25},{25,17},{2,10},{10... | collective-permute-start | bytes 417800 | tf_op jit(solution)/shard_map/ppermute | solution.py:280
  27.8 12.9 %collective-permute-start.7 = (bf16[272,256]{1,0:T(8,128)(2,1)}, bf16[272,256]{1,0:T(8,128)(2,1)}, u32[]{:S(2)}, u32[]{:S(2)}) collective-permute-start(bf16[272,256]{1,0:T(8,128)(2,1)} %collective-permute-done.3.refs_1_), channel_id=1, source_target_pairs={{0,16},{8,24},{16,0},{24,8},{1,17},{9,25},{17,1},{25,9},{2,18},{10... | collective-permute-start | bytes 417800 | tf_op jit(solution)/shard_map/ppermute | solution.py:280
  29.0 0.7 copy-start.4
  29.7 9.4 %collective-permute-start.8 = (bf16[256,256]{1,0:T(8,128)(2,1)}, bf16[256,256]{1,0:T(8,128)(2,1)}, u32[]{:S(2)}, u32[]{:S(2)}) collective-permute-start(bf16[256,256]{1,0:T(8,128)(2,1)} %get-tuple-element.52), channel_id=1, source_target_pairs={{0,16},{8,24},{16,0},{24,8},{1,17},{9,25},{17,1},{25,9},{2,18},{10... | collective-permute-start | bytes 393224 | tf_op jit(solution)/shard_map/ppermute | solution.py:280
  40.8 7.4 %copy-start.2 = (f32[256]{0:T(256)S(1)}, f32[256]{0:T(256)}, u32[]{:S(2)}) copy-start(f32[256]{0:T(256)} %param.13) | copy-start | bytes 3076
  40.8 6.4 %collective-permute-start.12 = (bf16[128,2048]{1,0:T(8,128)(2,1)S(1)}, bf16[128,2048]{1,0:T(8,128)(2,1)S(1)}, u32[]{:S(2)}, u32[]{:S(2)}) collective-permute-start(bf16[128,2048]{1,0:T(8,128)(2,1)S(1)} %collective-permute-done.10.far), channel_id=1, source_target_pairs={{0,1},{1,0},{2,3},{3,2},{4,5},{5,4},{6,7},{7,6},{8,9},{9,8},{10,11... | collective-permute-start | bytes 1572872 | tf_op jit(solution)/shard_map/ppermute | solution.py:277
  40.9 6.3 %collective-permute-start.11 = (bf16[272,256]{1,0:T(8,128)(2,1)}, bf16[272,256]{1,0:T(8,128)(2,1)S(1)}, u32[]{:S(2)}, u32[]{:S(2)}) collective-permute-start(bf16[272,256]{1,0:T(8,128)(2,1)} %collective-permute-done.7.refs_5_), channel_id=1, source_target_pairs={{0,8},{8,0},{16,24},{24,16},{1,9},{9,1},{17,25},{25,17},{2,10},{10... | collective-permute-start | bytes 417800 | tf_op jit(solution)/shard_map/ppermute | solution.py:280
  47.2 7.9 %collective-permute-start.16 = (bf16[256,512]{1,0:T(8,128)(2,1)S(1)}, bf16[256,512]{1,0:T(8,128)(2,1)S(1)}, u32[]{:S(2)}, u32[]{:S(2)}) collective-permute-start(bf16[256,512]{1,0:T(8,128)(2,1)S(1)} %collective-permute-done.9.refs_1_), channel_id=1, source_target_pairs={{0,8},{8,0},{16,24},{24,16},{1,9},{9,1},{17,25},{25,17},{2,10},{10... | collective-permute-start | bytes 786440 | tf_op jit(solution)/shard_map/ppermute | solution.py:280
  47.7 7.6 %collective-permute-start.17 = (bf16[256,512]{1,0:T(8,128)(2,1)S(1)}, bf16[256,512]{1,0:T(8,128)(2,1)S(1)}, u32[]{:S(2)}, u32[]{:S(2)}) collective-permute-start(bf16[256,512]{1,0:T(8,128)(2,1)S(1)} %collective-permute-done.9.refs_1_), channel_id=1, source_target_pairs={{0,16},{8,24},{16,0},{24,8},{1,17},{9,25},{17,1},{25,9},{2,18},{10... | collective-permute-start | bytes 786440 | tf_op jit(solution)/shard_map/ppermute | solution.py:280
  48.2 7.1 %copy-start.5 = (bf16[256,512]{1,0:T(8,128)(2,1)S(1)}, bf16[256,512]{1,0:T(8,128)(2,1)}, u32[]{:S(2)}) copy-start(bf16[256,512]{1,0:T(8,128)(2,1)} %copy-done.4) | copy-start | bytes 786436
  50.3 13.9 %collective-permute-start.13 = (bf16[512,256]{1,0:T(8,128)(2,1)S(1)}, bf16[512,256]{1,0:T(8,128)(2,1)S(1)}, u32[]{:S(2)}, u32[]{:S(2)}) collective-permute-start(bf16[512,256]{1,0:T(8,128)(2,1)S(1)} %project_kv.1.refs_0_), channel_id=1, source_target_pairs={{0,4},{1,5},{2,6},{3,7},{4,0},{5,1},{6,2},{7,3},{8,12},{9,13},{10,... | collective-permute-start | bytes 786440 | tf_op jit(solution)/shard_map/ppermute | solution.py:283
  55.3 8.9 %copy-start.3 = (f32[256]{0:T(256)S(1)}, f32[256]{0:T(256)}, u32[]{:S(2)}) copy-start(f32[256]{0:T(256)} %param.12) | copy-start | bytes 3076
  55.3 8.9 %collective-permute-start.18 = (bf16[256,512]{1,0:T(8,128)(2,1)S(1)}, bf16[256,512]{1,0:T(8,128)(2,1)S(1)}, u32[]{:S(2)}, u32[]{:S(2)}) collective-permute-start(bf16[256,512]{1,0:T(8,128)(2,1)S(1)} %copy-done.5), channel_id=1, source_target_pairs={{0,16},{8,24},{16,0},{24,8},{1,17},{9,25},{17,1},{25,9},{2,18},{10... | collective-permute-start | bytes 786440 | tf_op jit(solution)/shard_map/ppermute | solution.py:280
  55.8 8.4 %collective-permute-start.19 = (bf16[256,512]{1,0:T(8,128)(2,1)S(1)}, bf16[256,512]{1,0:T(8,128)(2,1)S(1)}, u32[]{:S(2)}, u32[]{:S(2)}) collective-permute-start(bf16[256,512]{1,0:T(8,128)(2,1)S(1)} %collective-permute-done.17.refs_5_), channel_id=1, source_target_pairs={{0,8},{8,0},{16,24},{24,16},{1,9},{9,1},{17,25},{25,17},{2,10},{10... | collective-permute-start | bytes 786440 | tf_op jit(solution)/shard_map/ppermute | solution.py:280
  57.3 9.1 %collective-permute-start.14 = (bf16[512,256]{1,0:T(8,128)(2,1)S(1)}, bf16[512,256]{1,0:T(8,128)(2,1)S(1)}, u32[]{:S(2)}, u32[]{:S(2)}) collective-permute-start(bf16[512,256]{1,0:T(8,128)(2,1)S(1)} %project_kv.1.refs_0_), channel_id=1, source_target_pairs={{0,1},{1,0},{2,3},{3,2},{4,5},{5,4},{6,7},{7,6},{8,9},{9,8},{10,11... | collective-permute-start | bytes 786440 | tf_op jit(solution)/shard_map/ppermute | solution.py:277
  64.2 2.2 %collective-permute-start.15 = (bf16[512,256]{1,0:T(8,128)(2,1)S(1)}, bf16[512,256]{1,0:T(8,128)(2,1)S(1)}, u32[]{:S(2)}, u32[]{:S(2)}) collective-permute-start(bf16[512,256]{1,0:T(8,128)(2,1)S(1)} %collective-permute-done.13.refs_1_), channel_id=1, source_target_pairs={{0,1},{1,0},{2,3},{3,2},{4,5},{5,4},{6,7},{7,6},{8,9},{9,8},{10,11... | collective-permute-start | bytes 786440 | tf_op jit(solution)/shard_map/ppermute | solution.py:277
  65.8 1.7 %collective-permute-start.20 = (bf16[256,512]{1,0:T(8,128)(2,1)S(1)}, bf16[256,512]{1,0:T(8,128)(2,1)S(1)}, u32[]{:S(2)}, u32[]{:S(2)}) collective-permute-start(bf16[256,512]{1,0:T(8,128)(2,1)S(1)} %get-tuple-element.73), channel_id=1, source_target_pairs={{0,1},{1,0},{2,3},{3,2},{4,5},{5,4},{6,7},{7,6},{8,9},{9,8},{10,11... | collective-permute-start | bytes 786440 | tf_op jit(solution)/shard_map/ppermute | solution.py:277
  67.1 9.2 %collective-permute-start.22 = (bf16[4,64,512]{2,1,0:T(8,128)(2,1)S(1)}, bf16[4,64,512]{2,1,0:T(8,128)(2,1)S(1)}, u32[]{:S(2)}, u32[]{:S(2)}) collective-permute-start(bf16[4,64,512]{2,1,0:T(8,128)(2,1)S(1)} %get-tuple-element.75), channel_id=1, source_target_pairs={{0,2},{1,3},{2,0},{3,1},{4,6},{5,7},{6,4},{7,5},{8,10},{9,11},{10,... | collective-permute-start | bytes 786440 | tf_op jit(solution)/shard_map/ppermute | solution.py:277
  69.5 11.5 %collective-permute-start.21 = (bf16[128,1024]{1,0:T(8,128)(2,1)S(1)}, bf16[128,1024]{1,0:T(8,128)(2,1)S(1)}, u32[]{:S(2)}, u32[]{:S(2)}) collective-permute-start(bf16[128,1024]{1,0:T(8,128)(2,1)S(1)} %attend.3), channel_id=1, source_target_pairs={{0,2},{1,3},{2,0},{3,1},{4,6},{5,7},{6,4},{7,5},{8,10},{9,11},{10,... | collective-permute-start | bytes 786440 | tf_op jit(solution)/shard_map/ppermute | solution.py:277

commit v9 on v8

--- a/solution.py
+++ b/solution.py
@@ -100,12 +100,14 @@
     kv_out[TEAM * rows :, :] = jnp.concatenate([ids] * (HD // LANES), 1)
 
 
-def cut_kernel(whole, kv_out, q_out):
-    kv_out[...] = whole[:, :HD]
-    q_out[...] = whole[:, HD:]
-
-
-def project_kernel(n_out, depth, first_row, is_kv, own, near, far, far_near, *refs):
+def regroup_kernel(kv_o, w_x, kv_out, q_out):
+    rows = kv_o.shape[0]
+    kv_out[:rows, :] = kv_o[...]
+    kv_out[rows:, :] = w_x[:, :HD]
+    q_out[...] = w_x[:, HD:]
+
+
+def project_kernel(n_out, depth, tall, starts, first_row, is_kv, own, near, far, far_near, *refs):
     n_outs = 1 if is_kv else 2
     weights, (gain_ref, cos_ref, sin_ref) = refs[: -5 - n_outs], refs[-5 - n_outs : -2 - n_outs]
     outs, (w_all, sems) = refs[-2 - n_outs : -2], refs[-2:]
@@ -119,11 +121,11 @@
     places = []
     for i, piece in enumerate(weights):
         from_req = req ^ (i // 2)
-        tall = piece.shape[0] // (n_out - 1 if i % 2 else 1)
         for n in range(n_out - 1 if i % 2 else 1):
             from_outer = lax.rem(outer + n_out - n - i % 2, n_out)
-            cols = slice(None) if piece.shape[1] == width else slice(*((0, HD) if is_kv else (HD, 3 * HD)))
-            places.append((piece.at[pl.ds(n * tall, depth), cols], from_req * n_out + from_outer))
+            row, column = starts[i]
+            part = piece.at[pl.ds(row + n * tall, depth), column : column + width]
+            places.append((part, from_req * n_out + from_outer))
     if not direct:
         run([
             pltpu.make_async_copy(piece, w_all.at[aligned(index, depth), :], sems.at[n])
@@ -353,29 +355,34 @@
     info = jnp.stack([flat // per_head, block, lengths[0] - block * blk_rows])
 
     kv_o, w_x, w_y = sync(kv_o, w_x, w_y)
-    kv_x, q_x = pl.pallas_call(
-        cut_kernel,
-        out_shape=[shape((w_x.shape[0], HD), bf16), shape((w_x.shape[0], 2 * HD), bf16)],
-        in_specs=[VMEM],
+    others = kv_o.shape[0]
+    kv_o_x, q_x = pl.pallas_call(
+        regroup_kernel,
+        out_shape=[shape((others + w_x.shape[0], HD), bf16), shape((w_x.shape[0], 2 * HD), bf16)],
+        in_specs=[VMEM] * 2,
         out_specs=[VMEM] * 2,
         compiler_params=params(1),
-        name="cut",
-    )(w_x)
-    kv_ox, kv_oy, kv_d = in_req(kv_o, 1), in_req(kv_o, 2), in_req(kv_x, 2)
-    kv_ox, kv_oy, kv_d, q_o, far, cosine, sine, all_ids, info = sync(
-        kv_ox, kv_oy, kv_d, q_o, far, cosine, sine, all_ids, info
+        name="regroup",
+    )(kv_o, w_x)
+    kv_ox, kv_oy_d, kv_od = in_req(kv_o, 1), in_req(kv_o_x, 2), in_req(kv_o, 3)
+    kv_ox, kv_oy_d, kv_od, q_o, far, cosine, sine, all_ids, info = sync(
+        kv_ox, kv_oy_d, kv_od, q_o, far, cosine, sine, all_ids, info
     )
-    kv_od, far_near = in_req(kv_oy, 1), in_team(far, 1)
-    kv_od, far_near, q_o = sync(kv_od, far_near, q_o)
+    far_near = in_team(far, 1)
+    far_near, q_o = sync(far_near, q_o)
     q_ox, q_oy = in_req(q_o, 1), in_req(q_o, 2)
-    kv_weight = [kv, kv_o, w_x, kv_ox, w_y, kv_oy, kv_d, kv_od]
+    kv_weight = [(kv, 0, 0), (kv_o, 0, 0), (w_x, 0, 0), (kv_ox, 0, 0)]
+    kv_weight += [(w_y, 0, 0), (kv_oy_d, 0, 0), (kv_oy_d, others, 0), (kv_od, 0, 0)]
 
     def project(weight, is_kv, gain):
+        starts = [part[1:] for part in weight]
+        weight = [part[0] for part in weight]
         width = weight[1].shape[1]
+        step = weight[1].shape[0] // (n_out - 1)
         depth = own.shape[1]
         n_outs = 1 if is_kv else 2
         return pl.pallas_call(
-            functools.partial(project_kernel, n_out, TEAM * w_rows, packed_rows, is_kv),
+            functools.partial(project_kernel, n_out, TEAM * w_rows, step, starts, packed_rows, is_kv),
             out_shape=[shape((TEAM * rows // n_outs, width), bf16)] * n_outs,
             in_specs=[VMEM] * (7 + len(weight)),
             out_specs=[VMEM] * n_outs,
@@ -393,7 +400,8 @@
     (made,) = project(kv_weight, True, k_gain)
     q_ox, q_oy, q_x = sync(q_ox, q_oy, q_x)
     q_od, q_d = in_req(q_oy, 1), in_req(q_x, 2)
-    q_weight = [q, q_o, w_x, q_ox, w_y, q_oy, q_d, q_od]
+    q_weight = [(q, 0, 0), (q_o, 0, 0), (w_x, 0, HD), (q_ox, 0, 0)]
+    q_weight += [(w_y, 0, HD), (q_oy, 0, 0), (q_d, 0, 0), (q_od, 0, 0)]
     mine = [made] + [across(made, k) for k in range(1, n_out)]
     other = [in_team(part, 1) for part in mine]
 

time: 82.8 us -> 79.2 us (0.957)
  waiting for transfers between devices: 40.8 us -> 36.6 us
  other arithmetic: 3.44 us -> 1.38 us
  starting transfers between devices: 21.2 us -> 23 us
  Pallas kernels: 13.8 us -> 14.8 us
    ppermute x10 -> x9, waiting for transfers between devices: 8.92 us -> 2.95 us  [in_req(): return lax.ppermute(array, 'req', [(i, i ^ k) for i in range(n_req)])]
    ppermute x3, starting transfers between devices: 4.73 us -> 5.73 us  [across(): lax.ppermute(array, 'blk', [(i, (i + TEAM * k) % n_blk) for i in range(n_...]
    ppermute x10, waiting for transfers between devices: 14.3 us -> 15.2 us  [in_team(): return lax.ppermute(array, 'blk', [(i, i ^ k) for i in range(n_blk)])]
    pallas_call x3, Pallas kernels: 4.37 us -> 5.27 us  [the longest x2 4.53 us: project(): pl.pallas_call(functools.partial(project_kernel, n_out, TEAM * w_rows, st...]
    ppermute x10 -> x9, starting transfers between devices: 9.15 us -> 9.64 us  [in_req(): return lax.ppermute(array, 'req', [(i, i ^ k) for i in range(n_req)])]
  transfers between devices with their start and end apart: 23 -> 22, of which waited for: 12 -> 11; matrix products, arithmetic and copies ran while one was open for 4% -> 2% of each run, Pallas kernels for 11% -> 13%
where the time goes in v9:
time: 79.2 us; the launch traced here: 79 us
  waiting for transfers between devices  36.6 us (46%)
  starting transfers between devices  23 us (29%)
  Pallas kernels  14.8 us (19%)
  local copies, waits for them, and re-layouts  1.86 us (2%)
  between operations  1.44 us (2%)
  other arithmetic  1.38 us (2%)
    ppermute x3, waiting for transfers between devices, across(): lax.ppermute(array, 'blk', [(i, (i + TEAM * k) % n_blk) for i in range(n_...  18.4 us
    ppermute x10, waiting for transfers between devices, in_team(): return lax.ppermute(array, 'blk', [(i, i ^ k) for i in range(n_blk)])  15.2 us
    ppermute x9, starting transfers between devices, in_req(): return lax.ppermute(array, 'req', [(i, i ^ k) for i in range(n_req)])  9.64 us
    ppermute x10, starting transfers between devices, in_team(): return lax.ppermute(array, 'blk', [(i, i ^ k) for i in range(n_blk)])  7.61 us
    ppermute x3, starting transfers between devices, across(): lax.ppermute(array, 'blk', [(i, (i + TEAM * k) % n_blk) for i in range(n_...  5.73 us
    pallas_call x2, Pallas kernels, project(): pl.pallas_call(functools.partial(project_kernel, n_out, TEAM * w_rows, st...  4.53 us
    pallas_call x2, Pallas kernels, attend(): pl.pallas_call(functools.partial(attend_kernel, blk_rows, step), out_shap...  4.04 us
    ppermute x9, waiting for transfers between devices, in_req(): return lax.ppermute(array, 'req', [(i, i ^ k) for i in range(n_req)])  2.95 us
  transfers between devices with their start and end apart: 22, of which 11 were waited for; matrix products, arithmetic and copies ran while one was open for 2% of the time, Pallas kernels for 13%

profile of v9, /device:TPU:0, one launch (start us, length us, event | category | flops | bytes accessed | tf_op | source)
XLA Modules:
  0.0 79.0 jit_solution(9356420095951853290)
XLA Ops:
  0.6 2.3 %pack.1 = (bf16[400,128]{1,0:T(8,128)(2,1)}, bf16[2448,128]{1,0:T(8,128)(2,1)}, bf16[400,128]{1,0:T(8,128)(2,1)}, bf16[400,128]{1,0:T(8,128)(2,1)}) custom-call(bf16[64,3072]{1,0:T(8,128)(2,1)} %w_hbm.1, s32[1,2]{1,0:T(1,128)} %ids_hbm.1, bf16[128,2048]{1,0:T(8,128)(2,1)} %bitcast.32), custom_call_target="tpu_custom_call" | custom-call | tf_op jit(solution)/shard_map/pack/pallas_call | solution.py:295
  3.5 2.7 %collective-permute-start.1 = (bf16[400,128]{1,0:T(8,128)(2,1)}, bf16[400,128]{1,0:T(8,128)(2,1)S(1)}, u32[]{:S(2)}, u32[]{:S(2)}) collective-permute-start(bf16[400,128]{1,0:T(8,128)(2,1)} %get-tuple-element.41), channel_id=1, source_target_pairs={{0,2},{1,3},{2,0},{3,1},{4,6},{5,7},{6,4},{7,5},{8,10},{9,11},{10,... | collective-permute-start | bytes 307208 | tf_op jit(solution)/shard_map/ppermute | solution.py:279
  7.3 2.8 %collective-permute-done.1.refs_2_ = bf16[400,128]{1,0:T(8,128)(2,1)S(1)} collective-permute-done((bf16[400,128]{1,0:T(8,128)(2,1)}, bf16[400,128]{1,0:T(8,128)(2,1)S(1)}, u32[]{:S(2)}, u32[]{:S(2)}) %collective-permute-start.1) | collective-permute-done | bytes 102432 | tf_op jit(solution)/shard_map/ppermute | solution.py:279
  10.1 1.7 %collective-permute-done.2.refs_3_ = bf16[400,128]{1,0:T(8,128)(2,1)S(1)} collective-permute-done((bf16[400,128]{1,0:T(8,128)(2,1)}, bf16[400,128]{1,0:T(8,128)(2,1)S(1)}, u32[]{:S(2)}, u32[]{:S(2)}) %collective-permute-start.2) | collective-permute-done | bytes 102432 | tf_op jit(solution)/shard_map/ppermute | solution.py:279
  11.8 0.9 %copy-done.1 = bf16[400,128]{1,0:T(8,128)(2,1)S(1)} copy-done((bf16[400,128]{1,0:T(8,128)(2,1)S(1)}, bf16[400,128]{1,0:T(8,128)(2,1)}, u32[]{:S(2)}) %copy-start.1) | copy-done | bytes 102424
  12.7 1.0 %team.1 = (bf16[272,256]{1,0:T(8,128)(2,1)S(1)}, bf16[256,512]{1,0:T(8,128)(2,1)}, bf16[256,768]{1,0:T(8,128)(2,1)}) custom-call(bf16[400,128]{1,0:T(8,128)(2,1)S(1)} %copy-done.1, bf16[2448,128]{1,0:T(8,128)(2,1)S(1)} %collective-permute-done.refs_1_.near, bf16[400,128]{1,0:T(8,128)(2,1)S(1)} %collective-permute-done.1.refs_2_, ...), custom_call_target="tpu_custom_call" | custom-call | tf_op jit(solution)/shard_map/team/pallas_call | solution.py:312
  13.6 1.5 %collective-permute-start.4 = (bf16[256,768]{1,0:T(8,128)(2,1)}, bf16[256,768]{1,0:T(8,128)(2,1)S(1)}, u32[]{:S(2)}, u32[]{:S(2)}) collective-permute-start(bf16[256,768]{1,0:T(8,128)(2,1)} %get-tuple-element.48), channel_id=1, source_target_pairs={{0,8},{8,0},{16,24},{24,16},{1,9},{9,1},{17,25},{25,17},{2,10},{10... | collective-permute-start | bytes 1179656 | tf_op jit(solution)/shard_map/ppermute | solution.py:282
  15.1 1.5 %collective-permute-start.5 = (bf16[256,768]{1,0:T(8,128)(2,1)}, bf16[256,768]{1,0:T(8,128)(2,1)S(1)}, u32[]{:S(2)}, u32[]{:S(2)}) collective-permute-start(bf16[256,768]{1,0:T(8,128)(2,1)} %get-tuple-element.48), channel_id=1, source_target_pairs={{0,16},{8,24},{16,0},{24,8},{1,17},{9,25},{17,1},{25,9},{2,18},{10... | collective-permute-start | bytes 1179656 | tf_op jit(solution)/shard_map/ppermute | solution.py:282
  16.6 2.6 %collective-permute-start.3 = (bf16[272,256]{1,0:T(8,128)(2,1)S(1)}, bf16[272,256]{1,0:T(8,128)(2,1)S(1)}, u32[]{:S(2)}, u32[]{:S(2)}) collective-permute-start(bf16[272,256]{1,0:T(8,128)(2,1)S(1)} %get-tuple-element.47.refs_0_), channel_id=1, source_target_pairs={{0,4},{1,5},{2,6},{3,7},{4,0},{5,1},{6,2},{7,3},{8,12},{9,13},{10,... | collective-permute-start | bytes 417800 | tf_op jit(solution)/shard_map/ppermute | solution.py:285
  19.4 1.6 %collective-permute-start.10 = (bf16[128,2048]{1,0:T(8,128)(2,1)S(1)}, bf16[128,2048]{1,0:T(8,128)(2,1)S(1)}, u32[]{:S(2)}, u32[]{:S(2)}) collective-permute-start(bf16[128,2048]{1,0:T(8,128)(2,1)S(1)} %bitcast.33), channel_id=1, source_target_pairs={{0,2},{1,3},{2,0},{3,1},{4,6},{5,7},{6,4},{7,5},{8,10},{9,11},{10,... | collective-permute-start | bytes 1572872 | tf_op jit(solution)/shard_map/ppermute | solution.py:279
  21.3 1.0 %multiply_sine_fusion = (f32[512,128]{1,0:T(8,128)S(1)}, f32[512,128]{1,0:T(8,128)S(1)}) fusion(f32[128]{0:T(128)S(1)} %multiply_power_fusion, f32[512]{0:T(512)S(1)} %convert_element_type.37), kind=kLoop, calls=%fused_computation | loop fusion | flops 65536 | bytes 526848 | tf_op jit(solution)/shard_map/sin | solution.py:343
  22.3 4.8 %collective-permute-done.3.kv_o.refs_1_ = bf16[272,256]{1,0:T(8,128)(2,1)S(1)} collective-permute-done((bf16[272,256]{1,0:T(8,128)(2,1)S(1)}, bf16[272,256]{1,0:T(8,128)(2,1)S(1)}, u32[]{:S(2)}, u32[]{:S(2)}) %collective-permute-start.3) | collective-permute-done | bytes 139296 | tf_op jit(solution)/shard_map/ppermute | solution.py:285
  27.6 1.7 %collective-permute-start.8 = (bf16[272,256]{1,0:T(8,128)(2,1)S(1)}, bf16[272,256]{1,0:T(8,128)(2,1)}, u32[]{:S(2)}, u32[]{:S(2)}) collective-permute-start(bf16[272,256]{1,0:T(8,128)(2,1)S(1)} %collective-permute-done.3.kv_o.refs_1_), channel_id=1, source_target_pairs={{0,24},{8,16},{16,8},{24,0},{1,25},{9,17},{17,9},{25,1},{2,26},{10... | collective-permute-start | bytes 417800 | tf_op jit(solution)/shard_map/ppermute | solution.py:282
  29.3 0.7 regroup.1
  30.7 1.2 %collective-permute-start.7 = (bf16[528,256]{1,0:T(8,128)(2,1)}, bf16[528,256]{1,0:T(8,128)(2,1)S(1)}, u32[]{:S(2)}, u32[]{:S(2)}) collective-permute-start(bf16[528,256]{1,0:T(8,128)(2,1)} %get-tuple-element.51), channel_id=1, source_target_pairs={{0,16},{8,24},{16,0},{24,8},{1,17},{9,25},{17,1},{25,9},{2,18},{10... | collective-permute-start | bytes 811016 | tf_op jit(solution)/shard_map/ppermute | solution.py:282
  32.1 6.9 %collective-permute-done.9.refs_1_ = bf16[256,512]{1,0:T(8,128)(2,1)} collective-permute-done((bf16[256,512]{1,0:T(8,128)(2,1)}, bf16[256,512]{1,0:T(8,128)(2,1)}, u32[]{:S(2)}, u32[]{:S(2)}) %collective-permute-start.9) | collective-permute-done | bytes 262176 | tf_op jit(solution)/shard_map/ppermute | solution.py:285
  39.0 1.1 %collective-permute-done.10.far = bf16[128,2048]{1,0:T(8,128)(2,1)S(1)} collective-permute-done((bf16[128,2048]{1,0:T(8,128)(2,1)S(1)}, bf16[128,2048]{1,0:T(8,128)(2,1)S(1)}, u32[]{:S(2)}, u32[]{:S(2)}) %collective-permute-start.10) | collective-permute-done | bytes 524320 | tf_op jit(solution)/shard_map/ppermute | solution.py:279
  40.2 1.9 %collective-permute-done.11.far_near = bf16[128,2048]{1,0:T(8,128)(2,1)S(1)} collective-permute-done((bf16[128,2048]{1,0:T(8,128)(2,1)S(1)}, bf16[128,2048]{1,0:T(8,128)(2,1)S(1)}, u32[]{:S(2)}, u32[]{:S(2)}) %collective-permute-start.11) | collective-permute-done | bytes 524320 | tf_op jit(solution)/shard_map/ppermute | solution.py:279
  43.3 1.9 %project_kv.1.refs_0_ = bf16[512,256]{1,0:T(8,128)(2,1)S(1)} custom-call(bf16[128,2048]{1,0:T(8,128)(2,1)S(1)} %bitcast.34, bf16[2448,128]{1,0:T(8,128)(2,1)S(1)} %collective-permute-done.refs_1_.near, bf16[128,2048]{1,0:T(8,128)(2,1)S(1)} %collective-permute-done.10.far, bf16[128,2048]{1,0:T(8,128)(2,1)S(1)} %collective-permute-done.11.far_near, ...), custom_call_target="tpu_custom_call" | custom-call | flops 536870912 | bytes 6291456 | tf_op jit(solution)/shard_map/project_kv/pallas_call | solution.py:384
  45.2 2.8 %collective-permute-start.12 = (bf16[512,256]{1,0:T(8,128)(2,1)S(1)}, bf16[512,256]{1,0:T(8,128)(2,1)S(1)}, u32[]{:S(2)}, u32[]{:S(2)}) collective-permute-start(bf16[512,256]{1,0:T(8,128)(2,1)S(1)} %project_kv.1.refs_0_), channel_id=1, source_target_pairs={{0,4},{1,5},{2,6},{3,7},{4,0},{5,1},{6,2},{7,3},{8,12},{9,13},{10,... | collective-permute-start | bytes 786440 | tf_op jit(solution)/shard_map/ppermute | solution.py:285
  48.0 2.7 %collective-permute-done.15.refs_3_ = bf16[256,512]{1,0:T(8,128)(2,1)S(1)} collective-permute-done((bf16[256,512]{1,0:T(8,128)(2,1)}, bf16[256,512]{1,0:T(8,128)(2,1)S(1)}, u32[]{:S(2)}, u32[]{:S(2)}) %collective-permute-start.15) | collective-permute-done | bytes 262176 | tf_op jit(solution)/shard_map/ppermute | solution.py:282
  51.6 1.4 %collective-permute-start.18 = (bf16[256,512]{1,0:T(8,128)(2,1)S(1)}, bf16[256,512]{1,0:T(8,128)(2,1)S(1)}, u32[]{:S(2)}, u32[]{:S(2)}) collective-permute-start(bf16[256,512]{1,0:T(8,128)(2,1)S(1)} %collective-permute-done.16.refs_5_), channel_id=1, source_target_pairs={{0,8},{8,0},{16,24},{24,16},{1,9},{9,1},{17,25},{25,17},{2,10},{10... | collective-permute-start | bytes 786440 | tf_op jit(solution)/shard_map/ppermute | solution.py:282
  52.9 6.7 %collective-permute-done.12.refs_1_ = bf16[512,256]{1,0:T(8,128)(2,1)S(1)} collective-permute-done((bf16[512,256]{1,0:T(8,128)(2,1)S(1)}, bf16[512,256]{1,0:T(8,128)(2,1)S(1)}, u32[]{:S(2)}, u32[]{:S(2)}) %collective-permute-start.12) | collective-permute-done | bytes 262176 | tf_op jit(solution)/shard_map/ppermute | solution.py:285
  59.7 2.6 %project_q.1 = (bf16[256,512]{1,0:T(8,128)(2,1)S(1)}, bf16[256,512]{1,0:T(8,128)(2,1)S(1)}) custom-call(bf16[128,2048]{1,0:T(8,128)(2,1)S(1)} %bitcast.35, bf16[2448,128]{1,0:T(8,128)(2,1)S(1)} %collective-permute-done.refs_1_.near, bf16[128,2048]{1,0:T(8,128)(2,1)S(1)} %collective-permute-done.10.far, ...), custom_call_target="tpu_custom_call" | custom-call | flops 1073741824 | bytes 6291456 | tf_op jit(solution)/shard_map/project_q/pallas_call | solution.py:384
  62.9 0.7 pages.1
  63.6 0.8 collective-permute-start.21
  64.4 2.0 %attend.3 = bf16[128,1024]{1,0:T(8,128)(2,1)S(1)} custom-call(bf16[2,1024,256]{2,1,0:T(8,128)(2,1)S(1)} %get-tuple-element.64.store, bf16[256,512]{1,0:T(8,128)(2,1)S(1)} %get-tuple-element.70.q_ref, bf16[256,512]{1,0:T(8,128)(2,1)S(1)} %collective-permute-done.19.near_ref, s32[16]{0:T(128)S(1)} %reshape.141.refs_4_.ids_ref, s32[1]{0:T(128)} %copy.9.length_ref), custom_call_target="tpu_custom_call" | custom-call | flops 536870912 | bytes 4194304 | tf_op jit(solution)/shard_map/attend/pallas_call | solution.py:426
  66.4 1.4 %collective-permute-start.20 = (bf16[128,1024]{1,0:T(8,128)(2,1)S(1)}, bf16[128,1024]{1,0:T(8,128)(2,1)S(1)}, u32[]{:S(2)}, u32[]{:S(2)}) collective-permute-start(bf16[128,1024]{1,0:T(8,128)(2,1)S(1)} %attend.3), channel_id=1, source_target_pairs={{0,2},{1,3},{2,0},{3,1},{4,6},{5,7},{6,4},{7,5},{8,10},{9,11},{10,... | collective-permute-start | bytes 786440 | tf_op jit(solution)/shard_map/ppermute | solution.py:279
  67.8 2.0 %attend.2.kept = bf16[128,1024]{1,0:T(8,128)(2,1)S(1)} custom-call(bf16[2,1024,256]{2,1,0:T(8,128)(2,1)S(1)} %get-tuple-element.64.store, bf16[256,512]{1,0:T(8,128)(2,1)S(1)} %get-tuple-element.70.q_ref, bf16[256,512]{1,0:T(8,128)(2,1)S(1)} %collective-permute-done.19.near_ref, s32[16]{0:T(128)S(1)} %reshape.141.refs_4_.ids_ref, s32[1]{0:T(128)} %copy.9.length_ref), custom_call_target="tpu_custom_call" | custom-call | flops 536870912 | bytes 4194304 | tf_op jit(solution)/shard_map/attend/pallas_call | solution.py:426
  69.8 3.0 %collective-permute-done.21.got_pages = bf16[4,64,512]{2,1,0:T(8,128)(2,1)S(1)} collective-permute-done((bf16[4,64,512]{2,1,0:T(8,128)(2,1)S(1)}, bf16[4,64,512]{2,1,0:T(8,128)(2,1)S(1)}, u32[]{:S(2)}, u32[]{:S(2)}) %collective-permute-start.21) | collective-permute-done | bytes 262176 | tf_op jit(solution)/shard_map/ppermute | solution.py:279
  72.8 4.7 %collective-permute-done.20.from_far = bf16[128,1024]{1,0:T(8,128)(2,1)S(1)} collective-permute-done((bf16[128,1024]{1,0:T(8,128)(2,1)S(1)}, bf16[128,1024]{1,0:T(8,128)(2,1)S(1)}, u32[]{:S(2)}, u32[]{:S(2)}) %collective-permute-start.20) | collective-permute-done | bytes 262176 | tf_op jit(solution)/shard_map/ppermute | solution.py:279
  77.5 1.5 %finish.1 = (bf16[128,2048]{1,0:T(8,128)(2,1)}, bf16[4,64,512]{2,1,0:T(8,128)(2,1)}) custom-call(bf16[128,1024]{1,0:T(8,128)(2,1)S(1)} %attend.2.kept, bf16[128,1024]{1,0:T(8,128)(2,1)S(1)} %collective-permute-done.20.from_far, bf16[4,64,512]{2,1,0:T(8,128)(2,1)S(1)} %get-tuple-element.72.own_pages, ...), custom_call_target="tpu_custom_call" | custom-call | tf_op jit(solution)/shard_map/finish/pallas_call | solution.py:441
  (50 shorter events, 5.5 us)
Async XLA Ops:
  0.6 5.6 %copy-start.6 = (s32[1,2,16]{2,1,0:T(2,128)S(1)}, s32[1,2,16]{2,1,0:T(2,128)}, u32[]{:S(2)}) copy-start(s32[1,2,16]{2,1,0:T(2,128)} %param.10) | copy-start | bytes 388
  3.0 16.4 %copy-start = (bf16[1,128,2048]{2,1,0:T(8,128)(2,1)S(1)}, bf16[1,128,2048]{2,1,0:T(8,128)(2,1)}, u32[]{:S(2)}) copy-start(bf16[1,128,2048]{2,1,0:T(8,128)(2,1)} %param.7) | copy-start | bytes 1572868
  3.0 8.8 %collective-permute-start = (bf16[2448,128]{1,0:T(8,128)(2,1)}, bf16[2448,128]{1,0:T(8,128)(2,1)S(1)}, u32[]{:S(2)}, u32[]{:S(2)}) collective-permute-start(bf16[2448,128]{1,0:T(8,128)(2,1)} %get-tuple-element.40), channel_id=1, source_target_pairs={{0,1},{1,0},{2,3},{3,2},{4,5},{5,4},{6,7},{7,6},{8,9},{9,8},{10,11... | collective-permute-start | bytes 1880072 | tf_op jit(solution)/shard_map/ppermute | solution.py:279
  3.5 6.6 %collective-permute-start.1 = (bf16[400,128]{1,0:T(8,128)(2,1)}, bf16[400,128]{1,0:T(8,128)(2,1)S(1)}, u32[]{:S(2)}, u32[]{:S(2)}) collective-permute-start(bf16[400,128]{1,0:T(8,128)(2,1)} %get-tuple-element.41), channel_id=1, source_target_pairs={{0,2},{1,3},{2,0},{3,1},{4,6},{5,7},{6,4},{7,5},{8,10},{9,11},{10,... | collective-permute-start | bytes 307208 | tf_op jit(solution)/shard_map/ppermute | solution.py:279
  6.1 5.6 %collective-permute-start.2 = (bf16[400,128]{1,0:T(8,128)(2,1)}, bf16[400,128]{1,0:T(8,128)(2,1)S(1)}, u32[]{:S(2)}, u32[]{:S(2)}) collective-permute-start(bf16[400,128]{1,0:T(8,128)(2,1)} %get-tuple-element.42), channel_id=1, source_target_pairs={{0,3},{1,2},{2,1},{3,0},{4,7},{5,6},{6,5},{7,4},{8,11},{9,10},{10,... | collective-permute-start | bytes 307208 | tf_op jit(solution)/shard_map/ppermute | solution.py:279
  11.8 0.9 %copy-start.1 = (bf16[400,128]{1,0:T(8,128)(2,1)S(1)}, bf16[400,128]{1,0:T(8,128)(2,1)}, u32[]{:S(2)}) copy-start(bf16[400,128]{1,0:T(8,128)(2,1)} %get-tuple-element.39.refs_0_) | copy-start | bytes 307204
  13.6 13.4 %collective-permute-start.4 = (bf16[256,768]{1,0:T(8,128)(2,1)}, bf16[256,768]{1,0:T(8,128)(2,1)S(1)}, u32[]{:S(2)}, u32[]{:S(2)}) collective-permute-start(bf16[256,768]{1,0:T(8,128)(2,1)} %get-tuple-element.48), channel_id=1, source_target_pairs={{0,8},{8,0},{16,24},{24,16},{1,9},{9,1},{17,25},{25,17},{2,10},{10... | collective-permute-start | bytes 1179656 | tf_op jit(solution)/shard_map/ppermute | solution.py:282
  15.1 11.9 %collective-permute-start.5 = (bf16[256,768]{1,0:T(8,128)(2,1)}, bf16[256,768]{1,0:T(8,128)(2,1)S(1)}, u32[]{:S(2)}, u32[]{:S(2)}) collective-permute-start(bf16[256,768]{1,0:T(8,128)(2,1)} %get-tuple-element.48), channel_id=1, source_target_pairs={{0,16},{8,24},{16,0},{24,8},{1,17},{9,25},{17,1},{25,9},{2,18},{10... | collective-permute-start | bytes 1179656 | tf_op jit(solution)/shard_map/ppermute | solution.py:282
  16.6 10.4 %collective-permute-start.3 = (bf16[272,256]{1,0:T(8,128)(2,1)S(1)}, bf16[272,256]{1,0:T(8,128)(2,1)S(1)}, u32[]{:S(2)}, u32[]{:S(2)}) collective-permute-start(bf16[272,256]{1,0:T(8,128)(2,1)S(1)} %get-tuple-element.47.refs_0_), channel_id=1, source_target_pairs={{0,4},{1,5},{2,6},{3,7},{4,0},{5,1},{6,2},{7,3},{8,12},{9,13},{10,... | collective-permute-start | bytes 417800 | tf_op jit(solution)/shard_map/ppermute | solution.py:285
  19.4 20.8 %collective-permute-start.10 = (bf16[128,2048]{1,0:T(8,128)(2,1)S(1)}, bf16[128,2048]{1,0:T(8,128)(2,1)S(1)}, u32[]{:S(2)}, u32[]{:S(2)}) collective-permute-start(bf16[128,2048]{1,0:T(8,128)(2,1)S(1)} %bitcast.33), channel_id=1, source_target_pairs={{0,2},{1,3},{2,0},{3,1},{4,6},{5,7},{6,4},{7,5},{8,10},{9,11},{10,... | collective-permute-start | bytes 1572872 | tf_op jit(solution)/shard_map/ppermute | solution.py:279
  20.9 18.0 %collective-permute-start.9 = (bf16[256,512]{1,0:T(8,128)(2,1)}, bf16[256,512]{1,0:T(8,128)(2,1)}, u32[]{:S(2)}, u32[]{:S(2)}) collective-permute-start(bf16[256,512]{1,0:T(8,128)(2,1)} %get-tuple-element.52.refs_0_), channel_id=1, source_target_pairs={{0,4},{1,5},{2,6},{3,7},{4,0},{5,1},{6,2},{7,3},{8,12},{9,13},{10,... | collective-permute-start | bytes 786440 | tf_op jit(solution)/shard_map/ppermute | solution.py:285
  27.0 13.1 %collective-permute-start.6 = (bf16[272,256]{1,0:T(8,128)(2,1)S(1)}, bf16[272,256]{1,0:T(8,128)(2,1)}, u32[]{:S(2)}, u32[]{:S(2)}) collective-permute-start(bf16[272,256]{1,0:T(8,128)(2,1)S(1)} %collective-permute-done.3.kv_o.refs_1_), channel_id=1, source_target_pairs={{0,8},{8,0},{16,24},{24,16},{1,9},{9,1},{17,25},{25,17},{2,10},{10... | collective-permute-start | bytes 417800 | tf_op jit(solution)/shard_map/ppermute | solution.py:282
  27.6 12.5 %collective-permute-start.8 = (bf16[272,256]{1,0:T(8,128)(2,1)S(1)}, bf16[272,256]{1,0:T(8,128)(2,1)}, u32[]{:S(2)}, u32[]{:S(2)}) collective-permute-start(bf16[272,256]{1,0:T(8,128)(2,1)S(1)} %collective-permute-done.3.kv_o.refs_1_), channel_id=1, source_target_pairs={{0,24},{8,16},{16,8},{24,0},{1,25},{9,17},{17,9},{25,1},{2,26},{10... | collective-permute-start | bytes 417800 | tf_op jit(solution)/shard_map/ppermute | solution.py:282
  30.0 0.7 copy-start.4
  30.7 9.4 %collective-permute-start.7 = (bf16[528,256]{1,0:T(8,128)(2,1)}, bf16[528,256]{1,0:T(8,128)(2,1)S(1)}, u32[]{:S(2)}, u32[]{:S(2)}) collective-permute-start(bf16[528,256]{1,0:T(8,128)(2,1)} %get-tuple-element.51), channel_id=1, source_target_pairs={{0,16},{8,24},{16,0},{24,8},{1,17},{9,25},{17,1},{25,9},{2,18},{10... | collective-permute-start | bytes 811016 | tf_op jit(solution)/shard_map/ppermute | solution.py:282
  40.1 3.1 %copy-start.2 = (f32[256]{0:T(256)S(1)}, f32[256]{0:T(256)}, u32[]{:S(2)}) copy-start(f32[256]{0:T(256)} %param.13) | copy-start | bytes 3076
  40.1 2.0 %collective-permute-start.11 = (bf16[128,2048]{1,0:T(8,128)(2,1)S(1)}, bf16[128,2048]{1,0:T(8,128)(2,1)S(1)}, u32[]{:S(2)}, u32[]{:S(2)}) collective-permute-start(bf16[128,2048]{1,0:T(8,128)(2,1)S(1)} %collective-permute-done.10.far), channel_id=1, source_target_pairs={{0,1},{1,0},{2,3},{3,2},{4,5},{5,4},{6,7},{7,6},{8,9},{9,8},{10,11... | collective-permute-start | bytes 1572872 | tf_op jit(solution)/shard_map/ppermute | solution.py:279
  42.1 8.6 %collective-permute-start.15 = (bf16[256,512]{1,0:T(8,128)(2,1)}, bf16[256,512]{1,0:T(8,128)(2,1)S(1)}, u32[]{:S(2)}, u32[]{:S(2)}) collective-permute-start(bf16[256,512]{1,0:T(8,128)(2,1)} %collective-permute-done.9.refs_1_), channel_id=1, source_target_pairs={{0,8},{8,0},{16,24},{24,16},{1,9},{9,1},{17,25},{25,17},{2,10},{10... | collective-permute-start | bytes 786440 | tf_op jit(solution)/shard_map/ppermute | solution.py:282
  42.7 8.3 %collective-permute-start.16 = (bf16[256,512]{1,0:T(8,128)(2,1)}, bf16[256,512]{1,0:T(8,128)(2,1)S(1)}, u32[]{:S(2)}, u32[]{:S(2)}) collective-permute-start(bf16[256,512]{1,0:T(8,128)(2,1)} %collective-permute-done.9.refs_1_), channel_id=1, source_target_pairs={{0,16},{8,24},{16,0},{24,8},{1,17},{9,25},{17,1},{25,9},{2,18},{10... | collective-permute-start | bytes 786440 | tf_op jit(solution)/shard_map/ppermute | solution.py:282
  43.3 7.7 %copy-start.5 = (bf16[256,512]{1,0:T(8,128)(2,1)S(1)}, bf16[256,512]{1,0:T(8,128)(2,1)}, u32[]{:S(2)}) copy-start(bf16[256,512]{1,0:T(8,128)(2,1)} %copy-done.4) | copy-start | bytes 786436
  45.2 14.5 %collective-permute-start.12 = (bf16[512,256]{1,0:T(8,128)(2,1)S(1)}, bf16[512,256]{1,0:T(8,128)(2,1)S(1)}, u32[]{:S(2)}, u32[]{:S(2)}) collective-permute-start(bf16[512,256]{1,0:T(8,128)(2,1)S(1)} %project_kv.1.refs_0_), channel_id=1, source_target_pairs={{0,4},{1,5},{2,6},{3,7},{4,0},{5,1},{6,2},{7,3},{8,12},{9,13},{10,... | collective-permute-start | bytes 786440 | tf_op jit(solution)/shard_map/ppermute | solution.py:285
  50.9 8.7 %copy-start.3 = (f32[256]{0:T(256)S(1)}, f32[256]{0:T(256)}, u32[]{:S(2)}) copy-start(f32[256]{0:T(256)} %param.12) | copy-start | bytes 3076
  50.9 8.7 %collective-permute-start.17 = (bf16[256,512]{1,0:T(8,128)(2,1)S(1)}, bf16[256,512]{1,0:T(8,128)(2,1)S(1)}, u32[]{:S(2)}, u32[]{:S(2)}) collective-permute-start(bf16[256,512]{1,0:T(8,128)(2,1)S(1)} %copy-done.5), channel_id=1, source_target_pairs={{0,16},{8,24},{16,0},{24,8},{1,17},{9,25},{17,1},{25,9},{2,18},{10... | collective-permute-start | bytes 786440 | tf_op jit(solution)/shard_map/ppermute | solution.py:282
  51.6 8.1 %collective-permute-start.18 = (bf16[256,512]{1,0:T(8,128)(2,1)S(1)}, bf16[256,512]{1,0:T(8,128)(2,1)S(1)}, u32[]{:S(2)}, u32[]{:S(2)}) collective-permute-start(bf16[256,512]{1,0:T(8,128)(2,1)S(1)} %collective-permute-done.16.refs_5_), channel_id=1, source_target_pairs={{0,8},{8,0},{16,24},{24,16},{1,9},{9,1},{17,25},{25,17},{2,10},{10... | collective-permute-start | bytes 786440 | tf_op jit(solution)/shard_map/ppermute | solution.py:282
  52.9 9.9 %collective-permute-start.13 = (bf16[512,256]{1,0:T(8,128)(2,1)S(1)}, bf16[512,256]{1,0:T(8,128)(2,1)S(1)}, u32[]{:S(2)}, u32[]{:S(2)}) collective-permute-start(bf16[512,256]{1,0:T(8,128)(2,1)S(1)} %project_kv.1.refs_0_), channel_id=1, source_target_pairs={{0,1},{1,0},{2,3},{3,2},{4,5},{5,4},{6,7},{7,6},{8,9},{9,8},{10,11... | collective-permute-start | bytes 786440 | tf_op jit(solution)/shard_map/ppermute | solution.py:279
  59.7 3.2 %collective-permute-start.14 = (bf16[512,256]{1,0:T(8,128)(2,1)S(1)}, bf16[512,256]{1,0:T(8,128)(2,1)S(1)}, u32[]{:S(2)}, u32[]{:S(2)}) collective-permute-start(bf16[512,256]{1,0:T(8,128)(2,1)S(1)} %collective-permute-done.12.refs_1_), channel_id=1, source_target_pairs={{0,1},{1,0},{2,3},{3,2},{4,5},{5,4},{6,7},{7,6},{8,9},{9,8},{10,11... | collective-permute-start | bytes 786440 | tf_op jit(solution)/shard_map/ppermute | solution.py:279
  62.3 2.1 %collective-permute-start.19 = (bf16[256,512]{1,0:T(8,128)(2,1)S(1)}, bf16[256,512]{1,0:T(8,128)(2,1)S(1)}, u32[]{:S(2)}, u32[]{:S(2)}) collective-permute-start(bf16[256,512]{1,0:T(8,128)(2,1)S(1)} %get-tuple-element.71), channel_id=1, source_target_pairs={{0,1},{1,0},{2,3},{3,2},{4,5},{5,4},{6,7},{7,6},{8,9},{9,8},{10,11... | collective-permute-start | bytes 786440 | tf_op jit(solution)/shard_map/ppermute | solution.py:279
  63.6 9.2 %collective-permute-start.21 = (bf16[4,64,512]{2,1,0:T(8,128)(2,1)S(1)}, bf16[4,64,512]{2,1,0:T(8,128)(2,1)S(1)}, u32[]{:S(2)}, u32[]{:S(2)}) collective-permute-start(bf16[4,64,512]{2,1,0:T(8,128)(2,1)S(1)} %get-tuple-element.73), channel_id=1, source_target_pairs={{0,2},{1,3},{2,0},{3,1},{4,6},{5,7},{6,4},{7,5},{8,10},{9,11},{10,... | collective-permute-start | bytes 786440 | tf_op jit(solution)/shard_map/ppermute | solution.py:279
  66.4 11.1 %collective-permute-start.20 = (bf16[128,1024]{1,0:T(8,128)(2,1)S(1)}, bf16[128,1024]{1,0:T(8,128)(2,1)S(1)}, u32[]{:S(2)}, u32[]{:S(2)}) collective-permute-start(bf16[128,1024]{1,0:T(8,128)(2,1)S(1)} %attend.3), channel_id=1, source_target_pairs={{0,2},{1,3},{2,0},{3,1},{4,6},{5,7},{6,4},{7,5},{8,10},{9,11},{10,... | collective-permute-start | bytes 786440 | tf_op jit(solution)/shard_map/ppermute | solution.py:279

commit v10 on v9

--- a/solution.py
+++ b/solution.py
@@ -107,15 +107,24 @@
     q_out[...] = w_x[:, HD:]
 
 
-def project_kernel(n_out, depth, tall, starts, first_row, is_kv, own, near, far, far_near, *refs):
-    n_outs = 1 if is_kv else 2
+def join_kernel(first, second, out):
+    rows = first.shape[0]
+    out[:rows, :] = first[...]
+    out[rows:, :] = second[...]
+
+
+def project_kernel(n_out, depth, tall, starts, first_row, sets, is_kv, *refs):
+    n_outs = len(sets)
+    n_tokens = sum(len(steps) for steps in sets)
+    tokens = dict(zip(sorted(sum(sets, ())), refs[:n_tokens]))
+    refs = refs[n_tokens:]
     weights, (gain_ref, cos_ref, sin_ref) = refs[: -5 - n_outs], refs[-5 - n_outs : -2 - n_outs]
     outs, (w_all, sems) = refs[-2 - n_outs : -2], refs[-2:]
     req = lax.axis_index("req")
     outer = lax.axis_index("blk") // TEAM
     _, pair, core = place()
     member = pair * 2 + core
-    rows = own.shape[0]
+    rows = tokens[0].shape[0] if 0 in tokens else tokens[2].shape[0]
     width = outs[0].shape[1]
     direct = depth % LANES == 0
     places = []
@@ -135,15 +144,15 @@
     gain = gain_ref[...]
     if is_kv:
         gain = jnp.where(core == 0, gain, 1.0)
-    for out, steps in zip(outs, [(0, 1, 2, 3)] if is_kv else [(1, 3), (0, 2)]):
+    for out, steps in zip(outs, sets):
 
         def token_rows(k, start, size):
             if k != 1:
-                return (own, None, far, far_near)[k][:, pl.ds(start, size)]
+                return tokens[k][:, pl.ds(start, size)]
             blocks = []
             for n in range(size // LANES):
                 first = pl.multiple_of(first_row + (start // LANES + n) * rows, 16)
-                blocks.append(near[pl.ds(first, rows), :])
+                blocks.append(tokens[k][pl.ds(first, rows), :])
             return jnp.concatenate(blocks, 1)
 
         def team_rows(start, size):
@@ -170,7 +179,7 @@
             turned = jnp.concatenate([front * cosine - second * sine, second * cosine + front * sine], 1)
             turned = turned.astype(jnp.bfloat16)
             for n, k in enumerate(steps):
-                there = aligned(member ^ k if is_kv else n, rows)
+                there = aligned((member ^ k) % 2 if is_kv else n, rows)
                 out[there, h * HD : (h + 1) * HD] = turned[n * rows : (n + 1) * rows]
 
 
@@ -219,16 +228,19 @@
 
 
 def pages_kernel(n_out, blk_rows, *refs):
-    mine, other = refs[:n_out], refs[n_out : 2 * n_out]
-    ids_ref, info_ref, own, away, store = refs[2 * n_out :]
-    _, _, core = place()
-    per_piece = mine[0].shape[0] // blk_rows
-    for k in range(n_out):
-        for j in range(per_piece):
-            there = aligned(ids_ref[k * per_piece + j], blk_rows)
+    mine, other = refs[: 2 * n_out], refs[2 * n_out : 4 * n_out - 1]
+    ids_ref, info_ref, own, away, store = refs[4 * n_out - 1 :]
+    _, pair, core = place()
+    per_half = mine[0].shape[0] // blk_rows
+    for n in range(2 * n_out):
+        side = pair if n % 2 == 0 else 1 - pair
+        for j in range(per_half):
+            there = aligned(ids_ref[(n // 2 * 2 + side) * per_half + j], blk_rows)
             here = slice(j * blk_rows, (j + 1) * blk_rows)
-            store[core, there, :] = mine[k][here, :]
-            store[1 - core, there, :] = other[k][here, :]
+            store[core, there, :] = mine[n][here, :]
+            if n < 2:
+                here = slice((n * per_half + j) * blk_rows, (n * per_half + j + 1) * blk_rows)
+            store[1 - core, there, :] = other[max(n - 1, 0)][here, :]
     slots = own.shape[0]
     row = lax.broadcasted_iota(jnp.int32, (blk_rows, HD), 0)
     for target, base in ((away, slots), (own, 0)):
@@ -368,44 +380,52 @@
     kv_ox, kv_oy_d, kv_od, q_o, far, cosine, sine, all_ids, info = sync(
         kv_ox, kv_oy_d, kv_od, q_o, far, cosine, sine, all_ids, info
     )
-    far_near = in_team(far, 1)
-    far_near, q_o = sync(far_near, q_o)
-    q_ox, q_oy = in_req(q_o, 1), in_req(q_o, 2)
+    far_near, q_ox, q_oy = in_team(far, 1), in_req(q_o, 1), in_req(q_o, 2)
+    team_tokens = [own, got[1], far, far_near]
     kv_weight = [(kv, 0, 0), (kv_o, 0, 0), (w_x, 0, 0), (kv_ox, 0, 0)]
     kv_weight += [(w_y, 0, 0), (kv_oy_d, 0, 0), (kv_oy_d, others, 0), (kv_od, 0, 0)]
 
-    def project(weight, is_kv, gain):
+    def project(weight, sets, is_kv, gain):
         starts = [part[1:] for part in weight]
         weight = [part[0] for part in weight]
         width = weight[1].shape[1]
         step = weight[1].shape[0] // (n_out - 1)
         depth = own.shape[1]
-        n_outs = 1 if is_kv else 2
+        n_outs = len(sets)
+        used = [team_tokens[k] for k in sorted(sum(sets, ()))]
         return pl.pallas_call(
-            functools.partial(project_kernel, n_out, TEAM * w_rows, step, starts, packed_rows, is_kv),
-            out_shape=[shape((TEAM * rows // n_outs, width), bf16)] * n_outs,
-            in_specs=[VMEM] * (7 + len(weight)),
+            functools.partial(project_kernel, n_out, TEAM * w_rows, step, starts, packed_rows, sets, is_kv),
+            out_shape=[shape((2 * rows, width), bf16)] * n_outs,
+            in_specs=[VMEM] * (3 + len(used) + len(weight)),
             out_specs=[VMEM] * n_outs,
             scratch_shapes=[
                 pltpu.VMEM((depth, width) if w_rows * TEAM % LANES else (ID_ROWS, LANES), bf16),
                 pltpu.SemaphoreType.DMA((n_req * n_out,)),
             ],
             cost_estimate=pl.CostEstimate(
-                flops=2 * TEAM * rows * depth * width, bytes_accessed=6 * MIB, transcendentals=0
+                flops=2 * len(used) * rows * depth * width, bytes_accessed=6 * MIB, transcendentals=0
             ),
             compiler_params=params(4 if w_rows * TEAM % LANES == 0 else 12),
             name="project_kv" if is_kv else "project_q",
-        )(own, got[1], far, far_near, *weight, gain[None, :], cosine, sine)
-
-    (made,) = project(kv_weight, True, k_gain)
-    q_ox, q_oy, q_x = sync(q_ox, q_oy, q_x)
+        )(*used, *weight, gain[None, :], cosine, sine)
+
+    halves = [project(kv_weight, [steps], True, k_gain)[0] for steps in ((0, 1), (2, 3))]
+    mine = halves + [across(half, k) for k in range(1, n_out) for half in halves]
+    q_ox, q_oy, q_x, mine[2], halves[1] = sync(q_ox, q_oy, q_x, mine[2], halves[1])
     q_od, q_d = in_req(q_oy, 1), in_req(q_x, 2)
     q_weight = [(q, 0, 0), (q_o, 0, 0), (w_x, 0, HD), (q_ox, 0, 0)]
     q_weight += [(w_y, 0, HD), (q_oy, 0, 0), (q_d, 0, 0), (q_od, 0, 0)]
-    mine = [made] + [across(made, k) for k in range(1, n_out)]
-    other = [in_team(part, 1) for part in mine]
-
-    to_near, queries = project(q_weight, False, q_gain)
+    made = pl.pallas_call(
+        join_kernel,
+        out_shape=shape((TEAM * rows, HD), bf16),
+        in_specs=[VMEM] * 2,
+        out_specs=VMEM,
+        compiler_params=params(1),
+        name="join",
+    )(*halves)
+    other = [in_team(made, 1)] + [in_team(half, 1) for half in mine[2:]]
+
+    to_near, queries = project(q_weight, [(1, 3), (0, 2)], False, q_gain)
     from_near = in_team(to_near, 1)
 
     total = TEAM * rows * n_out
@@ -414,7 +434,7 @@
     own_pages, away_pages, store = pl.pallas_call(
         functools.partial(pages_kernel, n_out, blk_rows),
         out_shape=[page_shape, page_shape, shape((2, total, HD), bf16)],
-        in_specs=[VMEM] * (2 * n_out) + [SMEM] * 2,
+        in_specs=[VMEM] * (4 * n_out - 1) + [SMEM] * 2,
         out_specs=[VMEM] * 3,
         cost_estimate=pl.CostEstimate(flops=0, bytes_accessed=4 * MIB, transcendentals=0),
         compiler_params=params(store_mib + 1),

time: 79.2 us -> 81.7 us (1.032)
  Pallas kernels: 14.8 us -> 16.1 us
  starting transfers between devices: 23 us -> 24 us
    ppermute x9, waiting for transfers between devices: 2.95 us -> 5.43 us  [in_req(): return lax.ppermute(array, 'req', [(i, i ^ k) for i in range(n_req)])]
    ppermute x3 -> x4, waiting for transfers between devices: 18.4 us -> 16.5 us  [across(): lax.ppermute(array, 'blk', [(i, (i + TEAM * k) % n_blk) for i in range(n_...]
    pallas_call x2 -> x3, Pallas kernels: 4.53 us -> 5.8 us  [project(): pl.pallas_call(functools.partial(project_kernel, n_out, TEAM * w_rows, st...]
    ppermute x9, starting transfers between devices: 9.64 us -> 10.5 us  [in_req(): return lax.ppermute(array, 'req', [(i, i ^ k) for i in range(n_req)])]
    ppermute x10 -> x11, waiting for transfers between devices: 15.2 us -> 14.8 us  [in_team(): return lax.ppermute(array, 'blk', [(i, i ^ k) for i in range(n_blk)])]
    ppermute x10 -> x11, starting transfers between devices: 7.61 us -> 7.75 us  [in_team(): return lax.ppermute(array, 'blk', [(i, i ^ k) for i in range(n_blk)])]
    ppermute x3 -> x4, starting transfers between devices: 5.73 us -> 5.73 us  [across(): lax.ppermute(array, 'blk', [(i, (i + TEAM * k) % n_blk) for i in range(n_...]
  transfers between devices with their start and end apart: 22 -> 24, of which waited for: 11 -> 12; matrix products, arithmetic and copies ran while one was open for 2% -> 2% of each run, Pallas kernels for 13% -> 14%
where the time goes in v10:
time: 81.7 us; the launch traced here: 81.5 us
  waiting for transfers between devices  36.7 us (45%)
  starting transfers between devices  24 us (29%)
  Pallas kernels  16.1 us (20%)
  local copies, waits for them, and re-layouts  1.87 us (2%)
  between operations  1.48 us (2%)
  other arithmetic  1.38 us (2%)
    ppermute x4, waiting for transfers between devices, across(): lax.ppermute(array, 'blk', [(i, (i + TEAM * k) % n_blk) for i in range(n_...  16.5 us
    ppermute x11, waiting for transfers between devices, in_team(): return lax.ppermute(array, 'blk', [(i, i ^ k) for i in range(n_blk)])  14.8 us
    ppermute x9, starting transfers between devices, in_req(): return lax.ppermute(array, 'req', [(i, i ^ k) for i in range(n_req)])  10.5 us
    ppermute x11, starting transfers between devices, in_team(): return lax.ppermute(array, 'blk', [(i, i ^ k) for i in range(n_blk)])  7.75 us
    pallas_call x3, Pallas kernels, project(): pl.pallas_call(functools.partial(project_kernel, n_out, TEAM * w_rows, st...  5.8 us
    ppermute x4, starting transfers between devices, across(): lax.ppermute(array, 'blk', [(i, (i + TEAM * k) % n_blk) for i in range(n_...  5.73 us
    ppermute x9, waiting for transfers between devices, in_req(): return lax.ppermute(array, 'req', [(i, i ^ k) for i in range(n_req)])  5.43 us
    pallas_call x2, Pallas kernels, attend(): pl.pallas_call(functools.partial(attend_kernel, blk_rows, step), out_shap...  4.05 us
  transfers between devices with their start and end apart: 24, of which 12 were waited for; matrix products, arithmetic and copies ran while one was open for 2% of the time, Pallas kernels for 14%

profile of v10, /device:TPU:0, one launch (start us, length us, event | category | flops | bytes accessed | tf_op | source)
XLA Modules:
  0.0 81.5 jit_solution(17933487111434623181)
XLA Ops:
  0.6 2.3 %pack.1 = (bf16[400,128]{1,0:T(8,128)(2,1)}, bf16[2448,128]{1,0:T(8,128)(2,1)}, bf16[400,128]{1,0:T(8,128)(2,1)}, bf16[400,128]{1,0:T(8,128)(2,1)}) custom-call(bf16[64,3072]{1,0:T(8,128)(2,1)} %w_hbm.1, s32[1,2]{1,0:T(1,128)} %ids_hbm.1, bf16[128,2048]{1,0:T(8,128)(2,1)} %bitcast.32), custom_call_target="tpu_custom_call" | custom-call | tf_op jit(solution)/shard_map/pack/pallas_call | solution.py:307
  3.5 2.7 %collective-permute-start.1 = (bf16[400,128]{1,0:T(8,128)(2,1)}, bf16[400,128]{1,0:T(8,128)(2,1)S(1)}, u32[]{:S(2)}, u32[]{:S(2)}) collective-permute-start(bf16[400,128]{1,0:T(8,128)(2,1)} %get-tuple-element.41), channel_id=1, source_target_pairs={{0,2},{1,3},{2,0},{3,1},{4,6},{5,7},{6,4},{7,5},{8,10},{9,11},{10,... | collective-permute-start | bytes 307208 | tf_op jit(solution)/shard_map/ppermute | solution.py:291
  7.2 2.8 %collective-permute-done.1.refs_2_ = bf16[400,128]{1,0:T(8,128)(2,1)S(1)} collective-permute-done((bf16[400,128]{1,0:T(8,128)(2,1)}, bf16[400,128]{1,0:T(8,128)(2,1)S(1)}, u32[]{:S(2)}, u32[]{:S(2)}) %collective-permute-start.1) | collective-permute-done | bytes 102432 | tf_op jit(solution)/shard_map/ppermute | solution.py:291
  10.1 1.7 %collective-permute-done.2.refs_3_ = bf16[400,128]{1,0:T(8,128)(2,1)S(1)} collective-permute-done((bf16[400,128]{1,0:T(8,128)(2,1)}, bf16[400,128]{1,0:T(8,128)(2,1)S(1)}, u32[]{:S(2)}, u32[]{:S(2)}) %collective-permute-start.2) | collective-permute-done | bytes 102432 | tf_op jit(solution)/shard_map/ppermute | solution.py:291
  11.7 0.9 %copy-done.1 = bf16[400,128]{1,0:T(8,128)(2,1)S(1)} copy-done((bf16[400,128]{1,0:T(8,128)(2,1)S(1)}, bf16[400,128]{1,0:T(8,128)(2,1)}, u32[]{:S(2)}) %copy-start.1) | copy-done | bytes 102424
  12.6 1.0 %team.1 = (bf16[272,256]{1,0:T(8,128)(2,1)S(1)}, bf16[256,512]{1,0:T(8,128)(2,1)}, bf16[256,768]{1,0:T(8,128)(2,1)}) custom-call(bf16[400,128]{1,0:T(8,128)(2,1)S(1)} %copy-done.1, bf16[2448,128]{1,0:T(8,128)(2,1)S(1)} %collective-permute-done.refs_1_, bf16[400,128]{1,0:T(8,128)(2,1)S(1)} %collective-permute-done.1.refs_2_, ...), custom_call_target="tpu_custom_call" | custom-call | tf_op jit(solution)/shard_map/team/pallas_call | solution.py:324
  13.6 1.5 %collective-permute-start.4 = (bf16[256,768]{1,0:T(8,128)(2,1)}, bf16[256,768]{1,0:T(8,128)(2,1)S(1)}, u32[]{:S(2)}, u32[]{:S(2)}) collective-permute-start(bf16[256,768]{1,0:T(8,128)(2,1)} %get-tuple-element.48), channel_id=1, source_target_pairs={{0,8},{8,0},{16,24},{24,16},{1,9},{9,1},{17,25},{25,17},{2,10},{10... | collective-permute-start | bytes 1179656 | tf_op jit(solution)/shard_map/ppermute | solution.py:294
  15.1 1.5 %collective-permute-start.5 = (bf16[256,768]{1,0:T(8,128)(2,1)}, bf16[256,768]{1,0:T(8,128)(2,1)S(1)}, u32[]{:S(2)}, u32[]{:S(2)}) collective-permute-start(bf16[256,768]{1,0:T(8,128)(2,1)} %get-tuple-element.48), channel_id=1, source_target_pairs={{0,16},{8,24},{16,0},{24,8},{1,17},{9,25},{17,1},{25,9},{2,18},{10... | collective-permute-start | bytes 1179656 | tf_op jit(solution)/shard_map/ppermute | solution.py:294
  16.6 2.6 %collective-permute-start.3 = (bf16[272,256]{1,0:T(8,128)(2,1)S(1)}, bf16[272,256]{1,0:T(8,128)(2,1)S(1)}, u32[]{:S(2)}, u32[]{:S(2)}) collective-permute-start(bf16[272,256]{1,0:T(8,128)(2,1)S(1)} %get-tuple-element.47.refs_2_), channel_id=1, source_target_pairs={{0,4},{1,5},{2,6},{3,7},{4,0},{5,1},{6,2},{7,3},{8,12},{9,13},{10,... | collective-permute-start | bytes 417800 | tf_op jit(solution)/shard_map/ppermute | solution.py:297
  19.3 1.6 %collective-permute-start.10 = (bf16[128,2048]{1,0:T(8,128)(2,1)S(1)}, bf16[128,2048]{1,0:T(8,128)(2,1)S(1)}, u32[]{:S(2)}, u32[]{:S(2)}) collective-permute-start(bf16[128,2048]{1,0:T(8,128)(2,1)S(1)} %bitcast.33), channel_id=1, source_target_pairs={{0,2},{1,3},{2,0},{3,1},{4,6},{5,7},{6,4},{7,5},{8,10},{9,11},{10,... | collective-permute-start | bytes 1572872 | tf_op jit(solution)/shard_map/ppermute | solution.py:291
  21.3 1.0 %multiply_sine_fusion = (f32[512,128]{1,0:T(8,128)S(1)}, f32[512,128]{1,0:T(8,128)S(1)}) fusion(f32[128]{0:T(128)S(1)} %multiply_power_fusion, f32[512]{0:T(512)S(1)} %convert_element_type.37), kind=kLoop, calls=%fused_computation | loop fusion | flops 65536 | bytes 526848 | tf_op jit(solution)/shard_map/sin | solution.py:355
  22.3 4.8 %collective-permute-done.3.kv_o.refs_3_ = bf16[272,256]{1,0:T(8,128)(2,1)S(1)} collective-permute-done((bf16[272,256]{1,0:T(8,128)(2,1)S(1)}, bf16[272,256]{1,0:T(8,128)(2,1)S(1)}, u32[]{:S(2)}, u32[]{:S(2)}) %collective-permute-start.3) | collective-permute-done | bytes 139296 | tf_op jit(solution)/shard_map/ppermute | solution.py:297
  27.6 1.7 %collective-permute-start.8 = (bf16[272,256]{1,0:T(8,128)(2,1)S(1)}, bf16[272,256]{1,0:T(8,128)(2,1)}, u32[]{:S(2)}, u32[]{:S(2)}) collective-permute-start(bf16[272,256]{1,0:T(8,128)(2,1)S(1)} %collective-permute-done.3.kv_o.refs_3_), channel_id=1, source_target_pairs={{0,24},{8,16},{16,8},{24,0},{1,25},{9,17},{17,9},{25,1},{2,26},{10... | collective-permute-start | bytes 417800 | tf_op jit(solution)/shard_map/ppermute | solution.py:294
  30.7 1.2 %collective-permute-start.7 = (bf16[528,256]{1,0:T(8,128)(2,1)}, bf16[528,256]{1,0:T(8,128)(2,1)S(1)}, u32[]{:S(2)}, u32[]{:S(2)}) collective-permute-start(bf16[528,256]{1,0:T(8,128)(2,1)} %get-tuple-element.51), channel_id=1, source_target_pairs={{0,16},{8,24},{16,0},{24,8},{1,17},{9,25},{17,1},{25,9},{2,18},{10... | collective-permute-start | bytes 811016 | tf_op jit(solution)/shard_map/ppermute | solution.py:294
  32.1 6.9 %collective-permute-done.9.refs_5_ = bf16[256,512]{1,0:T(8,128)(2,1)} collective-permute-done((bf16[256,512]{1,0:T(8,128)(2,1)}, bf16[256,512]{1,0:T(8,128)(2,1)}, u32[]{:S(2)}, u32[]{:S(2)}) %collective-permute-start.9) | collective-permute-done | bytes 262176 | tf_op jit(solution)/shard_map/ppermute | solution.py:297
  39.0 1.1 %collective-permute-done.10.refs_0_.refs_2_ = bf16[128,2048]{1,0:T(8,128)(2,1)S(1)} collective-permute-done((bf16[128,2048]{1,0:T(8,128)(2,1)S(1)}, bf16[128,2048]{1,0:T(8,128)(2,1)S(1)}, u32[]{:S(2)}, u32[]{:S(2)}) %collective-permute-start.10) | collective-permute-done | bytes 524320 | tf_op jit(solution)/shard_map/ppermute | solution.py:291
  41.4 1.6 %project_kv.2.first.refs_0_ = bf16[256,256]{1,0:T(8,128)(2,1)S(1)} custom-call(bf16[128,2048]{1,0:T(8,128)(2,1)S(1)} %bitcast.34, bf16[2448,128]{1,0:T(8,128)(2,1)S(1)} %collective-permute-done.refs_1_, bf16[272,256]{1,0:T(8,128)(2,1)S(1)} %get-tuple-element.47.refs_2_, bf16[272,256]{1,0:T(8,128)(2,1)S(1)} %collective-permute-done.3.kv_o.refs_3_, ...), custom_call_target="tpu_custom_call" | custom-call | flops 268435456 | bytes 6291456 | tf_op jit(solution)/shard_map/project_kv/pallas_call | solution.py:396
  43.0 2.8 %collective-permute-start.14 = (bf16[256,256]{1,0:T(8,128)(2,1)S(1)}, bf16[256,256]{1,0:T(8,128)(2,1)S(1)}, u32[]{:S(2)}, u32[]{:S(2)}) collective-permute-start(bf16[256,256]{1,0:T(8,128)(2,1)S(1)} %project_kv.2.first.refs_0_), channel_id=1, source_target_pairs={{0,4},{1,5},{2,6},{3,7},{4,0},{5,1},{6,2},{7,3},{8,12},{9,13},{10,... | collective-permute-start | bytes 393224 | tf_op jit(solution)/shard_map/ppermute | solution.py:297
  45.8 1.6 %project_kv.3.second.refs_1_ = bf16[256,256]{1,0:T(8,128)(2,1)S(1)} custom-call(bf16[128,2048]{1,0:T(8,128)(2,1)S(1)} %collective-permute-done.10.refs_0_.refs_2_, bf16[128,2048]{1,0:T(8,128)(2,1)S(1)} %collective-permute-done.11.refs_1_.refs_3_, bf16[272,256]{1,0:T(8,128)(2,1)S(1)} %get-tuple-element.47.refs_2_, ...), custom_call_target="tpu_custom_call" | custom-call | flops 268435456 | bytes 6291456 | tf_op jit(solution)/shard_map/project_kv/pallas_call | solution.py:396
  47.4 4.8 %collective-permute-done.14.refs_2_ = bf16[256,256]{1,0:T(8,128)(2,1)S(1)} collective-permute-done((bf16[256,256]{1,0:T(8,128)(2,1)S(1)}, bf16[256,256]{1,0:T(8,128)(2,1)S(1)}, u32[]{:S(2)}, u32[]{:S(2)}) %collective-permute-start.14) | collective-permute-done | bytes 131104 | tf_op jit(solution)/shard_map/ppermute | solution.py:297
  52.2 1.4 %collective-permute-start.19 = (bf16[256,512]{1,0:T(8,128)(2,1)S(1)}, bf16[256,512]{1,0:T(8,128)(2,1)S(1)}, u32[]{:S(2)}, u32[]{:S(2)}) collective-permute-start(bf16[256,512]{1,0:T(8,128)(2,1)S(1)} %copy-done.5), channel_id=1, source_target_pairs={{0,16},{8,24},{16,0},{24,8},{1,17},{9,25},{17,1},{25,9},{2,18},{10... | collective-permute-start | bytes 786440 | tf_op jit(solution)/shard_map/ppermute | solution.py:294
  53.6 1.5 %collective-permute-start.20 = (bf16[256,512]{1,0:T(8,128)(2,1)S(1)}, bf16[256,512]{1,0:T(8,128)(2,1)S(1)}, u32[]{:S(2)}, u32[]{:S(2)}) collective-permute-start(bf16[256,512]{1,0:T(8,128)(2,1)S(1)} %collective-permute-done.13.refs_9_), channel_id=1, source_target_pairs={{0,8},{8,0},{16,24},{24,16},{1,9},{9,1},{17,25},{25,17},{2,10},{10... | collective-permute-start | bytes 786440 | tf_op jit(solution)/shard_map/ppermute | solution.py:294
  55.2 4.5 %collective-permute-done.19.refs_10_ = bf16[256,512]{1,0:T(8,128)(2,1)S(1)} collective-permute-done((bf16[256,512]{1,0:T(8,128)(2,1)S(1)}, bf16[256,512]{1,0:T(8,128)(2,1)S(1)}, u32[]{:S(2)}, u32[]{:S(2)}) %collective-permute-start.19) | collective-permute-done | bytes 262176 | tf_op jit(solution)/shard_map/ppermute | solution.py:294
  59.7 1.0 %collective-permute-done.20.refs_11_ = bf16[256,512]{1,0:T(8,128)(2,1)S(1)} collective-permute-done((bf16[256,512]{1,0:T(8,128)(2,1)S(1)}, bf16[256,512]{1,0:T(8,128)(2,1)S(1)}, u32[]{:S(2)}, u32[]{:S(2)}) %collective-permute-start.20) | collective-permute-done | bytes 262176 | tf_op jit(solution)/shard_map/ppermute | solution.py:294
  60.6 2.6 %project_q.1 = (bf16[256,512]{1,0:T(8,128)(2,1)S(1)}, bf16[256,512]{1,0:T(8,128)(2,1)S(1)}) custom-call(bf16[128,2048]{1,0:T(8,128)(2,1)S(1)} %bitcast.35, bf16[2448,128]{1,0:T(8,128)(2,1)S(1)} %collective-permute-done.refs_1_, bf16[128,2048]{1,0:T(8,128)(2,1)S(1)} %collective-permute-done.10.refs_0_.refs_2_, ...), custom_call_target="tpu_custom_call" | custom-call | flops 1073741824 | bytes 6291456 | tf_op jit(solution)/shard_map/project_q/pallas_call | solution.py:396
  63.9 1.1 %collective-permute-done.17.refs_5_ = bf16[256,256]{1,0:T(8,128)(2,1)S(1)} collective-permute-done((bf16[256,256]{1,0:T(8,128)(2,1)S(1)}, bf16[256,256]{1,0:T(8,128)(2,1)S(1)}, u32[]{:S(2)}, u32[]{:S(2)}) %collective-permute-start.17) | collective-permute-done | bytes 131104 | tf_op jit(solution)/shard_map/ppermute | solution.py:291
  65.9 1.4 %collective-permute-start.23 = (bf16[4,64,512]{2,1,0:T(8,128)(2,1)S(1)}, bf16[4,64,512]{2,1,0:T(8,128)(2,1)S(1)}, u32[]{:S(2)}, u32[]{:S(2)}) collective-permute-start(bf16[4,64,512]{2,1,0:T(8,128)(2,1)S(1)} %get-tuple-element.73), channel_id=1, source_target_pairs={{0,2},{1,3},{2,0},{3,1},{4,6},{5,7},{6,4},{7,5},{8,10},{9,11},{10,... | collective-permute-start | bytes 786440 | tf_op jit(solution)/shard_map/ppermute | solution.py:291
  67.4 2.0 %attend.3 = bf16[128,1024]{1,0:T(8,128)(2,1)S(1)} custom-call(bf16[2,1024,256]{2,1,0:T(8,128)(2,1)S(1)} %get-tuple-element.66.store, bf16[256,512]{1,0:T(8,128)(2,1)S(1)} %get-tuple-element.70.q_ref, bf16[256,512]{1,0:T(8,128)(2,1)S(1)} %collective-permute-done.21.near_ref, s32[16]{0:T(128)S(1)} %reshape.141.refs_7_.ids_ref, s32[1]{0:T(128)} %copy.9.length_ref), custom_call_target="tpu_custom_call" | custom-call | flops 536870912 | bytes 4194304 | tf_op jit(solution)/shard_map/attend/pallas_call | solution.py:446
  70.1 2.0 %attend.2.kept = bf16[128,1024]{1,0:T(8,128)(2,1)S(1)} custom-call(bf16[2,1024,256]{2,1,0:T(8,128)(2,1)S(1)} %get-tuple-element.66.store, bf16[256,512]{1,0:T(8,128)(2,1)S(1)} %get-tuple-element.70.q_ref, bf16[256,512]{1,0:T(8,128)(2,1)S(1)} %collective-permute-done.21.near_ref, s32[16]{0:T(128)S(1)} %reshape.141.refs_7_.ids_ref, s32[1]{0:T(128)} %copy.9.length_ref), custom_call_target="tpu_custom_call" | custom-call | flops 536870912 | bytes 4194304 | tf_op jit(solution)/shard_map/attend/pallas_call | solution.py:446
  72.2 3.0 %collective-permute-done.23.got_pages = bf16[4,64,512]{2,1,0:T(8,128)(2,1)S(1)} collective-permute-done((bf16[4,64,512]{2,1,0:T(8,128)(2,1)S(1)}, bf16[4,64,512]{2,1,0:T(8,128)(2,1)S(1)}, u32[]{:S(2)}, u32[]{:S(2)}) %collective-permute-start.23) | collective-permute-done | bytes 262176 | tf_op jit(solution)/shard_map/ppermute | solution.py:291
  75.2 4.8 %collective-permute-done.22.from_far = bf16[128,1024]{1,0:T(8,128)(2,1)S(1)} collective-permute-done((bf16[128,1024]{1,0:T(8,128)(2,1)S(1)}, bf16[128,1024]{1,0:T(8,128)(2,1)S(1)}, u32[]{:S(2)}, u32[]{:S(2)}) %collective-permute-start.22) | collective-permute-done | bytes 262176 | tf_op jit(solution)/shard_map/ppermute | solution.py:291
  80.0 1.5 %finish.1 = (bf16[128,2048]{1,0:T(8,128)(2,1)}, bf16[4,64,512]{2,1,0:T(8,128)(2,1)}) custom-call(bf16[128,1024]{1,0:T(8,128)(2,1)S(1)} %attend.2.kept, bf16[128,1024]{1,0:T(8,128)(2,1)S(1)} %collective-permute-done.22.from_far, bf16[4,64,512]{2,1,0:T(8,128)(2,1)S(1)} %get-tuple-element.72.own_pages, ...), custom_call_target="tpu_custom_call" | custom-call | tf_op jit(solution)/shard_map/finish/pallas_call | solution.py:461
  (56 shorter events, 7.2 us)
Async XLA Ops:
  0.6 5.6 %copy-start.6 = (s32[1,2,16]{2,1,0:T(2,128)S(1)}, s32[1,2,16]{2,1,0:T(2,128)}, u32[]{:S(2)}) copy-start(s32[1,2,16]{2,1,0:T(2,128)} %param.10) | copy-start | bytes 388
  2.9 16.4 %copy-start = (bf16[1,128,2048]{2,1,0:T(8,128)(2,1)S(1)}, bf16[1,128,2048]{2,1,0:T(8,128)(2,1)}, u32[]{:S(2)}) copy-start(bf16[1,128,2048]{2,1,0:T(8,128)(2,1)} %param.7) | copy-start | bytes 1572868
  2.9 8.8 %collective-permute-start = (bf16[2448,128]{1,0:T(8,128)(2,1)}, bf16[2448,128]{1,0:T(8,128)(2,1)S(1)}, u32[]{:S(2)}, u32[]{:S(2)}) collective-permute-start(bf16[2448,128]{1,0:T(8,128)(2,1)} %get-tuple-element.40), channel_id=1, source_target_pairs={{0,1},{1,0},{2,3},{3,2},{4,5},{5,4},{6,7},{7,6},{8,9},{9,8},{10,11... | collective-permute-start | bytes 1880072 | tf_op jit(solution)/shard_map/ppermute | solution.py:291
  3.5 6.6 %collective-permute-start.1 = (bf16[400,128]{1,0:T(8,128)(2,1)}, bf16[400,128]{1,0:T(8,128)(2,1)S(1)}, u32[]{:S(2)}, u32[]{:S(2)}) collective-permute-start(bf16[400,128]{1,0:T(8,128)(2,1)} %get-tuple-element.41), channel_id=1, source_target_pairs={{0,2},{1,3},{2,0},{3,1},{4,6},{5,7},{6,4},{7,5},{8,10},{9,11},{10,... | collective-permute-start | bytes 307208 | tf_op jit(solution)/shard_map/ppermute | solution.py:291
  6.1 5.6 %collective-permute-start.2 = (bf16[400,128]{1,0:T(8,128)(2,1)}, bf16[400,128]{1,0:T(8,128)(2,1)S(1)}, u32[]{:S(2)}, u32[]{:S(2)}) collective-permute-start(bf16[400,128]{1,0:T(8,128)(2,1)} %get-tuple-element.42), channel_id=1, source_target_pairs={{0,3},{1,2},{2,1},{3,0},{4,7},{5,6},{6,5},{7,4},{8,11},{9,10},{10,... | collective-permute-start | bytes 307208 | tf_op jit(solution)/shard_map/ppermute | solution.py:291
  11.7 0.9 %copy-start.1 = (bf16[400,128]{1,0:T(8,128)(2,1)S(1)}, bf16[400,128]{1,0:T(8,128)(2,1)}, u32[]{:S(2)}) copy-start(bf16[400,128]{1,0:T(8,128)(2,1)} %get-tuple-element.39.refs_0_) | copy-start | bytes 307204
  13.6 13.4 %collective-permute-start.4 = (bf16[256,768]{1,0:T(8,128)(2,1)}, bf16[256,768]{1,0:T(8,128)(2,1)S(1)}, u32[]{:S(2)}, u32[]{:S(2)}) collective-permute-start(bf16[256,768]{1,0:T(8,128)(2,1)} %get-tuple-element.48), channel_id=1, source_target_pairs={{0,8},{8,0},{16,24},{24,16},{1,9},{9,1},{17,25},{25,17},{2,10},{10... | collective-permute-start | bytes 1179656 | tf_op jit(solution)/shard_map/ppermute | solution.py:294
  15.1 11.9 %collective-permute-start.5 = (bf16[256,768]{1,0:T(8,128)(2,1)}, bf16[256,768]{1,0:T(8,128)(2,1)S(1)}, u32[]{:S(2)}, u32[]{:S(2)}) collective-permute-start(bf16[256,768]{1,0:T(8,128)(2,1)} %get-tuple-element.48), channel_id=1, source_target_pairs={{0,16},{8,24},{16,0},{24,8},{1,17},{9,25},{17,1},{25,9},{2,18},{10... | collective-permute-start | bytes 1179656 | tf_op jit(solution)/shard_map/ppermute | solution.py:294
  16.6 10.4 %collective-permute-start.3 = (bf16[272,256]{1,0:T(8,128)(2,1)S(1)}, bf16[272,256]{1,0:T(8,128)(2,1)S(1)}, u32[]{:S(2)}, u32[]{:S(2)}) collective-permute-start(bf16[272,256]{1,0:T(8,128)(2,1)S(1)} %get-tuple-element.47.refs_2_), channel_id=1, source_target_pairs={{0,4},{1,5},{2,6},{3,7},{4,0},{5,1},{6,2},{7,3},{8,12},{9,13},{10,... | collective-permute-start | bytes 417800 | tf_op jit(solution)/shard_map/ppermute | solution.py:297
  19.3 20.8 %collective-permute-start.10 = (bf16[128,2048]{1,0:T(8,128)(2,1)S(1)}, bf16[128,2048]{1,0:T(8,128)(2,1)S(1)}, u32[]{:S(2)}, u32[]{:S(2)}) collective-permute-start(bf16[128,2048]{1,0:T(8,128)(2,1)S(1)} %bitcast.33), channel_id=1, source_target_pairs={{0,2},{1,3},{2,0},{3,1},{4,6},{5,7},{6,4},{7,5},{8,10},{9,11},{10,... | collective-permute-start | bytes 1572872 | tf_op jit(solution)/shard_map/ppermute | solution.py:291
  20.9 18.0 %collective-permute-start.9 = (bf16[256,512]{1,0:T(8,128)(2,1)}, bf16[256,512]{1,0:T(8,128)(2,1)}, u32[]{:S(2)}, u32[]{:S(2)}) collective-permute-start(bf16[256,512]{1,0:T(8,128)(2,1)} %get-tuple-element.52.refs_4_), channel_id=1, source_target_pairs={{0,4},{1,5},{2,6},{3,7},{4,0},{5,1},{6,2},{7,3},{8,12},{9,13},{10,... | collective-permute-start | bytes 786440 | tf_op jit(solution)/shard_map/ppermute | solution.py:297
  27.0 13.1 %collective-permute-start.6 = (bf16[272,256]{1,0:T(8,128)(2,1)S(1)}, bf16[272,256]{1,0:T(8,128)(2,1)}, u32[]{:S(2)}, u32[]{:S(2)}) collective-permute-start(bf16[272,256]{1,0:T(8,128)(2,1)S(1)} %collective-permute-done.3.kv_o.refs_3_), channel_id=1, source_target_pairs={{0,8},{8,0},{16,24},{24,16},{1,9},{9,1},{17,25},{25,17},{2,10},{10... | collective-permute-start | bytes 417800 | tf_op jit(solution)/shard_map/ppermute | solution.py:294
  27.6 12.5 %collective-permute-start.8 = (bf16[272,256]{1,0:T(8,128)(2,1)S(1)}, bf16[272,256]{1,0:T(8,128)(2,1)}, u32[]{:S(2)}, u32[]{:S(2)}) collective-permute-start(bf16[272,256]{1,0:T(8,128)(2,1)S(1)} %collective-permute-done.3.kv_o.refs_3_), channel_id=1, source_target_pairs={{0,24},{8,16},{16,8},{24,0},{1,25},{9,17},{17,9},{25,1},{2,26},{10... | collective-permute-start | bytes 417800 | tf_op jit(solution)/shard_map/ppermute | solution.py:294
  30.0 0.7 copy-start.4
  30.7 9.4 %collective-permute-start.7 = (bf16[528,256]{1,0:T(8,128)(2,1)}, bf16[528,256]{1,0:T(8,128)(2,1)S(1)}, u32[]{:S(2)}, u32[]{:S(2)}) collective-permute-start(bf16[528,256]{1,0:T(8,128)(2,1)} %get-tuple-element.51), channel_id=1, source_target_pairs={{0,16},{8,24},{16,0},{24,8},{1,17},{9,25},{17,1},{25,9},{2,18},{10... | collective-permute-start | bytes 811016 | tf_op jit(solution)/shard_map/ppermute | solution.py:294
  40.1 1.2 %copy-start.2 = (f32[256]{0:T(256)S(1)}, f32[256]{0:T(256)}, u32[]{:S(2)}) copy-start(f32[256]{0:T(256)} %param.13) | copy-start | bytes 3076
  40.1 5.6 %collective-permute-start.11 = (bf16[128,2048]{1,0:T(8,128)(2,1)S(1)}, bf16[128,2048]{1,0:T(8,128)(2,1)S(1)}, u32[]{:S(2)}, u32[]{:S(2)}) collective-permute-start(bf16[128,2048]{1,0:T(8,128)(2,1)S(1)} %collective-permute-done.10.refs_0_.refs_2_), channel_id=1, source_target_pairs={{0,1},{1,0},{2,3},{3,2},{4,5},{5,4},{6,7},{7,6},{8,9},{9,8},{10,11... | collective-permute-start | bytes 1572872 | tf_op jit(solution)/shard_map/ppermute | solution.py:291
  40.2 12.0 %collective-permute-start.12 = (bf16[256,512]{1,0:T(8,128)(2,1)}, bf16[256,512]{1,0:T(8,128)(2,1)S(1)}, u32[]{:S(2)}, u32[]{:S(2)}) collective-permute-start(bf16[256,512]{1,0:T(8,128)(2,1)} %collective-permute-done.9.refs_5_), channel_id=1, source_target_pairs={{0,8},{8,0},{16,24},{24,16},{1,9},{9,1},{17,25},{25,17},{2,10},{10... | collective-permute-start | bytes 786440 | tf_op jit(solution)/shard_map/ppermute | solution.py:294
  40.8 11.4 %collective-permute-start.13 = (bf16[256,512]{1,0:T(8,128)(2,1)}, bf16[256,512]{1,0:T(8,128)(2,1)S(1)}, u32[]{:S(2)}, u32[]{:S(2)}) collective-permute-start(bf16[256,512]{1,0:T(8,128)(2,1)} %collective-permute-done.9.refs_5_), channel_id=1, source_target_pairs={{0,16},{8,24},{16,0},{24,8},{1,17},{9,25},{17,1},{25,9},{2,18},{10... | collective-permute-start | bytes 786440 | tf_op jit(solution)/shard_map/ppermute | solution.py:294
  42.9 9.2 %copy-start.5 = (bf16[256,512]{1,0:T(8,128)(2,1)S(1)}, bf16[256,512]{1,0:T(8,128)(2,1)}, u32[]{:S(2)}) copy-start(bf16[256,512]{1,0:T(8,128)(2,1)} %copy-done.4) | copy-start | bytes 786436
  43.0 9.2 %collective-permute-start.14 = (bf16[256,256]{1,0:T(8,128)(2,1)S(1)}, bf16[256,256]{1,0:T(8,128)(2,1)S(1)}, u32[]{:S(2)}, u32[]{:S(2)}) collective-permute-start(bf16[256,256]{1,0:T(8,128)(2,1)S(1)} %project_kv.2.first.refs_0_), channel_id=1, source_target_pairs={{0,4},{1,5},{2,6},{3,7},{4,0},{5,1},{6,2},{7,3},{8,12},{9,13},{10,... | collective-permute-start | bytes 393224 | tf_op jit(solution)/shard_map/ppermute | solution.py:297
  52.2 7.5 %collective-permute-start.19 = (bf16[256,512]{1,0:T(8,128)(2,1)S(1)}, bf16[256,512]{1,0:T(8,128)(2,1)S(1)}, u32[]{:S(2)}, u32[]{:S(2)}) collective-permute-start(bf16[256,512]{1,0:T(8,128)(2,1)S(1)} %copy-done.5), channel_id=1, source_target_pairs={{0,16},{8,24},{16,0},{24,8},{1,17},{9,25},{17,1},{25,9},{2,18},{10... | collective-permute-start | bytes 786440 | tf_op jit(solution)/shard_map/ppermute | solution.py:294
  53.6 7.0 %collective-permute-start.20 = (bf16[256,512]{1,0:T(8,128)(2,1)S(1)}, bf16[256,512]{1,0:T(8,128)(2,1)S(1)}, u32[]{:S(2)}, u32[]{:S(2)}) collective-permute-start(bf16[256,512]{1,0:T(8,128)(2,1)S(1)} %collective-permute-done.13.refs_9_), channel_id=1, source_target_pairs={{0,8},{8,0},{16,24},{24,16},{1,9},{9,1},{17,25},{25,17},{2,10},{10... | collective-permute-start | bytes 786440 | tf_op jit(solution)/shard_map/ppermute | solution.py:294
  55.1 8.7 %collective-permute-start.15 = (bf16[256,256]{1,0:T(8,128)(2,1)S(1)}, bf16[256,256]{1,0:T(8,128)(2,1)S(1)}, u32[]{:S(2)}, u32[]{:S(2)}) collective-permute-start(bf16[256,256]{1,0:T(8,128)(2,1)S(1)} %project_kv.3.second.refs_1_), channel_id=1, source_target_pairs={{0,4},{1,5},{2,6},{3,7},{4,0},{5,1},{6,2},{7,3},{8,12},{9,13},{10,... | collective-permute-start | bytes 393224 | tf_op jit(solution)/shard_map/ppermute | solution.py:297
  55.1 5.5 %copy-start.3 = (f32[256]{0:T(256)S(1)}, f32[256]{0:T(256)}, u32[]{:S(2)}) copy-start(f32[256]{0:T(256)} %param.12) | copy-start | bytes 3076
  55.1 9.9 %collective-permute-start.16 = (bf16[512,256]{1,0:T(8,128)(2,1)S(1)}, bf16[512,256]{1,0:T(8,128)(2,1)S(1)}, u32[]{:S(2)}, u32[]{:S(2)}) collective-permute-start(bf16[512,256]{1,0:T(8,128)(2,1)S(1)} %join.1), channel_id=1, source_target_pairs={{0,1},{1,0},{2,3},{3,2},{4,5},{5,4},{6,7},{7,6},{8,9},{9,8},{10,11... | collective-permute-start | bytes 786440 | tf_op jit(solution)/shard_map/ppermute | solution.py:291
  63.2 4.1 %collective-permute-start.21 = (bf16[256,512]{1,0:T(8,128)(2,1)S(1)}, bf16[256,512]{1,0:T(8,128)(2,1)S(1)}, u32[]{:S(2)}, u32[]{:S(2)}) collective-permute-start(bf16[256,512]{1,0:T(8,128)(2,1)S(1)} %get-tuple-element.71), channel_id=1, source_target_pairs={{0,1},{1,0},{2,3},{3,2},{4,5},{5,4},{6,7},{7,6},{8,9},{9,8},{10,11... | collective-permute-start | bytes 786440 | tf_op jit(solution)/shard_map/ppermute | solution.py:291
  63.3 1.7 %collective-permute-start.17 = (bf16[256,256]{1,0:T(8,128)(2,1)S(1)}, bf16[256,256]{1,0:T(8,128)(2,1)S(1)}, u32[]{:S(2)}, u32[]{:S(2)}) collective-permute-start(bf16[256,256]{1,0:T(8,128)(2,1)S(1)} %collective-permute-done.14.refs_2_), channel_id=1, source_target_pairs={{0,1},{1,0},{2,3},{3,2},{4,5},{5,4},{6,7},{7,6},{8,9},{9,8},{10,11... | collective-permute-start | bytes 393224 | tf_op jit(solution)/shard_map/ppermute | solution.py:291
  63.8 1.4 %collective-permute-start.18 = (bf16[256,256]{1,0:T(8,128)(2,1)S(1)}, bf16[256,256]{1,0:T(8,128)(2,1)S(1)}, u32[]{:S(2)}, u32[]{:S(2)}) collective-permute-start(bf16[256,256]{1,0:T(8,128)(2,1)S(1)} %collective-permute-done.15.refs_3_), channel_id=1, source_target_pairs={{0,1},{1,0},{2,3},{3,2},{4,5},{5,4},{6,7},{7,6},{8,9},{9,8},{10,11... | collective-permute-start | bytes 393224 | tf_op jit(solution)/shard_map/ppermute | solution.py:291
  65.9 9.2 %collective-permute-start.23 = (bf16[4,64,512]{2,1,0:T(8,128)(2,1)S(1)}, bf16[4,64,512]{2,1,0:T(8,128)(2,1)S(1)}, u32[]{:S(2)}, u32[]{:S(2)}) collective-permute-start(bf16[4,64,512]{2,1,0:T(8,128)(2,1)S(1)} %get-tuple-element.73), channel_id=1, source_target_pairs={{0,2},{1,3},{2,0},{3,1},{4,6},{5,7},{6,4},{7,5},{8,10},{9,11},{10,... | collective-permute-start | bytes 786440 | tf_op jit(solution)/shard_map/ppermute | solution.py:291
  69.4 10.6 %collective-permute-start.22 = (bf16[128,1024]{1,0:T(8,128)(2,1)S(1)}, bf16[128,1024]{1,0:T(8,128)(2,1)S(1)}, u32[]{:S(2)}, u32[]{:S(2)}) collective-permute-start(bf16[128,1024]{1,0:T(8,128)(2,1)S(1)} %attend.3), channel_id=1, source_target_pairs={{0,2},{1,3},{2,0},{3,1},{4,6},{5,7},{6,4},{7,5},{8,10},{9,11},{10,... | collective-permute-start | bytes 786440 | tf_op jit(solution)/shard_map/ppermute | solution.py:291

commit v11 on v9

--- a/solution.py
+++ b/solution.py
@@ -2,6 +2,7 @@
 
 import jax
 import jax.numpy as jnp
+import numpy as np
 from jax import lax
 from jax.experimental import pallas as pl
 from jax.experimental.pallas import tpu as pltpu
@@ -81,6 +82,31 @@
         outs[1][first : first + token_rows, :] = tokens_ref[:, n * LANES : (n + 1) * LANES]
 
 
+def read_id(piece, row, n):
+    ids = piece[row : row + ID_ROWS, :LANES].astype(jnp.float32)[:1]
+    lane = lax.broadcasted_iota(jnp.int32, ids.shape, 1)
+    return jnp.sum(jnp.where(lane == n, ids, 0.0)).astype(jnp.int32)
+
+
+def angle_kernel(piece, first_cos, first_sin, off_cos, off_sin, cos_out, sin_out):
+    blk_rows = off_cos.shape[0]
+    for n in range(cos_out.shape[0] // blk_rows):
+        block = pl.ds(read_id(piece, piece.shape[0] - ID_ROWS, n), 1)
+        here = slice(n * blk_rows, (n + 1) * blk_rows)
+        cosine, sine = first_cos[block, :], first_sin[block, :]
+        cos_out[here, :] = cosine * off_cos[...] - sine * off_sin[...]
+        sin_out[here, :] = sine * off_cos[...] + cosine * off_sin[...]
+
+
+def invert_table(table, flat_of):
+    per_head = table.shape[2]
+    for head in range(table.shape[1]):
+
+        @pl.loop(0, per_head)
+        def _(block):
+            flat_of[table[0, head, block]] = head * per_head + block
+
+
 def team_kernel(*refs):
     _, pair, core = place()
     parts, (kv_out, q_out, whole) = refs[:TEAM], refs[TEAM:]
@@ -174,7 +200,7 @@
                 out[there, h * HD : (h + 1) * HD] = turned[n * rows : (n + 1) * rows]
 
 
-def attend_kernel(blk_rows, step, store, q_ref, near_ref, ids_ref, length_ref, out):
+def attend_kernel(blk_rows, step, store, q_ref, near_ref, piece, length_ref, out):
     _, pair, core = place()
     length = length_ref[0]
     rows = out.shape[0]
@@ -184,7 +210,7 @@
     heads = 2 * (out.shape[1] // (2 * HD))
     first = step // 2 * rows
     for j in range(rows // blk_rows):
-        block = ids_ref[member * (rows // blk_rows) + j]
+        block = read_id(piece, piece.shape[0] - ID_ROWS, member * (rows // blk_rows) + j)
         here = slice(first + j * blk_rows, first + (j + 1) * blk_rows)
         there = slice(j * blk_rows, (j + 1) * blk_rows)
         for variant in range(4):
@@ -220,28 +246,35 @@
 
 def pages_kernel(n_out, blk_rows, *refs):
     mine, other = refs[:n_out], refs[n_out : 2 * n_out]
-    ids_ref, info_ref, own, away, store = refs[2 * n_out :]
+    piece, piece_o, table, length_ref, own, away, store, flat_of = refs[2 * n_out :]
     _, _, core = place()
+    tall = piece.shape[0]
     per_piece = mine[0].shape[0] // blk_rows
     for k in range(n_out):
         for j in range(per_piece):
-            there = aligned(ids_ref[k * per_piece + j], blk_rows)
+            block = read_id(*((piece_o, k * tall - ID_ROWS) if k else (piece, tall - ID_ROWS)), j)
+            there = aligned(block, blk_rows)
             here = slice(j * blk_rows, (j + 1) * blk_rows)
             store[core, there, :] = mine[k][here, :]
             store[1 - core, there, :] = other[k][here, :]
     slots = own.shape[0]
     row = lax.broadcasted_iota(jnp.int32, (blk_rows, HD), 0)
-    for target, base in ((away, slots), (own, 0)):
+    invert_table(table, flat_of)
+    blk = lax.axis_index("blk")
+    for target, device in ((away, blk ^ 2), (own, blk)):
         for i in range(slots):
-            here = aligned(info_ref[1, base + i], blk_rows)
-            live = row < info_ref[2, base + i]
+            block = lax.rem(flat_of[device * slots + i], table.shape[2])
+            here = aligned(block, blk_rows)
+            live = row < length_ref[0] - block * blk_rows
             for half in range(2):
                 page = store[half, here, :]
                 target[i, :, half * HD : (half + 1) * HD] = jnp.where(live, page, jnp.zeros_like(page))
 
 
-def finish_kernel(kept, from_far, own_pages, got_pages, info_ref, att_out, page_out, sems):
+def finish_kernel(kept, from_far, own_pages, got_pages, table, att_out, page_out, flat_of, sems):
     _, pair, _ = place()
+    invert_table(table, flat_of)
+    slots = page_out.shape[0]
     width = kept.shape[1]
     copies = [
         pltpu.make_async_copy(kept, att_out.at[:, aligned(pair, width)], sems.at[0]),
@@ -250,7 +283,7 @@
     for copy in copies:
         copy.start()
     for i in range(page_out.shape[0]):
-        here = info_ref[0, i] == pair
+        here = lax.div(flat_of[lax.axis_index("blk") * slots + i], table.shape[2]) == pair
         ours = pltpu.make_async_copy(own_pages.at[i], page_out.at[i], sems.at[2 + i])
         theirs = pltpu.make_async_copy(got_pages.at[i], page_out.at[i], sems.at[2 + i])
         copies.append(ours)
@@ -331,28 +364,22 @@
     q_o, far = from_others(q), in_team(own, 2)
 
     blk_rows = rows // per_device
-    tall = kv.shape[0]
-    team_ids = kv[tall - ID_ROWS, : TEAM * per_device][None].astype(jnp.int32)
-    other_ids = kv_o.reshape(n_out - 1, tall, HD)[:, tall - ID_ROWS, : TEAM * per_device].astype(jnp.int32)
-    all_ids = jnp.concatenate([team_ids, other_ids], 0).reshape(-1)
-
-    offsets = jnp.arange(blk_rows, dtype=jnp.int32)
-    positions = (team_ids[0][:, None] * blk_rows + offsets[None, :]).reshape(-1, 1)
-    inverse = jnp.power(jnp.float32(ROPE_BASE), -2.0 * jnp.arange(HD // 2).astype(jnp.float32) / HD)
-    angles = positions.astype(jnp.float32) * inverse[None, :]
-    cosine, sine = jnp.cos(angles), jnp.sin(angles)
-
-    table = page_table[0].reshape(-1)
-    per_head = page_table.shape[2]
-    slot_count = page_table.shape[1] * per_head // n_blk
-    wanted = jnp.concatenate(
-        [b * slot_count + jnp.arange(slot_count, dtype=jnp.int32) for b in (blk, blk ^ 2)]
-    )
-    flat = jnp.sum(
-        jnp.where(wanted[:, None] == table[None, :], jnp.arange(table.shape[0], dtype=jnp.int32)[None, :], 0), 1
-    )
-    block = flat % per_head
-    info = jnp.stack([flat // per_head, block, lengths[0] - block * blk_rows])
+    half = HD // 2
+    inverse = np.float64(ROPE_BASE) ** (-2.0 * np.arange(half) / HD)
+    tables = []
+    for positions in (np.arange(per_device * n_blk) * blk_rows, np.arange(blk_rows)):
+        angles = positions[:, None] * inverse[None, :]
+        tables += [np.cos(angles).astype(np.float32), np.sin(angles).astype(np.float32)]
+    cosine, sine = pl.pallas_call(
+        angle_kernel,
+        out_shape=[shape((TEAM * rows, half), jnp.float32)] * 2,
+        in_specs=[VMEM] * 5,
+        out_specs=[VMEM] * 2,
+        cost_estimate=pl.CostEstimate(flops=0, bytes_accessed=38 * MIB, transcendentals=0),
+        compiler_params=params(2),
+        name="angles",
+    )(kv, *tables)
+    slot_count = page_table.shape[1] * page_table.shape[2] // n_blk
 
     kv_o, w_x, w_y = sync(kv_o, w_x, w_y)
     others = kv_o.shape[0]
@@ -365,9 +392,7 @@
         name="regroup",
     )(kv_o, w_x)
     kv_ox, kv_oy_d, kv_od = in_req(kv_o, 1), in_req(kv_o_x, 2), in_req(kv_o, 3)
-    kv_ox, kv_oy_d, kv_od, q_o, far, cosine, sine, all_ids, info = sync(
-        kv_ox, kv_oy_d, kv_od, q_o, far, cosine, sine, all_ids, info
-    )
+    kv_ox, kv_oy_d, kv_od, q_o, far, cosine, sine = sync(kv_ox, kv_oy_d, kv_od, q_o, far, cosine, sine)
     far_near = in_team(far, 1)
     far_near, q_o = sync(far_near, q_o)
     q_ox, q_oy = in_req(q_o, 1), in_req(q_o, 2)
@@ -414,26 +439,27 @@
     own_pages, away_pages, store = pl.pallas_call(
         functools.partial(pages_kernel, n_out, blk_rows),
         out_shape=[page_shape, page_shape, shape((2, total, HD), bf16)],
-        in_specs=[VMEM] * (2 * n_out) + [SMEM] * 2,
+        in_specs=[VMEM] * (2 * n_out + 2) + [SMEM] * 2,
         out_specs=[VMEM] * 3,
+        scratch_shapes=[pltpu.SMEM((page_table.size,), jnp.int32)],
         cost_estimate=pl.CostEstimate(flops=0, bytes_accessed=4 * MIB, transcendentals=0),
         compiler_params=params(store_mib + 1),
         name="pages",
-    )(*mine, *other, all_ids, info)
+    )(*mine, *other, kv, kv_o, page_table, lengths)
     got_pages = in_team(away_pages, 2)
 
     def attend(step):
         return pl.pallas_call(
             functools.partial(attend_kernel, blk_rows, step),
             out_shape=shape((rows, H // 2 * HD), bf16),
-            in_specs=[VMEM] * 3 + [SMEM] * 2,
+            in_specs=[VMEM] * 4 + [SMEM],
             out_specs=VMEM,
             cost_estimate=pl.CostEstimate(
                 flops=2 * H * HD * rows * total, bytes_accessed=4 * MIB, transcendentals=0
             ),
             compiler_params=params(store_mib + 2 + 3 * total // 1024),
             name="attend",
-        )(store, queries, from_near, all_ids, lengths)
+        )(store, queries, from_near, kv, lengths)
 
     from_far = in_team(attend(2), 2)
     kept = attend(0)
@@ -443,10 +469,10 @@
         out_shape=[shape((rows, H * HD), bf16), page_shape],
         in_specs=[ANY] * 4 + [SMEM],
         out_specs=[ANY] * 2,
-        scratch_shapes=[pltpu.SemaphoreType.DMA((2 + slot_count,))],
+        scratch_shapes=[pltpu.SMEM((page_table.size,), jnp.int32), pltpu.SemaphoreType.DMA((2 + slot_count,))],
         compiler_params=params(1),
         name="finish",
-    )(kept, from_far, own_pages, got_pages, info)
+    )(kept, from_far, own_pages, got_pages, page_table)
     return attended[None], pages[None]
 
 

time: 79.2 us -> 85.1 us (1.074)
  waiting for transfers between devices: 36.6 us -> 45.8 us
  Pallas kernels: 14.8 us -> 11.3 us
  starting transfers between devices: 23 us -> 25.4 us
  other arithmetic: 1.38 us -> 0 us
  local copies, waits for them, and re-layouts: 1.86 us -> 0.95 us
    ppermute x3, waiting for transfers between devices: 18.4 us -> 24.4 us  [across(): lax.ppermute(array, 'blk', [(i, (i + TEAM * k) % n_blk) for i in range(n_...]
    ppermute x9, waiting for transfers between devices: 2.95 us -> 5.58 us  [in_req(): return lax.ppermute(array, 'req', [(i, i ^ k) for i in range(n_req)])]
    pallas_call x2, Pallas kernels: 4.53 us -> 2.47 us  [project(): pl.pallas_call(functools.partial(project_kernel, n_out, TEAM * w_rows, st...]
    ppermute x9, starting transfers between devices: 9.64 us -> 11.7 us  [in_req(): return lax.ppermute(array, 'req', [(i, i ^ k) for i in range(n_req)])]
    sin x1 -> x0, other arithmetic: 0.98 us -> none  [body(): cosine, sine = (jnp.cos(angles), jnp.sin(angles))]
  transfers between devices with their start and end apart: 22 -> 22, of which waited for: 11 -> 10; matrix products, arithmetic and copies ran while one was open for 2% -> 0% of each run, Pallas kernels for 13% -> 8%
where the time goes in v11:
time: 85.1 us; the launch traced here: 84.9 us
  waiting for transfers between devices  45.8 us (54%)
  starting transfers between devices  25.4 us (30%)
  Pallas kernels  11.3 us (13%)
  between operations  1.5 us (2%)
  local copies, waits for them, and re-layouts  0.95 us (1%)
    ppermute x3, waiting for transfers between devices, across(): lax.ppermute(array, 'blk', [(i, (i + TEAM * k) % n_blk) for i in range(n_...  24.4 us
    ppermute x10, waiting for transfers between devices, in_team(): return lax.ppermute(array, 'blk', [(i, i ^ k) for i in range(n_blk)])  15.8 us
    ppermute x9, starting transfers between devices, in_req(): return lax.ppermute(array, 'req', [(i, i ^ k) for i in range(n_req)])  11.7 us
    ppermute x10, starting transfers between devices, in_team(): return lax.ppermute(array, 'blk', [(i, i ^ k) for i in range(n_blk)])  7.63 us
    ppermute x3, starting transfers between devices, across(): lax.ppermute(array, 'blk', [(i, (i + TEAM * k) % n_blk) for i in range(n_...  6.04 us
    ppermute x9, waiting for transfers between devices, in_req(): return lax.ppermute(array, 'req', [(i, i ^ k) for i in range(n_req)])  5.58 us
    pallas_call x2, Pallas kernels, attend(): pl.pallas_call(functools.partial(attend_kernel, blk_rows, step), out_shap...  3.39 us
    pallas_call x2, Pallas kernels, project(): pl.pallas_call(functools.partial(project_kernel, n_out, TEAM * w_rows, st...  2.47 us
  transfers between devices with their start and end apart: 22, of which 10 were waited for; matrix products, arithmetic and copies ran while one was open for 0% of the time, Pallas kernels for 8%

profile of v11, /device:TPU:0, one launch (start us, length us, event | category | flops | bytes accessed | tf_op | source)
XLA Modules:
  0.0 84.9 jit_solution(6582615372419133473)
XLA Ops:
  0.6 2.3 %pack.1 = (bf16[400,128]{1,0:T(8,128)(2,1)}, bf16[2448,128]{1,0:T(8,128)(2,1)}, bf16[400,128]{1,0:T(8,128)(2,1)}, bf16[400,128]{1,0:T(8,128)(2,1)}) custom-call(bf16[64,3072]{1,0:T(8,128)(2,1)} %w_hbm.1, s32[1,2]{1,0:T(1,128)} %ids_hbm.1, bf16[128,2048]{1,0:T(8,128)(2,1)} %bitcast.5), custom_call_target="tpu_custom_call" | custom-call | tf_op jit(solution)/shard_map/pack/pallas_call | solution.py:328
  3.4 2.7 %collective-permute-start.1 = (bf16[400,128]{1,0:T(8,128)(2,1)}, bf16[400,128]{1,0:T(8,128)(2,1)S(1)}, u32[]{:S(2)}, u32[]{:S(2)}) collective-permute-start(bf16[400,128]{1,0:T(8,128)(2,1)} %get-tuple-element.41), channel_id=1, source_target_pairs={{0,2},{1,3},{2,0},{3,1},{4,6},{5,7},{6,4},{7,5},{8,10},{9,11},{10,... | collective-permute-start | bytes 307208 | tf_op jit(solution)/shard_map/ppermute | solution.py:312
  6.2 3.9 %collective-permute-done.1.refs_2_ = bf16[400,128]{1,0:T(8,128)(2,1)S(1)} collective-permute-done((bf16[400,128]{1,0:T(8,128)(2,1)}, bf16[400,128]{1,0:T(8,128)(2,1)S(1)}, u32[]{:S(2)}, u32[]{:S(2)}) %collective-permute-start.1) | collective-permute-done | bytes 102432 | tf_op jit(solution)/shard_map/ppermute | solution.py:312
  10.0 1.7 %collective-permute-done.2.refs_3_ = bf16[400,128]{1,0:T(8,128)(2,1)S(1)} collective-permute-done((bf16[400,128]{1,0:T(8,128)(2,1)}, bf16[400,128]{1,0:T(8,128)(2,1)S(1)}, u32[]{:S(2)}, u32[]{:S(2)}) %collective-permute-start.2) | collective-permute-done | bytes 102432 | tf_op jit(solution)/shard_map/ppermute | solution.py:312
  11.7 0.9 %copy-done.1 = bf16[400,128]{1,0:T(8,128)(2,1)S(1)} copy-done((bf16[400,128]{1,0:T(8,128)(2,1)S(1)}, bf16[400,128]{1,0:T(8,128)(2,1)}, u32[]{:S(2)}) %copy-start.1) | copy-done | bytes 102424
  12.8 1.5 %collective-permute-start.4 = (bf16[256,768]{1,0:T(8,128)(2,1)S(1)}, bf16[256,768]{1,0:T(8,128)(2,1)S(1)}, u32[]{:S(2)}, u32[]{:S(2)}) collective-permute-start(bf16[256,768]{1,0:T(8,128)(2,1)S(1)} %get-tuple-element.48), channel_id=1, source_target_pairs={{0,8},{8,0},{16,24},{24,16},{1,9},{9,1},{17,25},{25,17},{2,10},{10... | collective-permute-start | bytes 1179656 | tf_op jit(solution)/shard_map/ppermute | solution.py:315
  14.3 1.5 %collective-permute-start.5 = (bf16[256,768]{1,0:T(8,128)(2,1)S(1)}, bf16[256,768]{1,0:T(8,128)(2,1)S(1)}, u32[]{:S(2)}, u32[]{:S(2)}) collective-permute-start(bf16[256,768]{1,0:T(8,128)(2,1)S(1)} %get-tuple-element.48), channel_id=1, source_target_pairs={{0,16},{8,24},{16,0},{24,8},{1,17},{9,25},{17,1},{25,9},{2,18},{10... | collective-permute-start | bytes 1179656 | tf_op jit(solution)/shard_map/ppermute | solution.py:315
  15.9 1.6 %collective-permute-start.10 = (bf16[128,2048]{1,0:T(8,128)(2,1)S(1)}, bf16[128,2048]{1,0:T(8,128)(2,1)S(1)}, u32[]{:S(2)}, u32[]{:S(2)}) collective-permute-start(bf16[128,2048]{1,0:T(8,128)(2,1)S(1)} %bitcast.6), channel_id=1, source_target_pairs={{0,2},{1,3},{2,0},{3,1},{4,6},{5,7},{6,4},{7,5},{8,10},{9,11},{10,... | collective-permute-start | bytes 1572872 | tf_op jit(solution)/shard_map/ppermute | solution.py:312
  17.4 2.6 %collective-permute-start.3 = (bf16[272,256]{1,0:T(8,128)(2,1)S(1)}, bf16[272,256]{1,0:T(8,128)(2,1)S(1)}, u32[]{:S(2)}, u32[]{:S(2)}) collective-permute-start(bf16[272,256]{1,0:T(8,128)(2,1)S(1)} %get-tuple-element.47.piece.refs_0_.refs_4_), channel_id=1, source_target_pairs={{0,4},{1,5},{2,6},{3,7},{4,0},{5,1},{6,2},{7,3},{8,12},{9,13},{10,... | collective-permute-start | bytes 417800 | tf_op jit(solution)/shard_map/ppermute | solution.py:318
  20.0 11.5 %collective-permute-done.3.kv_o.refs_1_.refs_5_ = bf16[272,256]{1,0:T(8,128)(2,1)S(1)} collective-permute-done((bf16[272,256]{1,0:T(8,128)(2,1)S(1)}, bf16[272,256]{1,0:T(8,128)(2,1)S(1)}, u32[]{:S(2)}, u32[]{:S(2)}) %collective-permute-start.3) | collective-permute-done | bytes 139296 | tf_op jit(solution)/shard_map/ppermute | solution.py:318
  31.5 0.6 collective-permute-start.7
  32.1 3.4 %collective-permute-start.9 = (bf16[256,512]{1,0:T(8,128)(2,1)S(1)}, bf16[256,512]{1,0:T(8,128)(2,1)S(1)}, u32[]{:S(2)}, u32[]{:S(2)}) collective-permute-start(bf16[256,512]{1,0:T(8,128)(2,1)S(1)} %get-tuple-element.52.refs_0_), channel_id=1, source_target_pairs={{0,4},{1,5},{2,6},{3,7},{4,0},{5,1},{6,2},{7,3},{8,12},{9,13},{10,... | collective-permute-start | bytes 786440 | tf_op jit(solution)/shard_map/ppermute | solution.py:318
  35.5 0.5 collective-permute-start.6
  36.0 2.4 %collective-permute-start.8 = (bf16[272,256]{1,0:T(8,128)(2,1)S(1)}, bf16[272,256]{1,0:T(8,128)(2,1)S(1)}, u32[]{:S(2)}, u32[]{:S(2)}) collective-permute-start(bf16[272,256]{1,0:T(8,128)(2,1)S(1)} %collective-permute-done.3.kv_o.refs_1_.refs_5_), channel_id=1, source_target_pairs={{0,24},{8,16},{16,8},{24,0},{1,25},{9,17},{17,9},{25,1},{2,26},{10... | collective-permute-start | bytes 417800 | tf_op jit(solution)/shard_map/ppermute | solution.py:315
  38.7 7.4 %collective-permute-done.9.refs_1_ = bf16[256,512]{1,0:T(8,128)(2,1)S(1)} collective-permute-done((bf16[256,512]{1,0:T(8,128)(2,1)S(1)}, bf16[256,512]{1,0:T(8,128)(2,1)S(1)}, u32[]{:S(2)}, u32[]{:S(2)}) %collective-permute-start.9) | collective-permute-done | bytes 262176 | tf_op jit(solution)/shard_map/ppermute | solution.py:318
  46.2 1.9 %collective-permute-done.11.far_near = bf16[128,2048]{1,0:T(8,128)(2,1)S(1)} collective-permute-done((bf16[128,2048]{1,0:T(8,128)(2,1)S(1)}, bf16[128,2048]{1,0:T(8,128)(2,1)S(1)}, u32[]{:S(2)}, u32[]{:S(2)}) %collective-permute-start.11) | collective-permute-done | bytes 524320 | tf_op jit(solution)/shard_map/ppermute | solution.py:312
  48.1 0.5 collective-permute-start.15
  48.7 1.5 %collective-permute-start.16 = (bf16[256,512]{1,0:T(8,128)(2,1)S(1)}, bf16[256,512]{1,0:T(8,128)(2,1)S(1)}, u32[]{:S(2)}, u32[]{:S(2)}) collective-permute-start(bf16[256,512]{1,0:T(8,128)(2,1)S(1)} %collective-permute-done.9.refs_1_), channel_id=1, source_target_pairs={{0,16},{8,24},{16,0},{24,8},{1,17},{9,25},{17,1},{25,9},{2,18},{10... | collective-permute-start | bytes 786440 | tf_op jit(solution)/shard_map/ppermute | solution.py:315
  50.2 0.9 %project_kv.1.refs_0_ = bf16[512,256]{1,0:T(8,128)(2,1)S(1)} custom-call(bf16[128,2048]{1,0:T(8,128)(2,1)S(1)} %bitcast.7, bf16[2448,128]{1,0:T(8,128)(2,1)S(1)} %collective-permute-done.refs_1_.near, bf16[128,2048]{1,0:T(8,128)(2,1)S(1)} %collective-permute-done.10.far, bf16[128,2048]{1,0:T(8,128)(2,1)S(1)} %collective-permute-done.11.far_near, ...), custom_call_target="tpu_custom_call" | custom-call | flops 536870912 | bytes 6291456 | tf_op jit(solution)/shard_map/project_kv/pallas_call | solution.py:409
  51.2 5.3 %collective-permute-done.15.refs_3_ = bf16[256,512]{1,0:T(8,128)(2,1)S(1)} collective-permute-done((bf16[256,512]{1,0:T(8,128)(2,1)S(1)}, bf16[256,512]{1,0:T(8,128)(2,1)S(1)}, u32[]{:S(2)}, u32[]{:S(2)}) %collective-permute-start.15) | collective-permute-done | bytes 262176 | tf_op jit(solution)/shard_map/ppermute | solution.py:315
  56.7 1.5 %collective-permute-start.17 = (bf16[256,512]{1,0:T(8,128)(2,1)S(1)}, bf16[256,512]{1,0:T(8,128)(2,1)S(1)}, u32[]{:S(2)}, u32[]{:S(2)}) collective-permute-start(bf16[256,512]{1,0:T(8,128)(2,1)S(1)} %get-tuple-element.69), channel_id=1, source_target_pairs={{0,16},{8,24},{16,0},{24,8},{1,17},{9,25},{17,1},{25,9},{2,18},{10... | collective-permute-start | bytes 786440 | tf_op jit(solution)/shard_map/ppermute | solution.py:315
  58.3 1.5 %collective-permute-start.18 = (bf16[256,512]{1,0:T(8,128)(2,1)S(1)}, bf16[256,512]{1,0:T(8,128)(2,1)S(1)}, u32[]{:S(2)}, u32[]{:S(2)}) collective-permute-start(bf16[256,512]{1,0:T(8,128)(2,1)S(1)} %collective-permute-done.16.refs_5_), channel_id=1, source_target_pairs={{0,8},{8,0},{16,24},{24,16},{1,9},{9,1},{17,25},{25,17},{2,10},{10... | collective-permute-start | bytes 786440 | tf_op jit(solution)/shard_map/ppermute | solution.py:315
  59.8 5.5 %collective-permute-done.12.refs_1_ = bf16[512,256]{1,0:T(8,128)(2,1)S(1)} collective-permute-done((bf16[512,256]{1,0:T(8,128)(2,1)S(1)}, bf16[512,256]{1,0:T(8,128)(2,1)S(1)}, u32[]{:S(2)}, u32[]{:S(2)}) %collective-permute-start.12) | collective-permute-done | bytes 262176 | tf_op jit(solution)/shard_map/ppermute | solution.py:318
  65.3 1.6 %project_q.1 = (bf16[256,512]{1,0:T(8,128)(2,1)S(1)}, bf16[256,512]{1,0:T(8,128)(2,1)S(1)}) custom-call(bf16[128,2048]{1,0:T(8,128)(2,1)S(1)} %bitcast.8, bf16[2448,128]{1,0:T(8,128)(2,1)S(1)} %collective-permute-done.refs_1_.near, bf16[128,2048]{1,0:T(8,128)(2,1)S(1)} %collective-permute-done.10.far, ...), custom_call_target="tpu_custom_call" | custom-call | flops 1073741824 | bytes 6291456 | tf_op jit(solution)/shard_map/project_q/pallas_call | solution.py:409
  66.9 0.6 collective-permute-start.19
  68.2 1.1 %pages.1 = (bf16[4,64,512]{2,1,0:T(8,128)(2,1)S(1)}, bf16[4,64,512]{2,1,0:T(8,128)(2,1)S(1)}, bf16[2,1024,256]{2,1,0:T(8,128)(2,1)S(1)}) custom-call(bf16[512,256]{1,0:T(8,128)(2,1)S(1)} %project_kv.1.refs_0_, bf16[512,256]{1,0:T(8,128)(2,1)S(1)} %collective-permute-done.12.refs_1_, bf16[512,256]{1,0:T(8,128)(2,1)S(1)} %collective-permute-done.13.refs_2_, ...), custom_call_target="tpu_custom_call" | custom-call | bytes 4194304 | tf_op jit(solution)/shard_map/pages/pallas_call | solution.py:439
  69.3 1.7 %attend.3 = bf16[128,1024]{1,0:T(8,128)(2,1)S(1)} custom-call(bf16[2,1024,256]{2,1,0:T(8,128)(2,1)S(1)} %get-tuple-element.64.store, bf16[256,512]{1,0:T(8,128)(2,1)S(1)} %get-tuple-element.70.q_ref, bf16[256,512]{1,0:T(8,128)(2,1)S(1)} %collective-permute-done.19.near_ref, bf16[272,256]{1,0:T(8,128)(2,1)S(1)} %get-tuple-element.47.piece.refs_0_.refs_4_, ...), custom_call_target="tpu_custom_call" | custom-call | flops 536870912 | bytes 4194304 | tf_op jit(solution)/shard_map/attend/pallas_call | solution.py:452
  71.0 2.1 %collective-permute-start.20 = (bf16[128,1024]{1,0:T(8,128)(2,1)S(1)}, bf16[128,1024]{1,0:T(8,128)(2,1)S(1)}, u32[]{:S(2)}, u32[]{:S(2)}) collective-permute-start(bf16[128,1024]{1,0:T(8,128)(2,1)S(1)} %attend.3), channel_id=1, source_target_pairs={{0,2},{1,3},{2,0},{3,1},{4,6},{5,7},{6,4},{7,5},{8,10},{9,11},{10,... | collective-permute-start | bytes 786440 | tf_op jit(solution)/shard_map/ppermute | solution.py:312
  73.1 1.7 %attend.2.kept = bf16[128,1024]{1,0:T(8,128)(2,1)S(1)} custom-call(bf16[2,1024,256]{2,1,0:T(8,128)(2,1)S(1)} %get-tuple-element.64.store, bf16[256,512]{1,0:T(8,128)(2,1)S(1)} %get-tuple-element.70.q_ref, bf16[256,512]{1,0:T(8,128)(2,1)S(1)} %collective-permute-done.19.near_ref, bf16[272,256]{1,0:T(8,128)(2,1)S(1)} %get-tuple-element.47.piece.refs_0_.refs_4_, ...), custom_call_target="tpu_custom_call" | custom-call | flops 536870912 | bytes 4194304 | tf_op jit(solution)/shard_map/attend/pallas_call | solution.py:452
  74.8 3.6 %collective-permute-done.21.got_pages = bf16[4,64,512]{2,1,0:T(8,128)(2,1)S(1)} collective-permute-done((bf16[4,64,512]{2,1,0:T(8,128)(2,1)S(1)}, bf16[4,64,512]{2,1,0:T(8,128)(2,1)S(1)}, u32[]{:S(2)}, u32[]{:S(2)}) %collective-permute-start.21) | collective-permute-done | bytes 262176 | tf_op jit(solution)/shard_map/ppermute | solution.py:312
  78.5 4.7 %collective-permute-done.20.from_far = bf16[128,1024]{1,0:T(8,128)(2,1)S(1)} collective-permute-done((bf16[128,1024]{1,0:T(8,128)(2,1)S(1)}, bf16[128,1024]{1,0:T(8,128)(2,1)S(1)}, u32[]{:S(2)}, u32[]{:S(2)}) %collective-permute-start.20) | collective-permute-done | bytes 262176 | tf_op jit(solution)/shard_map/ppermute | solution.py:312
  83.2 1.7 %finish.1 = (bf16[128,2048]{1,0:T(8,128)(2,1)}, bf16[4,64,512]{2,1,0:T(8,128)(2,1)}) custom-call(bf16[128,1024]{1,0:T(8,128)(2,1)S(1)} %attend.2.kept, bf16[128,1024]{1,0:T(8,128)(2,1)S(1)} %collective-permute-done.20.from_far, bf16[4,64,512]{2,1,0:T(8,128)(2,1)S(1)} %get-tuple-element.72.own_pages, ...), custom_call_target="tpu_custom_call" | custom-call | tf_op jit(solution)/shard_map/finish/pallas_call | solution.py:467
  (40 shorter events, 1.5 us)
Async XLA Ops:
  2.9 12.9 %copy-start = (bf16[1,128,2048]{2,1,0:T(8,128)(2,1)S(1)}, bf16[1,128,2048]{2,1,0:T(8,128)(2,1)}, u32[]{:S(2)}) copy-start(bf16[1,128,2048]{2,1,0:T(8,128)(2,1)} %param.11) | copy-start | bytes 1572868
  2.9 8.8 %collective-permute-start = (bf16[2448,128]{1,0:T(8,128)(2,1)}, bf16[2448,128]{1,0:T(8,128)(2,1)S(1)}, u32[]{:S(2)}, u32[]{:S(2)}) collective-permute-start(bf16[2448,128]{1,0:T(8,128)(2,1)} %get-tuple-element.40), channel_id=1, source_target_pairs={{0,1},{1,0},{2,3},{3,2},{4,5},{5,4},{6,7},{7,6},{8,9},{9,8},{10,11... | collective-permute-start | bytes 1880072 | tf_op jit(solution)/shard_map/ppermute | solution.py:312
  3.4 6.6 %collective-permute-start.1 = (bf16[400,128]{1,0:T(8,128)(2,1)}, bf16[400,128]{1,0:T(8,128)(2,1)S(1)}, u32[]{:S(2)}, u32[]{:S(2)}) collective-permute-start(bf16[400,128]{1,0:T(8,128)(2,1)} %get-tuple-element.41), channel_id=1, source_target_pairs={{0,2},{1,3},{2,0},{3,1},{4,6},{5,7},{6,4},{7,5},{8,10},{9,11},{10,... | collective-permute-start | bytes 307208 | tf_op jit(solution)/shard_map/ppermute | solution.py:312
  6.1 5.6 %collective-permute-start.2 = (bf16[400,128]{1,0:T(8,128)(2,1)}, bf16[400,128]{1,0:T(8,128)(2,1)S(1)}, u32[]{:S(2)}, u32[]{:S(2)}) collective-permute-start(bf16[400,128]{1,0:T(8,128)(2,1)} %get-tuple-element.42), channel_id=1, source_target_pairs={{0,3},{1,2},{2,1},{3,0},{4,7},{5,6},{6,5},{7,4},{8,11},{9,10},{10,... | collective-permute-start | bytes 307208 | tf_op jit(solution)/shard_map/ppermute | solution.py:312
  11.7 0.9 %copy-start.1 = (bf16[400,128]{1,0:T(8,128)(2,1)S(1)}, bf16[400,128]{1,0:T(8,128)(2,1)}, u32[]{:S(2)}) copy-start(bf16[400,128]{1,0:T(8,128)(2,1)} %get-tuple-element.39.refs_0_) | copy-start | bytes 307204
  12.7 25.7 %copy-start.2 = (f32[64,128]{1,0:T(8,128)S(1)}, f32[64,128]{1,0:T(8,128)}, u32[]{:S(2)}) copy-start(f32[64,128]{1,0:T(8,128)} %constant.10.clone.off_cos) | copy-start | bytes 98308
  12.8 25.7 %copy-start.3 = (f32[64,128]{1,0:T(8,128)S(1)}, f32[64,128]{1,0:T(8,128)}, u32[]{:S(2)}) copy-start(f32[64,128]{1,0:T(8,128)} %constant.11.clone.off_sin) | copy-start | bytes 98308
  12.8 25.7 %copy-start.4 = (f32[16,128]{1,0:T(8,128)S(1)}, f32[16,128]{1,0:T(8,128)}, u32[]{:S(2)}) copy-start(f32[16,128]{1,0:T(8,128)} %constant.8.clone.first_cos) | copy-start | bytes 24580
  12.8 25.7 %copy-start.5 = (f32[16,128]{1,0:T(8,128)S(1)}, f32[16,128]{1,0:T(8,128)}, u32[]{:S(2)}) copy-start(f32[16,128]{1,0:T(8,128)} %constant.9.clone.first_sin) | copy-start | bytes 24580
  12.8 18.7 %collective-permute-start.4 = (bf16[256,768]{1,0:T(8,128)(2,1)S(1)}, bf16[256,768]{1,0:T(8,128)(2,1)S(1)}, u32[]{:S(2)}, u32[]{:S(2)}) collective-permute-start(bf16[256,768]{1,0:T(8,128)(2,1)S(1)} %get-tuple-element.48), channel_id=1, source_target_pairs={{0,8},{8,0},{16,24},{24,16},{1,9},{9,1},{17,25},{25,17},{2,10},{10... | collective-permute-start | bytes 1179656 | tf_op jit(solution)/shard_map/ppermute | solution.py:315
  14.3 17.2 %collective-permute-start.5 = (bf16[256,768]{1,0:T(8,128)(2,1)S(1)}, bf16[256,768]{1,0:T(8,128)(2,1)S(1)}, u32[]{:S(2)}, u32[]{:S(2)}) collective-permute-start(bf16[256,768]{1,0:T(8,128)(2,1)S(1)} %get-tuple-element.48), channel_id=1, source_target_pairs={{0,16},{8,24},{16,0},{24,8},{1,17},{9,25},{17,1},{25,9},{2,18},{10... | collective-permute-start | bytes 1179656 | tf_op jit(solution)/shard_map/ppermute | solution.py:315
  15.9 30.3 %collective-permute-start.10 = (bf16[128,2048]{1,0:T(8,128)(2,1)S(1)}, bf16[128,2048]{1,0:T(8,128)(2,1)S(1)}, u32[]{:S(2)}, u32[]{:S(2)}) collective-permute-start(bf16[128,2048]{1,0:T(8,128)(2,1)S(1)} %bitcast.6), channel_id=1, source_target_pairs={{0,2},{1,3},{2,0},{3,1},{4,6},{5,7},{6,4},{7,5},{8,10},{9,11},{10,... | collective-permute-start | bytes 1572872 | tf_op jit(solution)/shard_map/ppermute | solution.py:312
  17.4 14.0 %collective-permute-start.3 = (bf16[272,256]{1,0:T(8,128)(2,1)S(1)}, bf16[272,256]{1,0:T(8,128)(2,1)S(1)}, u32[]{:S(2)}, u32[]{:S(2)}) collective-permute-start(bf16[272,256]{1,0:T(8,128)(2,1)S(1)} %get-tuple-element.47.piece.refs_0_.refs_4_), channel_id=1, source_target_pairs={{0,4},{1,5},{2,6},{3,7},{4,0},{5,1},{6,2},{7,3},{8,12},{9,13},{10,... | collective-permute-start | bytes 417800 | tf_op jit(solution)/shard_map/ppermute | solution.py:318
  31.5 14.6 %collective-permute-start.7 = (bf16[528,256]{1,0:T(8,128)(2,1)S(1)}, bf16[528,256]{1,0:T(8,128)(2,1)S(1)}, u32[]{:S(2)}, u32[]{:S(2)}) collective-permute-start(bf16[528,256]{1,0:T(8,128)(2,1)S(1)} %get-tuple-element.51), channel_id=1, source_target_pairs={{0,16},{8,24},{16,0},{24,8},{1,17},{9,25},{17,1},{25,9},{2,18},{10... | collective-permute-start | bytes 811016 | tf_op jit(solution)/shard_map/ppermute | solution.py:315
  32.1 14.0 %collective-permute-start.9 = (bf16[256,512]{1,0:T(8,128)(2,1)S(1)}, bf16[256,512]{1,0:T(8,128)(2,1)S(1)}, u32[]{:S(2)}, u32[]{:S(2)}) collective-permute-start(bf16[256,512]{1,0:T(8,128)(2,1)S(1)} %get-tuple-element.52.refs_0_), channel_id=1, source_target_pairs={{0,4},{1,5},{2,6},{3,7},{4,0},{5,1},{6,2},{7,3},{8,12},{9,13},{10,... | collective-permute-start | bytes 786440 | tf_op jit(solution)/shard_map/ppermute | solution.py:318
  35.5 10.6 %collective-permute-start.6 = (bf16[272,256]{1,0:T(8,128)(2,1)S(1)}, bf16[272,256]{1,0:T(8,128)(2,1)S(1)}, u32[]{:S(2)}, u32[]{:S(2)}) collective-permute-start(bf16[272,256]{1,0:T(8,128)(2,1)S(1)} %collective-permute-done.3.kv_o.refs_1_.refs_5_), channel_id=1, source_target_pairs={{0,8},{8,0},{16,24},{24,16},{1,9},{9,1},{17,25},{25,17},{2,10},{10... | collective-permute-start | bytes 417800 | tf_op jit(solution)/shard_map/ppermute | solution.py:315
  36.0 10.1 %collective-permute-start.8 = (bf16[272,256]{1,0:T(8,128)(2,1)S(1)}, bf16[272,256]{1,0:T(8,128)(2,1)S(1)}, u32[]{:S(2)}, u32[]{:S(2)}) collective-permute-start(bf16[272,256]{1,0:T(8,128)(2,1)S(1)} %collective-permute-done.3.kv_o.refs_1_.refs_5_), channel_id=1, source_target_pairs={{0,24},{8,16},{16,8},{24,0},{1,25},{9,17},{17,9},{25,1},{2,26},{10... | collective-permute-start | bytes 417800 | tf_op jit(solution)/shard_map/ppermute | solution.py:315
  46.1 4.0 %copy-start.7 = (f32[256]{0:T(256)S(1)}, f32[256]{0:T(256)}, u32[]{:S(2)}) copy-start(f32[256]{0:T(256)} %param.17) | copy-start | bytes 3076
  46.2 2.0 %collective-permute-start.11 = (bf16[128,2048]{1,0:T(8,128)(2,1)S(1)}, bf16[128,2048]{1,0:T(8,128)(2,1)S(1)}, u32[]{:S(2)}, u32[]{:S(2)}) collective-permute-start(bf16[128,2048]{1,0:T(8,128)(2,1)S(1)} %collective-permute-done.10.far), channel_id=1, source_target_pairs={{0,1},{1,0},{2,3},{3,2},{4,5},{5,4},{6,7},{7,6},{8,9},{9,8},{10,11... | collective-permute-start | bytes 1572872 | tf_op jit(solution)/shard_map/ppermute | solution.py:312
  48.1 8.3 %collective-permute-start.15 = (bf16[256,512]{1,0:T(8,128)(2,1)S(1)}, bf16[256,512]{1,0:T(8,128)(2,1)S(1)}, u32[]{:S(2)}, u32[]{:S(2)}) collective-permute-start(bf16[256,512]{1,0:T(8,128)(2,1)S(1)} %collective-permute-done.9.refs_1_), channel_id=1, source_target_pairs={{0,8},{8,0},{16,24},{24,16},{1,9},{9,1},{17,25},{25,17},{2,10},{10... | collective-permute-start | bytes 786440 | tf_op jit(solution)/shard_map/ppermute | solution.py:315
  48.7 8.1 %collective-permute-start.16 = (bf16[256,512]{1,0:T(8,128)(2,1)S(1)}, bf16[256,512]{1,0:T(8,128)(2,1)S(1)}, u32[]{:S(2)}, u32[]{:S(2)}) collective-permute-start(bf16[256,512]{1,0:T(8,128)(2,1)S(1)} %collective-permute-done.9.refs_1_), channel_id=1, source_target_pairs={{0,16},{8,24},{16,0},{24,8},{1,17},{9,25},{17,1},{25,9},{2,18},{10... | collective-permute-start | bytes 786440 | tf_op jit(solution)/shard_map/ppermute | solution.py:315
  51.1 14.2 %collective-permute-start.12 = (bf16[512,256]{1,0:T(8,128)(2,1)S(1)}, bf16[512,256]{1,0:T(8,128)(2,1)S(1)}, u32[]{:S(2)}, u32[]{:S(2)}) collective-permute-start(bf16[512,256]{1,0:T(8,128)(2,1)S(1)} %project_kv.1.refs_0_), channel_id=1, source_target_pairs={{0,4},{1,5},{2,6},{3,7},{4,0},{5,1},{6,2},{7,3},{8,12},{9,13},{10,... | collective-permute-start | bytes 786440 | tf_op jit(solution)/shard_map/ppermute | solution.py:318
  56.7 8.6 %copy-start.8 = (f32[256]{0:T(256)S(1)}, f32[256]{0:T(256)}, u32[]{:S(2)}) copy-start(f32[256]{0:T(256)} %param.16) | copy-start | bytes 3076
  56.7 8.6 %collective-permute-start.17 = (bf16[256,512]{1,0:T(8,128)(2,1)S(1)}, bf16[256,512]{1,0:T(8,128)(2,1)S(1)}, u32[]{:S(2)}, u32[]{:S(2)}) collective-permute-start(bf16[256,512]{1,0:T(8,128)(2,1)S(1)} %get-tuple-element.69), channel_id=1, source_target_pairs={{0,16},{8,24},{16,0},{24,8},{1,17},{9,25},{17,1},{25,9},{2,18},{10... | collective-permute-start | bytes 786440 | tf_op jit(solution)/shard_map/ppermute | solution.py:315
  58.3 7.1 %collective-permute-start.18 = (bf16[256,512]{1,0:T(8,128)(2,1)S(1)}, bf16[256,512]{1,0:T(8,128)(2,1)S(1)}, u32[]{:S(2)}, u32[]{:S(2)}) collective-permute-start(bf16[256,512]{1,0:T(8,128)(2,1)S(1)} %collective-permute-done.16.refs_5_), channel_id=1, source_target_pairs={{0,8},{8,0},{16,24},{24,16},{1,9},{9,1},{17,25},{25,17},{2,10},{10... | collective-permute-start | bytes 786440 | tf_op jit(solution)/shard_map/ppermute | solution.py:315
  59.8 8.4 %collective-permute-start.13 = (bf16[512,256]{1,0:T(8,128)(2,1)S(1)}, bf16[512,256]{1,0:T(8,128)(2,1)S(1)}, u32[]{:S(2)}, u32[]{:S(2)}) collective-permute-start(bf16[512,256]{1,0:T(8,128)(2,1)S(1)} %project_kv.1.refs_0_), channel_id=1, source_target_pairs={{0,1},{1,0},{2,3},{3,2},{4,5},{5,4},{6,7},{7,6},{8,9},{9,8},{10,11... | collective-permute-start | bytes 786440 | tf_op jit(solution)/shard_map/ppermute | solution.py:312
  65.3 2.9 %collective-permute-start.14 = (bf16[512,256]{1,0:T(8,128)(2,1)S(1)}, bf16[512,256]{1,0:T(8,128)(2,1)S(1)}, u32[]{:S(2)}, u32[]{:S(2)}) collective-permute-start(bf16[512,256]{1,0:T(8,128)(2,1)S(1)} %collective-permute-done.12.refs_1_), channel_id=1, source_target_pairs={{0,1},{1,0},{2,3},{3,2},{4,5},{5,4},{6,7},{7,6},{8,9},{9,8},{10,11... | collective-permute-start | bytes 786440 | tf_op jit(solution)/shard_map/ppermute | solution.py:312
  66.9 1.3 %copy-start.6 = (s32[1,2,16]{2,1,0:T(2,128)S(1)}, s32[1,2,16]{2,1,0:T(2,128)}, u32[]{:S(2)}) copy-start(s32[1,2,16]{2,1,0:T(2,128)} %table.1) | copy-start | bytes 388
  66.9 2.4 %collective-permute-start.19 = (bf16[256,512]{1,0:T(8,128)(2,1)S(1)}, bf16[256,512]{1,0:T(8,128)(2,1)S(1)}, u32[]{:S(2)}, u32[]{:S(2)}) collective-permute-start(bf16[256,512]{1,0:T(8,128)(2,1)S(1)} %get-tuple-element.71), channel_id=1, source_target_pairs={{0,1},{1,0},{2,3},{3,2},{4,5},{5,4},{6,7},{7,6},{8,9},{9,8},{10,11... | collective-permute-start | bytes 786440 | tf_op jit(solution)/shard_map/ppermute | solution.py:312
  69.2 9.2 %collective-permute-start.21 = (bf16[4,64,512]{2,1,0:T(8,128)(2,1)S(1)}, bf16[4,64,512]{2,1,0:T(8,128)(2,1)S(1)}, u32[]{:S(2)}, u32[]{:S(2)}) collective-permute-start(bf16[4,64,512]{2,1,0:T(8,128)(2,1)S(1)} %get-tuple-element.73), channel_id=1, source_target_pairs={{0,2},{1,3},{2,0},{3,1},{4,6},{5,7},{6,4},{7,5},{8,10},{9,11},{10,... | collective-permute-start | bytes 786440 | tf_op jit(solution)/shard_map/ppermute | solution.py:312
  71.0 12.1 %collective-permute-start.20 = (bf16[128,1024]{1,0:T(8,128)(2,1)S(1)}, bf16[128,1024]{1,0:T(8,128)(2,1)S(1)}, u32[]{:S(2)}, u32[]{:S(2)}) collective-permute-start(bf16[128,1024]{1,0:T(8,128)(2,1)S(1)} %attend.3), channel_id=1, source_target_pairs={{0,2},{1,3},{2,0},{3,1},{4,6},{5,7},{6,4},{7,5},{8,10},{9,11},{10,... | collective-permute-start | bytes 786440 | tf_op jit(solution)/shard_map/ppermute | solution.py:312

commit v12 on v11

--- a/solution.py
+++ b/solution.py
@@ -375,7 +375,7 @@
         out_shape=[shape((TEAM * rows, half), jnp.float32)] * 2,
         in_specs=[VMEM] * 5,
         out_specs=[VMEM] * 2,
-        cost_estimate=pl.CostEstimate(flops=0, bytes_accessed=38 * MIB, transcendentals=0),
+        cost_estimate=pl.CostEstimate(flops=10**10, bytes_accessed=40 * 10**6, transcendentals=0),
         compiler_params=params(2),
         name="angles",
     )(kv, *tables)

time: 85.1 us -> 77.2 us (0.907)
  waiting for transfers between devices: 45.8 us -> 40.7 us
  starting transfers between devices: 25.4 us -> 22.6 us
    ppermute x3, waiting for transfers between devices: 24.4 us -> 19.6 us  [across(): lax.ppermute(array, 'blk', [(i, (i + TEAM * k) % n_blk) for i in range(n_...]
    ppermute x9, starting transfers between devices: 11.7 us -> 9.61 us  [in_req(): return lax.ppermute(array, 'req', [(i, i ^ k) for i in range(n_req)])]
    ppermute x9, waiting for transfers between devices: 5.58 us -> 4.3 us  [in_req(): return lax.ppermute(array, 'req', [(i, i ^ k) for i in range(n_req)])]
    ppermute x10, waiting for transfers between devices: 15.8 us -> 16.8 us  [in_team(): return lax.ppermute(array, 'blk', [(i, i ^ k) for i in range(n_blk)])]
  transfers between devices with their start and end apart: 22 -> 22, of which waited for: 10 -> 11; matrix products, arithmetic and copies ran while one was open for 0% -> 0% of each run, Pallas kernels for 8% -> 9%
where the time goes in v12:
time: 77.2 us; the launch traced here: 77.1 us
  waiting for transfers between devices  40.7 us (53%)
  starting transfers between devices  22.6 us (29%)
  Pallas kernels  11.3 us (15%)
  between operations  1.47 us (2%)
  local copies, waits for them, and re-layouts  0.95 us (1%)
    ppermute x3, waiting for transfers between devices, across(): lax.ppermute(array, 'blk', [(i, (i + TEAM * k) % n_blk) for i in range(n_...  19.6 us
    ppermute x10, waiting for transfers between devices, in_team(): return lax.ppermute(array, 'blk', [(i, i ^ k) for i in range(n_blk)])  16.8 us
    ppermute x9, starting transfers between devices, in_req(): return lax.ppermute(array, 'req', [(i, i ^ k) for i in range(n_req)])  9.61 us
    ppermute x10, starting transfers between devices, in_team(): return lax.ppermute(array, 'blk', [(i, i ^ k) for i in range(n_blk)])  7.61 us
    ppermute x3, starting transfers between devices, across(): lax.ppermute(array, 'blk', [(i, (i + TEAM * k) % n_blk) for i in range(n_...  5.35 us
    ppermute x9, waiting for transfers between devices, in_req(): return lax.ppermute(array, 'req', [(i, i ^ k) for i in range(n_req)])  4.3 us
    pallas_call x2, Pallas kernels, attend(): pl.pallas_call(functools.partial(attend_kernel, blk_rows, step), out_shap...  3.42 us
    pallas_call x2, Pallas kernels, project(): pl.pallas_call(functools.partial(project_kernel, n_out, TEAM * w_rows, st...  2.47 us
  transfers between devices with their start and end apart: 22, of which 11 were waited for; matrix products, arithmetic and copies ran while one was open for 0% of the time, Pallas kernels for 9%

profile of v12, /device:TPU:0, one launch (start us, length us, event | category | flops | bytes accessed | tf_op | source)
XLA Modules:
  0.0 77.1 jit_solution(14483001467955555123)
XLA Ops:
  0.6 2.3 %pack.1 = (bf16[400,128]{1,0:T(8,128)(2,1)}, bf16[2448,128]{1,0:T(8,128)(2,1)}, bf16[400,128]{1,0:T(8,128)(2,1)}, bf16[400,128]{1,0:T(8,128)(2,1)}) custom-call(bf16[64,3072]{1,0:T(8,128)(2,1)} %w_hbm.1, s32[1,2]{1,0:T(1,128)} %ids_hbm.1, bf16[128,2048]{1,0:T(8,128)(2,1)} %bitcast.5), custom_call_target="tpu_custom_call" | custom-call | tf_op jit(solution)/shard_map/pack/pallas_call | solution.py:328
  3.4 2.7 %collective-permute-start.1 = (bf16[400,128]{1,0:T(8,128)(2,1)}, bf16[400,128]{1,0:T(8,128)(2,1)S(1)}, u32[]{:S(2)}, u32[]{:S(2)}) collective-permute-start(bf16[400,128]{1,0:T(8,128)(2,1)} %get-tuple-element.41), channel_id=1, source_target_pairs={{0,2},{1,3},{2,0},{3,1},{4,6},{5,7},{6,4},{7,5},{8,10},{9,11},{10,... | collective-permute-start | bytes 307208 | tf_op jit(solution)/shard_map/ppermute | solution.py:312
  6.2 3.9 %collective-permute-done.1.refs_2_ = bf16[400,128]{1,0:T(8,128)(2,1)S(1)} collective-permute-done((bf16[400,128]{1,0:T(8,128)(2,1)}, bf16[400,128]{1,0:T(8,128)(2,1)S(1)}, u32[]{:S(2)}, u32[]{:S(2)}) %collective-permute-start.1) | collective-permute-done | bytes 102432 | tf_op jit(solution)/shard_map/ppermute | solution.py:312
  10.0 1.7 %collective-permute-done.2.refs_3_ = bf16[400,128]{1,0:T(8,128)(2,1)S(1)} collective-permute-done((bf16[400,128]{1,0:T(8,128)(2,1)}, bf16[400,128]{1,0:T(8,128)(2,1)S(1)}, u32[]{:S(2)}, u32[]{:S(2)}) %collective-permute-start.2) | collective-permute-done | bytes 102432 | tf_op jit(solution)/shard_map/ppermute | solution.py:312
  11.7 0.9 %copy-done.1 = bf16[400,128]{1,0:T(8,128)(2,1)S(1)} copy-done((bf16[400,128]{1,0:T(8,128)(2,1)S(1)}, bf16[400,128]{1,0:T(8,128)(2,1)}, u32[]{:S(2)}) %copy-start.1) | copy-done | bytes 102424
  12.8 1.5 %collective-permute-start.4 = (bf16[256,768]{1,0:T(8,128)(2,1)S(1)}, bf16[256,768]{1,0:T(8,128)(2,1)S(1)}, u32[]{:S(2)}, u32[]{:S(2)}) collective-permute-start(bf16[256,768]{1,0:T(8,128)(2,1)S(1)} %get-tuple-element.48), channel_id=1, source_target_pairs={{0,8},{8,0},{16,24},{24,16},{1,9},{9,1},{17,25},{25,17},{2,10},{10... | collective-permute-start | bytes 1179656 | tf_op jit(solution)/shard_map/ppermute | solution.py:315
  14.3 1.5 %collective-permute-start.5 = (bf16[256,768]{1,0:T(8,128)(2,1)S(1)}, bf16[256,768]{1,0:T(8,128)(2,1)S(1)}, u32[]{:S(2)}, u32[]{:S(2)}) collective-permute-start(bf16[256,768]{1,0:T(8,128)(2,1)S(1)} %get-tuple-element.48), channel_id=1, source_target_pairs={{0,16},{8,24},{16,0},{24,8},{1,17},{9,25},{17,1},{25,9},{2,18},{10... | collective-permute-start | bytes 1179656 | tf_op jit(solution)/shard_map/ppermute | solution.py:315
  15.9 2.6 %collective-permute-start.3 = (bf16[272,256]{1,0:T(8,128)(2,1)S(1)}, bf16[272,256]{1,0:T(8,128)(2,1)S(1)}, u32[]{:S(2)}, u32[]{:S(2)}) collective-permute-start(bf16[272,256]{1,0:T(8,128)(2,1)S(1)} %get-tuple-element.47.piece.refs_0_.refs_4_), channel_id=1, source_target_pairs={{0,4},{1,5},{2,6},{3,7},{4,0},{5,1},{6,2},{7,3},{8,12},{9,13},{10,... | collective-permute-start | bytes 417800 | tf_op jit(solution)/shard_map/ppermute | solution.py:318
  18.5 1.6 %collective-permute-start.10 = (bf16[128,2048]{1,0:T(8,128)(2,1)S(1)}, bf16[128,2048]{1,0:T(8,128)(2,1)S(1)}, u32[]{:S(2)}, u32[]{:S(2)}) collective-permute-start(bf16[128,2048]{1,0:T(8,128)(2,1)S(1)} %bitcast.6), channel_id=1, source_target_pairs={{0,2},{1,3},{2,0},{3,1},{4,6},{5,7},{6,4},{7,5},{8,10},{9,11},{10,... | collective-permute-start | bytes 1572872 | tf_op jit(solution)/shard_map/ppermute | solution.py:312
  20.4 5.9 %collective-permute-done.3.kv_o.refs_1_.refs_5_ = bf16[272,256]{1,0:T(8,128)(2,1)S(1)} collective-permute-done((bf16[272,256]{1,0:T(8,128)(2,1)S(1)}, bf16[272,256]{1,0:T(8,128)(2,1)S(1)}, u32[]{:S(2)}, u32[]{:S(2)}) %collective-permute-start.3) | collective-permute-done | bytes 139296 | tf_op jit(solution)/shard_map/ppermute | solution.py:318
  26.3 0.5 collective-permute-start.6
  26.8 1.5 %collective-permute-start.8 = (bf16[272,256]{1,0:T(8,128)(2,1)S(1)}, bf16[272,256]{1,0:T(8,128)(2,1)S(1)}, u32[]{:S(2)}, u32[]{:S(2)}) collective-permute-start(bf16[272,256]{1,0:T(8,128)(2,1)S(1)} %collective-permute-done.3.kv_o.refs_1_.refs_5_), channel_id=1, source_target_pairs={{0,24},{8,16},{16,8},{24,0},{1,25},{9,17},{17,9},{25,1},{2,26},{10... | collective-permute-start | bytes 417800 | tf_op jit(solution)/shard_map/ppermute | solution.py:315
  28.4 1.5 %collective-permute-start.7 = (bf16[528,256]{1,0:T(8,128)(2,1)S(1)}, bf16[528,256]{1,0:T(8,128)(2,1)S(1)}, u32[]{:S(2)}, u32[]{:S(2)}) collective-permute-start(bf16[528,256]{1,0:T(8,128)(2,1)S(1)} %get-tuple-element.51), channel_id=1, source_target_pairs={{0,16},{8,24},{16,0},{24,8},{1,17},{9,25},{17,1},{25,9},{2,18},{10... | collective-permute-start | bytes 811016 | tf_op jit(solution)/shard_map/ppermute | solution.py:315
  30.1 8.0 %collective-permute-done.9.refs_1_ = bf16[256,512]{1,0:T(8,128)(2,1)S(1)} collective-permute-done((bf16[256,512]{1,0:T(8,128)(2,1)S(1)}, bf16[256,512]{1,0:T(8,128)(2,1)S(1)}, u32[]{:S(2)}, u32[]{:S(2)}) %collective-permute-start.9) | collective-permute-done | bytes 262176 | tf_op jit(solution)/shard_map/ppermute | solution.py:318
  38.1 1.1 %collective-permute-done.10.far = bf16[128,2048]{1,0:T(8,128)(2,1)S(1)} collective-permute-done((bf16[128,2048]{1,0:T(8,128)(2,1)S(1)}, bf16[128,2048]{1,0:T(8,128)(2,1)S(1)}, u32[]{:S(2)}, u32[]{:S(2)}) %collective-permute-start.10) | collective-permute-done | bytes 524320 | tf_op jit(solution)/shard_map/ppermute | solution.py:312
  39.3 1.9 %collective-permute-done.11.far_near = bf16[128,2048]{1,0:T(8,128)(2,1)S(1)} collective-permute-done((bf16[128,2048]{1,0:T(8,128)(2,1)S(1)}, bf16[128,2048]{1,0:T(8,128)(2,1)S(1)}, u32[]{:S(2)}, u32[]{:S(2)}) %collective-permute-start.11) | collective-permute-done | bytes 524320 | tf_op jit(solution)/shard_map/ppermute | solution.py:312
  41.2 0.5 collective-permute-start.15
  42.2 0.9 %project_kv.1.refs_0_ = bf16[512,256]{1,0:T(8,128)(2,1)S(1)} custom-call(bf16[128,2048]{1,0:T(8,128)(2,1)S(1)} %bitcast.7, bf16[2448,128]{1,0:T(8,128)(2,1)S(1)} %collective-permute-done.refs_1_.near, bf16[128,2048]{1,0:T(8,128)(2,1)S(1)} %collective-permute-done.10.far, bf16[128,2048]{1,0:T(8,128)(2,1)S(1)} %collective-permute-done.11.far_near, ...), custom_call_target="tpu_custom_call" | custom-call | flops 536870912 | bytes 6291456 | tf_op jit(solution)/shard_map/project_kv/pallas_call | solution.py:409
  43.1 2.4 %collective-permute-start.12 = (bf16[512,256]{1,0:T(8,128)(2,1)S(1)}, bf16[512,256]{1,0:T(8,128)(2,1)S(1)}, u32[]{:S(2)}, u32[]{:S(2)}) collective-permute-start(bf16[512,256]{1,0:T(8,128)(2,1)S(1)} %project_kv.1.refs_0_), channel_id=1, source_target_pairs={{0,4},{1,5},{2,6},{3,7},{4,0},{5,1},{6,2},{7,3},{8,12},{9,13},{10,... | collective-permute-start | bytes 786440 | tf_op jit(solution)/shard_map/ppermute | solution.py:318
  45.5 4.0 %collective-permute-done.15.refs_3_ = bf16[256,512]{1,0:T(8,128)(2,1)S(1)} collective-permute-done((bf16[256,512]{1,0:T(8,128)(2,1)S(1)}, bf16[256,512]{1,0:T(8,128)(2,1)S(1)}, u32[]{:S(2)}, u32[]{:S(2)}) %collective-permute-start.15) | collective-permute-done | bytes 262176 | tf_op jit(solution)/shard_map/ppermute | solution.py:315
  50.3 1.5 %collective-permute-start.18 = (bf16[256,512]{1,0:T(8,128)(2,1)S(1)}, bf16[256,512]{1,0:T(8,128)(2,1)S(1)}, u32[]{:S(2)}, u32[]{:S(2)}) collective-permute-start(bf16[256,512]{1,0:T(8,128)(2,1)S(1)} %collective-permute-done.16.refs_5_), channel_id=1, source_target_pairs={{0,8},{8,0},{16,24},{24,16},{1,9},{9,1},{17,25},{25,17},{2,10},{10... | collective-permute-start | bytes 786440 | tf_op jit(solution)/shard_map/ppermute | solution.py:315
  51.8 5.7 %collective-permute-done.12.refs_1_ = bf16[512,256]{1,0:T(8,128)(2,1)S(1)} collective-permute-done((bf16[512,256]{1,0:T(8,128)(2,1)S(1)}, bf16[512,256]{1,0:T(8,128)(2,1)S(1)}, u32[]{:S(2)}, u32[]{:S(2)}) %collective-permute-start.12) | collective-permute-done | bytes 262176 | tf_op jit(solution)/shard_map/ppermute | solution.py:318
  57.5 1.6 %project_q.1 = (bf16[256,512]{1,0:T(8,128)(2,1)S(1)}, bf16[256,512]{1,0:T(8,128)(2,1)S(1)}) custom-call(bf16[128,2048]{1,0:T(8,128)(2,1)S(1)} %bitcast.8, bf16[2448,128]{1,0:T(8,128)(2,1)S(1)} %collective-permute-done.refs_1_.near, bf16[128,2048]{1,0:T(8,128)(2,1)S(1)} %collective-permute-done.10.far, ...), custom_call_target="tpu_custom_call" | custom-call | flops 1073741824 | bytes 6291456 | tf_op jit(solution)/shard_map/project_q/pallas_call | solution.py:409
  59.1 0.6 collective-permute-start.19
  60.4 1.1 %pages.1 = (bf16[4,64,512]{2,1,0:T(8,128)(2,1)S(1)}, bf16[4,64,512]{2,1,0:T(8,128)(2,1)S(1)}, bf16[2,1024,256]{2,1,0:T(8,128)(2,1)S(1)}) custom-call(bf16[512,256]{1,0:T(8,128)(2,1)S(1)} %project_kv.1.refs_0_, bf16[512,256]{1,0:T(8,128)(2,1)S(1)} %collective-permute-done.12.refs_1_, bf16[512,256]{1,0:T(8,128)(2,1)S(1)} %collective-permute-done.13.refs_2_, ...), custom_call_target="tpu_custom_call" | custom-call | bytes 4194304 | tf_op jit(solution)/shard_map/pages/pallas_call | solution.py:439
  61.4 0.7 collective-permute-start.21
  62.1 1.7 %attend.3 = bf16[128,1024]{1,0:T(8,128)(2,1)S(1)} custom-call(bf16[2,1024,256]{2,1,0:T(8,128)(2,1)S(1)} %get-tuple-element.64.store, bf16[256,512]{1,0:T(8,128)(2,1)S(1)} %get-tuple-element.70.q_ref, bf16[256,512]{1,0:T(8,128)(2,1)S(1)} %collective-permute-done.19.near_ref, bf16[272,256]{1,0:T(8,128)(2,1)S(1)} %get-tuple-element.47.piece.refs_0_.refs_4_, ...), custom_call_target="tpu_custom_call" | custom-call | flops 536870912 | bytes 4194304 | tf_op jit(solution)/shard_map/attend/pallas_call | solution.py:452
  63.9 1.4 %collective-permute-start.20 = (bf16[128,1024]{1,0:T(8,128)(2,1)S(1)}, bf16[128,1024]{1,0:T(8,128)(2,1)S(1)}, u32[]{:S(2)}, u32[]{:S(2)}) collective-permute-start(bf16[128,1024]{1,0:T(8,128)(2,1)S(1)} %attend.3), channel_id=1, source_target_pairs={{0,2},{1,3},{2,0},{3,1},{4,6},{5,7},{6,4},{7,5},{8,10},{9,11},{10,... | collective-permute-start | bytes 786440 | tf_op jit(solution)/shard_map/ppermute | solution.py:312
  65.3 1.7 %attend.2.kept = bf16[128,1024]{1,0:T(8,128)(2,1)S(1)} custom-call(bf16[2,1024,256]{2,1,0:T(8,128)(2,1)S(1)} %get-tuple-element.64.store, bf16[256,512]{1,0:T(8,128)(2,1)S(1)} %get-tuple-element.70.q_ref, bf16[256,512]{1,0:T(8,128)(2,1)S(1)} %collective-permute-done.19.near_ref, bf16[272,256]{1,0:T(8,128)(2,1)S(1)} %get-tuple-element.47.piece.refs_0_.refs_4_, ...), custom_call_target="tpu_custom_call" | custom-call | flops 536870912 | bytes 4194304 | tf_op jit(solution)/shard_map/attend/pallas_call | solution.py:452
  67.0 3.6 %collective-permute-done.21.got_pages = bf16[4,64,512]{2,1,0:T(8,128)(2,1)S(1)} collective-permute-done((bf16[4,64,512]{2,1,0:T(8,128)(2,1)S(1)}, bf16[4,64,512]{2,1,0:T(8,128)(2,1)S(1)}, u32[]{:S(2)}, u32[]{:S(2)}) %collective-permute-start.21) | collective-permute-done | bytes 262176 | tf_op jit(solution)/shard_map/ppermute | solution.py:312
  70.7 4.7 %collective-permute-done.20.from_far = bf16[128,1024]{1,0:T(8,128)(2,1)S(1)} collective-permute-done((bf16[128,1024]{1,0:T(8,128)(2,1)S(1)}, bf16[128,1024]{1,0:T(8,128)(2,1)S(1)}, u32[]{:S(2)}, u32[]{:S(2)}) %collective-permute-start.20) | collective-permute-done | bytes 262176 | tf_op jit(solution)/shard_map/ppermute | solution.py:312
  75.3 1.7 %finish.1 = (bf16[128,2048]{1,0:T(8,128)(2,1)}, bf16[4,64,512]{2,1,0:T(8,128)(2,1)}) custom-call(bf16[128,1024]{1,0:T(8,128)(2,1)S(1)} %attend.2.kept, bf16[128,1024]{1,0:T(8,128)(2,1)S(1)} %collective-permute-done.20.from_far, bf16[4,64,512]{2,1,0:T(8,128)(2,1)S(1)} %get-tuple-element.72.own_pages, ...), custom_call_target="tpu_custom_call" | custom-call | tf_op jit(solution)/shard_map/finish/pallas_call | solution.py:467
  (40 shorter events, 2.6 us)
Async XLA Ops:
  2.9 15.5 %copy-start = (bf16[1,128,2048]{2,1,0:T(8,128)(2,1)S(1)}, bf16[1,128,2048]{2,1,0:T(8,128)(2,1)}, u32[]{:S(2)}) copy-start(bf16[1,128,2048]{2,1,0:T(8,128)(2,1)} %param.11) | copy-start | bytes 1572868
  2.9 8.8 %collective-permute-start = (bf16[2448,128]{1,0:T(8,128)(2,1)}, bf16[2448,128]{1,0:T(8,128)(2,1)S(1)}, u32[]{:S(2)}, u32[]{:S(2)}) collective-permute-start(bf16[2448,128]{1,0:T(8,128)(2,1)} %get-tuple-element.40), channel_id=1, source_target_pairs={{0,1},{1,0},{2,3},{3,2},{4,5},{5,4},{6,7},{7,6},{8,9},{9,8},{10,11... | collective-permute-start | bytes 1880072 | tf_op jit(solution)/shard_map/ppermute | solution.py:312
  3.4 6.6 %collective-permute-start.1 = (bf16[400,128]{1,0:T(8,128)(2,1)}, bf16[400,128]{1,0:T(8,128)(2,1)S(1)}, u32[]{:S(2)}, u32[]{:S(2)}) collective-permute-start(bf16[400,128]{1,0:T(8,128)(2,1)} %get-tuple-element.41), channel_id=1, source_target_pairs={{0,2},{1,3},{2,0},{3,1},{4,6},{5,7},{6,4},{7,5},{8,10},{9,11},{10,... | collective-permute-start | bytes 307208 | tf_op jit(solution)/shard_map/ppermute | solution.py:312
  6.1 5.6 %collective-permute-start.2 = (bf16[400,128]{1,0:T(8,128)(2,1)}, bf16[400,128]{1,0:T(8,128)(2,1)S(1)}, u32[]{:S(2)}, u32[]{:S(2)}) collective-permute-start(bf16[400,128]{1,0:T(8,128)(2,1)} %get-tuple-element.42), channel_id=1, source_target_pairs={{0,3},{1,2},{2,1},{3,0},{4,7},{5,6},{6,5},{7,4},{8,11},{9,10},{10,... | collective-permute-start | bytes 307208 | tf_op jit(solution)/shard_map/ppermute | solution.py:312
  11.7 0.9 %copy-start.1 = (bf16[400,128]{1,0:T(8,128)(2,1)S(1)}, bf16[400,128]{1,0:T(8,128)(2,1)}, u32[]{:S(2)}) copy-start(bf16[400,128]{1,0:T(8,128)(2,1)} %get-tuple-element.39.refs_0_) | copy-start | bytes 307204
  12.7 17.1 %copy-start.5 = (f32[64,128]{1,0:T(8,128)S(1)}, f32[64,128]{1,0:T(8,128)}, u32[]{:S(2)}) copy-start(f32[64,128]{1,0:T(8,128)} %constant.10.clone.off_cos) | copy-start | bytes 98308
  12.8 17.1 %copy-start.6 = (f32[64,128]{1,0:T(8,128)S(1)}, f32[64,128]{1,0:T(8,128)}, u32[]{:S(2)}) copy-start(f32[64,128]{1,0:T(8,128)} %constant.11.clone.off_sin) | copy-start | bytes 98308
  12.8 17.1 %copy-start.7 = (f32[16,128]{1,0:T(8,128)S(1)}, f32[16,128]{1,0:T(8,128)}, u32[]{:S(2)}) copy-start(f32[16,128]{1,0:T(8,128)} %constant.8.clone.first_cos) | copy-start | bytes 24580
  12.8 17.1 %copy-start.8 = (f32[16,128]{1,0:T(8,128)S(1)}, f32[16,128]{1,0:T(8,128)}, u32[]{:S(2)}) copy-start(f32[16,128]{1,0:T(8,128)} %constant.9.clone.first_sin) | copy-start | bytes 24580
  12.8 13.5 %collective-permute-start.4 = (bf16[256,768]{1,0:T(8,128)(2,1)S(1)}, bf16[256,768]{1,0:T(8,128)(2,1)S(1)}, u32[]{:S(2)}, u32[]{:S(2)}) collective-permute-start(bf16[256,768]{1,0:T(8,128)(2,1)S(1)} %get-tuple-element.48), channel_id=1, source_target_pairs={{0,8},{8,0},{16,24},{24,16},{1,9},{9,1},{17,25},{25,17},{2,10},{10... | collective-permute-start | bytes 1179656 | tf_op jit(solution)/shard_map/ppermute | solution.py:315
  14.3 11.9 %collective-permute-start.5 = (bf16[256,768]{1,0:T(8,128)(2,1)S(1)}, bf16[256,768]{1,0:T(8,128)(2,1)S(1)}, u32[]{:S(2)}, u32[]{:S(2)}) collective-permute-start(bf16[256,768]{1,0:T(8,128)(2,1)S(1)} %get-tuple-element.48), channel_id=1, source_target_pairs={{0,16},{8,24},{16,0},{24,8},{1,17},{9,25},{17,1},{25,9},{2,18},{10... | collective-permute-start | bytes 1179656 | tf_op jit(solution)/shard_map/ppermute | solution.py:315
  15.9 10.4 %collective-permute-start.3 = (bf16[272,256]{1,0:T(8,128)(2,1)S(1)}, bf16[272,256]{1,0:T(8,128)(2,1)S(1)}, u32[]{:S(2)}, u32[]{:S(2)}) collective-permute-start(bf16[272,256]{1,0:T(8,128)(2,1)S(1)} %get-tuple-element.47.piece.refs_0_.refs_4_), channel_id=1, source_target_pairs={{0,4},{1,5},{2,6},{3,7},{4,0},{5,1},{6,2},{7,3},{8,12},{9,13},{10,... | collective-permute-start | bytes 417800 | tf_op jit(solution)/shard_map/ppermute | solution.py:318
  18.5 20.8 %collective-permute-start.10 = (bf16[128,2048]{1,0:T(8,128)(2,1)S(1)}, bf16[128,2048]{1,0:T(8,128)(2,1)S(1)}, u32[]{:S(2)}, u32[]{:S(2)}) collective-permute-start(bf16[128,2048]{1,0:T(8,128)(2,1)S(1)} %bitcast.6), channel_id=1, source_target_pairs={{0,2},{1,3},{2,0},{3,1},{4,6},{5,7},{6,4},{7,5},{8,10},{9,11},{10,... | collective-permute-start | bytes 1572872 | tf_op jit(solution)/shard_map/ppermute | solution.py:312
  20.0 18.1 %collective-permute-start.9 = (bf16[256,512]{1,0:T(8,128)(2,1)S(1)}, bf16[256,512]{1,0:T(8,128)(2,1)S(1)}, u32[]{:S(2)}, u32[]{:S(2)}) collective-permute-start(bf16[256,512]{1,0:T(8,128)(2,1)S(1)} %get-tuple-element.52.refs_0_), channel_id=1, source_target_pairs={{0,4},{1,5},{2,6},{3,7},{4,0},{5,1},{6,2},{7,3},{8,12},{9,13},{10,... | collective-permute-start | bytes 786440 | tf_op jit(solution)/shard_map/ppermute | solution.py:318
  26.3 12.9 %collective-permute-start.6 = (bf16[272,256]{1,0:T(8,128)(2,1)S(1)}, bf16[272,256]{1,0:T(8,128)(2,1)S(1)}, u32[]{:S(2)}, u32[]{:S(2)}) collective-permute-start(bf16[272,256]{1,0:T(8,128)(2,1)S(1)} %collective-permute-done.3.kv_o.refs_1_.refs_5_), channel_id=1, source_target_pairs={{0,8},{8,0},{16,24},{24,16},{1,9},{9,1},{17,25},{25,17},{2,10},{10... | collective-permute-start | bytes 417800 | tf_op jit(solution)/shard_map/ppermute | solution.py:315
  26.8 12.4 %collective-permute-start.8 = (bf16[272,256]{1,0:T(8,128)(2,1)S(1)}, bf16[272,256]{1,0:T(8,128)(2,1)S(1)}, u32[]{:S(2)}, u32[]{:S(2)}) collective-permute-start(bf16[272,256]{1,0:T(8,128)(2,1)S(1)} %collective-permute-done.3.kv_o.refs_1_.refs_5_), channel_id=1, source_target_pairs={{0,24},{8,16},{16,8},{24,0},{1,25},{9,17},{17,9},{25,1},{2,26},{10... | collective-permute-start | bytes 417800 | tf_op jit(solution)/shard_map/ppermute | solution.py:315
  28.4 10.8 %collective-permute-start.7 = (bf16[528,256]{1,0:T(8,128)(2,1)S(1)}, bf16[528,256]{1,0:T(8,128)(2,1)S(1)}, u32[]{:S(2)}, u32[]{:S(2)}) collective-permute-start(bf16[528,256]{1,0:T(8,128)(2,1)S(1)} %get-tuple-element.51), channel_id=1, source_target_pairs={{0,16},{8,24},{16,0},{24,8},{1,17},{9,25},{17,1},{25,9},{2,18},{10... | collective-permute-start | bytes 811016 | tf_op jit(solution)/shard_map/ppermute | solution.py:315
  39.2 3.0 %copy-start.3 = (f32[256]{0:T(256)S(1)}, f32[256]{0:T(256)}, u32[]{:S(2)}) copy-start(f32[256]{0:T(256)} %param.17) | copy-start | bytes 3076
  39.2 2.0 %collective-permute-start.11 = (bf16[128,2048]{1,0:T(8,128)(2,1)S(1)}, bf16[128,2048]{1,0:T(8,128)(2,1)S(1)}, u32[]{:S(2)}, u32[]{:S(2)}) collective-permute-start(bf16[128,2048]{1,0:T(8,128)(2,1)S(1)} %collective-permute-done.10.far), channel_id=1, source_target_pairs={{0,1},{1,0},{2,3},{3,2},{4,5},{5,4},{6,7},{7,6},{8,9},{9,8},{10,11... | collective-permute-start | bytes 1572872 | tf_op jit(solution)/shard_map/ppermute | solution.py:312
  41.2 8.3 %collective-permute-start.15 = (bf16[256,512]{1,0:T(8,128)(2,1)S(1)}, bf16[256,512]{1,0:T(8,128)(2,1)S(1)}, u32[]{:S(2)}, u32[]{:S(2)}) collective-permute-start(bf16[256,512]{1,0:T(8,128)(2,1)S(1)} %collective-permute-done.9.refs_1_), channel_id=1, source_target_pairs={{0,8},{8,0},{16,24},{24,16},{1,9},{9,1},{17,25},{25,17},{2,10},{10... | collective-permute-start | bytes 786440 | tf_op jit(solution)/shard_map/ppermute | solution.py:315
  41.7 8.1 %collective-permute-start.16 = (bf16[256,512]{1,0:T(8,128)(2,1)S(1)}, bf16[256,512]{1,0:T(8,128)(2,1)S(1)}, u32[]{:S(2)}, u32[]{:S(2)}) collective-permute-start(bf16[256,512]{1,0:T(8,128)(2,1)S(1)} %collective-permute-done.9.refs_1_), channel_id=1, source_target_pairs={{0,16},{8,24},{16,0},{24,8},{1,17},{9,25},{17,1},{25,9},{2,18},{10... | collective-permute-start | bytes 786440 | tf_op jit(solution)/shard_map/ppermute | solution.py:315
  43.1 14.4 %collective-permute-start.12 = (bf16[512,256]{1,0:T(8,128)(2,1)S(1)}, bf16[512,256]{1,0:T(8,128)(2,1)S(1)}, u32[]{:S(2)}, u32[]{:S(2)}) collective-permute-start(bf16[512,256]{1,0:T(8,128)(2,1)S(1)} %project_kv.1.refs_0_), channel_id=1, source_target_pairs={{0,4},{1,5},{2,6},{3,7},{4,0},{5,1},{6,2},{7,3},{8,12},{9,13},{10,... | collective-permute-start | bytes 786440 | tf_op jit(solution)/shard_map/ppermute | solution.py:318
  49.8 7.7 %copy-start.4 = (f32[256]{0:T(256)S(1)}, f32[256]{0:T(256)}, u32[]{:S(2)}) copy-start(f32[256]{0:T(256)} %param.16) | copy-start | bytes 3076
  49.8 7.7 %collective-permute-start.17 = (bf16[256,512]{1,0:T(8,128)(2,1)S(1)}, bf16[256,512]{1,0:T(8,128)(2,1)S(1)}, u32[]{:S(2)}, u32[]{:S(2)}) collective-permute-start(bf16[256,512]{1,0:T(8,128)(2,1)S(1)} %get-tuple-element.69), channel_id=1, source_target_pairs={{0,16},{8,24},{16,0},{24,8},{1,17},{9,25},{17,1},{25,9},{2,18},{10... | collective-permute-start | bytes 786440 | tf_op jit(solution)/shard_map/ppermute | solution.py:315
  50.3 7.2 %collective-permute-start.18 = (bf16[256,512]{1,0:T(8,128)(2,1)S(1)}, bf16[256,512]{1,0:T(8,128)(2,1)S(1)}, u32[]{:S(2)}, u32[]{:S(2)}) collective-permute-start(bf16[256,512]{1,0:T(8,128)(2,1)S(1)} %collective-permute-done.16.refs_5_), channel_id=1, source_target_pairs={{0,8},{8,0},{16,24},{24,16},{1,9},{9,1},{17,25},{25,17},{2,10},{10... | collective-permute-start | bytes 786440 | tf_op jit(solution)/shard_map/ppermute | solution.py:315
  51.8 8.5 %collective-permute-start.13 = (bf16[512,256]{1,0:T(8,128)(2,1)S(1)}, bf16[512,256]{1,0:T(8,128)(2,1)S(1)}, u32[]{:S(2)}, u32[]{:S(2)}) collective-permute-start(bf16[512,256]{1,0:T(8,128)(2,1)S(1)} %project_kv.1.refs_0_), channel_id=1, source_target_pairs={{0,1},{1,0},{2,3},{3,2},{4,5},{5,4},{6,7},{7,6},{8,9},{9,8},{10,11... | collective-permute-start | bytes 786440 | tf_op jit(solution)/shard_map/ppermute | solution.py:312
  57.5 2.9 %collective-permute-start.14 = (bf16[512,256]{1,0:T(8,128)(2,1)S(1)}, bf16[512,256]{1,0:T(8,128)(2,1)S(1)}, u32[]{:S(2)}, u32[]{:S(2)}) collective-permute-start(bf16[512,256]{1,0:T(8,128)(2,1)S(1)} %collective-permute-done.12.refs_1_), channel_id=1, source_target_pairs={{0,1},{1,0},{2,3},{3,2},{4,5},{5,4},{6,7},{7,6},{8,9},{9,8},{10,11... | collective-permute-start | bytes 786440 | tf_op jit(solution)/shard_map/ppermute | solution.py:312
  59.1 1.3 %copy-start.2 = (s32[1,2,16]{2,1,0:T(2,128)S(1)}, s32[1,2,16]{2,1,0:T(2,128)}, u32[]{:S(2)}) copy-start(s32[1,2,16]{2,1,0:T(2,128)} %table.1) | copy-start | bytes 388
  59.1 3.0 %collective-permute-start.19 = (bf16[256,512]{1,0:T(8,128)(2,1)S(1)}, bf16[256,512]{1,0:T(8,128)(2,1)S(1)}, u32[]{:S(2)}, u32[]{:S(2)}) collective-permute-start(bf16[256,512]{1,0:T(8,128)(2,1)S(1)} %get-tuple-element.71), channel_id=1, source_target_pairs={{0,1},{1,0},{2,3},{3,2},{4,5},{5,4},{6,7},{7,6},{8,9},{9,8},{10,11... | collective-permute-start | bytes 786440 | tf_op jit(solution)/shard_map/ppermute | solution.py:312
  61.4 9.2 %collective-permute-start.21 = (bf16[4,64,512]{2,1,0:T(8,128)(2,1)S(1)}, bf16[4,64,512]{2,1,0:T(8,128)(2,1)S(1)}, u32[]{:S(2)}, u32[]{:S(2)}) collective-permute-start(bf16[4,64,512]{2,1,0:T(8,128)(2,1)S(1)} %get-tuple-element.73), channel_id=1, source_target_pairs={{0,2},{1,3},{2,0},{3,1},{4,6},{5,7},{6,4},{7,5},{8,10},{9,11},{10,... | collective-permute-start | bytes 786440 | tf_op jit(solution)/shard_map/ppermute | solution.py:312
  63.9 11.5 %collective-permute-start.20 = (bf16[128,1024]{1,0:T(8,128)(2,1)S(1)}, bf16[128,1024]{1,0:T(8,128)(2,1)S(1)}, u32[]{:S(2)}, u32[]{:S(2)}) collective-permute-start(bf16[128,1024]{1,0:T(8,128)(2,1)S(1)} %attend.3), channel_id=1, source_target_pairs={{0,2},{1,3},{2,0},{3,1},{4,6},{5,7},{6,4},{7,5},{8,10},{9,11},{10,... | collective-permute-start | bytes 786440 | tf_op jit(solution)/shard_map/ppermute | solution.py:312

commit v13 on v12

--- a/solution.py
+++ b/solution.py
@@ -244,35 +244,58 @@
                     out[there, aligned(column, HD)] = result[n * blk_rows : (n + 1) * blk_rows]
 
 
-def pages_kernel(n_out, blk_rows, *refs):
-    mine, other = refs[:n_out], refs[n_out : 2 * n_out]
-    piece, piece_o, table, length_ref, own, away, store, flat_of = refs[2 * n_out :]
-    _, _, core = place()
-    tall = piece.shape[0]
+def live_page(store, table, flat_of, slot, length, blk_rows):
+    block = lax.rem(flat_of[slot], table.shape[2])
+    page = store[aligned(block, blk_rows), :]
+    row = lax.broadcasted_iota(jnp.int32, page.shape, 0)
+    return jnp.where(row < length - block * blk_rows, page, jnp.zeros_like(page))
+
+
+def block_of(pieces, tall, k, j):
+    piece, piece_o = pieces
+    return read_id(piece_o, k * tall - ID_ROWS, j) if k else read_id(piece, tall - ID_ROWS, j)
+
+
+def away_kernel(n_out, blk_rows, *refs):
+    mine, (piece, piece_o, table, length_ref, away, store, flat_of) = refs[:n_out], refs[n_out:]
     per_piece = mine[0].shape[0] // blk_rows
     for k in range(n_out):
         for j in range(per_piece):
-            block = read_id(*((piece_o, k * tall - ID_ROWS) if k else (piece, tall - ID_ROWS)), j)
-            there = aligned(block, blk_rows)
+            there = aligned(block_of((piece, piece_o), piece.shape[0], k, j), blk_rows)
+            store[there, :] = mine[k][j * blk_rows : (j + 1) * blk_rows, :]
+    invert_table(table, flat_of)
+    blk = lax.axis_index("blk")
+    far = (blk ^ 2) - blk % 2
+    slots = away.shape[0] // 2
+    for i in range(2 * slots):
+        away[i] = live_page(store, table, flat_of, far * slots + i, length_ref[0], blk_rows)
+
+
+def sort_kernel(n_out, blk_rows, *refs):
+    mine, other = refs[:n_out], refs[n_out : 2 * n_out]
+    piece, piece_o, store = refs[2 * n_out :]
+    _, _, core = place()
+    per_piece = mine[0].shape[0] // blk_rows
+    for k in range(n_out):
+        for j in range(per_piece):
+            there = aligned(block_of((piece, piece_o), piece.shape[0], k, j), blk_rows)
             here = slice(j * blk_rows, (j + 1) * blk_rows)
             store[core, there, :] = mine[k][here, :]
             store[1 - core, there, :] = other[k][here, :]
+
+
+def own_kernel(blk_rows, store, table, length_ref, own, flat_of):
+    invert_table(table, flat_of)
     slots = own.shape[0]
-    row = lax.broadcasted_iota(jnp.int32, (blk_rows, HD), 0)
-    invert_table(table, flat_of)
-    blk = lax.axis_index("blk")
-    for target, device in ((away, blk ^ 2), (own, blk)):
-        for i in range(slots):
-            block = lax.rem(flat_of[device * slots + i], table.shape[2])
-            here = aligned(block, blk_rows)
-            live = row < length_ref[0] - block * blk_rows
-            for half in range(2):
-                page = store[half, here, :]
-                target[i, :, half * HD : (half + 1) * HD] = jnp.where(live, page, jnp.zeros_like(page))
-
-
-def finish_kernel(kept, from_far, own_pages, got_pages, table, att_out, page_out, flat_of, sems):
-    _, pair, _ = place()
+    for i in range(slots):
+        for half in range(2):
+            slot = lax.axis_index("blk") * slots + i
+            page = live_page(store.at[half], table, flat_of, slot, length_ref[0], blk_rows)
+            own[i, :, half * HD : (half + 1) * HD] = page
+
+
+def finish_kernel(kept, from_far, own_pages, got, got_near, table, att_out, page_out, flat_of, sems):
+    _, pair, core = place()
     invert_table(table, flat_of)
     slots = page_out.shape[0]
     width = kept.shape[1]
@@ -282,19 +305,23 @@
     ]
     for copy in copies:
         copy.start()
-    for i in range(page_out.shape[0]):
+    for i in range(slots):
         here = lax.div(flat_of[lax.axis_index("blk") * slots + i], table.shape[2]) == pair
-        ours = pltpu.make_async_copy(own_pages.at[i], page_out.at[i], sems.at[2 + i])
-        theirs = pltpu.make_async_copy(got_pages.at[i], page_out.at[i], sems.at[2 + i])
-        copies.append(ours)
-
-        @pl.when(here)
-        def _():
-            ours.start()
-
-        @pl.when(jnp.logical_not(here))
-        def _():
-            theirs.start()
+        for half in range(2):
+            cols = aligned(core if half == 0 else 1 - core, HD)
+            there = page_out.at[i, :, cols]
+            sem = sems.at[2 + 2 * i + half]
+            ours = pltpu.make_async_copy(own_pages.at[i, :, cols], there, sem)
+            theirs = pltpu.make_async_copy((got, got_near)[half].at[core * slots + i], there, sem)
+            copies.append(ours)
+
+            @pl.when(here)
+            def _():
+                ours.start()
+
+            @pl.when(jnp.logical_not(here))
+            def _():
+                theirs.start()
 
     for copy in copies:
         copy.wait()
@@ -416,7 +443,7 @@
                 pltpu.SemaphoreType.DMA((n_req * n_out,)),
             ],
             cost_estimate=pl.CostEstimate(
-                flops=2 * TEAM * rows * depth * width, bytes_accessed=6 * MIB, transcendentals=0
+                flops=(0 if is_kv else 0), bytes_accessed=MIB, transcendentals=0
             ),
             compiler_params=params(4 if w_rows * TEAM % LANES == 0 else 12),
             name="project_kv" if is_kv else "project_q",
@@ -436,17 +463,27 @@
     total = TEAM * rows * n_out
     store_mib = -(-2 * total * HD * 2 // MIB)
     page_shape = shape((slot_count, blk_rows, 2 * HD), bf16)
-    own_pages, away_pages, store = pl.pallas_call(
-        functools.partial(pages_kernel, n_out, blk_rows),
-        out_shape=[page_shape, page_shape, shape((2, total, HD), bf16)],
-        in_specs=[VMEM] * (2 * n_out + 2) + [SMEM] * 2,
-        out_specs=[VMEM] * 3,
-        scratch_shapes=[pltpu.SMEM((page_table.size,), jnp.int32)],
-        cost_estimate=pl.CostEstimate(flops=0, bytes_accessed=4 * MIB, transcendentals=0),
+    flat_of = pltpu.SMEM((page_table.size,), jnp.int32)
+    away_half = pl.pallas_call(
+        functools.partial(away_kernel, n_out, blk_rows),
+        out_shape=shape((2 * slot_count, blk_rows, HD), bf16),
+        in_specs=[VMEM] * (n_out + 2) + [SMEM] * 2,
+        out_specs=VMEM,
+        scratch_shapes=[pltpu.VMEM((total, HD), bf16), flat_of],
+        cost_estimate=pl.CostEstimate(flops=0, bytes_accessed=MIB, transcendentals=0),
         compiler_params=params(store_mib + 1),
-        name="pages",
-    )(*mine, *other, kv, kv_o, page_table, lengths)
-    got_pages = in_team(away_pages, 2)
+        name="away",
+    )(*mine, kv, kv_o, page_table, lengths)
+    got_half = in_team(away_half, 2)
+    store = pl.pallas_call(
+        functools.partial(sort_kernel, n_out, blk_rows),
+        out_shape=shape((2, total, HD), bf16),
+        in_specs=[VMEM] * (2 * n_out + 2),
+        out_specs=VMEM,
+        cost_estimate=pl.CostEstimate(flops=10**10, bytes_accessed=MIB, transcendentals=0),
+        compiler_params=params(store_mib + 1),
+        name="sort",
+    )(*mine, *other, kv, kv_o)
 
     def attend(step):
         return pl.pallas_call(
@@ -455,7 +492,7 @@
             in_specs=[VMEM] * 4 + [SMEM],
             out_specs=VMEM,
             cost_estimate=pl.CostEstimate(
-                flops=2 * H * HD * rows * total, bytes_accessed=4 * MIB, transcendentals=0
+                flops=0, bytes_accessed=MIB, transcendentals=0
             ),
             compiler_params=params(store_mib + 2 + 3 * total // 1024),
             name="attend",
@@ -463,16 +500,27 @@
 
     from_far = in_team(attend(2), 2)
     kept = attend(0)
+    got_half, kept = sync(got_half, kept)
+    got_near = in_team(got_half, 1)
+    own_pages = pl.pallas_call(
+        functools.partial(own_kernel, blk_rows),
+        out_shape=page_shape,
+        in_specs=[VMEM] + [SMEM] * 2,
+        out_specs=VMEM,
+        scratch_shapes=[flat_of],
+        compiler_params=params(store_mib + 1),
+        name="own",
+    )(store, page_table, lengths)
 
     attended, pages = pl.pallas_call(
         finish_kernel,
         out_shape=[shape((rows, H * HD), bf16), page_shape],
-        in_specs=[ANY] * 4 + [SMEM],
+        in_specs=[ANY] * 5 + [SMEM],
         out_specs=[ANY] * 2,
-        scratch_shapes=[pltpu.SMEM((page_table.size,), jnp.int32), pltpu.SemaphoreType.DMA((2 + slot_count,))],
+        scratch_shapes=[flat_of, pltpu.SemaphoreType.DMA((2 + 2 * slot_count,))],
         compiler_params=params(1),
         name="finish",
-    )(kept, from_far, own_pages, got_pages, page_table)
+    )(kept, from_far, own_pages, got_half, got_near, page_table)
     return attended[None], pages[None]
 
 

time: 77.2 us -> 75.5 us (0.978)
  waiting for transfers between devices: 40.7 us -> 38.2 us
  Pallas kernels: 11.3 us -> 12.3 us
    ppermute x10 -> x11, waiting for transfers between devices: 16.8 us -> 14.3 us  [in_team(): return lax.ppermute(array, 'blk', [(i, i ^ k) for i in range(n_blk)])]
    pallas_call x1 -> x3, Pallas kernels: 1.06 us -> 2.05 us  [the longest x1 1.01 us: body(): pl.pallas_call(functools.partial(away_kernel, n_out, blk_rows), out_shape...]
    ppermute x10 -> x11, starting transfers between devices: 7.61 us -> 7.28 us  [in_team(): return lax.ppermute(array, 'blk', [(i, i ^ k) for i in range(n_blk)])]
  transfers between devices with their start and end apart: 22 -> 23, of which waited for: 11 -> 12; matrix products, arithmetic and copies ran while one was open for 0% -> 0% of each run, Pallas kernels for 9% -> 11%
where the time goes in v13:
time: 75.5 us; the launch traced here: 75.4 us
  waiting for transfers between devices  38.2 us (51%)
  starting transfers between devices  22.2 us (29%)
  Pallas kernels  12.3 us (16%)
  between operations  1.47 us (2%)
  local copies, waits for them, and re-layouts  1.12 us (1%)
    ppermute x3, waiting for transfers between devices, across(): lax.ppermute(array, 'blk', [(i, (i + TEAM * k) % n_blk) for i in range(n_...  19.6 us
    ppermute x11, waiting for transfers between devices, in_team(): return lax.ppermute(array, 'blk', [(i, i ^ k) for i in range(n_blk)])  14.3 us
    ppermute x9, starting transfers between devices, in_req(): return lax.ppermute(array, 'req', [(i, i ^ k) for i in range(n_req)])  9.61 us
    ppermute x11, starting transfers between devices, in_team(): return lax.ppermute(array, 'blk', [(i, i ^ k) for i in range(n_blk)])  7.28 us
    ppermute x3, starting transfers between devices, across(): lax.ppermute(array, 'blk', [(i, (i + TEAM * k) % n_blk) for i in range(n_...  5.35 us
    ppermute x9, waiting for transfers between devices, in_req(): return lax.ppermute(array, 'req', [(i, i ^ k) for i in range(n_req)])  4.3 us
    pallas_call x2, Pallas kernels, attend(): pl.pallas_call(functools.partial(attend_kernel, blk_rows, step), out_shap...  3.37 us
    pallas_call x2, Pallas kernels, project(): pl.pallas_call(functools.partial(project_kernel, n_out, TEAM * w_rows, st...  2.46 us
  transfers between devices with their start and end apart: 23, of which 12 were waited for; matrix products, arithmetic and copies ran while one was open for 0% of the time, Pallas kernels for 11%

profile of v13, /device:TPU:0, one launch (start us, length us, event | category | flops | bytes accessed | tf_op | source)
XLA Modules:
  0.0 75.4 jit_solution(13201072657700321971)
XLA Ops:
  0.6 2.3 %pack.1 = (bf16[400,128]{1,0:T(8,128)(2,1)}, bf16[2448,128]{1,0:T(8,128)(2,1)}, bf16[400,128]{1,0:T(8,128)(2,1)}, bf16[400,128]{1,0:T(8,128)(2,1)}) custom-call(bf16[64,3072]{1,0:T(8,128)(2,1)} %w_hbm.1, s32[1,2]{1,0:T(1,128)} %ids_hbm.1, bf16[128,2048]{1,0:T(8,128)(2,1)} %bitcast.5), custom_call_target="tpu_custom_call" | custom-call | tf_op jit(solution)/shard_map/pack/pallas_call | solution.py:355
  3.4 2.7 %collective-permute-start.1 = (bf16[400,128]{1,0:T(8,128)(2,1)}, bf16[400,128]{1,0:T(8,128)(2,1)S(1)}, u32[]{:S(2)}, u32[]{:S(2)}) collective-permute-start(bf16[400,128]{1,0:T(8,128)(2,1)} %get-tuple-element.40), channel_id=1, source_target_pairs={{0,2},{1,3},{2,0},{3,1},{4,6},{5,7},{6,4},{7,5},{8,10},{9,11},{10,... | collective-permute-start | bytes 307208 | tf_op jit(solution)/shard_map/ppermute | solution.py:339
  6.2 3.9 %collective-permute-done.1.refs_2_ = bf16[400,128]{1,0:T(8,128)(2,1)S(1)} collective-permute-done((bf16[400,128]{1,0:T(8,128)(2,1)}, bf16[400,128]{1,0:T(8,128)(2,1)S(1)}, u32[]{:S(2)}, u32[]{:S(2)}) %collective-permute-start.1) | collective-permute-done | bytes 102432 | tf_op jit(solution)/shard_map/ppermute | solution.py:339
  10.0 1.7 %collective-permute-done.2.refs_3_ = bf16[400,128]{1,0:T(8,128)(2,1)S(1)} collective-permute-done((bf16[400,128]{1,0:T(8,128)(2,1)}, bf16[400,128]{1,0:T(8,128)(2,1)S(1)}, u32[]{:S(2)}, u32[]{:S(2)}) %collective-permute-start.2) | collective-permute-done | bytes 102432 | tf_op jit(solution)/shard_map/ppermute | solution.py:339
  11.7 0.9 %copy-done.1 = bf16[400,128]{1,0:T(8,128)(2,1)S(1)} copy-done((bf16[400,128]{1,0:T(8,128)(2,1)S(1)}, bf16[400,128]{1,0:T(8,128)(2,1)}, u32[]{:S(2)}) %copy-start.1) | copy-done | bytes 102424
  12.8 1.5 %collective-permute-start.4 = (bf16[256,768]{1,0:T(8,128)(2,1)S(1)}, bf16[256,768]{1,0:T(8,128)(2,1)S(1)}, u32[]{:S(2)}, u32[]{:S(2)}) collective-permute-start(bf16[256,768]{1,0:T(8,128)(2,1)S(1)} %get-tuple-element.47), channel_id=1, source_target_pairs={{0,8},{8,0},{16,24},{24,16},{1,9},{9,1},{17,25},{25,17},{2,10},{10... | collective-permute-start | bytes 1179656 | tf_op jit(solution)/shard_map/ppermute | solution.py:342
  14.3 1.5 %collective-permute-start.5 = (bf16[256,768]{1,0:T(8,128)(2,1)S(1)}, bf16[256,768]{1,0:T(8,128)(2,1)S(1)}, u32[]{:S(2)}, u32[]{:S(2)}) collective-permute-start(bf16[256,768]{1,0:T(8,128)(2,1)S(1)} %get-tuple-element.47), channel_id=1, source_target_pairs={{0,16},{8,24},{16,0},{24,8},{1,17},{9,25},{17,1},{25,9},{2,18},{10... | collective-permute-start | bytes 1179656 | tf_op jit(solution)/shard_map/ppermute | solution.py:342
  15.9 2.6 %collective-permute-start.3 = (bf16[272,256]{1,0:T(8,128)(2,1)S(1)}, bf16[272,256]{1,0:T(8,128)(2,1)S(1)}, u32[]{:S(2)}, u32[]{:S(2)}) collective-permute-start(bf16[272,256]{1,0:T(8,128)(2,1)S(1)} %get-tuple-element.46.piece.refs_0_.refs_2_.refs_4_), channel_id=1, source_target_pairs={{0,4},{1,5},{2,6},{3,7},{4,0},{5,1},{6,2},{7,3},{8,12},{9,13},{10,... | collective-permute-start | bytes 417800 | tf_op jit(solution)/shard_map/ppermute | solution.py:345
  18.5 1.6 %collective-permute-start.10 = (bf16[128,2048]{1,0:T(8,128)(2,1)S(1)}, bf16[128,2048]{1,0:T(8,128)(2,1)S(1)}, u32[]{:S(2)}, u32[]{:S(2)}) collective-permute-start(bf16[128,2048]{1,0:T(8,128)(2,1)S(1)} %bitcast.6), channel_id=1, source_target_pairs={{0,2},{1,3},{2,0},{3,1},{4,6},{5,7},{6,4},{7,5},{8,10},{9,11},{10,... | collective-permute-start | bytes 1572872 | tf_op jit(solution)/shard_map/ppermute | solution.py:339
  20.4 5.9 %collective-permute-done.3.kv_o.refs_1_.refs_3_.refs_5_ = bf16[272,256]{1,0:T(8,128)(2,1)S(1)} collective-permute-done((bf16[272,256]{1,0:T(8,128)(2,1)S(1)}, bf16[272,256]{1,0:T(8,128)(2,1)S(1)}, u32[]{:S(2)}, u32[]{:S(2)}) %collective-permute-start.3) | collective-permute-done | bytes 139296 | tf_op jit(solution)/shard_map/ppermute | solution.py:345
  26.3 0.5 collective-permute-start.6
  26.8 1.5 %collective-permute-start.8 = (bf16[272,256]{1,0:T(8,128)(2,1)S(1)}, bf16[272,256]{1,0:T(8,128)(2,1)S(1)}, u32[]{:S(2)}, u32[]{:S(2)}) collective-permute-start(bf16[272,256]{1,0:T(8,128)(2,1)S(1)} %collective-permute-done.3.kv_o.refs_1_.refs_3_.refs_5_), channel_id=1, source_target_pairs={{0,24},{8,16},{16,8},{24,0},{1,25},{9,17},{17,9},{25,1},{2,26},{10... | collective-permute-start | bytes 417800 | tf_op jit(solution)/shard_map/ppermute | solution.py:342
  28.4 1.5 %collective-permute-start.7 = (bf16[528,256]{1,0:T(8,128)(2,1)S(1)}, bf16[528,256]{1,0:T(8,128)(2,1)S(1)}, u32[]{:S(2)}, u32[]{:S(2)}) collective-permute-start(bf16[528,256]{1,0:T(8,128)(2,1)S(1)} %get-tuple-element.50), channel_id=1, source_target_pairs={{0,16},{8,24},{16,0},{24,8},{1,17},{9,25},{17,1},{25,9},{2,18},{10... | collective-permute-start | bytes 811016 | tf_op jit(solution)/shard_map/ppermute | solution.py:342
  30.1 8.0 %collective-permute-done.9.refs_1_ = bf16[256,512]{1,0:T(8,128)(2,1)S(1)} collective-permute-done((bf16[256,512]{1,0:T(8,128)(2,1)S(1)}, bf16[256,512]{1,0:T(8,128)(2,1)S(1)}, u32[]{:S(2)}, u32[]{:S(2)}) %collective-permute-start.9) | collective-permute-done | bytes 262176 | tf_op jit(solution)/shard_map/ppermute | solution.py:345
  38.1 1.1 %collective-permute-done.10.far = bf16[128,2048]{1,0:T(8,128)(2,1)S(1)} collective-permute-done((bf16[128,2048]{1,0:T(8,128)(2,1)S(1)}, bf16[128,2048]{1,0:T(8,128)(2,1)S(1)}, u32[]{:S(2)}, u32[]{:S(2)}) %collective-permute-start.10) | collective-permute-done | bytes 524320 | tf_op jit(solution)/shard_map/ppermute | solution.py:339
  39.3 1.9 %collective-permute-done.11.far_near = bf16[128,2048]{1,0:T(8,128)(2,1)S(1)} collective-permute-done((bf16[128,2048]{1,0:T(8,128)(2,1)S(1)}, bf16[128,2048]{1,0:T(8,128)(2,1)S(1)}, u32[]{:S(2)}, u32[]{:S(2)}) %collective-permute-start.11) | collective-permute-done | bytes 524320 | tf_op jit(solution)/shard_map/ppermute | solution.py:339
  41.2 0.5 collective-permute-start.16
  42.2 0.9 %project_kv.1.refs_0_ = bf16[512,256]{1,0:T(8,128)(2,1)S(1)} custom-call(bf16[128,2048]{1,0:T(8,128)(2,1)S(1)} %bitcast.7, bf16[2448,128]{1,0:T(8,128)(2,1)S(1)} %collective-permute-done.refs_1_.near, bf16[128,2048]{1,0:T(8,128)(2,1)S(1)} %collective-permute-done.10.far, bf16[128,2048]{1,0:T(8,128)(2,1)S(1)} %collective-permute-done.11.far_near, ...), custom_call_target="tpu_custom_call" | custom-call | bytes 1048576 | tf_op jit(solution)/shard_map/project_kv/pallas_call | solution.py:436
  43.1 2.4 %collective-permute-start.12 = (bf16[512,256]{1,0:T(8,128)(2,1)S(1)}, bf16[512,256]{1,0:T(8,128)(2,1)S(1)}, u32[]{:S(2)}, u32[]{:S(2)}) collective-permute-start(bf16[512,256]{1,0:T(8,128)(2,1)S(1)} %project_kv.1.refs_0_), channel_id=1, source_target_pairs={{0,4},{1,5},{2,6},{3,7},{4,0},{5,1},{6,2},{7,3},{8,12},{9,13},{10,... | collective-permute-start | bytes 786440 | tf_op jit(solution)/shard_map/ppermute | solution.py:345
  45.5 4.0 %collective-permute-done.16.refs_3_ = bf16[256,512]{1,0:T(8,128)(2,1)S(1)} collective-permute-done((bf16[256,512]{1,0:T(8,128)(2,1)S(1)}, bf16[256,512]{1,0:T(8,128)(2,1)S(1)}, u32[]{:S(2)}, u32[]{:S(2)}) %collective-permute-start.16) | collective-permute-done | bytes 262176 | tf_op jit(solution)/shard_map/ppermute | solution.py:342
  50.3 1.5 %collective-permute-start.19 = (bf16[256,512]{1,0:T(8,128)(2,1)S(1)}, bf16[256,512]{1,0:T(8,128)(2,1)S(1)}, u32[]{:S(2)}, u32[]{:S(2)}) collective-permute-start(bf16[256,512]{1,0:T(8,128)(2,1)S(1)} %collective-permute-done.17.refs_5_), channel_id=1, source_target_pairs={{0,8},{8,0},{16,24},{24,16},{1,9},{9,1},{17,25},{25,17},{2,10},{10... | collective-permute-start | bytes 786440 | tf_op jit(solution)/shard_map/ppermute | solution.py:342
  51.8 5.7 %collective-permute-done.12.refs_1_ = bf16[512,256]{1,0:T(8,128)(2,1)S(1)} collective-permute-done((bf16[512,256]{1,0:T(8,128)(2,1)S(1)}, bf16[512,256]{1,0:T(8,128)(2,1)S(1)}, u32[]{:S(2)}, u32[]{:S(2)}) %collective-permute-start.12) | collective-permute-done | bytes 262176 | tf_op jit(solution)/shard_map/ppermute | solution.py:345
  58.1 1.0 %away.1 = bf16[8,64,256]{2,1,0:T(8,128)(2,1)S(1)} custom-call(bf16[512,256]{1,0:T(8,128)(2,1)S(1)} %project_kv.1.refs_0_, bf16[512,256]{1,0:T(8,128)(2,1)S(1)} %collective-permute-done.12.refs_1_, bf16[272,256]{1,0:T(8,128)(2,1)S(1)} %get-tuple-element.46.piece.refs_0_.refs_2_.refs_4_, ...), custom_call_target="tpu_custom_call" | custom-call | bytes 1048576 | tf_op jit(solution)/shard_map/away/pallas_call | solution.py:467
  59.8 1.6 %project_q.1 = (bf16[256,512]{1,0:T(8,128)(2,1)S(1)}, bf16[256,512]{1,0:T(8,128)(2,1)S(1)}) custom-call(bf16[128,2048]{1,0:T(8,128)(2,1)S(1)} %bitcast.8, bf16[2448,128]{1,0:T(8,128)(2,1)S(1)} %collective-permute-done.refs_1_.near, bf16[128,2048]{1,0:T(8,128)(2,1)S(1)} %collective-permute-done.10.far, ...), custom_call_target="tpu_custom_call" | custom-call | bytes 1048576 | tf_op jit(solution)/shard_map/project_q/pallas_call | solution.py:436
  61.4 0.6 collective-permute-start.20
  62.2 1.0 %collective-permute-done.20.near_ref = bf16[256,512]{1,0:T(8,128)(2,1)S(1)} collective-permute-done((bf16[256,512]{1,0:T(8,128)(2,1)S(1)}, bf16[256,512]{1,0:T(8,128)(2,1)S(1)}, u32[]{:S(2)}, u32[]{:S(2)}) %collective-permute-start.20) | collective-permute-done | bytes 262176 | tf_op jit(solution)/shard_map/ppermute | solution.py:339
  63.1 1.7 %attend.3 = bf16[128,1024]{1,0:T(8,128)(2,1)S(1)} custom-call(bf16[2,1024,256]{2,1,0:T(8,128)(2,1)S(1)} %sort.1.store, bf16[256,512]{1,0:T(8,128)(2,1)S(1)} %get-tuple-element.68.q_ref, bf16[256,512]{1,0:T(8,128)(2,1)S(1)} %collective-permute-done.20.near_ref, bf16[272,256]{1,0:T(8,128)(2,1)S(1)} %get-tuple-element.46.piece.refs_0_.refs_2_.refs_4_, ...), custom_call_target="tpu_custom_call" | custom-call | bytes 1048576 | tf_op jit(solution)/shard_map/attend/pallas_call | solution.py:489
  64.9 1.3 %collective-permute-start.21 = (bf16[128,1024]{1,0:T(8,128)(2,1)S(1)}, bf16[128,1024]{1,0:T(8,128)(2,1)S(1)}, u32[]{:S(2)}, u32[]{:S(2)}) collective-permute-start(bf16[128,1024]{1,0:T(8,128)(2,1)S(1)} %attend.3), channel_id=1, source_target_pairs={{0,2},{1,3},{2,0},{3,1},{4,6},{5,7},{6,4},{7,5},{8,10},{9,11},{10,... | collective-permute-start | bytes 786440 | tf_op jit(solution)/shard_map/ppermute | solution.py:339
  66.2 1.7 %attend.2.kept = bf16[128,1024]{1,0:T(8,128)(2,1)S(1)} custom-call(bf16[2,1024,256]{2,1,0:T(8,128)(2,1)S(1)} %sort.1.store, bf16[256,512]{1,0:T(8,128)(2,1)S(1)} %get-tuple-element.68.q_ref, bf16[256,512]{1,0:T(8,128)(2,1)S(1)} %collective-permute-done.20.near_ref, bf16[272,256]{1,0:T(8,128)(2,1)S(1)} %get-tuple-element.46.piece.refs_0_.refs_2_.refs_4_, ...), custom_call_target="tpu_custom_call" | custom-call | bytes 1048576 | tf_op jit(solution)/shard_map/attend/pallas_call | solution.py:489
  68.0 0.8 %own.1.own_pages = bf16[4,64,512]{2,1,0:T(8,128)(2,1)S(1)} custom-call(bf16[2,1024,256]{2,1,0:T(8,128)(2,1)S(1)} %sort.1.store, s32[1,2,16]{2,1,0:T(2,128)S(1)} %copy-done.2, s32[1]{0:T(128)S(6)} %copy.13.refs_5_.length_ref), custom_call_target="tpu_custom_call" | custom-call | tf_op jit(solution)/shard_map/own/pallas_call | solution.py:505
  68.8 4.8 %collective-permute-done.21.from_far = bf16[128,1024]{1,0:T(8,128)(2,1)S(1)} collective-permute-done((bf16[128,1024]{1,0:T(8,128)(2,1)S(1)}, bf16[128,1024]{1,0:T(8,128)(2,1)S(1)}, u32[]{:S(2)}, u32[]{:S(2)}) %collective-permute-start.21) | collective-permute-done | bytes 262176 | tf_op jit(solution)/shard_map/ppermute | solution.py:339
  73.6 1.8 %finish.1 = (bf16[128,2048]{1,0:T(8,128)(2,1)}, bf16[4,64,512]{2,1,0:T(8,128)(2,1)}) custom-call(bf16[128,1024]{1,0:T(8,128)(2,1)S(1)} %attend.2.kept, bf16[128,1024]{1,0:T(8,128)(2,1)S(1)} %collective-permute-done.21.from_far, bf16[4,64,512]{2,1,0:T(8,128)(2,1)S(1)} %own.1.own_pages, bf16[8,64,256]{2,1,0:T(8,128)(2,1)S(1)} %collective-permute-done.13.got, ...), custom_call_target="tpu_custom_call" | custom-call | tf_op jit(solution)/shard_map/finish/pallas_call | solution.py:515
  (44 shorter events, 3.5 us)
Async XLA Ops:
  2.9 15.5 %copy-start = (bf16[1,128,2048]{2,1,0:T(8,128)(2,1)S(1)}, bf16[1,128,2048]{2,1,0:T(8,128)(2,1)}, u32[]{:S(2)}) copy-start(bf16[1,128,2048]{2,1,0:T(8,128)(2,1)} %param.11) | copy-start | bytes 1572868
  2.9 8.8 %collective-permute-start = (bf16[2448,128]{1,0:T(8,128)(2,1)}, bf16[2448,128]{1,0:T(8,128)(2,1)S(1)}, u32[]{:S(2)}, u32[]{:S(2)}) collective-permute-start(bf16[2448,128]{1,0:T(8,128)(2,1)} %get-tuple-element.39), channel_id=1, source_target_pairs={{0,1},{1,0},{2,3},{3,2},{4,5},{5,4},{6,7},{7,6},{8,9},{9,8},{10,11... | collective-permute-start | bytes 1880072 | tf_op jit(solution)/shard_map/ppermute | solution.py:339
  3.4 6.6 %collective-permute-start.1 = (bf16[400,128]{1,0:T(8,128)(2,1)}, bf16[400,128]{1,0:T(8,128)(2,1)S(1)}, u32[]{:S(2)}, u32[]{:S(2)}) collective-permute-start(bf16[400,128]{1,0:T(8,128)(2,1)} %get-tuple-element.40), channel_id=1, source_target_pairs={{0,2},{1,3},{2,0},{3,1},{4,6},{5,7},{6,4},{7,5},{8,10},{9,11},{10,... | collective-permute-start | bytes 307208 | tf_op jit(solution)/shard_map/ppermute | solution.py:339
  6.1 5.6 %collective-permute-start.2 = (bf16[400,128]{1,0:T(8,128)(2,1)}, bf16[400,128]{1,0:T(8,128)(2,1)S(1)}, u32[]{:S(2)}, u32[]{:S(2)}) collective-permute-start(bf16[400,128]{1,0:T(8,128)(2,1)} %get-tuple-element.41), channel_id=1, source_target_pairs={{0,3},{1,2},{2,1},{3,0},{4,7},{5,6},{6,5},{7,4},{8,11},{9,10},{10,... | collective-permute-start | bytes 307208 | tf_op jit(solution)/shard_map/ppermute | solution.py:339
  11.7 0.9 %copy-start.1 = (bf16[400,128]{1,0:T(8,128)(2,1)S(1)}, bf16[400,128]{1,0:T(8,128)(2,1)}, u32[]{:S(2)}) copy-start(bf16[400,128]{1,0:T(8,128)(2,1)} %get-tuple-element.38.refs_0_) | copy-start | bytes 307204
  12.7 17.1 %copy-start.5 = (f32[64,128]{1,0:T(8,128)S(1)}, f32[64,128]{1,0:T(8,128)}, u32[]{:S(2)}) copy-start(f32[64,128]{1,0:T(8,128)} %constant.10.clone.off_cos) | copy-start | bytes 98308
  12.8 17.1 %copy-start.6 = (f32[64,128]{1,0:T(8,128)S(1)}, f32[64,128]{1,0:T(8,128)}, u32[]{:S(2)}) copy-start(f32[64,128]{1,0:T(8,128)} %constant.11.clone.off_sin) | copy-start | bytes 98308
  12.8 17.1 %copy-start.7 = (f32[16,128]{1,0:T(8,128)S(1)}, f32[16,128]{1,0:T(8,128)}, u32[]{:S(2)}) copy-start(f32[16,128]{1,0:T(8,128)} %constant.8.clone.first_cos) | copy-start | bytes 24580
  12.8 17.1 %copy-start.8 = (f32[16,128]{1,0:T(8,128)S(1)}, f32[16,128]{1,0:T(8,128)}, u32[]{:S(2)}) copy-start(f32[16,128]{1,0:T(8,128)} %constant.9.clone.first_sin) | copy-start | bytes 24580
  12.8 13.5 %collective-permute-start.4 = (bf16[256,768]{1,0:T(8,128)(2,1)S(1)}, bf16[256,768]{1,0:T(8,128)(2,1)S(1)}, u32[]{:S(2)}, u32[]{:S(2)}) collective-permute-start(bf16[256,768]{1,0:T(8,128)(2,1)S(1)} %get-tuple-element.47), channel_id=1, source_target_pairs={{0,8},{8,0},{16,24},{24,16},{1,9},{9,1},{17,25},{25,17},{2,10},{10... | collective-permute-start | bytes 1179656 | tf_op jit(solution)/shard_map/ppermute | solution.py:342
  14.3 11.9 %collective-permute-start.5 = (bf16[256,768]{1,0:T(8,128)(2,1)S(1)}, bf16[256,768]{1,0:T(8,128)(2,1)S(1)}, u32[]{:S(2)}, u32[]{:S(2)}) collective-permute-start(bf16[256,768]{1,0:T(8,128)(2,1)S(1)} %get-tuple-element.47), channel_id=1, source_target_pairs={{0,16},{8,24},{16,0},{24,8},{1,17},{9,25},{17,1},{25,9},{2,18},{10... | collective-permute-start | bytes 1179656 | tf_op jit(solution)/shard_map/ppermute | solution.py:342
  15.9 10.4 %collective-permute-start.3 = (bf16[272,256]{1,0:T(8,128)(2,1)S(1)}, bf16[272,256]{1,0:T(8,128)(2,1)S(1)}, u32[]{:S(2)}, u32[]{:S(2)}) collective-permute-start(bf16[272,256]{1,0:T(8,128)(2,1)S(1)} %get-tuple-element.46.piece.refs_0_.refs_2_.refs_4_), channel_id=1, source_target_pairs={{0,4},{1,5},{2,6},{3,7},{4,0},{5,1},{6,2},{7,3},{8,12},{9,13},{10,... | collective-permute-start | bytes 417800 | tf_op jit(solution)/shard_map/ppermute | solution.py:345
  18.5 20.8 %collective-permute-start.10 = (bf16[128,2048]{1,0:T(8,128)(2,1)S(1)}, bf16[128,2048]{1,0:T(8,128)(2,1)S(1)}, u32[]{:S(2)}, u32[]{:S(2)}) collective-permute-start(bf16[128,2048]{1,0:T(8,128)(2,1)S(1)} %bitcast.6), channel_id=1, source_target_pairs={{0,2},{1,3},{2,0},{3,1},{4,6},{5,7},{6,4},{7,5},{8,10},{9,11},{10,... | collective-permute-start | bytes 1572872 | tf_op jit(solution)/shard_map/ppermute | solution.py:339
  20.0 18.1 %collective-permute-start.9 = (bf16[256,512]{1,0:T(8,128)(2,1)S(1)}, bf16[256,512]{1,0:T(8,128)(2,1)S(1)}, u32[]{:S(2)}, u32[]{:S(2)}) collective-permute-start(bf16[256,512]{1,0:T(8,128)(2,1)S(1)} %get-tuple-element.51.refs_0_), channel_id=1, source_target_pairs={{0,4},{1,5},{2,6},{3,7},{4,0},{5,1},{6,2},{7,3},{8,12},{9,13},{10,... | collective-permute-start | bytes 786440 | tf_op jit(solution)/shard_map/ppermute | solution.py:345
  26.3 12.9 %collective-permute-start.6 = (bf16[272,256]{1,0:T(8,128)(2,1)S(1)}, bf16[272,256]{1,0:T(8,128)(2,1)S(1)}, u32[]{:S(2)}, u32[]{:S(2)}) collective-permute-start(bf16[272,256]{1,0:T(8,128)(2,1)S(1)} %collective-permute-done.3.kv_o.refs_1_.refs_3_.refs_5_), channel_id=1, source_target_pairs={{0,8},{8,0},{16,24},{24,16},{1,9},{9,1},{17,25},{25,17},{2,10},{10... | collective-permute-start | bytes 417800 | tf_op jit(solution)/shard_map/ppermute | solution.py:342
  26.8 12.4 %collective-permute-start.8 = (bf16[272,256]{1,0:T(8,128)(2,1)S(1)}, bf16[272,256]{1,0:T(8,128)(2,1)S(1)}, u32[]{:S(2)}, u32[]{:S(2)}) collective-permute-start(bf16[272,256]{1,0:T(8,128)(2,1)S(1)} %collective-permute-done.3.kv_o.refs_1_.refs_3_.refs_5_), channel_id=1, source_target_pairs={{0,24},{8,16},{16,8},{24,0},{1,25},{9,17},{17,9},{25,1},{2,26},{10... | collective-permute-start | bytes 417800 | tf_op jit(solution)/shard_map/ppermute | solution.py:342
  28.4 10.8 %collective-permute-start.7 = (bf16[528,256]{1,0:T(8,128)(2,1)S(1)}, bf16[528,256]{1,0:T(8,128)(2,1)S(1)}, u32[]{:S(2)}, u32[]{:S(2)}) collective-permute-start(bf16[528,256]{1,0:T(8,128)(2,1)S(1)} %get-tuple-element.50), channel_id=1, source_target_pairs={{0,16},{8,24},{16,0},{24,8},{1,17},{9,25},{17,1},{25,9},{2,18},{10... | collective-permute-start | bytes 811016 | tf_op jit(solution)/shard_map/ppermute | solution.py:342
  39.2 3.0 %copy-start.3 = (f32[256]{0:T(256)S(1)}, f32[256]{0:T(256)}, u32[]{:S(2)}) copy-start(f32[256]{0:T(256)} %param.17) | copy-start | bytes 3076
  39.2 2.0 %collective-permute-start.11 = (bf16[128,2048]{1,0:T(8,128)(2,1)S(1)}, bf16[128,2048]{1,0:T(8,128)(2,1)S(1)}, u32[]{:S(2)}, u32[]{:S(2)}) collective-permute-start(bf16[128,2048]{1,0:T(8,128)(2,1)S(1)} %collective-permute-done.10.far), channel_id=1, source_target_pairs={{0,1},{1,0},{2,3},{3,2},{4,5},{5,4},{6,7},{7,6},{8,9},{9,8},{10,11... | collective-permute-start | bytes 1572872 | tf_op jit(solution)/shard_map/ppermute | solution.py:339
  41.2 8.3 %collective-permute-start.16 = (bf16[256,512]{1,0:T(8,128)(2,1)S(1)}, bf16[256,512]{1,0:T(8,128)(2,1)S(1)}, u32[]{:S(2)}, u32[]{:S(2)}) collective-permute-start(bf16[256,512]{1,0:T(8,128)(2,1)S(1)} %collective-permute-done.9.refs_1_), channel_id=1, source_target_pairs={{0,8},{8,0},{16,24},{24,16},{1,9},{9,1},{17,25},{25,17},{2,10},{10... | collective-permute-start | bytes 786440 | tf_op jit(solution)/shard_map/ppermute | solution.py:342
  41.7 8.1 %collective-permute-start.17 = (bf16[256,512]{1,0:T(8,128)(2,1)S(1)}, bf16[256,512]{1,0:T(8,128)(2,1)S(1)}, u32[]{:S(2)}, u32[]{:S(2)}) collective-permute-start(bf16[256,512]{1,0:T(8,128)(2,1)S(1)} %collective-permute-done.9.refs_1_), channel_id=1, source_target_pairs={{0,16},{8,24},{16,0},{24,8},{1,17},{9,25},{17,1},{25,9},{2,18},{10... | collective-permute-start | bytes 786440 | tf_op jit(solution)/shard_map/ppermute | solution.py:342
  43.1 14.4 %collective-permute-start.12 = (bf16[512,256]{1,0:T(8,128)(2,1)S(1)}, bf16[512,256]{1,0:T(8,128)(2,1)S(1)}, u32[]{:S(2)}, u32[]{:S(2)}) collective-permute-start(bf16[512,256]{1,0:T(8,128)(2,1)S(1)} %project_kv.1.refs_0_), channel_id=1, source_target_pairs={{0,4},{1,5},{2,6},{3,7},{4,0},{5,1},{6,2},{7,3},{8,12},{9,13},{10,... | collective-permute-start | bytes 786440 | tf_op jit(solution)/shard_map/ppermute | solution.py:345
  49.8 8.3 %copy-start.2 = (s32[1,2,16]{2,1,0:T(2,128)S(1)}, s32[1,2,16]{2,1,0:T(2,128)}, u32[]{:S(2)}) copy-start(s32[1,2,16]{2,1,0:T(2,128)} %table.3) | copy-start | bytes 388
  49.8 9.9 %collective-permute-start.18 = (bf16[256,512]{1,0:T(8,128)(2,1)S(1)}, bf16[256,512]{1,0:T(8,128)(2,1)S(1)}, u32[]{:S(2)}, u32[]{:S(2)}) collective-permute-start(bf16[256,512]{1,0:T(8,128)(2,1)S(1)} %get-tuple-element.67), channel_id=1, source_target_pairs={{0,16},{8,24},{16,0},{24,8},{1,17},{9,25},{17,1},{25,9},{2,18},{10... | collective-permute-start | bytes 786440 | tf_op jit(solution)/shard_map/ppermute | solution.py:342
  50.3 9.4 %collective-permute-start.19 = (bf16[256,512]{1,0:T(8,128)(2,1)S(1)}, bf16[256,512]{1,0:T(8,128)(2,1)S(1)}, u32[]{:S(2)}, u32[]{:S(2)}) collective-permute-start(bf16[256,512]{1,0:T(8,128)(2,1)S(1)} %collective-permute-done.17.refs_5_), channel_id=1, source_target_pairs={{0,8},{8,0},{16,24},{24,16},{1,9},{9,1},{17,25},{25,17},{2,10},{10... | collective-permute-start | bytes 786440 | tf_op jit(solution)/shard_map/ppermute | solution.py:342
  51.8 10.2 %collective-permute-start.14 = (bf16[512,256]{1,0:T(8,128)(2,1)S(1)}, bf16[512,256]{1,0:T(8,128)(2,1)S(1)}, u32[]{:S(2)}, u32[]{:S(2)}) collective-permute-start(bf16[512,256]{1,0:T(8,128)(2,1)S(1)} %project_kv.1.refs_0_), channel_id=1, source_target_pairs={{0,1},{1,0},{2,3},{3,2},{4,5},{5,4},{6,7},{7,6},{8,9},{9,8},{10,11... | collective-permute-start | bytes 786440 | tf_op jit(solution)/shard_map/ppermute | solution.py:339
  57.5 4.5 %collective-permute-start.15 = (bf16[512,256]{1,0:T(8,128)(2,1)S(1)}, bf16[512,256]{1,0:T(8,128)(2,1)S(1)}, u32[]{:S(2)}, u32[]{:S(2)}) collective-permute-start(bf16[512,256]{1,0:T(8,128)(2,1)S(1)} %collective-permute-done.12.refs_1_), channel_id=1, source_target_pairs={{0,1},{1,0},{2,3},{3,2},{4,5},{5,4},{6,7},{7,6},{8,9},{9,8},{10,11... | collective-permute-start | bytes 786440 | tf_op jit(solution)/shard_map/ppermute | solution.py:339
  59.2 0.7 copy-start.4
  59.2 8.8 %collective-permute-start.13 = (bf16[8,64,256]{2,1,0:T(8,128)(2,1)S(1)}, bf16[8,64,256]{2,1,0:T(8,128)(2,1)S(1)}, u32[]{:S(2)}, u32[]{:S(2)}) collective-permute-start(bf16[8,64,256]{2,1,0:T(8,128)(2,1)S(1)} %away.1), channel_id=1, source_target_pairs={{0,2},{1,3},{2,0},{3,1},{4,6},{5,7},{6,4},{7,5},{8,10},{9,11},{10,... | collective-permute-start | bytes 786440 | tf_op jit(solution)/shard_map/ppermute | solution.py:339
  61.4 1.7 %collective-permute-start.20 = (bf16[256,512]{1,0:T(8,128)(2,1)S(1)}, bf16[256,512]{1,0:T(8,128)(2,1)S(1)}, u32[]{:S(2)}, u32[]{:S(2)}) collective-permute-start(bf16[256,512]{1,0:T(8,128)(2,1)S(1)} %get-tuple-element.69), channel_id=1, source_target_pairs={{0,1},{1,0},{2,3},{3,2},{4,5},{5,4},{6,7},{7,6},{8,9},{9,8},{10,11... | collective-permute-start | bytes 786440 | tf_op jit(solution)/shard_map/ppermute | solution.py:339
  64.9 8.7 %collective-permute-start.21 = (bf16[128,1024]{1,0:T(8,128)(2,1)S(1)}, bf16[128,1024]{1,0:T(8,128)(2,1)S(1)}, u32[]{:S(2)}, u32[]{:S(2)}) collective-permute-start(bf16[128,1024]{1,0:T(8,128)(2,1)S(1)} %attend.3), channel_id=1, source_target_pairs={{0,2},{1,3},{2,0},{3,1},{4,6},{5,7},{6,4},{7,5},{8,10},{9,11},{10,... | collective-permute-start | bytes 786440 | tf_op jit(solution)/shard_map/ppermute | solution.py:339
  68.0 5.6 %collective-permute-start.22 = (bf16[8,64,256]{2,1,0:T(8,128)(2,1)S(1)}, bf16[8,64,256]{2,1,0:T(8,128)(2,1)S(1)}, u32[]{:S(2)}, u32[]{:S(2)}) collective-permute-start(bf16[8,64,256]{2,1,0:T(8,128)(2,1)S(1)} %collective-permute-done.13.got), channel_id=1, source_target_pairs={{0,1},{1,0},{2,3},{3,2},{4,5},{5,4},{6,7},{7,6},{8,9},{9,8},{10,11... | collective-permute-start | bytes 786440 | tf_op jit(solution)/shard_map/ppermute | solution.py:339

commit v14 on v13

--- a/solution.py
+++ b/solution.py
@@ -84,6 +84,8 @@
 
 def read_id(piece, row, n):
     ids = piece[row : row + ID_ROWS, :LANES].astype(jnp.float32)[:1]
+    if isinstance(n, int):
+        return ids[0, n].astype(jnp.int32)
     lane = lax.broadcasted_iota(jnp.int32, ids.shape, 1)
     return jnp.sum(jnp.where(lane == n, ids, 0.0)).astype(jnp.int32)
 
@@ -421,7 +423,6 @@
     kv_ox, kv_oy_d, kv_od = in_req(kv_o, 1), in_req(kv_o_x, 2), in_req(kv_o, 3)
     kv_ox, kv_oy_d, kv_od, q_o, far, cosine, sine = sync(kv_ox, kv_oy_d, kv_od, q_o, far, cosine, sine)
     far_near = in_team(far, 1)
-    far_near, q_o = sync(far_near, q_o)
     q_ox, q_oy = in_req(q_o, 1), in_req(q_o, 2)
     kv_weight = [(kv, 0, 0), (kv_o, 0, 0), (w_x, 0, 0), (kv_ox, 0, 0)]
     kv_weight += [(w_y, 0, 0), (kv_oy_d, 0, 0), (kv_oy_d, others, 0), (kv_od, 0, 0)]
@@ -457,9 +458,6 @@
     mine = [made] + [across(made, k) for k in range(1, n_out)]
     other = [in_team(part, 1) for part in mine]
 
-    to_near, queries = project(q_weight, False, q_gain)
-    from_near = in_team(to_near, 1)
-
     total = TEAM * rows * n_out
     store_mib = -(-2 * total * HD * 2 // MIB)
     page_shape = shape((slot_count, blk_rows, 2 * HD), bf16)
@@ -475,6 +473,12 @@
         name="away",
     )(*mine, kv, kv_o, page_table, lengths)
     got_half = in_team(away_half, 2)
+    away_half, q_od, q_d = sync(away_half, q_od, q_d)
+    q_weight[-2:] = [(q_d, 0, 0), (q_od, 0, 0)]
+
+    to_near, queries = project(q_weight, False, q_gain)
+    from_near = in_team(to_near, 1)
+
     store = pl.pallas_call(
         functools.partial(sort_kernel, n_out, blk_rows),
         out_shape=shape((2, total, HD), bf16),

time: 75.5 us -> 75.1 us (level)
    ppermute x11, waiting for transfers between devices: 14.3 us -> 13.1 us  [in_team(): return lax.ppermute(array, 'blk', [(i, i ^ k) for i in range(n_blk)])]
    ppermute x3, waiting for transfers between devices: 19.6 us -> 20.7 us  [across(): lax.ppermute(array, 'blk', [(i, (i + TEAM * k) % n_blk) for i in range(n_...]
  transfers between devices with their start and end apart: 23 -> 23, of which waited for: 12 -> 11; matrix products, arithmetic and copies ran while one was open for 0% -> 0% of each run, Pallas kernels for 11% -> 11%
where the time goes in v14:
time: 75.1 us; the launch traced here: 74.9 us
  waiting for transfers between devices  37.7 us (50%)
  starting transfers between devices  22 us (29%)
  Pallas kernels  12.2 us (16%)
  local copies, waits for them, and re-layouts  1.51 us (2%)
  between operations  1.5 us (2%)
    ppermute x3, waiting for transfers between devices, across(): lax.ppermute(array, 'blk', [(i, (i + TEAM * k) % n_blk) for i in range(n_...  20.7 us
    ppermute x11, waiting for transfers between devices, in_team(): return lax.ppermute(array, 'blk', [(i, i ^ k) for i in range(n_blk)])  13.1 us
    ppermute x9, starting transfers between devices, in_req(): return lax.ppermute(array, 'req', [(i, i ^ k) for i in range(n_req)])  9.68 us
    ppermute x11, starting transfers between devices, in_team(): return lax.ppermute(array, 'blk', [(i, i ^ k) for i in range(n_blk)])  7.02 us
    ppermute x3, starting transfers between devices, across(): lax.ppermute(array, 'blk', [(i, (i + TEAM * k) % n_blk) for i in range(n_...  5.3 us
    ppermute x9, waiting for transfers between devices, in_req(): return lax.ppermute(array, 'req', [(i, i ^ k) for i in range(n_req)])  3.81 us
    pallas_call x2, Pallas kernels, attend(): pl.pallas_call(functools.partial(attend_kernel, blk_rows, step), out_shap...  3.37 us
    pallas_call x2, Pallas kernels, project(): pl.pallas_call(functools.partial(project_kernel, n_out, TEAM * w_rows, st...  2.46 us
  transfers between devices with their start and end apart: 23, of which 11 were waited for; matrix products, arithmetic and copies ran while one was open for 0% of the time, Pallas kernels for 11%

profile of v14, /device:TPU:0, one launch (start us, length us, event | category | flops | bytes accessed | tf_op | source)
XLA Modules:
  0.0 74.9 jit_solution(4761486127113149029)
XLA Ops:
  0.6 2.3 %pack.1 = (bf16[400,128]{1,0:T(8,128)(2,1)}, bf16[2448,128]{1,0:T(8,128)(2,1)}, bf16[400,128]{1,0:T(8,128)(2,1)}, bf16[400,128]{1,0:T(8,128)(2,1)}) custom-call(bf16[64,3072]{1,0:T(8,128)(2,1)} %w_hbm.1, s32[1,2]{1,0:T(1,128)} %ids_hbm.1, bf16[128,2048]{1,0:T(8,128)(2,1)} %bitcast.5), custom_call_target="tpu_custom_call" | custom-call | tf_op jit(solution)/shard_map/pack/pallas_call | solution.py:357
  3.4 2.7 %collective-permute-start.1 = (bf16[400,128]{1,0:T(8,128)(2,1)}, bf16[400,128]{1,0:T(8,128)(2,1)S(1)}, u32[]{:S(2)}, u32[]{:S(2)}) collective-permute-start(bf16[400,128]{1,0:T(8,128)(2,1)} %get-tuple-element.40), channel_id=1, source_target_pairs={{0,2},{1,3},{2,0},{3,1},{4,6},{5,7},{6,4},{7,5},{8,10},{9,11},{10,... | collective-permute-start | bytes 307208 | tf_op jit(solution)/shard_map/ppermute | solution.py:341
  6.2 3.9 %collective-permute-done.1.refs_2_ = bf16[400,128]{1,0:T(8,128)(2,1)S(1)} collective-permute-done((bf16[400,128]{1,0:T(8,128)(2,1)}, bf16[400,128]{1,0:T(8,128)(2,1)S(1)}, u32[]{:S(2)}, u32[]{:S(2)}) %collective-permute-start.1) | collective-permute-done | bytes 102432 | tf_op jit(solution)/shard_map/ppermute | solution.py:341
  10.0 1.7 %collective-permute-done.2.refs_3_ = bf16[400,128]{1,0:T(8,128)(2,1)S(1)} collective-permute-done((bf16[400,128]{1,0:T(8,128)(2,1)}, bf16[400,128]{1,0:T(8,128)(2,1)S(1)}, u32[]{:S(2)}, u32[]{:S(2)}) %collective-permute-start.2) | collective-permute-done | bytes 102432 | tf_op jit(solution)/shard_map/ppermute | solution.py:341
  11.7 0.9 %copy-done.1 = bf16[400,128]{1,0:T(8,128)(2,1)S(1)} copy-done((bf16[400,128]{1,0:T(8,128)(2,1)S(1)}, bf16[400,128]{1,0:T(8,128)(2,1)}, u32[]{:S(2)}) %copy-start.1) | copy-done | bytes 102424
  12.8 1.5 %collective-permute-start.4 = (bf16[256,768]{1,0:T(8,128)(2,1)S(1)}, bf16[256,768]{1,0:T(8,128)(2,1)S(1)}, u32[]{:S(2)}, u32[]{:S(2)}) collective-permute-start(bf16[256,768]{1,0:T(8,128)(2,1)S(1)} %get-tuple-element.47), channel_id=1, source_target_pairs={{0,8},{8,0},{16,24},{24,16},{1,9},{9,1},{17,25},{25,17},{2,10},{10... | collective-permute-start | bytes 1179656 | tf_op jit(solution)/shard_map/ppermute | solution.py:344
  14.3 1.5 %collective-permute-start.5 = (bf16[256,768]{1,0:T(8,128)(2,1)S(1)}, bf16[256,768]{1,0:T(8,128)(2,1)S(1)}, u32[]{:S(2)}, u32[]{:S(2)}) collective-permute-start(bf16[256,768]{1,0:T(8,128)(2,1)S(1)} %get-tuple-element.47), channel_id=1, source_target_pairs={{0,16},{8,24},{16,0},{24,8},{1,17},{9,25},{17,1},{25,9},{2,18},{10... | collective-permute-start | bytes 1179656 | tf_op jit(solution)/shard_map/ppermute | solution.py:344
  15.9 2.6 %collective-permute-start.3 = (bf16[272,256]{1,0:T(8,128)(2,1)S(1)}, bf16[272,256]{1,0:T(8,128)(2,1)S(1)}, u32[]{:S(2)}, u32[]{:S(2)}) collective-permute-start(bf16[272,256]{1,0:T(8,128)(2,1)S(1)} %get-tuple-element.46.piece.refs_0_.refs_2_.refs_4_), channel_id=1, source_target_pairs={{0,4},{1,5},{2,6},{3,7},{4,0},{5,1},{6,2},{7,3},{8,12},{9,13},{10,... | collective-permute-start | bytes 417800 | tf_op jit(solution)/shard_map/ppermute | solution.py:347
  18.5 1.6 %collective-permute-start.10 = (bf16[128,2048]{1,0:T(8,128)(2,1)S(1)}, bf16[128,2048]{1,0:T(8,128)(2,1)S(1)}, u32[]{:S(2)}, u32[]{:S(2)}) collective-permute-start(bf16[128,2048]{1,0:T(8,128)(2,1)S(1)} %bitcast.6), channel_id=1, source_target_pairs={{0,2},{1,3},{2,0},{3,1},{4,6},{5,7},{6,4},{7,5},{8,10},{9,11},{10,... | collective-permute-start | bytes 1572872 | tf_op jit(solution)/shard_map/ppermute | solution.py:341
  20.4 5.9 %collective-permute-done.3.kv_o.refs_1_.refs_3_.refs_5_ = bf16[272,256]{1,0:T(8,128)(2,1)S(1)} collective-permute-done((bf16[272,256]{1,0:T(8,128)(2,1)S(1)}, bf16[272,256]{1,0:T(8,128)(2,1)S(1)}, u32[]{:S(2)}, u32[]{:S(2)}) %collective-permute-start.3) | collective-permute-done | bytes 139296 | tf_op jit(solution)/shard_map/ppermute | solution.py:347
  26.8 1.5 %collective-permute-start.8 = (bf16[272,256]{1,0:T(8,128)(2,1)S(1)}, bf16[272,256]{1,0:T(8,128)(2,1)S(1)}, u32[]{:S(2)}, u32[]{:S(2)}) collective-permute-start(bf16[272,256]{1,0:T(8,128)(2,1)S(1)} %collective-permute-done.3.kv_o.refs_1_.refs_3_.refs_5_), channel_id=1, source_target_pairs={{0,24},{8,16},{16,8},{24,0},{1,25},{9,17},{17,9},{25,1},{2,26},{10... | collective-permute-start | bytes 417800 | tf_op jit(solution)/shard_map/ppermute | solution.py:344
  28.4 1.5 %collective-permute-start.7 = (bf16[528,256]{1,0:T(8,128)(2,1)S(1)}, bf16[528,256]{1,0:T(8,128)(2,1)S(1)}, u32[]{:S(2)}, u32[]{:S(2)}) collective-permute-start(bf16[528,256]{1,0:T(8,128)(2,1)S(1)} %get-tuple-element.50), channel_id=1, source_target_pairs={{0,16},{8,24},{16,0},{24,8},{1,17},{9,25},{17,1},{25,9},{2,18},{10... | collective-permute-start | bytes 811016 | tf_op jit(solution)/shard_map/ppermute | solution.py:344
  30.1 8.1 %collective-permute-done.9.refs_1_ = bf16[256,512]{1,0:T(8,128)(2,1)S(1)} collective-permute-done((bf16[256,512]{1,0:T(8,128)(2,1)S(1)}, bf16[256,512]{1,0:T(8,128)(2,1)S(1)}, u32[]{:S(2)}, u32[]{:S(2)}) %collective-permute-start.9) | collective-permute-done | bytes 262176 | tf_op jit(solution)/shard_map/ppermute | solution.py:347
  38.1 1.1 %collective-permute-done.10.far = bf16[128,2048]{1,0:T(8,128)(2,1)S(1)} collective-permute-done((bf16[128,2048]{1,0:T(8,128)(2,1)S(1)}, bf16[128,2048]{1,0:T(8,128)(2,1)S(1)}, u32[]{:S(2)}, u32[]{:S(2)}) %collective-permute-start.10) | collective-permute-done | bytes 524320 | tf_op jit(solution)/shard_map/ppermute | solution.py:341
  39.3 0.6 collective-permute-start.16
  40.4 0.8 %collective-permute-done.11.far_near = bf16[128,2048]{1,0:T(8,128)(2,1)S(1)} collective-permute-done((bf16[128,2048]{1,0:T(8,128)(2,1)S(1)}, bf16[128,2048]{1,0:T(8,128)(2,1)S(1)}, u32[]{:S(2)}, u32[]{:S(2)}) %collective-permute-start.11) | collective-permute-done | bytes 524320 | tf_op jit(solution)/shard_map/ppermute | solution.py:341
  41.2 0.9 %project_kv.1.refs_0_ = bf16[512,256]{1,0:T(8,128)(2,1)S(1)} custom-call(bf16[128,2048]{1,0:T(8,128)(2,1)S(1)} %bitcast.7, bf16[2448,128]{1,0:T(8,128)(2,1)S(1)} %collective-permute-done.refs_1_.near, bf16[128,2048]{1,0:T(8,128)(2,1)S(1)} %collective-permute-done.10.far, bf16[128,2048]{1,0:T(8,128)(2,1)S(1)} %collective-permute-done.11.far_near, ...), custom_call_target="tpu_custom_call" | custom-call | bytes 1048576 | tf_op jit(solution)/shard_map/project_kv/pallas_call | solution.py:437
  42.1 2.4 %collective-permute-start.12 = (bf16[512,256]{1,0:T(8,128)(2,1)S(1)}, bf16[512,256]{1,0:T(8,128)(2,1)S(1)}, u32[]{:S(2)}, u32[]{:S(2)}) collective-permute-start(bf16[512,256]{1,0:T(8,128)(2,1)S(1)} %project_kv.1.refs_0_), channel_id=1, source_target_pairs={{0,4},{1,5},{2,6},{3,7},{4,0},{5,1},{6,2},{7,3},{8,12},{9,13},{10,... | collective-permute-start | bytes 786440 | tf_op jit(solution)/shard_map/ppermute | solution.py:347
  44.5 3.5 %collective-permute-done.16.refs_3_ = bf16[256,512]{1,0:T(8,128)(2,1)S(1)} collective-permute-done((bf16[256,512]{1,0:T(8,128)(2,1)S(1)}, bf16[256,512]{1,0:T(8,128)(2,1)S(1)}, u32[]{:S(2)}, u32[]{:S(2)}) %collective-permute-start.16) | collective-permute-done | bytes 262176 | tf_op jit(solution)/shard_map/ppermute | solution.py:344
  48.3 1.5 %collective-permute-start.18 = (bf16[256,512]{1,0:T(8,128)(2,1)S(1)}, bf16[256,512]{1,0:T(8,128)(2,1)S(1)}, u32[]{:S(2)}, u32[]{:S(2)}) collective-permute-start(bf16[256,512]{1,0:T(8,128)(2,1)S(1)} %collective-permute-done.17.refs_5_), channel_id=1, source_target_pairs={{0,8},{8,0},{16,24},{24,16},{1,9},{9,1},{17,25},{25,17},{2,10},{10... | collective-permute-start | bytes 786440 | tf_op jit(solution)/shard_map/ppermute | solution.py:344
  50.3 6.8 %collective-permute-done.12.refs_1_ = bf16[512,256]{1,0:T(8,128)(2,1)S(1)} collective-permute-done((bf16[512,256]{1,0:T(8,128)(2,1)S(1)}, bf16[512,256]{1,0:T(8,128)(2,1)S(1)}, u32[]{:S(2)}, u32[]{:S(2)}) %collective-permute-start.12) | collective-permute-done | bytes 262176 | tf_op jit(solution)/shard_map/ppermute | solution.py:347
  57.7 1.0 %away.1 = bf16[8,64,256]{2,1,0:T(8,128)(2,1)S(1)} custom-call(bf16[512,256]{1,0:T(8,128)(2,1)S(1)} %project_kv.1.refs_0_, bf16[512,256]{1,0:T(8,128)(2,1)S(1)} %collective-permute-done.12.refs_1_, bf16[272,256]{1,0:T(8,128)(2,1)S(1)} %get-tuple-element.46.piece.refs_0_.refs_2_.refs_4_, ...), custom_call_target="tpu_custom_call" | custom-call | bytes 1048576 | tf_op jit(solution)/shard_map/away/pallas_call | solution.py:465
  58.8 0.6 copy-done.4
  59.4 1.6 %project_q.1 = (bf16[256,512]{1,0:T(8,128)(2,1)S(1)}, bf16[256,512]{1,0:T(8,128)(2,1)S(1)}) custom-call(bf16[128,2048]{1,0:T(8,128)(2,1)S(1)} %bitcast.8, bf16[2448,128]{1,0:T(8,128)(2,1)S(1)} %collective-permute-done.refs_1_.near, bf16[128,2048]{1,0:T(8,128)(2,1)S(1)} %collective-permute-done.10.far, ...), custom_call_target="tpu_custom_call" | custom-call | bytes 1048576 | tf_op jit(solution)/shard_map/project_q/pallas_call | solution.py:437
  61.0 0.6 collective-permute-start.20
  61.7 1.0 %collective-permute-done.20.near_ref = bf16[256,512]{1,0:T(8,128)(2,1)S(1)} collective-permute-done((bf16[256,512]{1,0:T(8,128)(2,1)S(1)}, bf16[256,512]{1,0:T(8,128)(2,1)S(1)}, u32[]{:S(2)}, u32[]{:S(2)}) %collective-permute-start.20) | collective-permute-done | bytes 262176 | tf_op jit(solution)/shard_map/ppermute | solution.py:341
  62.7 1.7 %attend.3 = bf16[128,1024]{1,0:T(8,128)(2,1)S(1)} custom-call(bf16[2,1024,256]{2,1,0:T(8,128)(2,1)S(1)} %sort.1.store, bf16[256,512]{1,0:T(8,128)(2,1)S(1)} %get-tuple-element.68.q_ref, bf16[256,512]{1,0:T(8,128)(2,1)S(1)} %collective-permute-done.20.near_ref, bf16[272,256]{1,0:T(8,128)(2,1)S(1)} %get-tuple-element.46.piece.refs_0_.refs_2_.refs_4_, ...), custom_call_target="tpu_custom_call" | custom-call | bytes 1048576 | tf_op jit(solution)/shard_map/attend/pallas_call | solution.py:493
  64.4 1.4 %collective-permute-start.21 = (bf16[128,1024]{1,0:T(8,128)(2,1)S(1)}, bf16[128,1024]{1,0:T(8,128)(2,1)S(1)}, u32[]{:S(2)}, u32[]{:S(2)}) collective-permute-start(bf16[128,1024]{1,0:T(8,128)(2,1)S(1)} %attend.3), channel_id=1, source_target_pairs={{0,2},{1,3},{2,0},{3,1},{4,6},{5,7},{6,4},{7,5},{8,10},{9,11},{10,... | collective-permute-start | bytes 786440 | tf_op jit(solution)/shard_map/ppermute | solution.py:341
  65.8 1.7 %attend.2.kept = bf16[128,1024]{1,0:T(8,128)(2,1)S(1)} custom-call(bf16[2,1024,256]{2,1,0:T(8,128)(2,1)S(1)} %sort.1.store, bf16[256,512]{1,0:T(8,128)(2,1)S(1)} %get-tuple-element.68.q_ref, bf16[256,512]{1,0:T(8,128)(2,1)S(1)} %collective-permute-done.20.near_ref, bf16[272,256]{1,0:T(8,128)(2,1)S(1)} %get-tuple-element.46.piece.refs_0_.refs_2_.refs_4_, ...), custom_call_target="tpu_custom_call" | custom-call | bytes 1048576 | tf_op jit(solution)/shard_map/attend/pallas_call | solution.py:493
  67.6 0.9 %own.1.own_pages = bf16[4,64,512]{2,1,0:T(8,128)(2,1)S(1)} custom-call(bf16[2,1024,256]{2,1,0:T(8,128)(2,1)S(1)} %sort.1.store, s32[1,2,16]{2,1,0:T(2,128)S(1)} %copy-done.2, s32[1]{0:T(128)S(6)} %copy.13.refs_5_.length_ref), custom_call_target="tpu_custom_call" | custom-call | tf_op jit(solution)/shard_map/own/pallas_call | solution.py:509
  68.5 4.7 %collective-permute-done.21.from_far = bf16[128,1024]{1,0:T(8,128)(2,1)S(1)} collective-permute-done((bf16[128,1024]{1,0:T(8,128)(2,1)S(1)}, bf16[128,1024]{1,0:T(8,128)(2,1)S(1)}, u32[]{:S(2)}, u32[]{:S(2)}) %collective-permute-start.21) | collective-permute-done | bytes 262176 | tf_op jit(solution)/shard_map/ppermute | solution.py:341
  73.1 1.8 %finish.1 = (bf16[128,2048]{1,0:T(8,128)(2,1)}, bf16[4,64,512]{2,1,0:T(8,128)(2,1)}) custom-call(bf16[128,1024]{1,0:T(8,128)(2,1)S(1)} %attend.2.kept, bf16[128,1024]{1,0:T(8,128)(2,1)S(1)} %collective-permute-done.21.from_far, bf16[4,64,512]{2,1,0:T(8,128)(2,1)S(1)} %own.1.own_pages, bf16[8,64,256]{2,1,0:T(8,128)(2,1)S(1)} %collective-permute-done.13.got, ...), custom_call_target="tpu_custom_call" | custom-call | tf_op jit(solution)/shard_map/finish/pallas_call | solution.py:519
  (44 shorter events, 3.5 us)
Async XLA Ops:
  2.9 15.5 %copy-start = (bf16[1,128,2048]{2,1,0:T(8,128)(2,1)S(1)}, bf16[1,128,2048]{2,1,0:T(8,128)(2,1)}, u32[]{:S(2)}) copy-start(bf16[1,128,2048]{2,1,0:T(8,128)(2,1)} %param.11) | copy-start | bytes 1572868
  2.9 8.8 %collective-permute-start = (bf16[2448,128]{1,0:T(8,128)(2,1)}, bf16[2448,128]{1,0:T(8,128)(2,1)S(1)}, u32[]{:S(2)}, u32[]{:S(2)}) collective-permute-start(bf16[2448,128]{1,0:T(8,128)(2,1)} %get-tuple-element.39), channel_id=1, source_target_pairs={{0,1},{1,0},{2,3},{3,2},{4,5},{5,4},{6,7},{7,6},{8,9},{9,8},{10,11... | collective-permute-start | bytes 1880072 | tf_op jit(solution)/shard_map/ppermute | solution.py:341
  3.4 6.6 %collective-permute-start.1 = (bf16[400,128]{1,0:T(8,128)(2,1)}, bf16[400,128]{1,0:T(8,128)(2,1)S(1)}, u32[]{:S(2)}, u32[]{:S(2)}) collective-permute-start(bf16[400,128]{1,0:T(8,128)(2,1)} %get-tuple-element.40), channel_id=1, source_target_pairs={{0,2},{1,3},{2,0},{3,1},{4,6},{5,7},{6,4},{7,5},{8,10},{9,11},{10,... | collective-permute-start | bytes 307208 | tf_op jit(solution)/shard_map/ppermute | solution.py:341
  6.1 5.6 %collective-permute-start.2 = (bf16[400,128]{1,0:T(8,128)(2,1)}, bf16[400,128]{1,0:T(8,128)(2,1)S(1)}, u32[]{:S(2)}, u32[]{:S(2)}) collective-permute-start(bf16[400,128]{1,0:T(8,128)(2,1)} %get-tuple-element.41), channel_id=1, source_target_pairs={{0,3},{1,2},{2,1},{3,0},{4,7},{5,6},{6,5},{7,4},{8,11},{9,10},{10,... | collective-permute-start | bytes 307208 | tf_op jit(solution)/shard_map/ppermute | solution.py:341
  11.7 0.9 %copy-start.1 = (bf16[400,128]{1,0:T(8,128)(2,1)S(1)}, bf16[400,128]{1,0:T(8,128)(2,1)}, u32[]{:S(2)}) copy-start(bf16[400,128]{1,0:T(8,128)(2,1)} %get-tuple-element.38.refs_0_) | copy-start | bytes 307204
  12.7 17.1 %copy-start.5 = (f32[64,128]{1,0:T(8,128)S(1)}, f32[64,128]{1,0:T(8,128)}, u32[]{:S(2)}) copy-start(f32[64,128]{1,0:T(8,128)} %constant.10.clone.off_cos) | copy-start | bytes 98308
  12.8 17.1 %copy-start.6 = (f32[64,128]{1,0:T(8,128)S(1)}, f32[64,128]{1,0:T(8,128)}, u32[]{:S(2)}) copy-start(f32[64,128]{1,0:T(8,128)} %constant.11.clone.off_sin) | copy-start | bytes 98308
  12.8 17.1 %copy-start.7 = (f32[16,128]{1,0:T(8,128)S(1)}, f32[16,128]{1,0:T(8,128)}, u32[]{:S(2)}) copy-start(f32[16,128]{1,0:T(8,128)} %constant.8.clone.first_cos) | copy-start | bytes 24580
  12.8 17.1 %copy-start.8 = (f32[16,128]{1,0:T(8,128)S(1)}, f32[16,128]{1,0:T(8,128)}, u32[]{:S(2)}) copy-start(f32[16,128]{1,0:T(8,128)} %constant.9.clone.first_sin) | copy-start | bytes 24580
  12.8 13.5 %collective-permute-start.4 = (bf16[256,768]{1,0:T(8,128)(2,1)S(1)}, bf16[256,768]{1,0:T(8,128)(2,1)S(1)}, u32[]{:S(2)}, u32[]{:S(2)}) collective-permute-start(bf16[256,768]{1,0:T(8,128)(2,1)S(1)} %get-tuple-element.47), channel_id=1, source_target_pairs={{0,8},{8,0},{16,24},{24,16},{1,9},{9,1},{17,25},{25,17},{2,10},{10... | collective-permute-start | bytes 1179656 | tf_op jit(solution)/shard_map/ppermute | solution.py:344
  14.3 11.9 %collective-permute-start.5 = (bf16[256,768]{1,0:T(8,128)(2,1)S(1)}, bf16[256,768]{1,0:T(8,128)(2,1)S(1)}, u32[]{:S(2)}, u32[]{:S(2)}) collective-permute-start(bf16[256,768]{1,0:T(8,128)(2,1)S(1)} %get-tuple-element.47), channel_id=1, source_target_pairs={{0,16},{8,24},{16,0},{24,8},{1,17},{9,25},{17,1},{25,9},{2,18},{10... | collective-permute-start | bytes 1179656 | tf_op jit(solution)/shard_map/ppermute | solution.py:344
  15.9 10.4 %collective-permute-start.3 = (bf16[272,256]{1,0:T(8,128)(2,1)S(1)}, bf16[272,256]{1,0:T(8,128)(2,1)S(1)}, u32[]{:S(2)}, u32[]{:S(2)}) collective-permute-start(bf16[272,256]{1,0:T(8,128)(2,1)S(1)} %get-tuple-element.46.piece.refs_0_.refs_2_.refs_4_), channel_id=1, source_target_pairs={{0,4},{1,5},{2,6},{3,7},{4,0},{5,1},{6,2},{7,3},{8,12},{9,13},{10,... | collective-permute-start | bytes 417800 | tf_op jit(solution)/shard_map/ppermute | solution.py:347
  18.5 20.8 %collective-permute-start.10 = (bf16[128,2048]{1,0:T(8,128)(2,1)S(1)}, bf16[128,2048]{1,0:T(8,128)(2,1)S(1)}, u32[]{:S(2)}, u32[]{:S(2)}) collective-permute-start(bf16[128,2048]{1,0:T(8,128)(2,1)S(1)} %bitcast.6), channel_id=1, source_target_pairs={{0,2},{1,3},{2,0},{3,1},{4,6},{5,7},{6,4},{7,5},{8,10},{9,11},{10,... | collective-permute-start | bytes 1572872 | tf_op jit(solution)/shard_map/ppermute | solution.py:341
  20.0 18.1 %collective-permute-start.9 = (bf16[256,512]{1,0:T(8,128)(2,1)S(1)}, bf16[256,512]{1,0:T(8,128)(2,1)S(1)}, u32[]{:S(2)}, u32[]{:S(2)}) collective-permute-start(bf16[256,512]{1,0:T(8,128)(2,1)S(1)} %get-tuple-element.51.refs_0_), channel_id=1, source_target_pairs={{0,4},{1,5},{2,6},{3,7},{4,0},{5,1},{6,2},{7,3},{8,12},{9,13},{10,... | collective-permute-start | bytes 786440 | tf_op jit(solution)/shard_map/ppermute | solution.py:347
  26.3 12.9 %collective-permute-start.6 = (bf16[272,256]{1,0:T(8,128)(2,1)S(1)}, bf16[272,256]{1,0:T(8,128)(2,1)S(1)}, u32[]{:S(2)}, u32[]{:S(2)}) collective-permute-start(bf16[272,256]{1,0:T(8,128)(2,1)S(1)} %collective-permute-done.3.kv_o.refs_1_.refs_3_.refs_5_), channel_id=1, source_target_pairs={{0,8},{8,0},{16,24},{24,16},{1,9},{9,1},{17,25},{25,17},{2,10},{10... | collective-permute-start | bytes 417800 | tf_op jit(solution)/shard_map/ppermute | solution.py:344
  26.8 12.4 %collective-permute-start.8 = (bf16[272,256]{1,0:T(8,128)(2,1)S(1)}, bf16[272,256]{1,0:T(8,128)(2,1)S(1)}, u32[]{:S(2)}, u32[]{:S(2)}) collective-permute-start(bf16[272,256]{1,0:T(8,128)(2,1)S(1)} %collective-permute-done.3.kv_o.refs_1_.refs_3_.refs_5_), channel_id=1, source_target_pairs={{0,24},{8,16},{16,8},{24,0},{1,25},{9,17},{17,9},{25,1},{2,26},{10... | collective-permute-start | bytes 417800 | tf_op jit(solution)/shard_map/ppermute | solution.py:344
  28.4 10.8 %collective-permute-start.7 = (bf16[528,256]{1,0:T(8,128)(2,1)S(1)}, bf16[528,256]{1,0:T(8,128)(2,1)S(1)}, u32[]{:S(2)}, u32[]{:S(2)}) collective-permute-start(bf16[528,256]{1,0:T(8,128)(2,1)S(1)} %get-tuple-element.50), channel_id=1, source_target_pairs={{0,16},{8,24},{16,0},{24,8},{1,17},{9,25},{17,1},{25,9},{2,18},{10... | collective-permute-start | bytes 811016 | tf_op jit(solution)/shard_map/ppermute | solution.py:344
  39.2 2.0 %copy-start.3 = (f32[256]{0:T(256)S(1)}, f32[256]{0:T(256)}, u32[]{:S(2)}) copy-start(f32[256]{0:T(256)} %param.17) | copy-start | bytes 3076
  39.2 2.0 %collective-permute-start.11 = (bf16[128,2048]{1,0:T(8,128)(2,1)S(1)}, bf16[128,2048]{1,0:T(8,128)(2,1)S(1)}, u32[]{:S(2)}, u32[]{:S(2)}) collective-permute-start(bf16[128,2048]{1,0:T(8,128)(2,1)S(1)} %collective-permute-done.10.far), channel_id=1, source_target_pairs={{0,1},{1,0},{2,3},{3,2},{4,5},{5,4},{6,7},{7,6},{8,9},{9,8},{10,11... | collective-permute-start | bytes 1572872 | tf_op jit(solution)/shard_map/ppermute | solution.py:341
  39.3 8.7 %collective-permute-start.16 = (bf16[256,512]{1,0:T(8,128)(2,1)S(1)}, bf16[256,512]{1,0:T(8,128)(2,1)S(1)}, u32[]{:S(2)}, u32[]{:S(2)}) collective-permute-start(bf16[256,512]{1,0:T(8,128)(2,1)S(1)} %collective-permute-done.9.refs_1_), channel_id=1, source_target_pairs={{0,8},{8,0},{16,24},{24,16},{1,9},{9,1},{17,25},{25,17},{2,10},{10... | collective-permute-start | bytes 786440 | tf_op jit(solution)/shard_map/ppermute | solution.py:344
  39.9 8.4 %collective-permute-start.17 = (bf16[256,512]{1,0:T(8,128)(2,1)S(1)}, bf16[256,512]{1,0:T(8,128)(2,1)S(1)}, u32[]{:S(2)}, u32[]{:S(2)}) collective-permute-start(bf16[256,512]{1,0:T(8,128)(2,1)S(1)} %collective-permute-done.9.refs_1_), channel_id=1, source_target_pairs={{0,16},{8,24},{16,0},{24,8},{1,17},{9,25},{17,1},{25,9},{2,18},{10... | collective-permute-start | bytes 786440 | tf_op jit(solution)/shard_map/ppermute | solution.py:344
  42.1 14.9 %collective-permute-start.12 = (bf16[512,256]{1,0:T(8,128)(2,1)S(1)}, bf16[512,256]{1,0:T(8,128)(2,1)S(1)}, u32[]{:S(2)}, u32[]{:S(2)}) collective-permute-start(bf16[512,256]{1,0:T(8,128)(2,1)S(1)} %project_kv.1.refs_0_), channel_id=1, source_target_pairs={{0,4},{1,5},{2,6},{3,7},{4,0},{5,1},{6,2},{7,3},{8,12},{9,13},{10,... | collective-permute-start | bytes 786440 | tf_op jit(solution)/shard_map/ppermute | solution.py:347
  48.3 9.4 %copy-start.2 = (s32[1,2,16]{2,1,0:T(2,128)S(1)}, s32[1,2,16]{2,1,0:T(2,128)}, u32[]{:S(2)}) copy-start(s32[1,2,16]{2,1,0:T(2,128)} %table.3) | copy-start | bytes 388
  48.3 10.5 %collective-permute-start.18 = (bf16[256,512]{1,0:T(8,128)(2,1)S(1)}, bf16[256,512]{1,0:T(8,128)(2,1)S(1)}, u32[]{:S(2)}, u32[]{:S(2)}) collective-permute-start(bf16[256,512]{1,0:T(8,128)(2,1)S(1)} %collective-permute-done.17.refs_5_), channel_id=1, source_target_pairs={{0,8},{8,0},{16,24},{24,16},{1,9},{9,1},{17,25},{25,17},{2,10},{10... | collective-permute-start | bytes 786440 | tf_op jit(solution)/shard_map/ppermute | solution.py:344
  49.8 9.0 %collective-permute-start.19 = (bf16[256,512]{1,0:T(8,128)(2,1)S(1)}, bf16[256,512]{1,0:T(8,128)(2,1)S(1)}, u32[]{:S(2)}, u32[]{:S(2)}) collective-permute-start(bf16[256,512]{1,0:T(8,128)(2,1)S(1)} %get-tuple-element.65), channel_id=1, source_target_pairs={{0,16},{8,24},{16,0},{24,8},{1,17},{9,25},{17,1},{25,9},{2,18},{10... | collective-permute-start | bytes 786440 | tf_op jit(solution)/shard_map/ppermute | solution.py:344
  50.3 11.3 %collective-permute-start.14 = (bf16[512,256]{1,0:T(8,128)(2,1)S(1)}, bf16[512,256]{1,0:T(8,128)(2,1)S(1)}, u32[]{:S(2)}, u32[]{:S(2)}) collective-permute-start(bf16[512,256]{1,0:T(8,128)(2,1)S(1)} %project_kv.1.refs_0_), channel_id=1, source_target_pairs={{0,1},{1,0},{2,3},{3,2},{4,5},{5,4},{6,7},{7,6},{8,9},{9,8},{10,11... | collective-permute-start | bytes 786440 | tf_op jit(solution)/shard_map/ppermute | solution.py:341
  57.1 4.5 %collective-permute-start.15 = (bf16[512,256]{1,0:T(8,128)(2,1)S(1)}, bf16[512,256]{1,0:T(8,128)(2,1)S(1)}, u32[]{:S(2)}, u32[]{:S(2)}) collective-permute-start(bf16[512,256]{1,0:T(8,128)(2,1)S(1)} %collective-permute-done.12.refs_1_), channel_id=1, source_target_pairs={{0,1},{1,0},{2,3},{3,2},{4,5},{5,4},{6,7},{7,6},{8,9},{9,8},{10,11... | collective-permute-start | bytes 786440 | tf_op jit(solution)/shard_map/ppermute | solution.py:341
  58.7 0.7 copy-start.4
  58.7 8.8 %collective-permute-start.13 = (bf16[8,64,256]{2,1,0:T(8,128)(2,1)S(1)}, bf16[8,64,256]{2,1,0:T(8,128)(2,1)S(1)}, u32[]{:S(2)}, u32[]{:S(2)}) collective-permute-start(bf16[8,64,256]{2,1,0:T(8,128)(2,1)S(1)} %away.1), channel_id=1, source_target_pairs={{0,2},{1,3},{2,0},{3,1},{4,6},{5,7},{6,4},{7,5},{8,10},{9,11},{10,... | collective-permute-start | bytes 786440 | tf_op jit(solution)/shard_map/ppermute | solution.py:341
  61.0 1.7 %collective-permute-start.20 = (bf16[256,512]{1,0:T(8,128)(2,1)S(1)}, bf16[256,512]{1,0:T(8,128)(2,1)S(1)}, u32[]{:S(2)}, u32[]{:S(2)}) collective-permute-start(bf16[256,512]{1,0:T(8,128)(2,1)S(1)} %get-tuple-element.69), channel_id=1, source_target_pairs={{0,1},{1,0},{2,3},{3,2},{4,5},{5,4},{6,7},{7,6},{8,9},{9,8},{10,11... | collective-permute-start | bytes 786440 | tf_op jit(solution)/shard_map/ppermute | solution.py:341
  64.4 8.7 %collective-permute-start.21 = (bf16[128,1024]{1,0:T(8,128)(2,1)S(1)}, bf16[128,1024]{1,0:T(8,128)(2,1)S(1)}, u32[]{:S(2)}, u32[]{:S(2)}) collective-permute-start(bf16[128,1024]{1,0:T(8,128)(2,1)S(1)} %attend.3), channel_id=1, source_target_pairs={{0,2},{1,3},{2,0},{3,1},{4,6},{5,7},{6,4},{7,5},{8,10},{9,11},{10,... | collective-permute-start | bytes 786440 | tf_op jit(solution)/shard_map/ppermute | solution.py:341
  67.5 5.6 %collective-permute-start.22 = (bf16[8,64,256]{2,1,0:T(8,128)(2,1)S(1)}, bf16[8,64,256]{2,1,0:T(8,128)(2,1)S(1)}, u32[]{:S(2)}, u32[]{:S(2)}) collective-permute-start(bf16[8,64,256]{2,1,0:T(8,128)(2,1)S(1)} %collective-permute-done.13.got), channel_id=1, source_target_pairs={{0,1},{1,0},{2,3},{3,2},{4,5},{5,4},{6,7},{7,6},{8,9},{9,8},{10,11... | collective-permute-start | bytes 786440 | tf_op jit(solution)/shard_map/ppermute | solution.py:341

commit v15 on v14

--- a/solution.py
+++ b/solution.py
@@ -109,6 +109,10 @@
             flat_of[table[0, head, block]] = head * per_head + block
 
 
+def keep_kernel(part, out):
+    out[...] = part[...]
+
+
 def team_kernel(*refs):
     _, pair, core = place()
     parts, (kv_out, q_out, whole) = refs[:TEAM], refs[TEAM:]
@@ -370,7 +374,16 @@
         compiler_params=params(56),
         name="pack",
     )(qkv_weight, block_ids, own)
-    got = [parts[0]] + [in_team(parts[k], k) for k in range(1, TEAM)]
+    kept_part = pl.pallas_call(
+        keep_kernel,
+        out_shape=shape(parts[0].shape, bf16),
+        in_specs=[VMEM],
+        out_specs=VMEM,
+        cost_estimate=pl.CostEstimate(flops=10**10, bytes_accessed=MIB, transcendentals=0),
+        compiler_params=params(1),
+        name="keep",
+    )(parts[0])
+    got = [kept_part] + [in_team(parts[k], k) for k in range(1, TEAM)]
     kv, q, w = pl.pallas_call(
         team_kernel,
         out_shape=[

time: 75.1 us -> 74.2 us (0.988)
  waiting for transfers between devices: 37.7 us -> 36.8 us
    ppermute x11, waiting for transfers between devices: 13.1 us -> 12.2 us  [in_team(): return lax.ppermute(array, 'blk', [(i, i ^ k) for i in range(n_blk)])]
where the time goes in v15:
time: 74.2 us; the launch traced here: 74 us
  waiting for transfers between devices  36.8 us (50%)
  starting transfers between devices  21.9 us (30%)
  Pallas kernels  12.3 us (17%)
  local copies, waits for them, and re-layouts  1.51 us (2%)
  between operations  1.5 us (2%)
    ppermute x3, waiting for transfers between devices, across(): lax.ppermute(array, 'blk', [(i, (i + TEAM * k) % n_blk) for i in range(n_...  20.7 us
    ppermute x11, waiting for transfers between devices, in_team(): return lax.ppermute(array, 'blk', [(i, i ^ k) for i in range(n_blk)])  12.2 us
    ppermute x9, starting transfers between devices, in_req(): return lax.ppermute(array, 'req', [(i, i ^ k) for i in range(n_req)])  9.68 us
    ppermute x11, starting transfers between devices, in_team(): return lax.ppermute(array, 'blk', [(i, i ^ k) for i in range(n_blk)])  6.95 us
    ppermute x3, starting transfers between devices, across(): lax.ppermute(array, 'blk', [(i, (i + TEAM * k) % n_blk) for i in range(n_...  5.29 us
    ppermute x9, waiting for transfers between devices, in_req(): return lax.ppermute(array, 'req', [(i, i ^ k) for i in range(n_req)])  3.82 us
    pallas_call x2, Pallas kernels, attend(): pl.pallas_call(functools.partial(attend_kernel, blk_rows, step), out_shap...  3.41 us
    pallas_call x2, Pallas kernels, project(): pl.pallas_call(functools.partial(project_kernel, n_out, TEAM * w_rows, st...  2.47 us
  transfers between devices with their start and end apart: 23, of which 11 were waited for; matrix products, arithmetic and copies ran while one was open for 0% of the time, Pallas kernels for 11%

profile of v15, /device:TPU:0, one launch (start us, length us, event | category | flops | bytes accessed | tf_op | source)
XLA Modules:
  0.0 74.0 jit_solution(2462903148427770017)
XLA Ops:
  0.6 2.3 %pack.1 = (bf16[400,128]{1,0:T(8,128)(2,1)}, bf16[2448,128]{1,0:T(8,128)(2,1)}, bf16[400,128]{1,0:T(8,128)(2,1)}, bf16[400,128]{1,0:T(8,128)(2,1)}) custom-call(bf16[64,3072]{1,0:T(8,128)(2,1)} %w_hbm.1, s32[1,2]{1,0:T(1,128)} %ids_hbm.1, bf16[128,2048]{1,0:T(8,128)(2,1)} %bitcast.5), custom_call_target="tpu_custom_call" | custom-call | tf_op jit(solution)/shard_map/pack/pallas_call | solution.py:361
  3.4 2.7 %collective-permute-start.1 = (bf16[400,128]{1,0:T(8,128)(2,1)}, bf16[400,128]{1,0:T(8,128)(2,1)S(1)}, u32[]{:S(2)}, u32[]{:S(2)}) collective-permute-start(bf16[400,128]{1,0:T(8,128)(2,1)} %get-tuple-element.40), channel_id=1, source_target_pairs={{0,2},{1,3},{2,0},{3,1},{4,6},{5,7},{6,4},{7,5},{8,10},{9,11},{10,... | collective-permute-start | bytes 307208 | tf_op jit(solution)/shard_map/ppermute | solution.py:345
  6.2 0.9 %copy-done.4 = bf16[400,128]{1,0:T(8,128)(2,1)S(1)} copy-done((bf16[400,128]{1,0:T(8,128)(2,1)S(1)}, bf16[400,128]{1,0:T(8,128)(2,1)}, u32[]{:S(2)}) %copy-start.4) | copy-done | bytes 102424
  7.1 3.0 %collective-permute-done.1.refs_2_ = bf16[400,128]{1,0:T(8,128)(2,1)S(1)} collective-permute-done((bf16[400,128]{1,0:T(8,128)(2,1)}, bf16[400,128]{1,0:T(8,128)(2,1)S(1)}, u32[]{:S(2)}, u32[]{:S(2)}) %collective-permute-start.1) | collective-permute-done | bytes 102432 | tf_op jit(solution)/shard_map/ppermute | solution.py:345
  10.0 1.7 %collective-permute-done.2.refs_3_ = bf16[400,128]{1,0:T(8,128)(2,1)S(1)} collective-permute-done((bf16[400,128]{1,0:T(8,128)(2,1)}, bf16[400,128]{1,0:T(8,128)(2,1)S(1)}, u32[]{:S(2)}, u32[]{:S(2)}) %collective-permute-start.2) | collective-permute-done | bytes 102432 | tf_op jit(solution)/shard_map/ppermute | solution.py:345
  11.9 1.5 %collective-permute-start.4 = (bf16[256,768]{1,0:T(8,128)(2,1)S(1)}, bf16[256,768]{1,0:T(8,128)(2,1)S(1)}, u32[]{:S(2)}, u32[]{:S(2)}) collective-permute-start(bf16[256,768]{1,0:T(8,128)(2,1)S(1)} %get-tuple-element.47), channel_id=1, source_target_pairs={{0,8},{8,0},{16,24},{24,16},{1,9},{9,1},{17,25},{25,17},{2,10},{10... | collective-permute-start | bytes 1179656 | tf_op jit(solution)/shard_map/ppermute | solution.py:348
  13.4 1.5 %collective-permute-start.5 = (bf16[256,768]{1,0:T(8,128)(2,1)S(1)}, bf16[256,768]{1,0:T(8,128)(2,1)S(1)}, u32[]{:S(2)}, u32[]{:S(2)}) collective-permute-start(bf16[256,768]{1,0:T(8,128)(2,1)S(1)} %get-tuple-element.47), channel_id=1, source_target_pairs={{0,16},{8,24},{16,0},{24,8},{1,17},{9,25},{17,1},{25,9},{2,18},{10... | collective-permute-start | bytes 1179656 | tf_op jit(solution)/shard_map/ppermute | solution.py:348
  15.0 2.6 %collective-permute-start.3 = (bf16[272,256]{1,0:T(8,128)(2,1)S(1)}, bf16[272,256]{1,0:T(8,128)(2,1)S(1)}, u32[]{:S(2)}, u32[]{:S(2)}) collective-permute-start(bf16[272,256]{1,0:T(8,128)(2,1)S(1)} %get-tuple-element.46.piece.refs_0_.refs_2_.refs_4_), channel_id=1, source_target_pairs={{0,4},{1,5},{2,6},{3,7},{4,0},{5,1},{6,2},{7,3},{8,12},{9,13},{10,... | collective-permute-start | bytes 417800 | tf_op jit(solution)/shard_map/ppermute | solution.py:351
  17.6 1.6 %collective-permute-start.10 = (bf16[128,2048]{1,0:T(8,128)(2,1)S(1)}, bf16[128,2048]{1,0:T(8,128)(2,1)S(1)}, u32[]{:S(2)}, u32[]{:S(2)}) collective-permute-start(bf16[128,2048]{1,0:T(8,128)(2,1)S(1)} %bitcast.6), channel_id=1, source_target_pairs={{0,2},{1,3},{2,0},{3,1},{4,6},{5,7},{6,4},{7,5},{8,10},{9,11},{10,... | collective-permute-start | bytes 1572872 | tf_op jit(solution)/shard_map/ppermute | solution.py:345
  19.5 5.9 %collective-permute-done.3.kv_o.refs_1_.refs_3_.refs_5_ = bf16[272,256]{1,0:T(8,128)(2,1)S(1)} collective-permute-done((bf16[272,256]{1,0:T(8,128)(2,1)S(1)}, bf16[272,256]{1,0:T(8,128)(2,1)S(1)}, u32[]{:S(2)}, u32[]{:S(2)}) %collective-permute-start.3) | collective-permute-done | bytes 139296 | tf_op jit(solution)/shard_map/ppermute | solution.py:351
  25.9 1.5 %collective-permute-start.8 = (bf16[272,256]{1,0:T(8,128)(2,1)S(1)}, bf16[272,256]{1,0:T(8,128)(2,1)S(1)}, u32[]{:S(2)}, u32[]{:S(2)}) collective-permute-start(bf16[272,256]{1,0:T(8,128)(2,1)S(1)} %collective-permute-done.3.kv_o.refs_1_.refs_3_.refs_5_), channel_id=1, source_target_pairs={{0,24},{8,16},{16,8},{24,0},{1,25},{9,17},{17,9},{25,1},{2,26},{10... | collective-permute-start | bytes 417800 | tf_op jit(solution)/shard_map/ppermute | solution.py:348
  27.5 1.5 %collective-permute-start.7 = (bf16[528,256]{1,0:T(8,128)(2,1)S(1)}, bf16[528,256]{1,0:T(8,128)(2,1)S(1)}, u32[]{:S(2)}, u32[]{:S(2)}) collective-permute-start(bf16[528,256]{1,0:T(8,128)(2,1)S(1)} %get-tuple-element.50), channel_id=1, source_target_pairs={{0,16},{8,24},{16,0},{24,8},{1,17},{9,25},{17,1},{25,9},{2,18},{10... | collective-permute-start | bytes 811016 | tf_op jit(solution)/shard_map/ppermute | solution.py:348
  29.2 8.1 %collective-permute-done.9.refs_1_ = bf16[256,512]{1,0:T(8,128)(2,1)S(1)} collective-permute-done((bf16[256,512]{1,0:T(8,128)(2,1)S(1)}, bf16[256,512]{1,0:T(8,128)(2,1)S(1)}, u32[]{:S(2)}, u32[]{:S(2)}) %collective-permute-start.9) | collective-permute-done | bytes 262176 | tf_op jit(solution)/shard_map/ppermute | solution.py:351
  37.2 1.1 %collective-permute-done.10.far = bf16[128,2048]{1,0:T(8,128)(2,1)S(1)} collective-permute-done((bf16[128,2048]{1,0:T(8,128)(2,1)S(1)}, bf16[128,2048]{1,0:T(8,128)(2,1)S(1)}, u32[]{:S(2)}, u32[]{:S(2)}) %collective-permute-start.10) | collective-permute-done | bytes 524320 | tf_op jit(solution)/shard_map/ppermute | solution.py:345
  38.4 0.6 collective-permute-start.16
  39.5 0.8 %collective-permute-done.11.far_near = bf16[128,2048]{1,0:T(8,128)(2,1)S(1)} collective-permute-done((bf16[128,2048]{1,0:T(8,128)(2,1)S(1)}, bf16[128,2048]{1,0:T(8,128)(2,1)S(1)}, u32[]{:S(2)}, u32[]{:S(2)}) %collective-permute-start.11) | collective-permute-done | bytes 524320 | tf_op jit(solution)/shard_map/ppermute | solution.py:345
  40.3 0.9 %project_kv.1.refs_0_ = bf16[512,256]{1,0:T(8,128)(2,1)S(1)} custom-call(bf16[128,2048]{1,0:T(8,128)(2,1)S(1)} %bitcast.7, bf16[2448,128]{1,0:T(8,128)(2,1)S(1)} %collective-permute-done.refs_1_.near, bf16[128,2048]{1,0:T(8,128)(2,1)S(1)} %collective-permute-done.10.far, bf16[128,2048]{1,0:T(8,128)(2,1)S(1)} %collective-permute-done.11.far_near, ...), custom_call_target="tpu_custom_call" | custom-call | bytes 1048576 | tf_op jit(solution)/shard_map/project_kv/pallas_call | solution.py:450
  41.2 2.4 %collective-permute-start.12 = (bf16[512,256]{1,0:T(8,128)(2,1)S(1)}, bf16[512,256]{1,0:T(8,128)(2,1)S(1)}, u32[]{:S(2)}, u32[]{:S(2)}) collective-permute-start(bf16[512,256]{1,0:T(8,128)(2,1)S(1)} %project_kv.1.refs_0_), channel_id=1, source_target_pairs={{0,4},{1,5},{2,6},{3,7},{4,0},{5,1},{6,2},{7,3},{8,12},{9,13},{10,... | collective-permute-start | bytes 786440 | tf_op jit(solution)/shard_map/ppermute | solution.py:351
  43.6 3.5 %collective-permute-done.16.refs_3_ = bf16[256,512]{1,0:T(8,128)(2,1)S(1)} collective-permute-done((bf16[256,512]{1,0:T(8,128)(2,1)S(1)}, bf16[256,512]{1,0:T(8,128)(2,1)S(1)}, u32[]{:S(2)}, u32[]{:S(2)}) %collective-permute-start.16) | collective-permute-done | bytes 262176 | tf_op jit(solution)/shard_map/ppermute | solution.py:348
  47.4 1.5 %collective-permute-start.18 = (bf16[256,512]{1,0:T(8,128)(2,1)S(1)}, bf16[256,512]{1,0:T(8,128)(2,1)S(1)}, u32[]{:S(2)}, u32[]{:S(2)}) collective-permute-start(bf16[256,512]{1,0:T(8,128)(2,1)S(1)} %collective-permute-done.17.refs_5_), channel_id=1, source_target_pairs={{0,8},{8,0},{16,24},{24,16},{1,9},{9,1},{17,25},{25,17},{2,10},{10... | collective-permute-start | bytes 786440 | tf_op jit(solution)/shard_map/ppermute | solution.py:348
  49.4 6.8 %collective-permute-done.12.refs_1_ = bf16[512,256]{1,0:T(8,128)(2,1)S(1)} collective-permute-done((bf16[512,256]{1,0:T(8,128)(2,1)S(1)}, bf16[512,256]{1,0:T(8,128)(2,1)S(1)}, u32[]{:S(2)}, u32[]{:S(2)}) %collective-permute-start.12) | collective-permute-done | bytes 262176 | tf_op jit(solution)/shard_map/ppermute | solution.py:351
  56.8 1.0 %away.1 = bf16[8,64,256]{2,1,0:T(8,128)(2,1)S(1)} custom-call(bf16[512,256]{1,0:T(8,128)(2,1)S(1)} %project_kv.1.refs_0_, bf16[512,256]{1,0:T(8,128)(2,1)S(1)} %collective-permute-done.12.refs_1_, bf16[272,256]{1,0:T(8,128)(2,1)S(1)} %get-tuple-element.46.piece.refs_0_.refs_2_.refs_4_, ...), custom_call_target="tpu_custom_call" | custom-call | bytes 1048576 | tf_op jit(solution)/shard_map/away/pallas_call | solution.py:478
  57.9 0.6 copy-done.3
  58.5 1.6 %project_q.1 = (bf16[256,512]{1,0:T(8,128)(2,1)S(1)}, bf16[256,512]{1,0:T(8,128)(2,1)S(1)}) custom-call(bf16[128,2048]{1,0:T(8,128)(2,1)S(1)} %bitcast.8, bf16[2448,128]{1,0:T(8,128)(2,1)S(1)} %collective-permute-done.refs_1_.near, bf16[128,2048]{1,0:T(8,128)(2,1)S(1)} %collective-permute-done.10.far, ...), custom_call_target="tpu_custom_call" | custom-call | bytes 1048576 | tf_op jit(solution)/shard_map/project_q/pallas_call | solution.py:450
  60.1 0.6 collective-permute-start.20
  60.8 1.0 %collective-permute-done.20.near_ref = bf16[256,512]{1,0:T(8,128)(2,1)S(1)} collective-permute-done((bf16[256,512]{1,0:T(8,128)(2,1)S(1)}, bf16[256,512]{1,0:T(8,128)(2,1)S(1)}, u32[]{:S(2)}, u32[]{:S(2)}) %collective-permute-start.20) | collective-permute-done | bytes 262176 | tf_op jit(solution)/shard_map/ppermute | solution.py:345
  61.8 1.7 %attend.3 = bf16[128,1024]{1,0:T(8,128)(2,1)S(1)} custom-call(bf16[2,1024,256]{2,1,0:T(8,128)(2,1)S(1)} %sort.1.store, bf16[256,512]{1,0:T(8,128)(2,1)S(1)} %get-tuple-element.68.q_ref, bf16[256,512]{1,0:T(8,128)(2,1)S(1)} %collective-permute-done.20.near_ref, bf16[272,256]{1,0:T(8,128)(2,1)S(1)} %get-tuple-element.46.piece.refs_0_.refs_2_.refs_4_, ...), custom_call_target="tpu_custom_call" | custom-call | bytes 1048576 | tf_op jit(solution)/shard_map/attend/pallas_call | solution.py:506
  63.5 1.4 %collective-permute-start.21 = (bf16[128,1024]{1,0:T(8,128)(2,1)S(1)}, bf16[128,1024]{1,0:T(8,128)(2,1)S(1)}, u32[]{:S(2)}, u32[]{:S(2)}) collective-permute-start(bf16[128,1024]{1,0:T(8,128)(2,1)S(1)} %attend.3), channel_id=1, source_target_pairs={{0,2},{1,3},{2,0},{3,1},{4,6},{5,7},{6,4},{7,5},{8,10},{9,11},{10,... | collective-permute-start | bytes 786440 | tf_op jit(solution)/shard_map/ppermute | solution.py:345
  64.9 1.7 %attend.2.kept = bf16[128,1024]{1,0:T(8,128)(2,1)S(1)} custom-call(bf16[2,1024,256]{2,1,0:T(8,128)(2,1)S(1)} %sort.1.store, bf16[256,512]{1,0:T(8,128)(2,1)S(1)} %get-tuple-element.68.q_ref, bf16[256,512]{1,0:T(8,128)(2,1)S(1)} %collective-permute-done.20.near_ref, bf16[272,256]{1,0:T(8,128)(2,1)S(1)} %get-tuple-element.46.piece.refs_0_.refs_2_.refs_4_, ...), custom_call_target="tpu_custom_call" | custom-call | bytes 1048576 | tf_op jit(solution)/shard_map/attend/pallas_call | solution.py:506
  66.7 0.9 %own.1.own_pages = bf16[4,64,512]{2,1,0:T(8,128)(2,1)S(1)} custom-call(bf16[2,1024,256]{2,1,0:T(8,128)(2,1)S(1)} %sort.1.store, s32[1,2,16]{2,1,0:T(2,128)S(1)} %copy-done.1, s32[1]{0:T(128)S(6)} %copy.13.refs_5_.length_ref), custom_call_target="tpu_custom_call" | custom-call | tf_op jit(solution)/shard_map/own/pallas_call | solution.py:522
  67.6 4.7 %collective-permute-done.21.from_far = bf16[128,1024]{1,0:T(8,128)(2,1)S(1)} collective-permute-done((bf16[128,1024]{1,0:T(8,128)(2,1)S(1)}, bf16[128,1024]{1,0:T(8,128)(2,1)S(1)}, u32[]{:S(2)}, u32[]{:S(2)}) %collective-permute-start.21) | collective-permute-done | bytes 262176 | tf_op jit(solution)/shard_map/ppermute | solution.py:345
  72.2 1.8 %finish.1 = (bf16[128,2048]{1,0:T(8,128)(2,1)}, bf16[4,64,512]{2,1,0:T(8,128)(2,1)}) custom-call(bf16[128,1024]{1,0:T(8,128)(2,1)S(1)} %attend.2.kept, bf16[128,1024]{1,0:T(8,128)(2,1)S(1)} %collective-permute-done.21.from_far, bf16[4,64,512]{2,1,0:T(8,128)(2,1)S(1)} %own.1.own_pages, bf16[8,64,256]{2,1,0:T(8,128)(2,1)S(1)} %collective-permute-done.13.got, ...), custom_call_target="tpu_custom_call" | custom-call | tf_op jit(solution)/shard_map/finish/pallas_call | solution.py:532
  (45 shorter events, 3.5 us)
Async XLA Ops:
  2.9 8.8 %collective-permute-start = (bf16[2448,128]{1,0:T(8,128)(2,1)}, bf16[2448,128]{1,0:T(8,128)(2,1)S(1)}, u32[]{:S(2)}, u32[]{:S(2)}) collective-permute-start(bf16[2448,128]{1,0:T(8,128)(2,1)} %get-tuple-element.39), channel_id=1, source_target_pairs={{0,1},{1,0},{2,3},{3,2},{4,5},{5,4},{6,7},{7,6},{8,9},{9,8},{10,11... | collective-permute-start | bytes 1880072 | tf_op jit(solution)/shard_map/ppermute | solution.py:345
  3.4 6.6 %collective-permute-start.1 = (bf16[400,128]{1,0:T(8,128)(2,1)}, bf16[400,128]{1,0:T(8,128)(2,1)S(1)}, u32[]{:S(2)}, u32[]{:S(2)}) collective-permute-start(bf16[400,128]{1,0:T(8,128)(2,1)} %get-tuple-element.40), channel_id=1, source_target_pairs={{0,2},{1,3},{2,0},{3,1},{4,6},{5,7},{6,4},{7,5},{8,10},{9,11},{10,... | collective-permute-start | bytes 307208 | tf_op jit(solution)/shard_map/ppermute | solution.py:345
  6.1 5.6 %collective-permute-start.2 = (bf16[400,128]{1,0:T(8,128)(2,1)}, bf16[400,128]{1,0:T(8,128)(2,1)S(1)}, u32[]{:S(2)}, u32[]{:S(2)}) collective-permute-start(bf16[400,128]{1,0:T(8,128)(2,1)} %get-tuple-element.41), channel_id=1, source_target_pairs={{0,3},{1,2},{2,1},{3,0},{4,7},{5,6},{6,5},{7,4},{8,11},{9,10},{10,... | collective-permute-start | bytes 307208 | tf_op jit(solution)/shard_map/ppermute | solution.py:345
  6.2 0.9 %copy-start.4 = (bf16[400,128]{1,0:T(8,128)(2,1)S(1)}, bf16[400,128]{1,0:T(8,128)(2,1)}, u32[]{:S(2)}) copy-start(bf16[400,128]{1,0:T(8,128)(2,1)} %get-tuple-element.38.part) | copy-start | bytes 307204
  7.1 10.5 %copy-start = (bf16[1,128,2048]{2,1,0:T(8,128)(2,1)S(1)}, bf16[1,128,2048]{2,1,0:T(8,128)(2,1)}, u32[]{:S(2)}) copy-start(bf16[1,128,2048]{2,1,0:T(8,128)(2,1)} %param.11) | copy-start | bytes 1572868
  11.8 17.1 %copy-start.5 = (f32[64,128]{1,0:T(8,128)S(1)}, f32[64,128]{1,0:T(8,128)}, u32[]{:S(2)}) copy-start(f32[64,128]{1,0:T(8,128)} %constant.10.clone.off_cos) | copy-start | bytes 98308
  11.9 17.1 %copy-start.6 = (f32[64,128]{1,0:T(8,128)S(1)}, f32[64,128]{1,0:T(8,128)}, u32[]{:S(2)}) copy-start(f32[64,128]{1,0:T(8,128)} %constant.11.clone.off_sin) | copy-start | bytes 98308
  11.9 17.1 %copy-start.7 = (f32[16,128]{1,0:T(8,128)S(1)}, f32[16,128]{1,0:T(8,128)}, u32[]{:S(2)}) copy-start(f32[16,128]{1,0:T(8,128)} %constant.8.clone.first_cos) | copy-start | bytes 24580
  11.9 17.1 %copy-start.8 = (f32[16,128]{1,0:T(8,128)S(1)}, f32[16,128]{1,0:T(8,128)}, u32[]{:S(2)}) copy-start(f32[16,128]{1,0:T(8,128)} %constant.9.clone.first_sin) | copy-start | bytes 24580
  11.9 13.5 %collective-permute-start.4 = (bf16[256,768]{1,0:T(8,128)(2,1)S(1)}, bf16[256,768]{1,0:T(8,128)(2,1)S(1)}, u32[]{:S(2)}, u32[]{:S(2)}) collective-permute-start(bf16[256,768]{1,0:T(8,128)(2,1)S(1)} %get-tuple-element.47), channel_id=1, source_target_pairs={{0,8},{8,0},{16,24},{24,16},{1,9},{9,1},{17,25},{25,17},{2,10},{10... | collective-permute-start | bytes 1179656 | tf_op jit(solution)/shard_map/ppermute | solution.py:348
  13.4 11.9 %collective-permute-start.5 = (bf16[256,768]{1,0:T(8,128)(2,1)S(1)}, bf16[256,768]{1,0:T(8,128)(2,1)S(1)}, u32[]{:S(2)}, u32[]{:S(2)}) collective-permute-start(bf16[256,768]{1,0:T(8,128)(2,1)S(1)} %get-tuple-element.47), channel_id=1, source_target_pairs={{0,16},{8,24},{16,0},{24,8},{1,17},{9,25},{17,1},{25,9},{2,18},{10... | collective-permute-start | bytes 1179656 | tf_op jit(solution)/shard_map/ppermute | solution.py:348
  15.0 10.4 %collective-permute-start.3 = (bf16[272,256]{1,0:T(8,128)(2,1)S(1)}, bf16[272,256]{1,0:T(8,128)(2,1)S(1)}, u32[]{:S(2)}, u32[]{:S(2)}) collective-permute-start(bf16[272,256]{1,0:T(8,128)(2,1)S(1)} %get-tuple-element.46.piece.refs_0_.refs_2_.refs_4_), channel_id=1, source_target_pairs={{0,4},{1,5},{2,6},{3,7},{4,0},{5,1},{6,2},{7,3},{8,12},{9,13},{10,... | collective-permute-start | bytes 417800 | tf_op jit(solution)/shard_map/ppermute | solution.py:351
  17.6 20.8 %collective-permute-start.10 = (bf16[128,2048]{1,0:T(8,128)(2,1)S(1)}, bf16[128,2048]{1,0:T(8,128)(2,1)S(1)}, u32[]{:S(2)}, u32[]{:S(2)}) collective-permute-start(bf16[128,2048]{1,0:T(8,128)(2,1)S(1)} %bitcast.6), channel_id=1, source_target_pairs={{0,2},{1,3},{2,0},{3,1},{4,6},{5,7},{6,4},{7,5},{8,10},{9,11},{10,... | collective-permute-start | bytes 1572872 | tf_op jit(solution)/shard_map/ppermute | solution.py:345
  19.1 18.1 %collective-permute-start.9 = (bf16[256,512]{1,0:T(8,128)(2,1)S(1)}, bf16[256,512]{1,0:T(8,128)(2,1)S(1)}, u32[]{:S(2)}, u32[]{:S(2)}) collective-permute-start(bf16[256,512]{1,0:T(8,128)(2,1)S(1)} %get-tuple-element.51.refs_0_), channel_id=1, source_target_pairs={{0,4},{1,5},{2,6},{3,7},{4,0},{5,1},{6,2},{7,3},{8,12},{9,13},{10,... | collective-permute-start | bytes 786440 | tf_op jit(solution)/shard_map/ppermute | solution.py:351
  25.4 12.9 %collective-permute-start.6 = (bf16[272,256]{1,0:T(8,128)(2,1)S(1)}, bf16[272,256]{1,0:T(8,128)(2,1)S(1)}, u32[]{:S(2)}, u32[]{:S(2)}) collective-permute-start(bf16[272,256]{1,0:T(8,128)(2,1)S(1)} %collective-permute-done.3.kv_o.refs_1_.refs_3_.refs_5_), channel_id=1, source_target_pairs={{0,8},{8,0},{16,24},{24,16},{1,9},{9,1},{17,25},{25,17},{2,10},{10... | collective-permute-start | bytes 417800 | tf_op jit(solution)/shard_map/ppermute | solution.py:348
  25.9 12.4 %collective-permute-start.8 = (bf16[272,256]{1,0:T(8,128)(2,1)S(1)}, bf16[272,256]{1,0:T(8,128)(2,1)S(1)}, u32[]{:S(2)}, u32[]{:S(2)}) collective-permute-start(bf16[272,256]{1,0:T(8,128)(2,1)S(1)} %collective-permute-done.3.kv_o.refs_1_.refs_3_.refs_5_), channel_id=1, source_target_pairs={{0,24},{8,16},{16,8},{24,0},{1,25},{9,17},{17,9},{25,1},{2,26},{10... | collective-permute-start | bytes 417800 | tf_op jit(solution)/shard_map/ppermute | solution.py:348
  27.5 10.8 %collective-permute-start.7 = (bf16[528,256]{1,0:T(8,128)(2,1)S(1)}, bf16[528,256]{1,0:T(8,128)(2,1)S(1)}, u32[]{:S(2)}, u32[]{:S(2)}) collective-permute-start(bf16[528,256]{1,0:T(8,128)(2,1)S(1)} %get-tuple-element.50), channel_id=1, source_target_pairs={{0,16},{8,24},{16,0},{24,8},{1,17},{9,25},{17,1},{25,9},{2,18},{10... | collective-permute-start | bytes 811016 | tf_op jit(solution)/shard_map/ppermute | solution.py:348
  38.3 2.0 %copy-start.2 = (f32[256]{0:T(256)S(1)}, f32[256]{0:T(256)}, u32[]{:S(2)}) copy-start(f32[256]{0:T(256)} %param.17) | copy-start | bytes 3076
  38.3 2.0 %collective-permute-start.11 = (bf16[128,2048]{1,0:T(8,128)(2,1)S(1)}, bf16[128,2048]{1,0:T(8,128)(2,1)S(1)}, u32[]{:S(2)}, u32[]{:S(2)}) collective-permute-start(bf16[128,2048]{1,0:T(8,128)(2,1)S(1)} %collective-permute-done.10.far), channel_id=1, source_target_pairs={{0,1},{1,0},{2,3},{3,2},{4,5},{5,4},{6,7},{7,6},{8,9},{9,8},{10,11... | collective-permute-start | bytes 1572872 | tf_op jit(solution)/shard_map/ppermute | solution.py:345
  38.4 8.7 %collective-permute-start.16 = (bf16[256,512]{1,0:T(8,128)(2,1)S(1)}, bf16[256,512]{1,0:T(8,128)(2,1)S(1)}, u32[]{:S(2)}, u32[]{:S(2)}) collective-permute-start(bf16[256,512]{1,0:T(8,128)(2,1)S(1)} %collective-permute-done.9.refs_1_), channel_id=1, source_target_pairs={{0,8},{8,0},{16,24},{24,16},{1,9},{9,1},{17,25},{25,17},{2,10},{10... | collective-permute-start | bytes 786440 | tf_op jit(solution)/shard_map/ppermute | solution.py:348
  39.0 8.4 %collective-permute-start.17 = (bf16[256,512]{1,0:T(8,128)(2,1)S(1)}, bf16[256,512]{1,0:T(8,128)(2,1)S(1)}, u32[]{:S(2)}, u32[]{:S(2)}) collective-permute-start(bf16[256,512]{1,0:T(8,128)(2,1)S(1)} %collective-permute-done.9.refs_1_), channel_id=1, source_target_pairs={{0,16},{8,24},{16,0},{24,8},{1,17},{9,25},{17,1},{25,9},{2,18},{10... | collective-permute-start | bytes 786440 | tf_op jit(solution)/shard_map/ppermute | solution.py:348
  41.2 14.9 %collective-permute-start.12 = (bf16[512,256]{1,0:T(8,128)(2,1)S(1)}, bf16[512,256]{1,0:T(8,128)(2,1)S(1)}, u32[]{:S(2)}, u32[]{:S(2)}) collective-permute-start(bf16[512,256]{1,0:T(8,128)(2,1)S(1)} %project_kv.1.refs_0_), channel_id=1, source_target_pairs={{0,4},{1,5},{2,6},{3,7},{4,0},{5,1},{6,2},{7,3},{8,12},{9,13},{10,... | collective-permute-start | bytes 786440 | tf_op jit(solution)/shard_map/ppermute | solution.py:351
  47.4 9.4 %copy-start.1 = (s32[1,2,16]{2,1,0:T(2,128)S(1)}, s32[1,2,16]{2,1,0:T(2,128)}, u32[]{:S(2)}) copy-start(s32[1,2,16]{2,1,0:T(2,128)} %table.3) | copy-start | bytes 388
  47.4 10.5 %collective-permute-start.18 = (bf16[256,512]{1,0:T(8,128)(2,1)S(1)}, bf16[256,512]{1,0:T(8,128)(2,1)S(1)}, u32[]{:S(2)}, u32[]{:S(2)}) collective-permute-start(bf16[256,512]{1,0:T(8,128)(2,1)S(1)} %collective-permute-done.17.refs_5_), channel_id=1, source_target_pairs={{0,8},{8,0},{16,24},{24,16},{1,9},{9,1},{17,25},{25,17},{2,10},{10... | collective-permute-start | bytes 786440 | tf_op jit(solution)/shard_map/ppermute | solution.py:348
  48.9 9.0 %collective-permute-start.19 = (bf16[256,512]{1,0:T(8,128)(2,1)S(1)}, bf16[256,512]{1,0:T(8,128)(2,1)S(1)}, u32[]{:S(2)}, u32[]{:S(2)}) collective-permute-start(bf16[256,512]{1,0:T(8,128)(2,1)S(1)} %get-tuple-element.65), channel_id=1, source_target_pairs={{0,16},{8,24},{16,0},{24,8},{1,17},{9,25},{17,1},{25,9},{2,18},{10... | collective-permute-start | bytes 786440 | tf_op jit(solution)/shard_map/ppermute | solution.py:348
  49.4 11.2 %collective-permute-start.14 = (bf16[512,256]{1,0:T(8,128)(2,1)S(1)}, bf16[512,256]{1,0:T(8,128)(2,1)S(1)}, u32[]{:S(2)}, u32[]{:S(2)}) collective-permute-start(bf16[512,256]{1,0:T(8,128)(2,1)S(1)} %project_kv.1.refs_0_), channel_id=1, source_target_pairs={{0,1},{1,0},{2,3},{3,2},{4,5},{5,4},{6,7},{7,6},{8,9},{9,8},{10,11... | collective-permute-start | bytes 786440 | tf_op jit(solution)/shard_map/ppermute | solution.py:345
  56.1 4.5 %collective-permute-start.15 = (bf16[512,256]{1,0:T(8,128)(2,1)S(1)}, bf16[512,256]{1,0:T(8,128)(2,1)S(1)}, u32[]{:S(2)}, u32[]{:S(2)}) collective-permute-start(bf16[512,256]{1,0:T(8,128)(2,1)S(1)} %collective-permute-done.12.refs_1_), channel_id=1, source_target_pairs={{0,1},{1,0},{2,3},{3,2},{4,5},{5,4},{6,7},{7,6},{8,9},{9,8},{10,11... | collective-permute-start | bytes 786440 | tf_op jit(solution)/shard_map/ppermute | solution.py:345
  57.8 0.7 copy-start.3
  57.8 8.8 %collective-permute-start.13 = (bf16[8,64,256]{2,1,0:T(8,128)(2,1)S(1)}, bf16[8,64,256]{2,1,0:T(8,128)(2,1)S(1)}, u32[]{:S(2)}, u32[]{:S(2)}) collective-permute-start(bf16[8,64,256]{2,1,0:T(8,128)(2,1)S(1)} %away.1), channel_id=1, source_target_pairs={{0,2},{1,3},{2,0},{3,1},{4,6},{5,7},{6,4},{7,5},{8,10},{9,11},{10,... | collective-permute-start | bytes 786440 | tf_op jit(solution)/shard_map/ppermute | solution.py:345
  60.1 1.7 %collective-permute-start.20 = (bf16[256,512]{1,0:T(8,128)(2,1)S(1)}, bf16[256,512]{1,0:T(8,128)(2,1)S(1)}, u32[]{:S(2)}, u32[]{:S(2)}) collective-permute-start(bf16[256,512]{1,0:T(8,128)(2,1)S(1)} %get-tuple-element.69), channel_id=1, source_target_pairs={{0,1},{1,0},{2,3},{3,2},{4,5},{5,4},{6,7},{7,6},{8,9},{9,8},{10,11... | collective-permute-start | bytes 786440 | tf_op jit(solution)/shard_map/ppermute | solution.py:345
  63.5 8.7 %collective-permute-start.21 = (bf16[128,1024]{1,0:T(8,128)(2,1)S(1)}, bf16[128,1024]{1,0:T(8,128)(2,1)S(1)}, u32[]{:S(2)}, u32[]{:S(2)}) collective-permute-start(bf16[128,1024]{1,0:T(8,128)(2,1)S(1)} %attend.3), channel_id=1, source_target_pairs={{0,2},{1,3},{2,0},{3,1},{4,6},{5,7},{6,4},{7,5},{8,10},{9,11},{10,... | collective-permute-start | bytes 786440 | tf_op jit(solution)/shard_map/ppermute | solution.py:345
  66.6 5.6 %collective-permute-start.22 = (bf16[8,64,256]{2,1,0:T(8,128)(2,1)S(1)}, bf16[8,64,256]{2,1,0:T(8,128)(2,1)S(1)}, u32[]{:S(2)}, u32[]{:S(2)}) collective-permute-start(bf16[8,64,256]{2,1,0:T(8,128)(2,1)S(1)} %collective-permute-done.13.got), channel_id=1, source_target_pairs={{0,1},{1,0},{2,3},{3,2},{4,5},{5,4},{6,7},{7,6},{8,9},{9,8},{10,11... | collective-permute-start | bytes 786440 | tf_op jit(solution)/shard_map/ppermute | solution.py:345

commit v16 on v15

--- a/solution.py
+++ b/solution.py
@@ -457,14 +457,14 @@
                 pltpu.SemaphoreType.DMA((n_req * n_out,)),
             ],
             cost_estimate=pl.CostEstimate(
-                flops=(0 if is_kv else 0), bytes_accessed=MIB, transcendentals=0
+                flops=(0 if is_kv else 4 * 10**9), bytes_accessed=MIB, transcendentals=0
             ),
             compiler_params=params(4 if w_rows * TEAM % LANES == 0 else 12),
             name="project_kv" if is_kv else "project_q",
         )(own, got[1], far, far_near, *weight, gain[None, :], cosine, sine)
 
     (made,) = project(kv_weight, True, k_gain)
-    q_ox, q_oy, q_x = sync(q_ox, q_oy, q_x)
+    q_ox, q_oy, q_x, _ = sync(q_ox, q_oy, q_x, made)
     q_od, q_d = in_req(q_oy, 1), in_req(q_x, 2)
     q_weight = [(q, 0, 0), (q_o, 0, 0), (w_x, 0, HD), (q_ox, 0, 0)]
     q_weight += [(w_y, 0, HD), (q_oy, 0, 0), (q_d, 0, 0), (q_od, 0, 0)]

time: 74.2 us -> 73.2 us (0.987)
  waiting for transfers between devices: 36.8 us -> 35.8 us
where the time goes in v16:
time: 73.2 us; the launch traced here: 73 us
  waiting for transfers between devices  35.8 us (49%)
  starting transfers between devices  21.9 us (30%)
  Pallas kernels  12.3 us (17%)
  between operations  1.52 us (2%)
  local copies, waits for them, and re-layouts  1.43 us (2%)
    ppermute x3, waiting for transfers between devices, across(): lax.ppermute(array, 'blk', [(i, (i + TEAM * k) % n_blk) for i in range(n_...  20 us
    ppermute x11, waiting for transfers between devices, in_team(): return lax.ppermute(array, 'blk', [(i, i ^ k) for i in range(n_blk)])  12 us
    ppermute x9, starting transfers between devices, in_req(): return lax.ppermute(array, 'req', [(i, i ^ k) for i in range(n_req)])  9.68 us
    ppermute x11, starting transfers between devices, in_team(): return lax.ppermute(array, 'blk', [(i, i ^ k) for i in range(n_blk)])  6.97 us
    ppermute x3, starting transfers between devices, across(): lax.ppermute(array, 'blk', [(i, (i + TEAM * k) % n_blk) for i in range(n_...  5.29 us
    ppermute x9, waiting for transfers between devices, in_req(): return lax.ppermute(array, 'req', [(i, i ^ k) for i in range(n_req)])  3.82 us
    pallas_call x2, Pallas kernels, attend(): pl.pallas_call(functools.partial(attend_kernel, blk_rows, step), out_shap...  3.42 us
    pallas_call x2, Pallas kernels, project(): pl.pallas_call(functools.partial(project_kernel, n_out, TEAM * w_rows, st...  2.48 us
  transfers between devices with their start and end apart: 23, of which 11 were waited for; matrix products, arithmetic and copies ran while one was open for 0% of the time, Pallas kernels for 11%

profile of v16, /device:TPU:0, one launch (start us, length us, event | category | flops | bytes accessed | tf_op | source)
XLA Modules:
  0.0 73.0 jit_solution(8898385070566292139)
XLA Ops:
  0.6 2.3 %pack.1 = (bf16[400,128]{1,0:T(8,128)(2,1)}, bf16[2448,128]{1,0:T(8,128)(2,1)}, bf16[400,128]{1,0:T(8,128)(2,1)}, bf16[400,128]{1,0:T(8,128)(2,1)}) custom-call(bf16[64,3072]{1,0:T(8,128)(2,1)} %w_hbm.1, s32[1,2]{1,0:T(1,128)} %ids_hbm.1, bf16[128,2048]{1,0:T(8,128)(2,1)} %bitcast.5), custom_call_target="tpu_custom_call" | custom-call | tf_op jit(solution)/shard_map/pack/pallas_call | solution.py:361
  2.9 0.5 collective-permute-start
  3.4 2.7 %collective-permute-start.1 = (bf16[400,128]{1,0:T(8,128)(2,1)}, bf16[400,128]{1,0:T(8,128)(2,1)S(1)}, u32[]{:S(2)}, u32[]{:S(2)}) collective-permute-start(bf16[400,128]{1,0:T(8,128)(2,1)} %get-tuple-element.40), channel_id=1, source_target_pairs={{0,2},{1,3},{2,0},{3,1},{4,6},{5,7},{6,4},{7,5},{8,10},{9,11},{10,... | collective-permute-start | bytes 307208 | tf_op jit(solution)/shard_map/ppermute | solution.py:345
  6.2 0.9 %copy-done.3 = bf16[400,128]{1,0:T(8,128)(2,1)S(1)} copy-done((bf16[400,128]{1,0:T(8,128)(2,1)S(1)}, bf16[400,128]{1,0:T(8,128)(2,1)}, u32[]{:S(2)}) %copy-start.3) | copy-done | bytes 102424
  7.1 3.0 %collective-permute-done.1.refs_2_ = bf16[400,128]{1,0:T(8,128)(2,1)S(1)} collective-permute-done((bf16[400,128]{1,0:T(8,128)(2,1)}, bf16[400,128]{1,0:T(8,128)(2,1)S(1)}, u32[]{:S(2)}, u32[]{:S(2)}) %collective-permute-start.1) | collective-permute-done | bytes 102432 | tf_op jit(solution)/shard_map/ppermute | solution.py:345
  10.0 1.7 %collective-permute-done.2.refs_3_ = bf16[400,128]{1,0:T(8,128)(2,1)S(1)} collective-permute-done((bf16[400,128]{1,0:T(8,128)(2,1)}, bf16[400,128]{1,0:T(8,128)(2,1)S(1)}, u32[]{:S(2)}, u32[]{:S(2)}) %collective-permute-start.2) | collective-permute-done | bytes 102432 | tf_op jit(solution)/shard_map/ppermute | solution.py:345
  11.9 1.5 %collective-permute-start.4 = (bf16[256,768]{1,0:T(8,128)(2,1)S(1)}, bf16[256,768]{1,0:T(8,128)(2,1)S(1)}, u32[]{:S(2)}, u32[]{:S(2)}) collective-permute-start(bf16[256,768]{1,0:T(8,128)(2,1)S(1)} %get-tuple-element.47), channel_id=1, source_target_pairs={{0,8},{8,0},{16,24},{24,16},{1,9},{9,1},{17,25},{25,17},{2,10},{10... | collective-permute-start | bytes 1179656 | tf_op jit(solution)/shard_map/ppermute | solution.py:348
  13.4 1.5 %collective-permute-start.5 = (bf16[256,768]{1,0:T(8,128)(2,1)S(1)}, bf16[256,768]{1,0:T(8,128)(2,1)S(1)}, u32[]{:S(2)}, u32[]{:S(2)}) collective-permute-start(bf16[256,768]{1,0:T(8,128)(2,1)S(1)} %get-tuple-element.47), channel_id=1, source_target_pairs={{0,16},{8,24},{16,0},{24,8},{1,17},{9,25},{17,1},{25,9},{2,18},{10... | collective-permute-start | bytes 1179656 | tf_op jit(solution)/shard_map/ppermute | solution.py:348
  15.0 2.6 %collective-permute-start.3 = (bf16[272,256]{1,0:T(8,128)(2,1)S(1)}, bf16[272,256]{1,0:T(8,128)(2,1)S(1)}, u32[]{:S(2)}, u32[]{:S(2)}) collective-permute-start(bf16[272,256]{1,0:T(8,128)(2,1)S(1)} %get-tuple-element.46.piece.refs_0_.refs_2_.refs_4_), channel_id=1, source_target_pairs={{0,4},{1,5},{2,6},{3,7},{4,0},{5,1},{6,2},{7,3},{8,12},{9,13},{10,... | collective-permute-start | bytes 417800 | tf_op jit(solution)/shard_map/ppermute | solution.py:351
  17.6 1.6 %collective-permute-start.10 = (bf16[128,2048]{1,0:T(8,128)(2,1)S(1)}, bf16[128,2048]{1,0:T(8,128)(2,1)S(1)}, u32[]{:S(2)}, u32[]{:S(2)}) collective-permute-start(bf16[128,2048]{1,0:T(8,128)(2,1)S(1)} %bitcast.6), channel_id=1, source_target_pairs={{0,2},{1,3},{2,0},{3,1},{4,6},{5,7},{6,4},{7,5},{8,10},{9,11},{10,... | collective-permute-start | bytes 1572872 | tf_op jit(solution)/shard_map/ppermute | solution.py:345
  19.5 5.9 %collective-permute-done.3.kv_o.refs_1_.refs_3_.refs_5_ = bf16[272,256]{1,0:T(8,128)(2,1)S(1)} collective-permute-done((bf16[272,256]{1,0:T(8,128)(2,1)S(1)}, bf16[272,256]{1,0:T(8,128)(2,1)S(1)}, u32[]{:S(2)}, u32[]{:S(2)}) %collective-permute-start.3) | collective-permute-done | bytes 139296 | tf_op jit(solution)/shard_map/ppermute | solution.py:351
  25.4 0.5 collective-permute-start.6
  25.9 1.5 %collective-permute-start.8 = (bf16[272,256]{1,0:T(8,128)(2,1)S(1)}, bf16[272,256]{1,0:T(8,128)(2,1)S(1)}, u32[]{:S(2)}, u32[]{:S(2)}) collective-permute-start(bf16[272,256]{1,0:T(8,128)(2,1)S(1)} %collective-permute-done.3.kv_o.refs_1_.refs_3_.refs_5_), channel_id=1, source_target_pairs={{0,24},{8,16},{16,8},{24,0},{1,25},{9,17},{17,9},{25,1},{2,26},{10... | collective-permute-start | bytes 417800 | tf_op jit(solution)/shard_map/ppermute | solution.py:348
  27.5 1.5 %collective-permute-start.7 = (bf16[528,256]{1,0:T(8,128)(2,1)S(1)}, bf16[528,256]{1,0:T(8,128)(2,1)S(1)}, u32[]{:S(2)}, u32[]{:S(2)}) collective-permute-start(bf16[528,256]{1,0:T(8,128)(2,1)S(1)} %get-tuple-element.50), channel_id=1, source_target_pairs={{0,16},{8,24},{16,0},{24,8},{1,17},{9,25},{17,1},{25,9},{2,18},{10... | collective-permute-start | bytes 811016 | tf_op jit(solution)/shard_map/ppermute | solution.py:348
  29.2 8.1 %collective-permute-done.9.refs_1_ = bf16[256,512]{1,0:T(8,128)(2,1)S(1)} collective-permute-done((bf16[256,512]{1,0:T(8,128)(2,1)S(1)}, bf16[256,512]{1,0:T(8,128)(2,1)S(1)}, u32[]{:S(2)}, u32[]{:S(2)}) %collective-permute-start.9) | collective-permute-done | bytes 262176 | tf_op jit(solution)/shard_map/ppermute | solution.py:351
  37.2 1.1 %collective-permute-done.10.far = bf16[128,2048]{1,0:T(8,128)(2,1)S(1)} collective-permute-done((bf16[128,2048]{1,0:T(8,128)(2,1)S(1)}, bf16[128,2048]{1,0:T(8,128)(2,1)S(1)}, u32[]{:S(2)}, u32[]{:S(2)}) %collective-permute-start.10) | collective-permute-done | bytes 524320 | tf_op jit(solution)/shard_map/ppermute | solution.py:345
  38.4 0.6 collective-permute-start.16
  39.5 0.8 %collective-permute-done.11.far_near = bf16[128,2048]{1,0:T(8,128)(2,1)S(1)} collective-permute-done((bf16[128,2048]{1,0:T(8,128)(2,1)S(1)}, bf16[128,2048]{1,0:T(8,128)(2,1)S(1)}, u32[]{:S(2)}, u32[]{:S(2)}) %collective-permute-start.11) | collective-permute-done | bytes 524320 | tf_op jit(solution)/shard_map/ppermute | solution.py:345
  40.3 0.9 %project_kv.1.refs_0_ = bf16[512,256]{1,0:T(8,128)(2,1)S(1)} custom-call(bf16[128,2048]{1,0:T(8,128)(2,1)S(1)} %bitcast.7, bf16[2448,128]{1,0:T(8,128)(2,1)S(1)} %collective-permute-done.refs_1_.near, bf16[128,2048]{1,0:T(8,128)(2,1)S(1)} %collective-permute-done.10.far, bf16[128,2048]{1,0:T(8,128)(2,1)S(1)} %collective-permute-done.11.far_near, ...), custom_call_target="tpu_custom_call" | custom-call | bytes 1048576 | tf_op jit(solution)/shard_map/project_kv/pallas_call | solution.py:450
  41.2 2.4 %collective-permute-start.12 = (bf16[512,256]{1,0:T(8,128)(2,1)S(1)}, bf16[512,256]{1,0:T(8,128)(2,1)S(1)}, u32[]{:S(2)}, u32[]{:S(2)}) collective-permute-start(bf16[512,256]{1,0:T(8,128)(2,1)S(1)} %project_kv.1.refs_0_), channel_id=1, source_target_pairs={{0,4},{1,5},{2,6},{3,7},{4,0},{5,1},{6,2},{7,3},{8,12},{9,13},{10,... | collective-permute-start | bytes 786440 | tf_op jit(solution)/shard_map/ppermute | solution.py:351
  43.6 3.5 %collective-permute-done.16.refs_3_ = bf16[256,512]{1,0:T(8,128)(2,1)S(1)} collective-permute-done((bf16[256,512]{1,0:T(8,128)(2,1)S(1)}, bf16[256,512]{1,0:T(8,128)(2,1)S(1)}, u32[]{:S(2)}, u32[]{:S(2)}) %collective-permute-start.16) | collective-permute-done | bytes 262176 | tf_op jit(solution)/shard_map/ppermute | solution.py:348
  47.4 1.5 %collective-permute-start.18 = (bf16[256,512]{1,0:T(8,128)(2,1)S(1)}, bf16[256,512]{1,0:T(8,128)(2,1)S(1)}, u32[]{:S(2)}, u32[]{:S(2)}) collective-permute-start(bf16[256,512]{1,0:T(8,128)(2,1)S(1)} %collective-permute-done.17.refs_5_), channel_id=1, source_target_pairs={{0,8},{8,0},{16,24},{24,16},{1,9},{9,1},{17,25},{25,17},{2,10},{10... | collective-permute-start | bytes 786440 | tf_op jit(solution)/shard_map/ppermute | solution.py:348
  50.1 6.0 %collective-permute-done.12.refs_1_ = bf16[512,256]{1,0:T(8,128)(2,1)S(1)} collective-permute-done((bf16[512,256]{1,0:T(8,128)(2,1)S(1)}, bf16[512,256]{1,0:T(8,128)(2,1)S(1)}, u32[]{:S(2)}, u32[]{:S(2)}) %collective-permute-start.12) | collective-permute-done | bytes 262176 | tf_op jit(solution)/shard_map/ppermute | solution.py:351
  56.1 1.0 %away.1 = bf16[8,64,256]{2,1,0:T(8,128)(2,1)S(1)} custom-call(bf16[512,256]{1,0:T(8,128)(2,1)S(1)} %project_kv.1.refs_0_, bf16[512,256]{1,0:T(8,128)(2,1)S(1)} %collective-permute-done.12.refs_1_, bf16[272,256]{1,0:T(8,128)(2,1)S(1)} %get-tuple-element.46.piece.refs_0_.refs_2_.refs_4_, ...), custom_call_target="tpu_custom_call" | custom-call | bytes 1048576 | tf_op jit(solution)/shard_map/away/pallas_call | solution.py:478
  57.8 1.6 %project_q.1 = (bf16[256,512]{1,0:T(8,128)(2,1)S(1)}, bf16[256,512]{1,0:T(8,128)(2,1)S(1)}) custom-call(bf16[128,2048]{1,0:T(8,128)(2,1)S(1)} %bitcast.8, bf16[2448,128]{1,0:T(8,128)(2,1)S(1)} %collective-permute-done.refs_1_.near, bf16[128,2048]{1,0:T(8,128)(2,1)S(1)} %collective-permute-done.10.far, ...), custom_call_target="tpu_custom_call" | custom-call | flops 4000000000 | bytes 1048576 | tf_op jit(solution)/shard_map/project_q/pallas_call | solution.py:450
  59.7 1.3 %collective-permute-done.20.near_ref = bf16[256,512]{1,0:T(8,128)(2,1)S(1)} collective-permute-done((bf16[256,512]{1,0:T(8,128)(2,1)S(1)}, bf16[256,512]{1,0:T(8,128)(2,1)S(1)}, u32[]{:S(2)}, u32[]{:S(2)}) %collective-permute-start.20) | collective-permute-done | bytes 262176 | tf_op jit(solution)/shard_map/ppermute | solution.py:345
  61.0 1.7 %attend.3 = bf16[128,1024]{1,0:T(8,128)(2,1)S(1)} custom-call(bf16[2,1024,256]{2,1,0:T(8,128)(2,1)S(1)} %sort.1.store, bf16[256,512]{1,0:T(8,128)(2,1)S(1)} %get-tuple-element.68.q_ref, bf16[256,512]{1,0:T(8,128)(2,1)S(1)} %collective-permute-done.20.near_ref, bf16[272,256]{1,0:T(8,128)(2,1)S(1)} %get-tuple-element.46.piece.refs_0_.refs_2_.refs_4_, ...), custom_call_target="tpu_custom_call" | custom-call | bytes 1048576 | tf_op jit(solution)/shard_map/attend/pallas_call | solution.py:506
  62.7 1.7 %collective-permute-start.21 = (bf16[128,1024]{1,0:T(8,128)(2,1)S(1)}, bf16[128,1024]{1,0:T(8,128)(2,1)S(1)}, u32[]{:S(2)}, u32[]{:S(2)}) collective-permute-start(bf16[128,1024]{1,0:T(8,128)(2,1)S(1)} %attend.3), channel_id=1, source_target_pairs={{0,2},{1,3},{2,0},{3,1},{4,6},{5,7},{6,4},{7,5},{8,10},{9,11},{10,... | collective-permute-start | bytes 786440 | tf_op jit(solution)/shard_map/ppermute | solution.py:345
  64.4 1.7 %attend.2.kept = bf16[128,1024]{1,0:T(8,128)(2,1)S(1)} custom-call(bf16[2,1024,256]{2,1,0:T(8,128)(2,1)S(1)} %sort.1.store, bf16[256,512]{1,0:T(8,128)(2,1)S(1)} %get-tuple-element.68.q_ref, bf16[256,512]{1,0:T(8,128)(2,1)S(1)} %collective-permute-done.20.near_ref, bf16[272,256]{1,0:T(8,128)(2,1)S(1)} %get-tuple-element.46.piece.refs_0_.refs_2_.refs_4_, ...), custom_call_target="tpu_custom_call" | custom-call | bytes 1048576 | tf_op jit(solution)/shard_map/attend/pallas_call | solution.py:506
  66.2 0.8 %own.1.own_pages = bf16[4,64,512]{2,1,0:T(8,128)(2,1)S(1)} custom-call(bf16[2,1024,256]{2,1,0:T(8,128)(2,1)S(1)} %sort.1.store, s32[1,2,16]{2,1,0:T(2,128)S(1)} %copy-done.1, s32[1]{0:T(128)S(6)} %copy.13.refs_5_.length_ref), custom_call_target="tpu_custom_call" | custom-call | tf_op jit(solution)/shard_map/own/pallas_call | solution.py:522
  67.1 4.1 %collective-permute-done.21.from_far = bf16[128,1024]{1,0:T(8,128)(2,1)S(1)} collective-permute-done((bf16[128,1024]{1,0:T(8,128)(2,1)S(1)}, bf16[128,1024]{1,0:T(8,128)(2,1)S(1)}, u32[]{:S(2)}, u32[]{:S(2)}) %collective-permute-start.21) | collective-permute-done | bytes 262176 | tf_op jit(solution)/shard_map/ppermute | solution.py:345
  71.2 1.8 %finish.1 = (bf16[128,2048]{1,0:T(8,128)(2,1)}, bf16[4,64,512]{2,1,0:T(8,128)(2,1)}) custom-call(bf16[128,1024]{1,0:T(8,128)(2,1)S(1)} %attend.2.kept, bf16[128,1024]{1,0:T(8,128)(2,1)S(1)} %collective-permute-done.21.from_far, bf16[4,64,512]{2,1,0:T(8,128)(2,1)S(1)} %own.1.own_pages, bf16[8,64,256]{2,1,0:T(8,128)(2,1)S(1)} %collective-permute-done.13.got, ...), custom_call_target="tpu_custom_call" | custom-call | tf_op jit(solution)/shard_map/finish/pallas_call | solution.py:532
  (45 shorter events, 3.2 us)
Async XLA Ops:
  2.9 8.8 %collective-permute-start = (bf16[2448,128]{1,0:T(8,128)(2,1)}, bf16[2448,128]{1,0:T(8,128)(2,1)S(1)}, u32[]{:S(2)}, u32[]{:S(2)}) collective-permute-start(bf16[2448,128]{1,0:T(8,128)(2,1)} %get-tuple-element.39), channel_id=1, source_target_pairs={{0,1},{1,0},{2,3},{3,2},{4,5},{5,4},{6,7},{7,6},{8,9},{9,8},{10,11... | collective-permute-start | bytes 1880072 | tf_op jit(solution)/shard_map/ppermute | solution.py:345
  3.4 6.6 %collective-permute-start.1 = (bf16[400,128]{1,0:T(8,128)(2,1)}, bf16[400,128]{1,0:T(8,128)(2,1)S(1)}, u32[]{:S(2)}, u32[]{:S(2)}) collective-permute-start(bf16[400,128]{1,0:T(8,128)(2,1)} %get-tuple-element.40), channel_id=1, source_target_pairs={{0,2},{1,3},{2,0},{3,1},{4,6},{5,7},{6,4},{7,5},{8,10},{9,11},{10,... | collective-permute-start | bytes 307208 | tf_op jit(solution)/shard_map/ppermute | solution.py:345
  6.1 5.6 %collective-permute-start.2 = (bf16[400,128]{1,0:T(8,128)(2,1)}, bf16[400,128]{1,0:T(8,128)(2,1)S(1)}, u32[]{:S(2)}, u32[]{:S(2)}) collective-permute-start(bf16[400,128]{1,0:T(8,128)(2,1)} %get-tuple-element.41), channel_id=1, source_target_pairs={{0,3},{1,2},{2,1},{3,0},{4,7},{5,6},{6,5},{7,4},{8,11},{9,10},{10,... | collective-permute-start | bytes 307208 | tf_op jit(solution)/shard_map/ppermute | solution.py:345
  6.2 0.9 %copy-start.3 = (bf16[400,128]{1,0:T(8,128)(2,1)S(1)}, bf16[400,128]{1,0:T(8,128)(2,1)}, u32[]{:S(2)}) copy-start(bf16[400,128]{1,0:T(8,128)(2,1)} %get-tuple-element.38.part) | copy-start | bytes 307204
  7.1 10.5 %copy-start = (bf16[1,128,2048]{2,1,0:T(8,128)(2,1)S(1)}, bf16[1,128,2048]{2,1,0:T(8,128)(2,1)}, u32[]{:S(2)}) copy-start(bf16[1,128,2048]{2,1,0:T(8,128)(2,1)} %param.11) | copy-start | bytes 1572868
  11.8 17.1 %copy-start.5 = (f32[64,128]{1,0:T(8,128)S(1)}, f32[64,128]{1,0:T(8,128)}, u32[]{:S(2)}) copy-start(f32[64,128]{1,0:T(8,128)} %constant.10.clone.off_cos) | copy-start | bytes 98308
  11.9 17.1 %copy-start.6 = (f32[64,128]{1,0:T(8,128)S(1)}, f32[64,128]{1,0:T(8,128)}, u32[]{:S(2)}) copy-start(f32[64,128]{1,0:T(8,128)} %constant.11.clone.off_sin) | copy-start | bytes 98308
  11.9 17.1 %copy-start.7 = (f32[16,128]{1,0:T(8,128)S(1)}, f32[16,128]{1,0:T(8,128)}, u32[]{:S(2)}) copy-start(f32[16,128]{1,0:T(8,128)} %constant.8.clone.first_cos) | copy-start | bytes 24580
  11.9 17.1 %copy-start.8 = (f32[16,128]{1,0:T(8,128)S(1)}, f32[16,128]{1,0:T(8,128)}, u32[]{:S(2)}) copy-start(f32[16,128]{1,0:T(8,128)} %constant.9.clone.first_sin) | copy-start | bytes 24580
  11.9 13.5 %collective-permute-start.4 = (bf16[256,768]{1,0:T(8,128)(2,1)S(1)}, bf16[256,768]{1,0:T(8,128)(2,1)S(1)}, u32[]{:S(2)}, u32[]{:S(2)}) collective-permute-start(bf16[256,768]{1,0:T(8,128)(2,1)S(1)} %get-tuple-element.47), channel_id=1, source_target_pairs={{0,8},{8,0},{16,24},{24,16},{1,9},{9,1},{17,25},{25,17},{2,10},{10... | collective-permute-start | bytes 1179656 | tf_op jit(solution)/shard_map/ppermute | solution.py:348
  13.4 11.9 %collective-permute-start.5 = (bf16[256,768]{1,0:T(8,128)(2,1)S(1)}, bf16[256,768]{1,0:T(8,128)(2,1)S(1)}, u32[]{:S(2)}, u32[]{:S(2)}) collective-permute-start(bf16[256,768]{1,0:T(8,128)(2,1)S(1)} %get-tuple-element.47), channel_id=1, source_target_pairs={{0,16},{8,24},{16,0},{24,8},{1,17},{9,25},{17,1},{25,9},{2,18},{10... | collective-permute-start | bytes 1179656 | tf_op jit(solution)/shard_map/ppermute | solution.py:348
  15.0 10.4 %collective-permute-start.3 = (bf16[272,256]{1,0:T(8,128)(2,1)S(1)}, bf16[272,256]{1,0:T(8,128)(2,1)S(1)}, u32[]{:S(2)}, u32[]{:S(2)}) collective-permute-start(bf16[272,256]{1,0:T(8,128)(2,1)S(1)} %get-tuple-element.46.piece.refs_0_.refs_2_.refs_4_), channel_id=1, source_target_pairs={{0,4},{1,5},{2,6},{3,7},{4,0},{5,1},{6,2},{7,3},{8,12},{9,13},{10,... | collective-permute-start | bytes 417800 | tf_op jit(solution)/shard_map/ppermute | solution.py:351
  17.6 20.8 %collective-permute-start.10 = (bf16[128,2048]{1,0:T(8,128)(2,1)S(1)}, bf16[128,2048]{1,0:T(8,128)(2,1)S(1)}, u32[]{:S(2)}, u32[]{:S(2)}) collective-permute-start(bf16[128,2048]{1,0:T(8,128)(2,1)S(1)} %bitcast.6), channel_id=1, source_target_pairs={{0,2},{1,3},{2,0},{3,1},{4,6},{5,7},{6,4},{7,5},{8,10},{9,11},{10,... | collective-permute-start | bytes 1572872 | tf_op jit(solution)/shard_map/ppermute | solution.py:345
  19.1 18.1 %collective-permute-start.9 = (bf16[256,512]{1,0:T(8,128)(2,1)S(1)}, bf16[256,512]{1,0:T(8,128)(2,1)S(1)}, u32[]{:S(2)}, u32[]{:S(2)}) collective-permute-start(bf16[256,512]{1,0:T(8,128)(2,1)S(1)} %get-tuple-element.51.refs_0_), channel_id=1, source_target_pairs={{0,4},{1,5},{2,6},{3,7},{4,0},{5,1},{6,2},{7,3},{8,12},{9,13},{10,... | collective-permute-start | bytes 786440 | tf_op jit(solution)/shard_map/ppermute | solution.py:351
  25.4 12.9 %collective-permute-start.6 = (bf16[272,256]{1,0:T(8,128)(2,1)S(1)}, bf16[272,256]{1,0:T(8,128)(2,1)S(1)}, u32[]{:S(2)}, u32[]{:S(2)}) collective-permute-start(bf16[272,256]{1,0:T(8,128)(2,1)S(1)} %collective-permute-done.3.kv_o.refs_1_.refs_3_.refs_5_), channel_id=1, source_target_pairs={{0,8},{8,0},{16,24},{24,16},{1,9},{9,1},{17,25},{25,17},{2,10},{10... | collective-permute-start | bytes 417800 | tf_op jit(solution)/shard_map/ppermute | solution.py:348
  25.9 12.4 %collective-permute-start.8 = (bf16[272,256]{1,0:T(8,128)(2,1)S(1)}, bf16[272,256]{1,0:T(8,128)(2,1)S(1)}, u32[]{:S(2)}, u32[]{:S(2)}) collective-permute-start(bf16[272,256]{1,0:T(8,128)(2,1)S(1)} %collective-permute-done.3.kv_o.refs_1_.refs_3_.refs_5_), channel_id=1, source_target_pairs={{0,24},{8,16},{16,8},{24,0},{1,25},{9,17},{17,9},{25,1},{2,26},{10... | collective-permute-start | bytes 417800 | tf_op jit(solution)/shard_map/ppermute | solution.py:348
  27.5 10.8 %collective-permute-start.7 = (bf16[528,256]{1,0:T(8,128)(2,1)S(1)}, bf16[528,256]{1,0:T(8,128)(2,1)S(1)}, u32[]{:S(2)}, u32[]{:S(2)}) collective-permute-start(bf16[528,256]{1,0:T(8,128)(2,1)S(1)} %get-tuple-element.50), channel_id=1, source_target_pairs={{0,16},{8,24},{16,0},{24,8},{1,17},{9,25},{17,1},{25,9},{2,18},{10... | collective-permute-start | bytes 811016 | tf_op jit(solution)/shard_map/ppermute | solution.py:348
  38.3 2.0 %copy-start.2 = (f32[256]{0:T(256)S(1)}, f32[256]{0:T(256)}, u32[]{:S(2)}) copy-start(f32[256]{0:T(256)} %param.17) | copy-start | bytes 3076
  38.3 2.0 %collective-permute-start.11 = (bf16[128,2048]{1,0:T(8,128)(2,1)S(1)}, bf16[128,2048]{1,0:T(8,128)(2,1)S(1)}, u32[]{:S(2)}, u32[]{:S(2)}) collective-permute-start(bf16[128,2048]{1,0:T(8,128)(2,1)S(1)} %collective-permute-done.10.far), channel_id=1, source_target_pairs={{0,1},{1,0},{2,3},{3,2},{4,5},{5,4},{6,7},{7,6},{8,9},{9,8},{10,11... | collective-permute-start | bytes 1572872 | tf_op jit(solution)/shard_map/ppermute | solution.py:345
  38.4 8.7 %collective-permute-start.16 = (bf16[256,512]{1,0:T(8,128)(2,1)S(1)}, bf16[256,512]{1,0:T(8,128)(2,1)S(1)}, u32[]{:S(2)}, u32[]{:S(2)}) collective-permute-start(bf16[256,512]{1,0:T(8,128)(2,1)S(1)} %collective-permute-done.9.refs_1_), channel_id=1, source_target_pairs={{0,8},{8,0},{16,24},{24,16},{1,9},{9,1},{17,25},{25,17},{2,10},{10... | collective-permute-start | bytes 786440 | tf_op jit(solution)/shard_map/ppermute | solution.py:348
  39.0 8.4 %collective-permute-start.17 = (bf16[256,512]{1,0:T(8,128)(2,1)S(1)}, bf16[256,512]{1,0:T(8,128)(2,1)S(1)}, u32[]{:S(2)}, u32[]{:S(2)}) collective-permute-start(bf16[256,512]{1,0:T(8,128)(2,1)S(1)} %collective-permute-done.9.refs_1_), channel_id=1, source_target_pairs={{0,16},{8,24},{16,0},{24,8},{1,17},{9,25},{17,1},{25,9},{2,18},{10... | collective-permute-start | bytes 786440 | tf_op jit(solution)/shard_map/ppermute | solution.py:348
  41.2 14.9 %collective-permute-start.12 = (bf16[512,256]{1,0:T(8,128)(2,1)S(1)}, bf16[512,256]{1,0:T(8,128)(2,1)S(1)}, u32[]{:S(2)}, u32[]{:S(2)}) collective-permute-start(bf16[512,256]{1,0:T(8,128)(2,1)S(1)} %project_kv.1.refs_0_), channel_id=1, source_target_pairs={{0,4},{1,5},{2,6},{3,7},{4,0},{5,1},{6,2},{7,3},{8,12},{9,13},{10,... | collective-permute-start | bytes 786440 | tf_op jit(solution)/shard_map/ppermute | solution.py:351
  47.4 8.8 %copy-start.1 = (s32[1,2,16]{2,1,0:T(2,128)S(1)}, s32[1,2,16]{2,1,0:T(2,128)}, u32[]{:S(2)}) copy-start(s32[1,2,16]{2,1,0:T(2,128)} %table.3) | copy-start | bytes 388
  47.4 9.8 %collective-permute-start.18 = (bf16[256,512]{1,0:T(8,128)(2,1)S(1)}, bf16[256,512]{1,0:T(8,128)(2,1)S(1)}, u32[]{:S(2)}, u32[]{:S(2)}) collective-permute-start(bf16[256,512]{1,0:T(8,128)(2,1)S(1)} %collective-permute-done.17.refs_5_), channel_id=1, source_target_pairs={{0,8},{8,0},{16,24},{24,16},{1,9},{9,1},{17,25},{25,17},{2,10},{10... | collective-permute-start | bytes 786440 | tf_op jit(solution)/shard_map/ppermute | solution.py:348
  48.9 8.4 %collective-permute-start.19 = (bf16[256,512]{1,0:T(8,128)(2,1)S(1)}, bf16[256,512]{1,0:T(8,128)(2,1)S(1)}, u32[]{:S(2)}, u32[]{:S(2)}) collective-permute-start(bf16[256,512]{1,0:T(8,128)(2,1)S(1)} %get-tuple-element.65), channel_id=1, source_target_pairs={{0,16},{8,24},{16,0},{24,8},{1,17},{9,25},{17,1},{25,9},{2,18},{10... | collective-permute-start | bytes 786440 | tf_op jit(solution)/shard_map/ppermute | solution.py:348
  50.0 9.5 %collective-permute-start.14 = (bf16[512,256]{1,0:T(8,128)(2,1)S(1)}, bf16[512,256]{1,0:T(8,128)(2,1)S(1)}, u32[]{:S(2)}, u32[]{:S(2)}) collective-permute-start(bf16[512,256]{1,0:T(8,128)(2,1)S(1)} %project_kv.1.refs_0_), channel_id=1, source_target_pairs={{0,1},{1,0},{2,3},{3,2},{4,5},{5,4},{6,7},{7,6},{8,9},{9,8},{10,11... | collective-permute-start | bytes 786440 | tf_op jit(solution)/shard_map/ppermute | solution.py:345
  57.1 0.7 copy-start.4
  57.2 8.9 %collective-permute-start.13 = (bf16[8,64,256]{2,1,0:T(8,128)(2,1)S(1)}, bf16[8,64,256]{2,1,0:T(8,128)(2,1)S(1)}, u32[]{:S(2)}, u32[]{:S(2)}) collective-permute-start(bf16[8,64,256]{2,1,0:T(8,128)(2,1)S(1)} %away.1), channel_id=1, source_target_pairs={{0,2},{1,3},{2,0},{3,1},{4,6},{5,7},{6,4},{7,5},{8,10},{9,11},{10,... | collective-permute-start | bytes 786440 | tf_op jit(solution)/shard_map/ppermute | solution.py:345
  57.3 2.2 %collective-permute-start.15 = (bf16[512,256]{1,0:T(8,128)(2,1)S(1)}, bf16[512,256]{1,0:T(8,128)(2,1)S(1)}, u32[]{:S(2)}, u32[]{:S(2)}) collective-permute-start(bf16[512,256]{1,0:T(8,128)(2,1)S(1)} %collective-permute-done.12.refs_1_), channel_id=1, source_target_pairs={{0,1},{1,0},{2,3},{3,2},{4,5},{5,4},{6,7},{7,6},{8,9},{9,8},{10,11... | collective-permute-start | bytes 786440 | tf_op jit(solution)/shard_map/ppermute | solution.py:345
  59.4 1.6 %collective-permute-start.20 = (bf16[256,512]{1,0:T(8,128)(2,1)S(1)}, bf16[256,512]{1,0:T(8,128)(2,1)S(1)}, u32[]{:S(2)}, u32[]{:S(2)}) collective-permute-start(bf16[256,512]{1,0:T(8,128)(2,1)S(1)} %get-tuple-element.69), channel_id=1, source_target_pairs={{0,1},{1,0},{2,3},{3,2},{4,5},{5,4},{6,7},{7,6},{8,9},{9,8},{10,11... | collective-permute-start | bytes 786440 | tf_op jit(solution)/shard_map/ppermute | solution.py:345
  62.7 8.5 %collective-permute-start.21 = (bf16[128,1024]{1,0:T(8,128)(2,1)S(1)}, bf16[128,1024]{1,0:T(8,128)(2,1)S(1)}, u32[]{:S(2)}, u32[]{:S(2)}) collective-permute-start(bf16[128,1024]{1,0:T(8,128)(2,1)S(1)} %attend.3), channel_id=1, source_target_pairs={{0,2},{1,3},{2,0},{3,1},{4,6},{5,7},{6,4},{7,5},{8,10},{9,11},{10,... | collective-permute-start | bytes 786440 | tf_op jit(solution)/shard_map/ppermute | solution.py:345
  66.1 5.1 %collective-permute-start.22 = (bf16[8,64,256]{2,1,0:T(8,128)(2,1)S(1)}, bf16[8,64,256]{2,1,0:T(8,128)(2,1)S(1)}, u32[]{:S(2)}, u32[]{:S(2)}) collective-permute-start(bf16[8,64,256]{2,1,0:T(8,128)(2,1)S(1)} %collective-permute-done.13.got), channel_id=1, source_target_pairs={{0,1},{1,0},{2,3},{3,2},{4,5},{5,4},{6,7},{7,6},{8,9},{9,8},{10,11... | collective-permute-start | bytes 786440 | tf_op jit(solution)/shard_map/ppermute | solution.py:345
